TPU v7x, 32 devices: a whole 2x2x4 slice. The times are simulated.
32 devices in a mesh: dp: 8 (over z, y), mp: 4 (over x, core).
Axes of the slice: x: 2, y: 2, z: 4, core: 2. Of those that a mesh axis runs over, the one named last changes fastest.
Arguments:
- patches: bfloat16 [8192, 1024], P('dp')
- cotangent: bfloat16 [8192, 512], P('dp')
- item_lengths: int32 [8, 8], P('dp'), may hold values from 0 to 784, as said below
- enc_master: float32 [1024, 12800], P('dp', 'mp')
- dec_master: float32 [512, 6144], P('dp', 'mp')
- enc_norms: float32 [4, 1024], P(None, 'dp')
- dec_norms: float32 [4, 512], P(None, 'dp')
- enc_moment: float32 [1024, 12800], P('dp', 'mp')
- dec_moment: float32 [512, 6144], P('dp', 'mp')
- enc_norm_moment: float32 [4, 1024], P(None, 'dp')
- dec_norm_moment: float32 [4, 512], P(None, 'dp')
Outputs:
- block_out: float32 [8192, 512], P('dp')
- input_grad: float32 [8192, 1024], P('dp')
- enc_grad: float32 [1024, 12800], P('dp', 'mp')
- dec_grad: float32 [512, 6144], P('dp', 'mp')
- enc_norm_grad: float32 [4, 1024], P(None, 'dp')
- dec_norm_grad: float32 [4, 512], P(None, 'dp')
- dec_shift_grad: float32 [512], P('dp')
- enc_moment_new: float32 [1024, 12800], P('dp', 'mp')
- dec_moment_new: float32 [512, 6144], P('dp', 'mp')
- enc_norm_moment_new: float32 [4, 1024], P(None, 'dp')
- dec_norm_moment_new: float32 [4, 512], P(None, 'dp')
- enc_master_new: float32 [1024, 12800], P('dp', 'mp')
- dec_master_new: float32 [512, 6144], P('dp', 'mp')
- enc_norms_new: float32 [4, 1024], P(None, 'dp')
- dec_norms_new: float32 [4, 512], P(None, 'dp')
- enc_copy: bfloat16 [1024, 12800], P('dp', 'mp')
- dec_copy: bfloat16 [512, 6144], P('dp', 'mp')
- enc_norms_copy: bfloat16 [4, 1024], P(None, 'dp')
- dec_norms_copy: bfloat16 [4, 512], P(None, 'dp')
- grad_norm: float32 [], replicated
Inputs may be any that keep to these rules, and one draw needn't show every extreme that they name: `item_lengths`: row r lists the items placed on index r of dp: each entry is 64, 196, 784 or 0, the zeros after all nonzero entries, and a row sums to at most 1024; the last row always holds an item of 784 patches.
All inputs are finite; a program needn't handle non-finite values.
Results may differ from a plain program's by a relative error of at most 0.029.
Values may be sent and summed in bfloat16 or wider, within the bound.
No kernel may reach another device: no remote copies, remote signals or barrier semaphores. Data moves between devices by JAX's collectives and lax.ppermute only.
A program may use at most 192 MiB of HBM per device.

v0:
```python
import math

import jax
import jax.numpy as jnp
from jax import lax
from jax.sharding import PartitionSpec as P

D = 1024
HD = 64
FF = 4096
DD = 512
DHD = 32
DFF = 2048
NS_STEPS = 5


highest = lax.Precision.HIGHEST
ln_eps = 1e-06
masked_score = -1e30
newton_first = 3.4445
newton_second = -4.775
newton_third = 2.0315
momentum_keep = 0.5
clip_bound = 100.0
rate_enc = 0.2
rate_dec = 0.3
rate_norm = 1.0
decay_rate = 0.01


def shortened(array):

    def short(part):
        return part.astype(jnp.bfloat16) if part.dtype == jnp.float32 else part

    return jax.tree.map(short, array)


def broadcast(value, axis, source):
    kept = jnp.where(lax.axis_index(axis) == source, value, 0).astype(value.dtype)
    return lax.psum(kept, axis)


def layer_norm(values, gain_row, shift_row):
    center = values - jnp.mean(values, axis=-1, keepdims=True)
    spread = jnp.mean(center * center, axis=-1, keepdims=True)
    return center * lax.rsqrt(spread + ln_eps) * gain_row + shift_row


def exact_gelu(hidden_in):
    return jax.nn.gelu(hidden_in, approximate=False)


def model_sum(partial_term):
    share = lax.psum_scatter(
        partial_term.astype(jnp.bfloat16), "mp", scatter_dimension=0, tiled=True
    ).astype(jnp.float32)
    return lax.all_gather(share.astype(jnp.bfloat16), "mp", axis=0, tiled=True).astype(share.dtype)


def model_back(partial_term):
    share = lax.psum_scatter(
        partial_term.astype(jnp.bfloat16), "mp", scatter_dimension=0, tiled=True
    ).astype(jnp.float32)
    return lax.all_gather(share.astype(jnp.bfloat16), "mp", axis=0, tiled=True).astype(share.dtype)


def segments_of(lengths, row_count):
    item_ends = jnp.cumsum(lengths)
    position = jnp.arange(row_count, dtype=jnp.int32)
    segment = jnp.sum((position[:, None] >= item_ends[None, :]).astype(jnp.int32), axis=1)
    live_mask = (position < item_ends[-1]).astype(jnp.float32)
    return (segment, live_mask)


def split_columns(whole_cols, widths):
    pieces = []
    start_col = 0
    for piece_width in widths:
        pieces.append(whole_cols[:, start_col : start_col + piece_width])
        start_col += piece_width
    return pieces


def attend_forward(query_part, key_part, value_part, segment, head_count, head_width, block_rows):
    row_count = query_part.shape[0]
    blocks = row_count // block_rows
    score_scale = head_width ** (-0.5)
    key_heads = key_part.reshape(row_count, head_count, head_width)
    value_heads = value_part.reshape(row_count, head_count, head_width)
    query_blocks = query_part.reshape(blocks, block_rows, head_count, head_width)
    segment_blocks = segment.reshape(blocks, block_rows)

    def attend_block(block_inputs):
        query_block, segment_block = block_inputs
        scores = (
            jnp.einsum("qhd,khd->hqk", query_block, key_heads, preferred_element_type=jnp.float32)
            * score_scale
        )
        scores = jnp.where((segment_block[:, None] == segment[None, :])[None], scores, masked_score)
        row_max = jnp.max(scores, axis=-1, keepdims=True)
        shifted = jnp.exp(scores - row_max)
        row_total = jnp.sum(shifted, axis=-1, keepdims=True)
        attention = (shifted / row_total).astype(jnp.bfloat16)
        block_out = jnp.einsum(
            "hqk,khd->qhd", attention, value_heads, preferred_element_type=jnp.float32
        )
        return (block_out.astype(jnp.bfloat16), row_max + jnp.log(row_total))

    block_outs, logsum = lax.map(attend_block, (query_blocks, segment_blocks))
    return (block_outs.reshape(row_count, head_count * head_width), logsum)


def attend_backward(
    heads_grad,
    query_part,
    key_part,
    value_part,
    segment,
    logsum,
    head_count,
    head_width,
    block_rows,
):
    row_count = query_part.shape[0]
    blocks = row_count // block_rows
    score_scale = head_width ** (-0.5)
    key_heads = key_part.reshape(row_count, head_count, head_width)
    value_heads = value_part.reshape(row_count, head_count, head_width)
    query_blocks = query_part.reshape(blocks, block_rows, head_count, head_width)
    grad_blocks = heads_grad.reshape(blocks, block_rows, head_count, head_width)
    segment_blocks = segment.reshape(blocks, block_rows)

    def backward_block(carried, block_inputs):
        key_total, value_total = carried
        query_block, grad_block, segment_block, logsum_block = block_inputs
        scores = (
            jnp.einsum("qhd,khd->hqk", query_block, key_heads, preferred_element_type=jnp.float32)
            * score_scale
        )
        scores = jnp.where((segment_block[:, None] == segment[None, :])[None], scores, masked_score)
        attention = jnp.exp(scores - logsum_block)
        grad_soft = jnp.einsum(
            "qhd,khd->hqk", grad_block, value_heads, preferred_element_type=jnp.float32
        )
        row_dot = jnp.sum(attention * grad_soft, axis=-1, keepdims=True)
        score_grad = (attention * (grad_soft - row_dot)).astype(jnp.bfloat16)
        query_grad = (
            jnp.einsum("hqk,khd->qhd", score_grad, key_heads, preferred_element_type=jnp.float32)
            * score_scale
        )
        key_total = (
            key_total
            + jnp.einsum(
                "hqk,qhd->khd", score_grad, query_block, preferred_element_type=jnp.float32
            )
            * score_scale
        )
        value_total = value_total + jnp.einsum(
            "hqk,qhd->khd",
            attention.astype(jnp.bfloat16),
            grad_block,
            preferred_element_type=jnp.float32,
        )
        return ((key_total, value_total), query_grad.astype(jnp.bfloat16))

    zeros = jnp.zeros((row_count, head_count, head_width), jnp.float32)
    (key_total, value_total), query_grads = lax.scan(
        backward_block, (zeros, zeros), (query_blocks, grad_blocks, segment_blocks, logsum)
    )
    return (
        query_grads.reshape(row_count, head_count * head_width),
        key_total.reshape(row_count, head_count * head_width).astype(jnp.bfloat16),
        value_total.reshape(row_count, head_count * head_width).astype(jnp.bfloat16),
    )


def block_forward(values, segment, pieces, norm_values, head_width, block_rows):
    qkv_proj, out_proj, up_proj, down_proj = pieces
    inner_width = out_proj.shape[1]
    head_count = inner_width // head_width
    normed_half = layer_norm(values, norm_values[0], norm_values[1]).astype(jnp.bfloat16)
    mixed_all = jnp.dot(normed_half, qkv_proj, preferred_element_type=jnp.float32)
    query_part = mixed_all[:, :inner_width].astype(jnp.bfloat16)
    key_part = mixed_all[:, inner_width : 2 * inner_width].astype(jnp.bfloat16)
    value_part = mixed_all[:, 2 * inner_width :].astype(jnp.bfloat16)
    heads_out, logsum = attend_forward(
        query_part, key_part, value_part, segment, head_count, head_width, block_rows
    )
    middle = values + model_sum(
        jnp.einsum("ti,di->td", heads_out, out_proj, preferred_element_type=jnp.float32)
    )
    normed_two = layer_norm(middle, norm_values[2], norm_values[3]).astype(jnp.bfloat16)
    hidden = jnp.dot(normed_two, up_proj, preferred_element_type=jnp.float32)
    activated = exact_gelu(hidden).astype(jnp.bfloat16)
    output = middle + model_sum(
        jnp.einsum("tf,df->td", activated, down_proj, preferred_element_type=jnp.float32)
    )
    return (
        output,
        (
            normed_half,
            query_part,
            key_part,
            value_part,
            heads_out,
            logsum,
            middle,
            normed_two,
            hidden,
            activated,
        ),
    )


def block_backward(upstream, saved, values, pieces, norm_values, segment, head_width, block_rows):
    (
        normed_half,
        query_part,
        key_part,
        value_part,
        heads_out,
        logsum,
        middle,
        normed_two,
        hidden,
        activated,
    ) = saved
    qkv_proj, out_proj, up_proj, down_proj = pieces
    inner_width = out_proj.shape[1]
    head_count = inner_width // head_width
    upstream_half = upstream.astype(jnp.bfloat16)
    down_grad = jnp.einsum(
        "td,tf->df", upstream_half, activated, preferred_element_type=jnp.float32
    )
    act_grad = jnp.einsum("td,df->tf", upstream_half, down_proj, preferred_element_type=jnp.float32)
    gelu_pull = jax.vjp(exact_gelu, hidden)[1]
    hidden_half = gelu_pull(act_grad)[0].astype(jnp.bfloat16)
    up_grad = jnp.einsum("td,tf->df", normed_two, hidden_half, preferred_element_type=jnp.float32)
    normed_two_grad = model_back(
        jnp.einsum("tf,df->td", hidden_half, up_proj, preferred_element_type=jnp.float32)
    )
    second_pull = jax.vjp(layer_norm, middle, norm_values[2], norm_values[3])[1]
    middle_part, gain_two, shift_two = second_pull(normed_two_grad)
    middle_grad = upstream + middle_part
    middle_half = middle_grad.astype(jnp.bfloat16)
    out_grad = jnp.einsum("td,ti->di", middle_half, heads_out, preferred_element_type=jnp.float32)
    heads_grad = jnp.einsum(
        "td,di->ti", middle_half, out_proj, preferred_element_type=jnp.float32
    ).astype(jnp.bfloat16)
    query_grad, key_grad, value_grad = attend_backward(
        heads_grad,
        query_part,
        key_part,
        value_part,
        segment,
        logsum,
        head_count,
        head_width,
        block_rows,
    )
    mixed_grad = jnp.concatenate([query_grad, key_grad, value_grad], axis=1)
    qkv_grad = jnp.einsum("td,tf->df", normed_half, mixed_grad, preferred_element_type=jnp.float32)
    normed_grad = model_back(
        jnp.einsum("tf,df->td", mixed_grad, qkv_proj, preferred_element_type=jnp.float32)
    )
    first_pull = jax.vjp(layer_norm, values, norm_values[0], norm_values[1])[1]
    values_part, gain_one, shift_one = first_pull(normed_grad)
    return (
        middle_grad + values_part,
        [qkv_grad, out_grad, up_grad, down_grad],
        jnp.stack([gain_one, shift_one, gain_two, shift_two]),
    )


def newton_apply(iterate, gram):
    mix_matrix = newton_second * gram + newton_third * jnp.dot(gram, gram, precision=highest)
    return newton_first * iterate + jnp.dot(mix_matrix, iterate, precision=highest)


def newton(enc_iterate, dec_iterate):
    for newton_step in range(NS_STEPS):
        enc_part, dec_part = (
            lax.psum_scatter(
                jnp.dot(enc_iterate, enc_iterate.T, precision=highest).astype(jnp.bfloat16),
                "mp",
                scatter_dimension=0,
                tiled=True,
            ).astype(jnp.float32),
            lax.psum_scatter(
                jnp.dot(dec_iterate, dec_iterate.T, precision=highest).astype(jnp.bfloat16),
                "mp",
                scatter_dimension=0,
                tiled=True,
            ).astype(jnp.float32),
        )
        enc_gram, dec_gram = (
            lax.all_gather(enc_part.astype(jnp.bfloat16), "mp", axis=0, tiled=True).astype(
                enc_part.dtype
            ),
            lax.all_gather(dec_part.astype(jnp.bfloat16), "mp", axis=0, tiled=True).astype(
                dec_part.dtype
            ),
        )
        if newton_step == 0:
            enc_size = jnp.sqrt(jnp.trace(enc_gram)) + 1e-07
            dec_size = jnp.sqrt(jnp.trace(dec_gram)) + 1e-07
            enc_iterate = enc_iterate / enc_size
            dec_iterate = dec_iterate / dec_size
            enc_gram = enc_gram / (enc_size * enc_size)
            dec_gram = dec_gram / (dec_size * dec_size)
        enc_iterate = newton_apply(enc_iterate, enc_gram)
        dec_iterate = newton_apply(dec_iterate, dec_gram)
    return (enc_iterate, dec_iterate)


def own_slot(whole_rows, widths, owner_rank, slot_width):
    starts = []
    start_col = 0
    for piece_width in widths:
        starts.append(start_col)
        start_col += piece_width
    chosen = jnp.arange(len(widths), dtype=jnp.int32) == owner_rank
    first_col = jnp.sum(jnp.where(chosen, jnp.array(starts, jnp.int32), 0))
    live_width = jnp.sum(jnp.where(chosen, jnp.array(widths, jnp.int32), 0))
    padded = jnp.pad(whole_rows, ((0, 0), (0, slot_width)))
    slot_cols = lax.dynamic_slice_in_dim(padded, first_col, slot_width, 1)
    keep = jnp.arange(slot_width, dtype=jnp.int32)[None, :] < live_width
    return jnp.where(keep, slot_cols, 0.0)


def apply_step(master, ortho_rows, widths, model_width, rate, model_ranks):
    steps_all = [
        orthogonal * (0.2 * math.sqrt(max(model_width, piece_width * model_ranks)))
        for orthogonal, piece_width in zip(ortho_rows, widths)
    ]
    return master * (1.0 - rate * decay_rate) - rate * jnp.concatenate(steps_all, axis=1)


def local(
    patches,
    cotangent,
    item_lengths,
    enc_master,
    dec_master,
    enc_norms,
    dec_norms,
    enc_moment,
    dec_moment,
    enc_norm_moment,
    dec_norm_moment,
):
    model_ranks = lax.axis_size("mp")
    data_ranks = lax.axis_size("dp")
    enc_widths = [
        3 * D // model_ranks,
        D // model_ranks,
        FF // model_ranks,
        FF // model_ranks,
        DD // model_ranks,
    ]
    dec_widths = [3 * DD // model_ranks, DD // model_ranks, DFF // model_ranks, DFF // model_ranks]
    enc_low, dec_low, enc_norm_low, dec_norm_low = (
        lax.all_gather(enc_master.astype(jnp.bfloat16), "dp", axis=0, tiled=True),
        lax.all_gather(dec_master.astype(jnp.bfloat16), "dp", axis=0, tiled=True),
        lax.all_gather(enc_norms.astype(jnp.bfloat16), "dp", axis=1, tiled=True),
        lax.all_gather(dec_norms.astype(jnp.bfloat16), "dp", axis=1, tiled=True),
    )
    enc_pieces = split_columns(enc_low, enc_widths)
    dec_pieces = split_columns(dec_low, dec_widths)
    enc_norm_values = enc_norm_low.astype(jnp.float32)
    dec_norm_values = dec_norm_low.astype(jnp.float32)
    row_count = patches.shape[0]
    block_rows = min(512, row_count)
    segment, live_mask = segments_of(item_lengths[0], row_count)
    inputs = patches.astype(jnp.float32)
    encoded, enc_saved = block_forward(
        inputs, segment, enc_pieces[:4], enc_norm_values, HD, block_rows
    )
    encoded_half = encoded.astype(jnp.bfloat16)
    bridge = enc_pieces[4]
    bridged = jnp.dot(encoded_half, bridge, preferred_element_type=jnp.float32).astype(jnp.bfloat16)
    joined = lax.all_gather(bridged, "mp", axis=1, tiled=True)
    decoder_in = joined.astype(jnp.float32)
    decoded, dec_saved = block_forward(
        decoder_in, segment, dec_pieces, dec_norm_values, DHD, block_rows
    )
    upstream = cotangent.astype(jnp.float32) * live_mask[:, None]
    dec_in_grad, dec_grads, dec_norm_grads = block_backward(
        upstream, dec_saved, decoder_in, dec_pieces, dec_norm_values, segment, DHD, block_rows
    )
    share_width = bridge.shape[1]
    bridge_in_grad = lax.dynamic_slice_in_dim(
        dec_in_grad, lax.axis_index("mp") * share_width, share_width, 1
    ).astype(jnp.bfloat16)
    bridge_grad = jnp.einsum(
        "td,tf->df", encoded_half, bridge_in_grad, preferred_element_type=jnp.float32
    )
    encoded_grad = model_back(
        jnp.einsum("tf,df->td", bridge_in_grad, bridge, preferred_element_type=jnp.float32)
    )
    input_grad, enc_grads, enc_norm_grads = block_backward(
        encoded_grad, enc_saved, inputs, enc_pieces[:4], enc_norm_values, segment, HD, block_rows
    )
    enc_sum_rows, dec_sum_rows, enc_norm_rows, dec_norm_rows = (
        lax.psum_scatter(
            jnp.concatenate(enc_grads + [bridge_grad], axis=1),
            "dp",
            scatter_dimension=0,
            tiled=True,
        ),
        lax.psum_scatter(jnp.concatenate(dec_grads, axis=1), "dp", scatter_dimension=0, tiled=True),
        lax.psum_scatter(enc_norm_grads, "dp", scatter_dimension=1, tiled=True),
        lax.psum_scatter(dec_norm_grads, "dp", scatter_dimension=1, tiled=True),
    )
    local_sum = (
        jnp.sum(enc_sum_rows * enc_sum_rows)
        + jnp.sum(dec_sum_rows * dec_sum_rows)
        + (jnp.sum(enc_norm_rows * enc_norm_rows) + jnp.sum(dec_norm_rows * dec_norm_rows))
        / model_ranks
    )
    squares = lax.psum(local_sum, ("dp", "mp"))
    grad_norm = jnp.sqrt(squares)
    factor = clip_bound * lax.rsqrt(squares + 1e-06)
    enc_grad = enc_sum_rows * factor
    dec_grad = dec_sum_rows * factor
    enc_norm_grad = enc_norm_rows * factor
    dec_norm_grad = dec_norm_rows * factor
    dec_shift_grad = dec_norm_grad[3]
    enc_moment_new = momentum_keep * enc_moment + enc_grad
    dec_moment_new = momentum_keep * dec_moment + dec_grad
    enc_norm_moment_new = momentum_keep * enc_norm_moment + enc_norm_grad
    dec_norm_moment_new = momentum_keep * dec_norm_moment + dec_norm_grad
    enc_slot_width = max(enc_widths)
    dec_slot_width = max(dec_widths)
    enc_rows = enc_master.shape[0]
    dec_rows = dec_master.shape[0]
    first_dec = len(enc_widths)
    enc_whole, dec_whole = (
        lax.all_gather(enc_moment_new.astype(jnp.bfloat16), "dp", axis=0, tiled=True).astype(
            enc_moment_new.dtype
        ),
        lax.all_gather(dec_moment_new.astype(jnp.bfloat16), "dp", axis=0, tiled=True).astype(
            dec_moment_new.dtype
        ),
    )
    data_rank = lax.axis_index("dp")
    enc_orth, dec_orth = newton(
        own_slot(enc_whole, enc_widths, data_rank, enc_slot_width),
        own_slot(dec_whole, dec_widths, jnp.mod(data_rank - first_dec, data_ranks), dec_slot_width),
    )
    sources = [
        (enc_orth, matrix_index, enc_rows, piece_width)
        for matrix_index, piece_width in enumerate(enc_widths)
    ]
    sources = sources + [
        (dec_orth, (first_dec + matrix_index) % data_ranks, dec_rows, piece_width)
        for matrix_index, piece_width in enumerate(dec_widths)
    ]
    results = []
    for orthogonal, owner_root, own_rows, piece_width in sources:
        whole_rows = broadcast(shortened(orthogonal), "dp", owner_root).astype(orthogonal.dtype)
        results.append(
            lax.dynamic_slice_in_dim(whole_rows, data_rank * own_rows, own_rows, 0)[:, :piece_width]
        )
    enc_results = results[:first_dec]
    dec_results = results[first_dec:]
    enc_master_new = apply_step(enc_master, enc_results, enc_widths, D, rate_enc, model_ranks)
    dec_master_new = apply_step(dec_master, dec_results, dec_widths, DD, rate_dec, model_ranks)
    enc_norms_new = enc_norms - rate_norm * enc_norm_moment_new
    dec_norms_new = dec_norms - rate_norm * dec_norm_moment_new
    return (
        decoded,
        input_grad,
        enc_grad,
        dec_grad,
        enc_norm_grad,
        dec_norm_grad,
        dec_shift_grad,
        enc_moment_new,
        dec_moment_new,
        enc_norm_moment_new,
        dec_norm_moment_new,
        enc_master_new,
        dec_master_new,
        enc_norms_new,
        dec_norms_new,
        enc_master_new.astype(jnp.bfloat16),
        dec_master_new.astype(jnp.bfloat16),
        enc_norms_new.astype(jnp.bfloat16),
        dec_norms_new.astype(jnp.bfloat16),
        grad_norm,
    )


def solution(mesh):
    return jax.shard_map(
        local,
        mesh=mesh,
        in_specs=(
            P("dp", None),
            P("dp", None),
            P("dp", None),
            P("dp", "mp"),
            P("dp", "mp"),
            P(None, "dp"),
            P(None, "dp"),
            P("dp", "mp"),
            P("dp", "mp"),
            P(None, "dp"),
            P(None, "dp"),
        ),
        out_specs=(
            P("dp", None),
            P("dp", None),
            P("dp", "mp"),
            P("dp", "mp"),
            P(None, "dp"),
            P(None, "dp"),
            P("dp"),
            P("dp", "mp"),
            P("dp", "mp"),
            P(None, "dp"),
            P(None, "dp"),
            P("dp", "mp"),
            P("dp", "mp"),
            P(None, "dp"),
            P(None, "dp"),
            P("dp", "mp"),
            P("dp", "mp"),
            P(None, "dp"),
            P(None, "dp"),
            P(),
        ),
        check_vma=False,
    )
```

profile of v0, /device:TPU:0, one launch (start us, length us, event | category | flops | bytes accessed | tf_op | source)
XLA Modules:
  0.0 2457.7 jit_solution(5264142338597294741)
XLA Ops:
  11.9 22.5 all_gather.78
  36.1 79.7 %all-gather.21.cloned.1.call-done = bf16[1024,3200]{1,0:T(8,128)(2,1)} async-done(((bf16[128,3200]{1,0:T(8,128)(2,1)}), bf16[1024,3200]{1,0:T(8,128)(2,1)}) %all-gather.21.cloned.1.call-update) | async-done | bytes 6553616 | tf_op jit(solution)/shard_map/all_gather | solution.py:364
  149.2 29.7 %reduce-scatter.40.cloned.1.call-done = bf16[256,1024]{1,0:T(8,128)(2,1)} async-done(((bf16[1024,1024]{1,0:T(8,128)(2,1)}), bf16[256,1024]{1,0:T(8,128)(2,1)}) %reduce-scatter.40.cloned.1.call-update) | async-done | bytes 524304 | tf_op jit(solution)/shard_map/reduce_scatter | solution.py:55
  179.2 24.0 all-gather.23.cloned.1.call-done
  228.2 31.5 %reduce-scatter.42.cloned.1.call-done = bf16[256,1024]{1,0:T(8,128)(2,1)} async-done(((bf16[1024,1024]{1,0:T(8,128)(2,1)}), bf16[256,1024]{1,0:T(8,128)(2,1)}) %reduce-scatter.42.cloned.1.call-update) | async-done | bytes 524304 | tf_op jit(solution)/shard_map/reduce_scatter | solution.py:55
  259.8 24.0 all-gather.25.cloned.1.call-done
  312.7 38.9 %all-gather.29.cloned.1.call-done = bf16[512,1536]{1,0:T(8,128)(2,1)} async-done(((bf16[64,1536]{1,0:T(8,128)(2,1)}), bf16[512,1536]{1,0:T(8,128)(2,1)}) %all-gather.29.cloned.1.call-update) | async-done | bytes 1572880 | tf_op jit(solution)/shard_map/all_gather | solution.py:365
  376.4 23.8 reduce-scatter.44.cloned.1.call-done
  444.7 21.9 reduce-scatter.48.cloned.1.call-done
  466.7 28.0 %reduce-scatter.46.cloned.1.call-done = bf16[256,512]{1,0:T(8,128)(2,1)} async-done(((bf16[1024,512]{1,0:T(8,128)(2,1)}), bf16[256,512]{1,0:T(8,128)(2,1)}) %reduce-scatter.46.cloned.1.call-update) | async-done | bytes 262160 | tf_op jit(solution)/shard_map/reduce_scatter | solution.py:55
  537.9 41.0 %while.56 = (s32[]{:T(128)}, f32[1024,4,32]{0,2,1:T(8,128)S(1)}, f32[1024,4,32]{0,2,1:T(8,128)}, bf16[2,512,4,32]{1,3,2,0:T(8,128)(2,1)S(1)}, bf16[2,512,4,32]{1...) while((s32[]{:T(128)}, f32[1024,4,32]{0,2,1:T(8,128)S(1)}, ...), condition=%wide.region_27.28_spmd.clone, body=%wide.region_25.27_spmd.clone.sunk | while | flops 703854592 | bytes 152505584 | solution.py:168
  583.4 25.0 %reduce-scatter.50.cloned.1.call-done = bf16[256,512]{1,0:T(8,128)(2,1)} async-done(((bf16[1024,512]{1,0:T(8,128)(2,1)}), bf16[256,512]{1,0:T(8,128)(2,1)}) %reduce-scatter.50.cloned.1.call-update) | async-done | bytes 262160 | tf_op jit(solution)/shard_map/reduce_scatter | solution.py:62
  636.2 31.5 %reduce-scatter.52.cloned.1.call-done = bf16[256,1024]{1,0:T(8,128)(2,1)} async-done(((bf16[1024,1024]{1,0:T(8,128)(2,1)}), bf16[256,1024]{1,0:T(8,128)(2,1)}) %reduce-scatter.52.cloned.1.call-update) | async-done | bytes 524304 | tf_op jit(solution)/shard_map/reduce_scatter | solution.py:62
  667.8 24.0 all-gather.39.cloned.1.call-done
  706.7 31.5 %reduce-scatter.54.cloned.1.call-done = bf16[256,1024]{1,0:T(8,128)(2,1)} async-done(((bf16[1024,1024]{1,0:T(8,128)(2,1)}), bf16[256,1024]{1,0:T(8,128)(2,1)}) %reduce-scatter.54.cloned.1.call-update) | async-done | bytes 524304 | tf_op jit(solution)/shard_map/reduce_scatter | solution.py:62
  738.3 24.1 all-gather.41.cloned.1.call-done
  779.1 45.1 %while.57 = (s32[]{:T(128)}, f32[1024,4,64]{0,2,1:T(8,128)}, f32[1024,4,64]{0,2,1:T(8,128)}, bf16[2,512,4,64]{1,3,2,0:T(8,128)(2,1)}, bf16[2,512,4,64]{1,3,2,0:T...) while((s32[]{:T(128)}, f32[1024,4,64]{0,2,1:T(8,128)}, ...), condition=%wide.region_37.38_spmd.clone, body=%wide.region_35.37_spmd.clone.sunk | while | flops 1375729664 | bytes 145559344 | solution.py:168
  834.4 31.5 %reduce-scatter.56.cloned.1.call-done = bf16[256,1024]{1,0:T(8,128)(2,1)} async-done(((bf16[1024,1024]{1,0:T(8,128)(2,1)}), bf16[256,1024]{1,0:T(8,128)(2,1)}) %reduce-scatter.56.cloned.1.call-update) | async-done | bytes 524304 | tf_op jit(solution)/shard_map/reduce_scatter | solution.py:62
  911.2 44.5 %reduce-scatter.74.cloned.1.call-done = f32[64,4]{1,0:T(8,128)} async-done(((f32[512,4]{1,0:T(8,128)}), f32[64,4]{1,0:T(8,128)}) %reduce-scatter.74.cloned.1.call-update) | async-done | bytes 1040
  957.1 76.0 %reduce-scatter.70.cloned.1.call-done = f32[64,1536]{1,0:T(8,128)} async-done(((f32[512,1536]{1,0:T(8,128)}), f32[64,1536]{1,0:T(8,128)}) %reduce-scatter.70.cloned.1.call-update) | async-done | bytes 393232
  1035.2 63.1 %reduce-scatter.72.cloned.1.call-done = f32[128,4]{1,0:T(8,128)} async-done(((f32[1024,4]{1,0:T(8,128)}), f32[128,4]{1,0:T(8,128)}) %reduce-scatter.72.cloned.1.call-update) | async-done | bytes 2064
  1101.2 214.4 %reduce-scatter.58.cloned.1.call-done = f32[128,3200]{1,0:T(8,128)} async-done(((f32[1024,3200]{1,0:T(8,128)}), f32[128,3200]{1,0:T(8,128)}) %reduce-scatter.58.cloned.1.call-update) | async-done | bytes 1638416 | tf_op jit(solution)/shard_map/reduce_scatter | solution.py:406
  1319.4 39.4 %psum.70 = f32[]{:T(128)} all-reduce(f32[]{:T(128)S(6)} %add.376), channel_id=1, replica_groups=mesh['dp'=8,'mp'=4] {'dp','mp'}, use_global_device_ids=true, to_apply=%region_57.58 | all-reduce | flops 1 | bytes 8 | tf_op jit(solution)/shard_map/psum | solution.py:422
  1367.0 99.1 %all-gather.45.cloned.1.call-done = bf16[1024,3200]{1,0:T(8,128)(2,1)} async-done(((bf16[128,3200]{1,0:T(8,128)(2,1)}), bf16[1024,3200]{1,0:T(8,128)(2,1)}) %all-gather.45.cloned.1.call-update) | async-done | bytes 6553616 | tf_op jit(solution)/shard_map/all_gather | solution.py:440
  1484.5 29.7 %reduce-scatter.60.cloned.1.call-done = bf16[256,1024]{1,0:T(8,128)(2,1)} async-done(((bf16[1024,1024]{1,0:T(8,128)(2,1)}), bf16[256,1024]{1,0:T(8,128)(2,1)}) %reduce-scatter.60.cloned.1.call-update) | async-done | bytes 524304 | tf_op jit(solution)/shard_map/reduce_scatter | solution.py:284
  1514.4 24.0 all-gather.47.cloned.1.call-done
  1594.6 31.5 %reduce-scatter.62.cloned.1.call-done = bf16[256,1024]{1,0:T(8,128)(2,1)} async-done(((bf16[1024,1024]{1,0:T(8,128)(2,1)}), bf16[256,1024]{1,0:T(8,128)(2,1)}) %reduce-scatter.62.cloned.1.call-update) | async-done | bytes 524304 | tf_op jit(solution)/shard_map/reduce_scatter | solution.py:284
  1701.5 28.5 %reduce-scatter.64.cloned.1.call-done = bf16[256,1024]{1,0:T(8,128)(2,1)} async-done(((bf16[1024,1024]{1,0:T(8,128)(2,1)}), bf16[256,1024]{1,0:T(8,128)(2,1)}) %reduce-scatter.64.cloned.1.call-update) | async-done | bytes 524304 | tf_op jit(solution)/shard_map/reduce_scatter | solution.py:284
  1730.1 24.7 %reduce-scatter.76.cloned.1.call-done = bf16[128,512]{1,0:T(8,128)(2,1)} async-done(((bf16[512,512]{1,0:T(8,128)(2,1)}), bf16[128,512]{1,0:T(8,128)(2,1)}) %reduce-scatter.76.cloned.1.call-update) | async-done | bytes 131088 | tf_op jit(solution)/shard_map/reduce_scatter | solution.py:290
  1846.4 24.0 reduce-scatter.80.cloned.1.call-done
  1962.3 24.2 reduce-scatter.84.cloned.1.call-done
  2044.5 394.2 %all-reduce.5.cloned.1.call-done = (bf16[1024,1024]{1,0:T(8,128)(2,1)}, bf16[1024,1024]{1,0:T(8,128)(2,1)}, bf16[1024,1024]{1,0:T(8,128)(2,1)}, bf16[1024,1024]{...) async-done(((bf16[1024,1024]{1,0:T(8,128)(2,1)}, ...) | async-done | bytes 12582928 | tf_op jit(solution)/shard_map/psum | solution.py:41
  (620 shorter events, 856.3 us)
Async XLA Ops:
  7.2 108.6 %all-gather.21.cloned.1.call-start = ((), (), s32[]{:S(2)}) async-start(), calls=%async_computation.23 | async-start | bytes 7372800 | tf_op jit(solution)/shard_map/all_gather | solution.py:364
  9.8 169.1 %reduce-scatter.40.cloned.1.call-start = ((), (), s32[]{:S(2)}) async-start(), calls=%async_computation.24 | async-start | bytes 2621440 | tf_op jit(solution)/shard_map/reduce_scatter | solution.py:55
  178.9 80.8 %reduce-scatter.42.cloned.1.call-start = ((), (), s32[]{:S(2)}) async-start(), calls=%async_computation.26 | async-start | bytes 2621440 | tf_op jit(solution)/shard_map/reduce_scatter | solution.py:55
  287.6 64.0 %all-gather.29.cloned.1.call-start = ((), (), s32[]{:S(2)}) async-start(), calls=%async_computation.29 | async-start | bytes 1769472 | tf_op jit(solution)/shard_map/all_gather | solution.py:365
  288.4 111.9 %reduce-scatter.44.cloned.1.call-start = ((), (), s32[]{:S(2)}) async-start(), calls=%async_computation.30 | async-start | bytes 1310720 | tf_op jit(solution)/shard_map/reduce_scatter | solution.py:55
  400.3 66.3 %reduce-scatter.48.cloned.1.call-start = ((), (), s32[]{:S(2)}) async-start(), calls=%async_computation.34 | async-start | bytes 1310720 | tf_op jit(solution)/shard_map/reduce_scatter | solution.py:62
  444.7 68.2 %all-gather.35.cloned.1.call-start = ((), (), s32[]{:S(2)}) async-start(), calls=%async_computation.35 | async-start | bytes 1310720 | tf_op jit(solution)/shard_map/all_gather | solution.py:65
  466.6 64.7 %all-gather.33.cloned.1.call-start = ((), (), s32[]{:S(2)}) async-start(), calls=%async_computation.33 | async-start | bytes 1310720 | tf_op jit(solution)/shard_map/all_gather | solution.py:58
  494.7 113.7 %reduce-scatter.50.cloned.1.call-start = ((), (), s32[]{:S(2)}) async-start(), calls=%async_computation.36 | async-start | bytes 1310720 | tf_op jit(solution)/shard_map/reduce_scatter | solution.py:62
  608.4 59.3 %reduce-scatter.52.cloned.1.call-start = ((), (), s32[]{:S(2)}) async-start(), calls=%async_computation.38 | async-start | bytes 2621440 | tf_op jit(solution)/shard_map/reduce_scatter | solution.py:62
  667.7 70.5 %reduce-scatter.54.cloned.1.call-start = ((), (), s32[]{:S(2)}) async-start(), calls=%async_computation.40 | async-start | bytes 2621440 | tf_op jit(solution)/shard_map/reduce_scatter | solution.py:62
  738.2 127.7 %reduce-scatter.56.cloned.1.call-start = ((), (), s32[]{:S(2)}) async-start(), calls=%async_computation.42 | async-start | bytes 2621440 | tf_op jit(solution)/shard_map/reduce_scatter | solution.py:62
  834.3 65.3 %all-gather.43.cloned.1.call-start = ((), (), s32[]{:S(2)}) async-start(), calls=%async_computation.43 | async-start | bytes 2621440 | tf_op jit(solution)/shard_map/all_gather | solution.py:65
  866.0 89.7 %reduce-scatter.74.cloned.1.call-start = ((), (), s32[]{:S(2)}) async-start(), calls=%async_computation.59 | async-start | bytes 294912
  874.5 158.7 %reduce-scatter.70.cloned.1.call-start = ((), (), s32[]{:S(2)}) async-start(), calls=%async_computation.57 | async-start | bytes 3538944
  882.2 216.1 %reduce-scatter.72.cloned.1.call-start = ((), (), s32[]{:S(2)}) async-start(), calls=%async_computation.58 | async-start | bytes 589824
  906.1 409.5 %reduce-scatter.58.cloned.1.call-start = ((), (), s32[]{:S(2)}) async-start(), calls=%async_computation.44 | async-start | bytes 14745600 | tf_op jit(solution)/shard_map/reduce_scatter | solution.py:406
  910.7 555.4 %all-gather.45.cloned.1.call-start = ((), (), s32[]{:S(2)}) async-start(), calls=%async_computation.45 | async-start | bytes 7372800 | tf_op jit(solution)/shard_map/all_gather | solution.py:440
  1363.6 150.6 %reduce-scatter.60.cloned.1.call-start = ((), (), s32[]{:S(2)}) async-start(), calls=%async_computation.46 | async-start | bytes 2621440 | tf_op jit(solution)/shard_map/reduce_scatter | solution.py:284
  1514.2 111.9 %reduce-scatter.62.cloned.1.call-start = ((), (), s32[]{:S(2)}) async-start(), calls=%async_computation.48 | async-start | bytes 2621440 | tf_op jit(solution)/shard_map/reduce_scatter | solution.py:284
  1626.2 71.0 %all-gather.57.cloned.1.call-start = ((), (), s32[]{:S(2)}) async-start(), calls=%async_computation.56 | async-start | bytes 1769472 | tf_op jit(solution)/shard_map/all_gather | solution.py:443
  1630.7 99.3 %reduce-scatter.64.cloned.1.call-start = ((), (), s32[]{:S(2)}) async-start(), calls=%async_computation.50 | async-start | bytes 2621440 | tf_op jit(solution)/shard_map/reduce_scatter | solution.py:284
  1686.3 68.5 %reduce-scatter.76.cloned.1.call-start = ((), (), s32[]{:S(2)}) async-start(), calls=%async_computation.60 | async-start | bytes 655360 | tf_op jit(solution)/shard_map/reduce_scatter | solution.py:290
  1701.5 77.5 %all-gather.51.cloned.1.call-start = ((), (), s32[]{:S(2)}) async-start(), calls=%async_computation.51 | async-start | bytes 2621440 | tf_op jit(solution)/shard_map/all_gather | solution.py:298
  1730.0 84.8 %reduce-scatter.78.cloned.1.call-start = ((), (), s32[]{:S(2)}) async-start(), calls=%async_computation.61 | async-start | bytes 655360 | tf_op jit(solution)/shard_map/reduce_scatter | solution.py:290
  1769.9 76.4 %reduce-scatter.66.cloned.1.call-start = ((), (), s32[]{:S(2)}) async-start(), calls=%async_computation.52 | async-start | bytes 2621440 | tf_op jit(solution)/shard_map/reduce_scatter | solution.py:284
  1828.7 66.0 %all-gather.53.cloned.1.call-start = ((), (), s32[]{:S(2)}) async-start(), calls=%async_computation.53 | async-start | bytes 2621440 | tf_op jit(solution)/shard_map/all_gather | solution.py:298
  1846.4 84.2 %reduce-scatter.82.cloned.1.call-start = ((), (), s32[]{:S(2)}) async-start(), calls=%async_computation.63 | async-start | bytes 655360 | tf_op jit(solution)/shard_map/reduce_scatter | solution.py:290
  1884.1 78.1 %reduce-scatter.68.cloned.1.call-start = ((), (), s32[]{:S(2)}) async-start(), calls=%async_computation.54 | async-start | bytes 2621440 | tf_op jit(solution)/shard_map/reduce_scatter | solution.py:284
  1930.6 55.9 %reduce-scatter.84.cloned.1.call-start = ((), (), s32[]{:S(2)}) async-start(), calls=%async_computation.64 | async-start | bytes 655360 | tf_op jit(solution)/shard_map/reduce_scatter | solution.py:290
  1944.0 66.6 %all-gather.55.cloned.1.call-start = ((), (), s32[]{:S(2)}) async-start(), calls=%async_computation.55 | async-start | bytes 2621440 | tf_op jit(solution)/shard_map/all_gather | solution.py:298
  1962.2 476.6 %all-reduce.5.cloned.1.call-start = ((), (), s32[]{:S(2)}) async-start(), calls=%async_computation.65 | async-start | bytes 25165824 | tf_op jit(solution)/shard_map/psum | solution.py:41
  (147 other events, 4199.1 us)
Sparse Core Ops, SparseCore 0:
  10.8 104.9 all-gather.20
  149.3 29.5 reduce-scatter.39
  180.5 22.5 all-gather.22
  228.2 31.4 reduce-scatter.41
  261.1 22.5 all-gather.24
  307.4 44.1 all-gather.28
  376.5 23.7 reduce-scatter.43
  441.7 24.8 reduce-scatter.47
  469.7 24.8 reduce-scatter.45
  583.5 24.8 reduce-scatter.49
  636.3 31.4 reduce-scatter.51
  669.2 22.5 all-gather.38
  706.7 31.4 reduce-scatter.53
  739.8 22.5 all-gather.40
  834.4 31.4 reduce-scatter.55
  867.5 22.5 all-gather.42
  894.4 61.2 reduce-scatter.73
  959.7 73.4 reduce-scatter.69
  1037.3 61.0 reduce-scatter.71
  1102.0 213.5 reduce-scatter.57
  1363.8 102.2 all-gather.44
  1484.6 29.5 reduce-scatter.59
  1515.8 22.5 all-gather.46
  1594.7 31.4 reduce-scatter.61
  1627.6 22.5 all-gather.48
  1653.0 44.1 all-gather.56
  1699.7 30.2 reduce-scatter.63
  1756.3 22.5 all-gather.50
  1814.9 31.4 reduce-scatter.65
  1930.7 31.4 reduce-scatter.67
  1988.1 22.5 all-gather.54
  2032.5 406.2 all-reduce.4
  (11 shorter events, 214.0 us)
where the time goes:
time: 2470 us; the launch traced here: 2460 us
  waiting for transfers between devices  1710 us (69%)
  matrix products  426 us (17%)
  blocking collectives  119 us (5%)
  other arithmetic  114 us (5%)
  local copies, waits for them, and re-layouts  57.3 us (2%)
  between operations  27.4 us (1%)
    psum x1, waiting for transfers between devices, broadcast(): return lax.psum(kept, axis)  394 us
    reduce_scatter x1, waiting for transfers between devices, local(): lax.psum_scatter(jnp.concatenate(enc_grads + [bridge_grad], axis=1), 'dp'...  214 us
    unnamed x46, waiting for transfers between devices  184 us
    reduce_scatter x5, waiting for transfers between devices, model_back(): lax.psum_scatter(partial_term.astype(jnp.bfloat16), 'mp', scatter_dimensi...  141 us
    reduce_scatter x5, waiting for transfers between devices, newton(): lax.psum_scatter(jnp.dot(enc_iterate, enc_iterate.T, precision=highest).a...  125 us
    reduce_scatter x4, waiting for transfers between devices, model_sum(): lax.psum_scatter(partial_term.astype(jnp.bfloat16), 'mp', scatter_dimensi...  113 us
    all_gather x1, waiting for transfers between devices, local(): lax.all_gather(enc_moment_new.astype(jnp.bfloat16), 'dp', axis=0, tiled=T...  99.1 us
    dot_general x10, matrix products, newton_apply(): jnp.dot(mix_matrix, iterate, precision=highest)  93.6 us
  transfers between devices with their start and end apart: 43, of which 39 were waited for; matrix products, arithmetic and copies ran while one was open for 9% of the time, Pallas kernels for 0%

commit v1 on v0

--- a/solution.py
+++ b/solution.py
@@ -34,11 +34,6 @@
         return part.astype(jnp.bfloat16) if part.dtype == jnp.float32 else part
 
     return jax.tree.map(short, array)
-
-
-def broadcast(value, axis, source):
-    kept = jnp.where(lax.axis_index(axis) == source, value, 0).astype(value.dtype)
-    return lax.psum(kept, axis)
 
 
 def layer_norm(values, gain_row, shift_row):
@@ -273,60 +268,60 @@
     )
 
 
-def newton_apply(iterate, gram):
-    mix_matrix = newton_second * gram + newton_third * jnp.dot(gram, gram, precision=highest)
-    return newton_first * iterate + jnp.dot(mix_matrix, iterate, precision=highest)
-
-
-def newton(enc_iterate, dec_iterate):
+def gram_newton(gram):
+    total = None
     for newton_step in range(NS_STEPS):
-        enc_part, dec_part = (
-            lax.psum_scatter(
-                jnp.dot(enc_iterate, enc_iterate.T, precision=highest).astype(jnp.bfloat16),
-                "mp",
-                scatter_dimension=0,
-                tiled=True,
-            ).astype(jnp.float32),
-            lax.psum_scatter(
-                jnp.dot(dec_iterate, dec_iterate.T, precision=highest).astype(jnp.bfloat16),
-                "mp",
-                scatter_dimension=0,
-                tiled=True,
-            ).astype(jnp.float32),
-        )
-        enc_gram, dec_gram = (
-            lax.all_gather(enc_part.astype(jnp.bfloat16), "mp", axis=0, tiled=True).astype(
-                enc_part.dtype
-            ),
-            lax.all_gather(dec_part.astype(jnp.bfloat16), "mp", axis=0, tiled=True).astype(
-                dec_part.dtype
-            ),
-        )
-        if newton_step == 0:
-            enc_size = jnp.sqrt(jnp.trace(enc_gram)) + 1e-07
-            dec_size = jnp.sqrt(jnp.trace(dec_gram)) + 1e-07
-            enc_iterate = enc_iterate / enc_size
-            dec_iterate = dec_iterate / dec_size
-            enc_gram = enc_gram / (enc_size * enc_size)
-            dec_gram = dec_gram / (dec_size * dec_size)
-        enc_iterate = newton_apply(enc_iterate, enc_gram)
-        dec_iterate = newton_apply(dec_iterate, dec_gram)
-    return (enc_iterate, dec_iterate)
-
-
-def own_slot(whole_rows, widths, owner_rank, slot_width):
-    starts = []
-    start_col = 0
-    for piece_width in widths:
-        starts.append(start_col)
-        start_col += piece_width
-    chosen = jnp.arange(len(widths), dtype=jnp.int32) == owner_rank
-    first_col = jnp.sum(jnp.where(chosen, jnp.array(starts, jnp.int32), 0))
-    live_width = jnp.sum(jnp.where(chosen, jnp.array(widths, jnp.int32), 0))
-    padded = jnp.pad(whole_rows, ((0, 0), (0, slot_width)))
-    slot_cols = lax.dynamic_slice_in_dim(padded, first_col, slot_width, 1)
-    keep = jnp.arange(slot_width, dtype=jnp.int32)[None, :] < live_width
-    return jnp.where(keep, slot_cols, 0.0)
+        gram_half = gram.astype(jnp.bfloat16)
+        square = jnp.dot(gram_half, gram_half, preferred_element_type=jnp.float32)
+        mix_matrix = newton_second * gram + newton_third * square
+        mix_half = mix_matrix.astype(jnp.bfloat16)
+        if total is None:
+            total = newton_first * jnp.eye(gram.shape[0], dtype=jnp.float32) + mix_matrix
+        else:
+            total = newton_first * total + jnp.dot(
+                mix_half, total.astype(jnp.bfloat16), preferred_element_type=jnp.float32
+            )
+        if newton_step < NS_STEPS - 1:
+            left = newton_first * gram + jnp.dot(
+                mix_half, gram_half, preferred_element_type=jnp.float32
+            )
+            gram = newton_first * left + jnp.dot(
+                left.astype(jnp.bfloat16), mix_half, preferred_element_type=jnp.float32
+            )
+    return total
+
+
+def slot_rows(enc_rows_half, dec_rows_half, enc_widths, dec_widths, slot_width, data_ranks):
+    enc_parts = split_columns(enc_rows_half, enc_widths)
+    dec_parts = split_columns(dec_rows_half, dec_widths)
+    half_width = slot_width // 2
+
+    def widened(part, width):
+        return jnp.pad(part, ((0, 0), (0, width - part.shape[1])))
+
+    slots = [widened(part, slot_width) for part in enc_parts]
+    for first in range(0, len(dec_parts), 2):
+        upper = jnp.pad(widened(dec_parts[first], half_width), ((0, 0), (0, half_width)))
+        lower = jnp.pad(widened(dec_parts[first + 1], half_width), ((0, 0), (half_width, 0)))
+        slots.append(jnp.concatenate([upper, lower], axis=0))
+    empty = jnp.zeros_like(slots[0])
+    return jnp.stack(slots + [empty] * (data_ranks - len(slots)))
+
+
+def unslot(rows_back, enc_widths, dec_widths, dec_rows):
+    slot_width = rows_back.shape[2]
+    enc_results = [rows_back[k][:, :width] for k, width in enumerate(enc_widths)]
+    dec_results = []
+    for place, width in enumerate(dec_widths):
+        slot = rows_back[len(enc_widths) + place // 2]
+        odd = place % 2
+        dec_results.append(
+            slot[
+                odd * dec_rows : (odd + 1) * dec_rows,
+                odd * (slot_width // 2) : odd * (slot_width // 2) + width,
+            ]
+        )
+    return enc_results, dec_results
 
 
 def apply_step(master, ortho_rows, widths, model_width, rate, model_ranks):
@@ -404,12 +399,14 @@
     )
     enc_sum_rows, dec_sum_rows, enc_norm_rows, dec_norm_rows = (
         lax.psum_scatter(
-            jnp.concatenate(enc_grads + [bridge_grad], axis=1),
+            shortened(jnp.concatenate(enc_grads + [bridge_grad], axis=1)),
             "dp",
             scatter_dimension=0,
             tiled=True,
-        ),
-        lax.psum_scatter(jnp.concatenate(dec_grads, axis=1), "dp", scatter_dimension=0, tiled=True),
+        ).astype(jnp.float32),
+        lax.psum_scatter(
+            shortened(jnp.concatenate(dec_grads, axis=1)), "dp", scatter_dimension=0, tiled=True
+        ).astype(jnp.float32),
         lax.psum_scatter(enc_norm_grads, "dp", scatter_dimension=1, tiled=True),
         lax.psum_scatter(dec_norm_grads, "dp", scatter_dimension=1, tiled=True),
     )
@@ -431,40 +428,47 @@
     dec_moment_new = momentum_keep * dec_moment + dec_grad
     enc_norm_moment_new = momentum_keep * enc_norm_moment + enc_norm_grad
     dec_norm_moment_new = momentum_keep * dec_norm_moment + dec_norm_grad
-    enc_slot_width = max(enc_widths)
-    dec_slot_width = max(dec_widths)
+    slot_width = max(enc_widths)
     enc_rows = enc_master.shape[0]
     dec_rows = dec_master.shape[0]
-    first_dec = len(enc_widths)
-    enc_whole, dec_whole = (
-        lax.all_gather(enc_moment_new.astype(jnp.bfloat16), "dp", axis=0, tiled=True).astype(
-            enc_moment_new.dtype
+    slots = slot_rows(
+        enc_moment_new.astype(jnp.bfloat16),
+        dec_moment_new.astype(jnp.bfloat16),
+        enc_widths,
+        dec_widths,
+        slot_width,
+        data_ranks,
+    )
+    own = lax.all_to_all(slots, "dp", 0, 0).reshape(data_ranks * enc_rows, slot_width)
+    gram = lax.psum(
+        lax.dot_general(
+            own, own, (((1,), (1,)), ((), ())), preferred_element_type=jnp.float32
         ),
-        lax.all_gather(dec_moment_new.astype(jnp.bfloat16), "dp", axis=0, tiled=True).astype(
-            dec_moment_new.dtype
-        ),
+        "mp",
     )
     data_rank = lax.axis_index("dp")
-    enc_orth, dec_orth = newton(
-        own_slot(enc_whole, enc_widths, data_rank, enc_slot_width),
-        own_slot(dec_whole, dec_widths, jnp.mod(data_rank - first_dec, data_ranks), dec_slot_width),
-    )
-    sources = [
-        (enc_orth, matrix_index, enc_rows, piece_width)
-        for matrix_index, piece_width in enumerate(enc_widths)
-    ]
-    sources = sources + [
-        (dec_orth, (first_dec + matrix_index) % data_ranks, dec_rows, piece_width)
-        for matrix_index, piece_width in enumerate(dec_widths)
-    ]
-    results = []
-    for orthogonal, owner_root, own_rows, piece_width in sources:
-        whole_rows = broadcast(shortened(orthogonal), "dp", owner_root).astype(orthogonal.dtype)
-        results.append(
-            lax.dynamic_slice_in_dim(whole_rows, data_rank * own_rows, own_rows, 0)[:, :piece_width]
-        )
-    enc_results = results[:first_dec]
-    dec_results = results[first_dec:]
+    paired = jnp.logical_and(
+        data_rank >= len(enc_widths), data_rank < len(enc_widths) + len(dec_widths) // 2
+    )
+    row_index = jnp.arange(gram.shape[0], dtype=jnp.int32)
+    upper_row = (row_index % enc_rows) < dec_rows
+    diagonal = jnp.sum(jnp.where(row_index[:, None] == row_index[None, :], gram, 0.0), axis=1)
+    upper_trace = jnp.sum(jnp.where(upper_row, diagonal, 0.0))
+    lower_trace = jnp.sum(jnp.where(upper_row, 0.0, diagonal))
+    row_trace = jnp.where(
+        paired, jnp.where(upper_row, upper_trace, lower_trace), upper_trace + lower_trace
+    )
+    row_scale = 1.0 / (jnp.sqrt(row_trace) + 1e-07)
+    product = gram_newton(gram * row_scale[:, None] * row_scale[None, :])
+    orthogonal = jnp.dot(
+        (product * row_scale[None, :]).astype(jnp.bfloat16),
+        own,
+        preferred_element_type=jnp.float32,
+    ).astype(jnp.bfloat16)
+    rows_back = lax.all_to_all(
+        orthogonal.reshape(data_ranks, enc_rows, slot_width), "dp", 0, 0
+    ).astype(jnp.float32)
+    enc_results, dec_results = unslot(rows_back, enc_widths, dec_widths, dec_rows)
     enc_master_new = apply_step(enc_master, enc_results, enc_widths, D, rate_enc, model_ranks)
     dec_master_new = apply_step(dec_master, dec_results, dec_widths, DD, rate_dec, model_ranks)
     enc_norms_new = enc_norms - rate_norm * enc_norm_moment_new

time: 2470 us -> 1510 us (0.61)
  waiting for transfers between devices: 1710 us -> 958 us
  matrix products: 426 us -> 231 us
    psum x1, waiting for transfers between devices: 394 us -> 84.6 us  [local(): lax.psum(lax.dot_general(own, own, (((1,), (1,)), ((), ())), preferred_el...]
    reduce_scatter x11 -> x2, waiting for transfers between devices: 413 us -> 171 us  [the longest x1 122 us: local(): lax.psum_scatter(shortened(jnp.concatenate(enc_grads + [bridge_grad], axi...]
    all_gather x7 -> x0, waiting for transfers between devices: 182 us -> none  [the longest x1 99.1 us: local(): lax.all_gather(enc_moment_new.astype(jnp.bfloat16), 'dp', axis=0, tiled=T...]
    dot_general x30 -> x18, matrix products: 224 us -> 63.8 us  [the longest x5 19.1 us: gram_newton(): square = jnp.dot(gram_half, gram_half, preferred_element_type=jnp.float32)]
    unnamed x46 -> x28, waiting for transfers between devices: 184 us -> 126 us
    all_to_all x0 -> x1, blocking collectives: none -> 51.8 us  [local(): lax.all_to_all(slots, 'dp', 0, 0).reshape(data_ranks * enc_rows, slot_width)]
    all_to_all x0 -> x1, waiting for transfers between devices: none -> 40 us  [local(): lax.all_to_all(orthogonal.reshape(data_ranks, enc_rows, slot_width), 'dp'...]
    all_gather x5 -> x0, blocking collectives: 36.4 us -> none  [newton(): lax.all_gather(dec_part.astype(jnp.bfloat16), 'mp', axis=0, tiled=True)]
  transfers between devices with their start and end apart: 43 -> 27, of which waited for: 39 -> 25; matrix products, arithmetic and copies ran while one was open for 9% -> 5% of each run, Pallas kernels for 0% -> 0%
where the time goes in v1:
time: 1510 us; the launch traced here: 1500 us
  waiting for transfers between devices  958 us (63%)
  matrix products  231 us (15%)
  blocking collectives  134 us (9%)
  other arithmetic  97.7 us (6%)
  local copies, waits for them, and re-layouts  48.8 us (3%)
  between operations  22.6 us (1%)
    reduce_scatter x5, waiting for transfers between devices, model_back(): lax.psum_scatter(partial_term.astype(jnp.bfloat16), 'mp', scatter_dimensi...  141 us
    unnamed x28, waiting for transfers between devices  126 us
    reduce_scatter x1, waiting for transfers between devices, local(): lax.psum_scatter(shortened(jnp.concatenate(enc_grads + [bridge_grad], axi...  122 us
    reduce_scatter x4, waiting for transfers between devices, model_sum(): lax.psum_scatter(partial_term.astype(jnp.bfloat16), 'mp', scatter_dimensi...  113 us
    psum x1, waiting for transfers between devices, local(): lax.psum(lax.dot_general(own, own, (((1,), (1,)), ((), ())), preferred_el...  84.6 us
    all_gather x5, waiting for transfers between devices, model_back(): lax.all_gather(share.astype(jnp.bfloat16), 'mp', axis=0, tiled=True)  84.4 us
    all_gather x1, waiting for transfers between devices, local(): lax.all_gather(enc_master.astype(jnp.bfloat16), 'dp', axis=0, tiled=True)  80 us
    all_gather x4, waiting for transfers between devices, model_sum(): lax.all_gather(share.astype(jnp.bfloat16), 'mp', axis=0, tiled=True)  77.9 us
  transfers between devices with their start and end apart: 27, of which 25 were waited for; matrix products, arithmetic and copies ran while one was open for 5% of the time, Pallas kernels for 0%

profile of v1, /device:TPU:0, one launch (start us, length us, event | category | flops | bytes accessed | tf_op | source)
XLA Modules:
  0.0 1500.9 jit_solution(3267360049680055320)
XLA Ops:
  11.5 22.6 %all_gather.42 = bf16[4,1024]{1,0:T(4,128)(2,1)S(1)} all-gather(bf16[4,128]{1,0:T(4,128)(2,1)S(1)} %convert_element_type.338), channel_id=1, replica_groups=mesh['dp'=8,'mp'=4] {'dp'}, dimensions={1}, use_global_device_ids=true | all-gather | bytes 9216 | tf_op jit(solution)/shard_map/all_gather | solution.py:361
  35.8 80.0 %all-gather.14.cloned.1.call-done = bf16[1024,3200]{1,0:T(8,128)(2,1)} async-done(((bf16[128,3200]{1,0:T(8,128)(2,1)}), bf16[1024,3200]{1,0:T(8,128)(2,1)}) %all-gather.14.cloned.1.call-update) | async-done | bytes 6553616 | tf_op jit(solution)/shard_map/all_gather | solution.py:359
  123.5 16.5 %while.54 = (s32[]{:T(128)}, bf16[2,512,4,64]{1,3,2,0:T(8,128)(2,1)}, f32[2,4,512,1]{2,1,3,0:T(4,128)S(1)}, s32[2,512]{1,0:T(2,128)S(1)}, s32[1024]{0:T(1024)S(1...) while((s32[]{:T(128)}, ...), condition=%wide.region_7.8_spmd, body=%wide.region_4.7_spmd.sunk | while | flops 562690048 | bytes 35203272 | solution.py:105
  146.0 29.7 %reduce-scatter.22.cloned.1.call-done = bf16[256,1024]{1,0:T(8,128)(2,1)} async-done(((bf16[1024,1024]{1,0:T(8,128)(2,1)}), bf16[256,1024]{1,0:T(8,128)(2,1)}) %reduce-scatter.22.cloned.1.call-update) | async-done | bytes 524304 | tf_op jit(solution)/shard_map/reduce_scatter | solution.py:50
  175.9 24.0 %all-gather.16.cloned.1.call-done = bf16[1024,1024]{1,0:T(8,128)(2,1)} async-done(((bf16[256,1024]{1,0:T(8,128)(2,1)}), bf16[1024,1024]{1,0:T(8,128)(2,1)}) %all-gather.16.cloned.1.call-update) | async-done | bytes 2097168 | tf_op jit(solution)/shard_map/all_gather | solution.py:53
  225.0 31.5 %reduce-scatter.24.cloned.1.call-done = bf16[256,1024]{1,0:T(8,128)(2,1)} async-done(((bf16[1024,1024]{1,0:T(8,128)(2,1)}), bf16[256,1024]{1,0:T(8,128)(2,1)}) %reduce-scatter.24.cloned.1.call-update) | async-done | bytes 524304 | tf_op jit(solution)/shard_map/reduce_scatter | solution.py:50
  256.6 24.0 %all-gather.18.cloned.1.call-done = bf16[1024,1024]{1,0:T(8,128)(2,1)} async-done(((bf16[256,1024]{1,0:T(8,128)(2,1)}), bf16[1024,1024]{1,0:T(8,128)(2,1)}) %all-gather.18.cloned.1.call-update) | async-done | bytes 2097168 | tf_op jit(solution)/shard_map/all_gather | solution.py:53
  285.3 20.7 %all-gather = bf16[8,64,4]{1,2,0:T(4,128)(2,1)S(1)} all-gather(bf16[1,64,4]{1,2,0:T(4,128)(2,1)S(1)} %convert_bitcast_fusion), channel_id=1, replica_groups=mesh['dp'=8,'mp'=4] {'dp'}, dimensions={0}, use_global_device_ids=true | all-gather | bytes 4608 | tf_op jit(solution)/shard_map/all_gather | solution.py:362
  309.3 39.1 %all-gather.22.cloned.1.call-done = bf16[512,1536]{1,0:T(8,128)(2,1)} async-done(((bf16[64,1536]{1,0:T(8,128)(2,1)}), bf16[512,1536]{1,0:T(8,128)(2,1)}) %all-gather.22.cloned.1.call-update) | async-done | bytes 1572880 | tf_op jit(solution)/shard_map/all_gather | solution.py:360
  351.0 15.1 %while.55 = (s32[]{:T(128)}, bf16[2,512,4,32]{1,3,2,0:T(8,128)(2,1)S(1)}, f32[2,4,512,1]{2,1,3,0:T(4,128)S(1)}, s32[2,512]{1,0:T(2,128)S(1)}, s32[1024]{0:T(1024...) while((s32[]{:T(128)}, ...), condition=%wide.region_17.18_spmd, body=%wide.region_14.17_spmd.sunk | while | flops 294189056 | bytes 28125300 | solution.py:105
  368.9 23.8 %reduce-scatter.26.cloned.1.call-done = bf16[256,512]{1,0:T(8,128)(2,1)} async-done(((bf16[1024,512]{1,0:T(8,128)(2,1)}), bf16[256,512]{1,0:T(8,128)(2,1)}) %reduce-scatter.26.cloned.1.call-update) | async-done | bytes 262160 | tf_op jit(solution)/shard_map/reduce_scatter | solution.py:50
  394.5 16.7 %all-gather.24.cloned.1.call-done = bf16[1024,512]{1,0:T(8,128)(2,1)} async-done(((bf16[256,512]{1,0:T(8,128)(2,1)}), bf16[1024,512]{1,0:T(8,128)(2,1)}) %all-gather.24.cloned.1.call-update) | async-done | bytes 1048592 | tf_op jit(solution)/shard_map/all_gather | solution.py:53
  436.1 21.9 %reduce-scatter.30.cloned.1.call-done = bf16[256,512]{1,0:T(8,128)(2,1)} async-done(((bf16[1024,512]{1,0:T(8,128)(2,1)}), bf16[256,512]{1,0:T(8,128)(2,1)}) %reduce-scatter.30.cloned.1.call-update) | async-done | bytes 262160 | tf_op jit(solution)/shard_map/reduce_scatter | solution.py:57
  458.0 28.0 %reduce-scatter.28.cloned.1.call-done = bf16[256,512]{1,0:T(8,128)(2,1)} async-done(((bf16[1024,512]{1,0:T(8,128)(2,1)}), bf16[256,512]{1,0:T(8,128)(2,1)}) %reduce-scatter.28.cloned.1.call-update) | async-done | bytes 262160 | tf_op jit(solution)/shard_map/reduce_scatter | solution.py:50
  486.1 18.2 %all-gather.28.cloned.1.call-done = bf16[1024,512]{1,0:T(8,128)(2,1)} async-done(((bf16[256,512]{1,0:T(8,128)(2,1)}), bf16[1024,512]{1,0:T(8,128)(2,1)}) %all-gather.28.cloned.1.call-update) | async-done | bytes 1048592 | tf_op jit(solution)/shard_map/all_gather | solution.py:60
  529.3 24.6 %while.56 = (s32[]{:T(128)}, f32[1024,4,32]{0,2,1:T(8,128)S(1)}, f32[1024,4,32]{0,2,1:T(8,128)}, bf16[2,512,4,32]{1,3,2,0:T(8,128)(2,1)S(1)}, bf16[2,512,4,32]{1...) while((s32[]{:T(128)}, f32[1024,4,32]{0,2,1:T(8,128)S(1)}, ...), condition=%wide.region_27.28_spmd.clone, body=%wide.region_25.27_spmd.clone.sunk | while | flops 703854592 | bytes 72812768 | solution.py:163
  558.4 25.0 %reduce-scatter.32.cloned.1.call-done = bf16[256,512]{1,0:T(8,128)(2,1)} async-done(((bf16[1024,512]{1,0:T(8,128)(2,1)}), bf16[256,512]{1,0:T(8,128)(2,1)}) %reduce-scatter.32.cloned.1.call-update) | async-done | bytes 262160 | tf_op jit(solution)/shard_map/reduce_scatter | solution.py:57
  583.5 18.1 %all-gather.30.cloned.1.call-done = bf16[1024,512]{1,0:T(8,128)(2,1)} async-done(((bf16[256,512]{1,0:T(8,128)(2,1)}), bf16[1024,512]{1,0:T(8,128)(2,1)}) %all-gather.30.cloned.1.call-update) | async-done | bytes 1048592 | tf_op jit(solution)/shard_map/all_gather | solution.py:60
  611.7 31.5 %reduce-scatter.34.cloned.1.call-done = bf16[256,1024]{1,0:T(8,128)(2,1)} async-done(((bf16[1024,1024]{1,0:T(8,128)(2,1)}), bf16[256,1024]{1,0:T(8,128)(2,1)}) %reduce-scatter.34.cloned.1.call-update) | async-done | bytes 524304 | tf_op jit(solution)/shard_map/reduce_scatter | solution.py:57
  643.3 24.0 %all-gather.32.cloned.1.call-done = bf16[1024,1024]{1,0:T(8,128)(2,1)} async-done(((bf16[256,1024]{1,0:T(8,128)(2,1)}), bf16[1024,1024]{1,0:T(8,128)(2,1)}) %all-gather.32.cloned.1.call-update) | async-done | bytes 2097168 | tf_op jit(solution)/shard_map/all_gather | solution.py:60
  682.3 31.5 %reduce-scatter.36.cloned.1.call-done = bf16[256,1024]{1,0:T(8,128)(2,1)} async-done(((bf16[1024,1024]{1,0:T(8,128)(2,1)}), bf16[256,1024]{1,0:T(8,128)(2,1)}) %reduce-scatter.36.cloned.1.call-update) | async-done | bytes 524304 | tf_op jit(solution)/shard_map/reduce_scatter | solution.py:57
  713.9 24.1 %all-gather.34.cloned.1.call-done = bf16[1024,1024]{1,0:T(8,128)(2,1)} async-done(((bf16[256,1024]{1,0:T(8,128)(2,1)}), bf16[1024,1024]{1,0:T(8,128)(2,1)}) %all-gather.34.cloned.1.call-update) | async-done | bytes 2097168 | tf_op jit(solution)/shard_map/all_gather | solution.py:60
  756.4 32.1 %while.57 = (s32[]{:T(128)}, f32[1024,4,64]{0,2,1:T(8,128)}, f32[1024,4,64]{0,2,1:T(8,128)}, bf16[2,512,4,64]{1,3,2,0:T(8,128)(2,1)}, bf16[2,512,4,64]{1,3,2,0:T...) while((s32[]{:T(128)}, f32[1024,4,64]{0,2,1:T(8,128)}, ...), condition=%wide.region_37.38_spmd.clone, body=%wide.region_35.37_spmd.clone.sunk | while | flops 1375729664 | bytes 93129096 | solution.py:163
  798.6 31.5 %reduce-scatter.38.cloned.1.call-done = bf16[256,1024]{1,0:T(8,128)(2,1)} async-done(((bf16[1024,1024]{1,0:T(8,128)(2,1)}), bf16[256,1024]{1,0:T(8,128)(2,1)}) %reduce-scatter.38.cloned.1.call-update) | async-done | bytes 524304 | tf_op jit(solution)/shard_map/reduce_scatter | solution.py:57
  874.3 49.4 %reduce-scatter.42.cloned.1.call-done = bf16[64,1536]{1,0:T(8,128)(2,1)} async-done(((bf16[512,1536]{1,0:T(8,128)(2,1)}), bf16[64,1536]{1,0:T(8,128)(2,1)}) %reduce-scatter.42.cloned.1.call-update) | async-done | bytes 196624 | tf_op jit(solution)/shard_map/reduce_scatter | solution.py:407
  925.4 62.4 %reduce-scatter.46.cloned.1.call-done = f32[64,4]{1,0:T(8,128)} async-done(((f32[512,4]{1,0:T(8,128)}), f32[64,4]{1,0:T(8,128)}) %reduce-scatter.46.cloned.1.call-update) | async-done | bytes 1040
  989.2 63.3 %reduce-scatter.44.cloned.1.call-done = f32[128,4]{1,0:T(8,128)} async-done(((f32[1024,4]{1,0:T(8,128)}), f32[128,4]{1,0:T(8,128)}) %reduce-scatter.44.cloned.1.call-update) | async-done | bytes 2064
  1055.4 122.0 %reduce-scatter.40.cloned.1.call-done = bf16[128,3200]{1,0:T(8,128)(2,1)} async-done(((bf16[1024,3200]{1,0:T(8,128)(2,1)}), bf16[128,3200]{1,0:T(8,128)(2,1)}) %reduce-scatter.40.cloned.1.call-update) | async-done | bytes 819216 | tf_op jit(solution)/shard_map/reduce_scatter | solution.py:401
  1180.8 39.4 %psum.14 = f32[]{:T(128)} all-reduce(f32[]{:T(128)S(6)} %add.349), channel_id=1, replica_groups=mesh['dp'=8,'mp'=4] {'dp','mp'}, use_global_device_ids=true, to_apply=%region_57.58 | all-reduce | flops 1 | bytes 8 | tf_op jit(solution)/shard_map/psum | solution.py:419
  1225.8 51.8 %all_to_all.10 = bf16[8,128,1024]{2,1,0:T(8,128)(2,1)S(1)} all-to-all(bf16[8,128,1024]{2,1,0:T(8,128)(2,1)S(1)} %broadcast_dynamic-update-slice_fusion), channel_id=1, replica_groups=mesh['dp'=8,'mp'=4] {'dp'}, dimensions={0} | all-to-all | bytes 4194304 | tf_op jit(solution)/shard_map/all_to_all | solution.py:442
  1283.3 84.6 %all-reduce.9.cloned.1.call-done = f32[1024,1024]{1,0:T(8,128)} async-done(((f32[1024,1024]{1,0:T(8,128)}), f32[1024,1024]{1,0:T(8,128)}) %all-reduce.9.cloned.1.call-update) | async-done | bytes 4194320 | tf_op jit(solution)/shard_map/psum | solution.py:443
  1447.0 40.0 %all-to-all-done.1 = bf16[8,128,1024]{2,1,0:T(8,128)(2,1)} async-done(((bf16[8,128,1024]{2,1,0:T(8,128)(2,1)}), bf16[8,128,1024]{2,1,0:T(8,128)(2,1)}, u32[]{:S(2)}, u32[]{:S(2)}) %all-to-all-start.1) | async-done | bytes 2097184 | tf_op jit(solution)/shard_map/all_to_all | solution.py:468
  (543 shorter events, 398.3 us)
Async XLA Ops:
  7.2 108.6 %all-gather.14.cloned.1.call-start = ((), (), s32[]{:S(2)}) async-start(), calls=%async_computation.15 | async-start | bytes 7372800 | tf_op jit(solution)/shard_map/all_gather | solution.py:359
  9.8 165.9 %reduce-scatter.22.cloned.1.call-start = ((), (), s32[]{:S(2)}) async-start(), calls=%async_computation.16 | async-start | bytes 2621440 | tf_op jit(solution)/shard_map/reduce_scatter | solution.py:50
  35.8 167.6 %copy-start.70 = (f32[1,1024]{1,0:T(1,128)}, f32[1,1024]{1,0:T(1,128)S(1)}, u32[]{:S(2)}) copy-start(f32[1,1024]{1,0:T(1,128)S(1)} %get-tuple-element.682) | copy-start | bytes 12292
  35.8 167.6 %copy-start.95 = (f32[1,1024]{1,0:T(1,128)}, f32[1,1024]{1,0:T(1,128)S(1)}, u32[]{:S(2)}) copy-start(f32[1,1024]{1,0:T(1,128)S(1)} %get-tuple-element.683) | copy-start | bytes 12292
  146.0 54.0 %all-gather.16.cloned.1.call-start = ((), (), s32[]{:S(2)}) async-start(), calls=%async_computation.17 | async-start | bytes 2621440 | tf_op jit(solution)/shard_map/all_gather | solution.py:53
  175.7 80.8 %reduce-scatter.24.cloned.1.call-start = ((), (), s32[]{:S(2)}) async-start(), calls=%async_computation.18 | async-start | bytes 2621440 | tf_op jit(solution)/shard_map/reduce_scatter | solution.py:50
  224.9 55.6 %all-gather.18.cloned.1.call-start = ((), (), s32[]{:S(2)}) async-start(), calls=%async_computation.19 | async-start | bytes 2621440 | tf_op jit(solution)/shard_map/all_gather | solution.py:53
  256.5 49.6 %all-gather.20.cloned.1.call-start = ((), (), s32[]{:S(2)}) async-start(), calls=%async_computation.20 | async-start | bytes 1310720 | tf_op jit(solution)/shard_map/all_gather | solution.py:378
  284.4 64.0 %all-gather.22.cloned.1.call-start = ((), (), s32[]{:S(2)}) async-start(), calls=%async_computation.21 | async-start | bytes 1769472 | tf_op jit(solution)/shard_map/all_gather | solution.py:360
  285.2 107.6 %reduce-scatter.26.cloned.1.call-start = ((), (), s32[]{:S(2)}) async-start(), calls=%async_computation.22 | async-start | bytes 1310720 | tf_op jit(solution)/shard_map/reduce_scatter | solution.py:50
  368.9 42.3 %all-gather.24.cloned.1.call-start = ((), (), s32[]{:S(2)}) async-start(), calls=%async_computation.23 | async-start | bytes 1310720 | tf_op jit(solution)/shard_map/all_gather | solution.py:53
  392.8 65.2 %reduce-scatter.30.cloned.1.call-start = ((), (), s32[]{:S(2)}) async-start(), calls=%async_computation.26 | async-start | bytes 1310720 | tf_op jit(solution)/shard_map/reduce_scatter | solution.py:57
  394.5 128.2 %copy-start.86 = (f32[1024]{0:T(1024)}, f32[1024]{0:T(1024)S(1)}, u32[]{:S(2)}) copy-start(f32[1024]{0:T(1024)S(1)} %fusion.257) | copy-start | bytes 12292
  432.9 53.1 %reduce-scatter.28.cloned.1.call-start = ((), (), s32[]{:S(2)}) async-start(), calls=%async_computation.24 | async-start | bytes 1310720 | tf_op jit(solution)/shard_map/reduce_scatter | solution.py:50
  436.0 68.2 %all-gather.28.cloned.1.call-start = ((), (), s32[]{:S(2)}) async-start(), calls=%async_computation.27 | async-start | bytes 1310720 | tf_op jit(solution)/shard_map/all_gather | solution.py:60
  458.0 64.7 %all-gather.26.cloned.1.call-start = ((), (), s32[]{:S(2)}) async-start(), calls=%async_computation.25 | async-start | bytes 1310720 | tf_op jit(solution)/shard_map/all_gather | solution.py:53
  486.0 97.4 %reduce-scatter.32.cloned.1.call-start = ((), (), s32[]{:S(2)}) async-start(), calls=%async_computation.28 | async-start | bytes 1310720 | tf_op jit(solution)/shard_map/reduce_scatter | solution.py:57
  558.4 43.2 %all-gather.30.cloned.1.call-start = ((), (), s32[]{:S(2)}) async-start(), calls=%async_computation.29 | async-start | bytes 1310720 | tf_op jit(solution)/shard_map/all_gather | solution.py:60
  583.5 59.8 %reduce-scatter.34.cloned.1.call-start = ((), (), s32[]{:S(2)}) async-start(), calls=%async_computation.30 | async-start | bytes 2621440 | tf_op jit(solution)/shard_map/reduce_scatter | solution.py:57
  611.7 55.7 %all-gather.32.cloned.1.call-start = ((), (), s32[]{:S(2)}) async-start(), calls=%async_computation.31 | async-start | bytes 2621440 | tf_op jit(solution)/shard_map/all_gather | solution.py:60
  643.3 70.5 %reduce-scatter.36.cloned.1.call-start = ((), (), s32[]{:S(2)}) async-start(), calls=%async_computation.32 | async-start | bytes 2621440 | tf_op jit(solution)/shard_map/reduce_scatter | solution.py:57
  682.2 55.8 %all-gather.34.cloned.1.call-start = ((), (), s32[]{:S(2)}) async-start(), calls=%async_computation.33 | async-start | bytes 2621440 | tf_op jit(solution)/shard_map/all_gather | solution.py:60
  713.9 116.3 %reduce-scatter.38.cloned.1.call-start = ((), (), s32[]{:S(2)}) async-start(), calls=%async_computation.34 | async-start | bytes 2621440 | tf_op jit(solution)/shard_map/reduce_scatter | solution.py:57
  798.6 55.9 %all-gather.36.cloned.1.call-start = ((), (), s32[]{:S(2)}) async-start(), calls=%async_computation.35 | async-start | bytes 2621440 | tf_op jit(solution)/shard_map/all_gather | solution.py:60
  830.2 93.5 %reduce-scatter.42.cloned.1.call-start = ((), (), s32[]{:S(2)}) async-start(), calls=%async_computation.38 | async-start | bytes 1769472 | tf_op jit(solution)/shard_map/reduce_scatter | solution.py:407
  838.8 149.0 %reduce-scatter.46.cloned.1.call-start = ((), (), s32[]{:S(2)}) async-start(), calls=%async_computation.40 | async-start | bytes 294912
  839.8 212.8 %reduce-scatter.44.cloned.1.call-start = ((), (), s32[]{:S(2)}) async-start(), calls=%async_computation.39 | async-start | bytes 589824
  860.9 316.4 %reduce-scatter.40.cloned.1.call-start = ((), (), s32[]{:S(2)}) async-start(), calls=%async_computation.37 | async-start | bytes 7372800 | tf_op jit(solution)/shard_map/reduce_scatter | solution.py:401
  874.2 350.3 %copy-start.50 = (f32[64,1536]{1,0:T(8,128)S(1)}, f32[64,1536]{1,0:T(8,128)}, u32[]{:S(2)}) copy-start(f32[64,1536]{1,0:T(8,128)} %param.27) | copy-start | bytes 1179652
  874.2 493.7 %all-reduce.9.cloned.1.call-start = ((), (), s32[]{:S(2)}) async-start(), calls=%async_computation.36 | async-start | bytes 8388608 | tf_op jit(solution)/shard_map/psum | solution.py:443
  923.7 300.8 %copy-start.43 = (bf16[64,1536]{1,0:T(8,128)(2,1)S(1)}, bf16[64,1536]{1,0:T(8,128)(2,1)}, u32[]{:S(2)}) copy-start(bf16[64,1536]{1,0:T(8,128)(2,1)} %reduce-scatter.42.cloned.1.call-done) | copy-start | bytes 589828
  1433.2 53.8 %all-to-all-start.1 = ((bf16[8,128,1024]{2,1,0:T(8,128)(2,1)}), bf16[8,128,1024]{2,1,0:T(8,128)(2,1)}, u32[]{:S(2)}, u32[]{:S(2)}) async-start(bf16[8,128,1024]{2,1,0:T(8,128)(2,1)} %bitcast.333), calls=%async_computation.10 | async-start | bytes 4194304 | tf_op jit(solution)/shard_map/all_to_all | solution.py:468
  (122 other events, 2092.1 us)
Sparse Core Ops, SparseCore 0:
  10.8 104.9 all-gather.13
  146.1 29.5 reduce-scatter.21
  177.3 22.5 all-gather.15
  225.0 31.4 reduce-scatter.23
  257.9 22.5 all-gather.17
  284.5 16.8 all-gather.19
  304.2 44.1 all-gather.21
  369.0 23.6 reduce-scatter.25
  394.4 16.7 all-gather.23
  433.0 24.8 reduce-scatter.29
  461.1 24.8 reduce-scatter.27
  487.5 16.7 all-gather.27
  505.9 16.7 all-gather.25
  558.5 24.8 reduce-scatter.31
  584.8 16.7 all-gather.29
  611.8 31.4 reduce-scatter.33
  644.8 22.5 all-gather.31
  682.4 31.4 reduce-scatter.35
  715.4 22.5 all-gather.33
  798.7 31.4 reduce-scatter.37
  831.8 22.5 all-gather.35
  858.8 64.8 reduce-scatter.41
  927.6 60.1 reduce-scatter.45
  991.6 60.9 reduce-scatter.43
  1056.6 120.6 reduce-scatter.39
  1283.5 84.4 all-reduce.8

commit v2 on v1

--- a/solution.py
+++ b/solution.py
@@ -36,28 +36,79 @@
     return jax.tree.map(short, array)
 
 
-def layer_norm(values, gain_row, shift_row):
+def pair_swap(array, axis, bit):
+    size = lax.axis_size(axis)
+    return lax.ppermute(array, axis, [(rank, rank ^ bit) for rank in range(size)])
+
+
+def core_swap(array):
+    return pair_swap(array, "mp", 1)
+
+
+def far_swap(array):
+    return pair_swap(array, "mp", 2)
+
+
+def far_sum(chip_term):
+    half = chip_term.astype(jnp.bfloat16)
+    return half.astype(jnp.float32) + far_swap(half).astype(jnp.float32)
+
+
+def chip_sum(partial_term):
+    own_rows = partial_term.shape[0] // 2
+    received = core_swap(partial_term[own_rows:].astype(jnp.bfloat16))
+    return partial_term[:own_rows] + received.astype(jnp.float32)
+
+
+def both_halves(own_part):
+    return jnp.concatenate([own_part, core_swap(own_part)], axis=0)
+
+
+def sum_everywhere(array):
+    for axis in ("mp", "dp"):
+        bit = 1
+        while bit < lax.axis_size(axis):
+            array = array + pair_swap(array, axis, bit)
+            bit *= 2
+    return array
+
+
+def gather_small(array):
+    rank = lax.axis_index("dp")
+    gathered = array[None]
+    bit = 1
+    while bit < lax.axis_size("dp"):
+        other = pair_swap(gathered, "dp", bit)
+        lower = (rank & bit) == 0
+        gathered = jnp.concatenate(
+            [jnp.where(lower, gathered, other), jnp.where(lower, other, gathered)], axis=0
+        )
+        bit *= 2
+    return gathered
+
+
+def normalize(values):
     center = values - jnp.mean(values, axis=-1, keepdims=True)
-    spread = jnp.mean(center * center, axis=-1, keepdims=True)
-    return center * lax.rsqrt(spread + ln_eps) * gain_row + shift_row
-
-
-def exact_gelu(hidden_in):
-    return jax.nn.gelu(hidden_in, approximate=False)
-
-
-def model_sum(partial_term):
-    share = lax.psum_scatter(
-        partial_term.astype(jnp.bfloat16), "mp", scatter_dimension=0, tiled=True
-    ).astype(jnp.float32)
-    return lax.all_gather(share.astype(jnp.bfloat16), "mp", axis=0, tiled=True).astype(share.dtype)
-
-
-def model_back(partial_term):
-    share = lax.psum_scatter(
-        partial_term.astype(jnp.bfloat16), "mp", scatter_dimension=0, tiled=True
-    ).astype(jnp.float32)
-    return lax.all_gather(share.astype(jnp.bfloat16), "mp", axis=0, tiled=True).astype(share.dtype)
+    inverse = lax.rsqrt(jnp.mean(center * center, axis=-1, keepdims=True) + ln_eps)
+    return center * inverse, inverse
+
+
+def normalize_back(normal, inverse, gain_row, out_grad):
+    scaled = out_grad * gain_row
+    mean_grad = jnp.mean(scaled, axis=-1, keepdims=True)
+    mean_dot = jnp.mean(scaled * normal, axis=-1, keepdims=True)
+    return inverse * (scaled - mean_grad - normal * mean_dot)
+
+
+def gelu_and_slope(hidden):
+    spread = 0.5 + 0.5 * lax.erf(hidden * math.sqrt(0.5))
+    density = jnp.exp(-0.5 * hidden * hidden) * (1.0 / math.sqrt(2.0 * math.pi))
+    return hidden * spread, spread + hidden * density
+
+
+def swap_halves(array, chunk_rows, core):
+    parts = array.reshape((-1, 2, chunk_rows // 2) + array.shape[1:])
+    return jnp.where(core == 0, parts, parts[:, ::-1]).reshape(array.shape)
 
 
 def segments_of(lengths, row_count):
@@ -170,78 +221,109 @@
     )
 
 
-def block_forward(values, segment, pieces, norm_values, head_width, block_rows):
+def attention_input(own_chunks, norm_values):
+    normals = [normalize(own) for own in own_chunks]
+    halves = [
+        both_halves((normal * norm_values[0] + norm_values[1]).astype(jnp.bfloat16))
+        for normal, _ in normals
+    ]
+    return normals, halves
+
+
+def block_forward(own_chunks, halves, segment, pieces, norm_values, head_width, block_rows):
     qkv_proj, out_proj, up_proj, down_proj = pieces
     inner_width = out_proj.shape[1]
     head_count = inner_width // head_width
-    normed_half = layer_norm(values, norm_values[0], norm_values[1]).astype(jnp.bfloat16)
-    mixed_all = jnp.dot(normed_half, qkv_proj, preferred_element_type=jnp.float32)
-    query_part = mixed_all[:, :inner_width].astype(jnp.bfloat16)
-    key_part = mixed_all[:, inner_width : 2 * inner_width].astype(jnp.bfloat16)
-    value_part = mixed_all[:, 2 * inner_width :].astype(jnp.bfloat16)
+    chunk_rows = halves[0].shape[0]
+    normed_half = jnp.concatenate(halves, axis=0)
+    mixed_all = jnp.dot(normed_half, qkv_proj, preferred_element_type=jnp.float32).astype(
+        jnp.bfloat16
+    )
+    query_part = mixed_all[:, :inner_width]
+    key_part = mixed_all[:, inner_width : 2 * inner_width]
+    value_part = mixed_all[:, 2 * inner_width :]
     heads_out, logsum = attend_forward(
         query_part, key_part, value_part, segment, head_count, head_width, block_rows
     )
-    middle = values + model_sum(
-        jnp.einsum("ti,di->td", heads_out, out_proj, preferred_element_type=jnp.float32)
-    )
-    normed_two = layer_norm(middle, norm_values[2], norm_values[3]).astype(jnp.bfloat16)
-    hidden = jnp.dot(normed_two, up_proj, preferred_element_type=jnp.float32)
-    activated = exact_gelu(hidden).astype(jnp.bfloat16)
-    output = middle + model_sum(
-        jnp.einsum("tf,df->td", activated, down_proj, preferred_element_type=jnp.float32)
-    )
+    middles = []
+    for place, own in enumerate(own_chunks):
+        rows = heads_out[place * chunk_rows : (place + 1) * chunk_rows]
+        chip_term = chip_sum(
+            jnp.einsum("ti,di->td", rows, out_proj, preferred_element_type=jnp.float32)
+        )
+        middles.append(own + far_sum(chip_term))
+    seconds, outputs, ups = [], [], []
+    for middle in middles:
+        normal, inverse = normalize(middle)
+        normed_two = both_halves((normal * norm_values[2] + norm_values[3]).astype(jnp.bfloat16))
+        hidden = jnp.dot(normed_two, up_proj, preferred_element_type=jnp.float32)
+        activated, slope = gelu_and_slope(hidden)
+        activated = activated.astype(jnp.bfloat16)
+        chip_term = chip_sum(
+            jnp.einsum("tf,df->td", activated, down_proj, preferred_element_type=jnp.float32)
+        )
+        outputs.append(middle + far_sum(chip_term))
+        seconds.append((normal, inverse))
+        ups.append((normed_two, activated, slope))
     return (
-        output,
-        (
-            normed_half,
-            query_part,
-            key_part,
-            value_part,
-            heads_out,
-            logsum,
-            middle,
-            normed_two,
-            hidden,
-            activated,
-        ),
-    )
-
-
-def block_backward(upstream, saved, values, pieces, norm_values, segment, head_width, block_rows):
-    (
-        normed_half,
-        query_part,
-        key_part,
-        value_part,
-        heads_out,
-        logsum,
-        middle,
-        normed_two,
-        hidden,
-        activated,
-    ) = saved
+        outputs,
+        (normed_half, query_part, key_part, value_part, heads_out, logsum, seconds, ups),
+    )
+
+
+def block_backward(
+    own_grads, half_grads, saved, firsts, pieces, norm_values, segment, head_width, block_rows
+):
+    normed_half, query_part, key_part, value_part, heads_out, logsum, seconds, ups = saved
     qkv_proj, out_proj, up_proj, down_proj = pieces
     inner_width = out_proj.shape[1]
     head_count = inner_width // head_width
-    upstream_half = upstream.astype(jnp.bfloat16)
+    chunk_rows = half_grads[0].shape[0]
+    hidden_halves, chip_terms = [], []
+    for half_grad, (_, _, slope) in zip(half_grads, ups):
+        act_grad = jnp.einsum("td,df->tf", half_grad, down_proj, preferred_element_type=jnp.float32)
+        hidden_half = (act_grad * slope).astype(jnp.bfloat16)
+        hidden_halves.append(hidden_half)
+        chip_terms.append(
+            chip_sum(
+                jnp.einsum("tf,df->td", hidden_half, up_proj, preferred_element_type=jnp.float32)
+            )
+        )
+    middle_grads, middle_halves, gain_two, shift_two = [], [], 0.0, 0.0
+    for own_grad, chip_term, (normal, inverse) in zip(own_grads, chip_terms, seconds):
+        gain_two = gain_two + jnp.sum(chip_term * normal, axis=0)
+        shift_two = shift_two + jnp.sum(chip_term, axis=0)
+        middle_grad = own_grad + normalize_back(
+            normal, inverse, norm_values[2], far_sum(chip_term)
+        )
+        middle_grads.append(middle_grad)
+        middle_halves.append(both_halves(middle_grad.astype(jnp.bfloat16)))
+    heads_grad = jnp.concatenate(
+        [
+            jnp.einsum("td,di->ti", half, out_proj, preferred_element_type=jnp.float32).astype(
+                jnp.bfloat16
+            )
+            for half in middle_halves
+        ],
+        axis=0,
+    )
     down_grad = jnp.einsum(
-        "td,tf->df", upstream_half, activated, preferred_element_type=jnp.float32
-    )
-    act_grad = jnp.einsum("td,df->tf", upstream_half, down_proj, preferred_element_type=jnp.float32)
-    gelu_pull = jax.vjp(exact_gelu, hidden)[1]
-    hidden_half = gelu_pull(act_grad)[0].astype(jnp.bfloat16)
-    up_grad = jnp.einsum("td,tf->df", normed_two, hidden_half, preferred_element_type=jnp.float32)
-    normed_two_grad = model_back(
-        jnp.einsum("tf,df->td", hidden_half, up_proj, preferred_element_type=jnp.float32)
-    )
-    second_pull = jax.vjp(layer_norm, middle, norm_values[2], norm_values[3])[1]
-    middle_part, gain_two, shift_two = second_pull(normed_two_grad)
-    middle_grad = upstream + middle_part
-    middle_half = middle_grad.astype(jnp.bfloat16)
-    out_grad = jnp.einsum("td,ti->di", middle_half, heads_out, preferred_element_type=jnp.float32)
-    heads_grad = jnp.einsum(
-        "td,di->ti", middle_half, out_proj, preferred_element_type=jnp.float32
+        "td,tf->df",
+        jnp.concatenate(half_grads, axis=0),
+        jnp.concatenate([activated for _, activated, _ in ups], axis=0),
+        preferred_element_type=jnp.float32,
+    ).astype(jnp.bfloat16)
+    up_grad = jnp.einsum(
+        "td,tf->df",
+        jnp.concatenate([normed_two for normed_two, _, _ in ups], axis=0),
+        jnp.concatenate(hidden_halves, axis=0),
+        preferred_element_type=jnp.float32,
+    ).astype(jnp.bfloat16)
+    out_grad = jnp.einsum(
+        "td,ti->di",
+        jnp.concatenate(middle_halves, axis=0),
+        heads_out,
+        preferred_element_type=jnp.float32,
     ).astype(jnp.bfloat16)
     query_grad, key_grad, value_grad = attend_backward(
         heads_grad,
@@ -255,14 +337,30 @@
         block_rows,
     )
     mixed_grad = jnp.concatenate([query_grad, key_grad, value_grad], axis=1)
-    qkv_grad = jnp.einsum("td,tf->df", normed_half, mixed_grad, preferred_element_type=jnp.float32)
-    normed_grad = model_back(
-        jnp.einsum("tf,df->td", mixed_grad, qkv_proj, preferred_element_type=jnp.float32)
-    )
-    first_pull = jax.vjp(layer_norm, values, norm_values[0], norm_values[1])[1]
-    values_part, gain_one, shift_one = first_pull(normed_grad)
+    chip_terms = [
+        chip_sum(
+            jnp.einsum(
+                "tf,df->td",
+                mixed_grad[place * chunk_rows : (place + 1) * chunk_rows],
+                qkv_proj,
+                preferred_element_type=jnp.float32,
+            )
+        )
+        for place in range(len(own_grads))
+    ]
+    qkv_grad = jnp.einsum(
+        "td,tf->df", normed_half, mixed_grad, preferred_element_type=jnp.float32
+    ).astype(jnp.bfloat16)
+    input_grads, gain_one, shift_one = [], 0.0, 0.0
+    for middle_grad, chip_term, (normal, inverse) in zip(middle_grads, chip_terms, firsts):
+        gain_one = gain_one + jnp.sum(chip_term * normal, axis=0)
+        shift_one = shift_one + jnp.sum(chip_term, axis=0)
+        input_grads.append(
+            middle_grad
+            + normalize_back(normal, inverse, norm_values[0], far_sum(chip_term))
+        )
     return (
-        middle_grad + values_part,
+        input_grads,
         [qkv_grad, out_grad, up_grad, down_grad],
         jnp.stack([gain_one, shift_one, gain_two, shift_two]),
     )
@@ -355,68 +453,145 @@
         DD // model_ranks,
     ]
     dec_widths = [3 * DD // model_ranks, DD // model_ranks, DFF // model_ranks, DFF // model_ranks]
-    enc_low, dec_low, enc_norm_low, dec_norm_low = (
-        lax.all_gather(enc_master.astype(jnp.bfloat16), "dp", axis=0, tiled=True),
+    first_cols = enc_widths[0] + enc_widths[1]
+    norm_parts = gather_small(
+        jnp.concatenate([enc_norms, dec_norms], axis=1).astype(jnp.bfloat16)
+    ).astype(jnp.float32)
+    enc_share, dec_share = enc_norms.shape[1], dec_norms.shape[1]
+    enc_norm_values = jnp.moveaxis(norm_parts[:, :, :enc_share], 0, 1).reshape(4, D)
+    dec_norm_values = jnp.moveaxis(norm_parts[:, :, enc_share:], 0, 1).reshape(4, DD)
+    first_low, rest_low, dec_low = (
+        lax.all_gather(
+            enc_master[:, :first_cols].astype(jnp.bfloat16), "dp", axis=0, tiled=True
+        ),
+        lax.all_gather(
+            enc_master[:, first_cols:].astype(jnp.bfloat16), "dp", axis=0, tiled=True
+        ),
         lax.all_gather(dec_master.astype(jnp.bfloat16), "dp", axis=0, tiled=True),
-        lax.all_gather(enc_norms.astype(jnp.bfloat16), "dp", axis=1, tiled=True),
-        lax.all_gather(dec_norms.astype(jnp.bfloat16), "dp", axis=1, tiled=True),
-    )
-    enc_pieces = split_columns(enc_low, enc_widths)
+    )
+    enc_pieces = split_columns(first_low, enc_widths[:2]) + split_columns(rest_low, enc_widths[2:])
     dec_pieces = split_columns(dec_low, dec_widths)
-    enc_norm_values = enc_norm_low.astype(jnp.float32)
-    dec_norm_values = dec_norm_low.astype(jnp.float32)
+    model_rank = lax.axis_index("mp")
+    core = model_rank % 2
+    upper_chip = model_rank // 2
     row_count = patches.shape[0]
     block_rows = min(512, row_count)
+    chunk_count = 2
+    chunk_rows = row_count // chunk_count
+    own_count = chunk_rows // 2
     segment, live_mask = segments_of(item_lengths[0], row_count)
-    inputs = patches.astype(jnp.float32)
+    segment = swap_halves(segment, chunk_rows, core)
+    live_mask = swap_halves(live_mask, chunk_rows, core)
+    inputs = swap_halves(patches, chunk_rows, core)
+    upstream = swap_halves(cotangent, chunk_rows, core) * live_mask.astype(jnp.bfloat16)[:, None]
+
+    def chunked(array):
+        return [array[k * chunk_rows : (k + 1) * chunk_rows] for k in range(chunk_count)]
+
+    bridge = enc_pieces[4]
+    bridge_far = far_swap(bridge)
+    bridge_pair = jnp.where(
+        upper_chip == 0, jnp.stack([bridge, bridge_far]), jnp.stack([bridge_far, bridge])
+    )
+    pair_other = core_swap(bridge_pair)
+    bridge_all = jnp.stack(
+        [
+            jnp.where(core == 0, bridge_pair, pair_other),
+            jnp.where(core == 0, pair_other, bridge_pair),
+        ],
+        axis=1,
+    )
+    share_width = bridge.shape[1]
+    bridge_all = jnp.moveaxis(bridge_all.reshape(-1, D, share_width), 0, 1).reshape(D, DD)
+
+    input_chunks = [chunk.astype(jnp.float32) for chunk in chunked(inputs)]
+    normals_all = [normalize(chunk) for chunk in input_chunks]
+    enc_firsts = [(normal[:own_count], inverse[:own_count]) for normal, inverse in normals_all]
+    enc_halves = [
+        (normal * enc_norm_values[0] + enc_norm_values[1]).astype(jnp.bfloat16)
+        for normal, _ in normals_all
+    ]
     encoded, enc_saved = block_forward(
-        inputs, segment, enc_pieces[:4], enc_norm_values, HD, block_rows
-    )
-    encoded_half = encoded.astype(jnp.bfloat16)
-    bridge = enc_pieces[4]
-    bridged = jnp.dot(encoded_half, bridge, preferred_element_type=jnp.float32).astype(jnp.bfloat16)
-    joined = lax.all_gather(bridged, "mp", axis=1, tiled=True)
-    decoder_in = joined.astype(jnp.float32)
+        [chunk[:own_count] for chunk in input_chunks],
+        enc_halves,
+        segment,
+        enc_pieces[:4],
+        enc_norm_values,
+        HD,
+        block_rows,
+    )
+    encoded_own = [chunk.astype(jnp.bfloat16) for chunk in encoded]
+    decoder_in = [
+        jnp.dot(chunk, bridge_all, preferred_element_type=jnp.float32)
+        .astype(jnp.bfloat16)
+        .astype(jnp.float32)
+        for chunk in encoded_own
+    ]
+    encoded_half = jnp.concatenate([both_halves(chunk) for chunk in encoded_own], axis=0)
+    dec_firsts, dec_halves = attention_input(decoder_in, dec_norm_values)
     decoded, dec_saved = block_forward(
-        decoder_in, segment, dec_pieces, dec_norm_values, DHD, block_rows
-    )
-    upstream = cotangent.astype(jnp.float32) * live_mask[:, None]
-    dec_in_grad, dec_grads, dec_norm_grads = block_backward(
-        upstream, dec_saved, decoder_in, dec_pieces, dec_norm_values, segment, DHD, block_rows
-    )
-    share_width = bridge.shape[1]
+        decoder_in, dec_halves, segment, dec_pieces, dec_norm_values, DHD, block_rows
+    )
+    upstream_halves = chunked(upstream)
+    dec_in_grads, dec_grads, dec_norm_grads = block_backward(
+        [half[:own_count].astype(jnp.float32) for half in upstream_halves],
+        upstream_halves,
+        dec_saved,
+        dec_firsts,
+        dec_pieces,
+        dec_norm_values,
+        segment,
+        DHD,
+        block_rows,
+    )
+    bridge_halves = [both_halves(grad.astype(jnp.bfloat16)) for grad in dec_in_grads]
+    encoded_grads = [
+        jnp.einsum("tf,df->td", half, bridge_all, preferred_element_type=jnp.float32)
+        for half in bridge_halves
+    ]
     bridge_in_grad = lax.dynamic_slice_in_dim(
-        dec_in_grad, lax.axis_index("mp") * share_width, share_width, 1
-    ).astype(jnp.bfloat16)
+        jnp.concatenate(bridge_halves, axis=0), model_rank * share_width, share_width, 1
+    )
     bridge_grad = jnp.einsum(
         "td,tf->df", encoded_half, bridge_in_grad, preferred_element_type=jnp.float32
-    )
-    encoded_grad = model_back(
-        jnp.einsum("tf,df->td", bridge_in_grad, bridge, preferred_element_type=jnp.float32)
-    )
-    input_grad, enc_grads, enc_norm_grads = block_backward(
-        encoded_grad, enc_saved, inputs, enc_pieces[:4], enc_norm_values, segment, HD, block_rows
-    )
-    enc_sum_rows, dec_sum_rows, enc_norm_rows, dec_norm_rows = (
-        lax.psum_scatter(
-            shortened(jnp.concatenate(enc_grads + [bridge_grad], axis=1)),
-            "dp",
-            scatter_dimension=0,
-            tiled=True,
-        ).astype(jnp.float32),
-        lax.psum_scatter(
-            shortened(jnp.concatenate(dec_grads, axis=1)), "dp", scatter_dimension=0, tiled=True
-        ).astype(jnp.float32),
-        lax.psum_scatter(enc_norm_grads, "dp", scatter_dimension=1, tiled=True),
-        lax.psum_scatter(dec_norm_grads, "dp", scatter_dimension=1, tiled=True),
-    )
-    local_sum = (
-        jnp.sum(enc_sum_rows * enc_sum_rows)
-        + jnp.sum(dec_sum_rows * dec_sum_rows)
-        + (jnp.sum(enc_norm_rows * enc_norm_rows) + jnp.sum(dec_norm_rows * dec_norm_rows))
-        / model_ranks
-    )
-    squares = lax.psum(local_sum, ("dp", "mp"))
+    ).astype(jnp.bfloat16)
+    input_grads, enc_grads, enc_norm_grads = block_backward(
+        [grad[:own_count] for grad in encoded_grads],
+        [grad.astype(jnp.bfloat16) for grad in encoded_grads],
+        enc_saved,
+        enc_firsts,
+        enc_pieces[:4],
+        enc_norm_values,
+        segment,
+        HD,
+        block_rows,
+    )
+
+    def natural(own_chunks):
+        return swap_halves(
+            jnp.concatenate([both_halves(own) for own in own_chunks], axis=0), chunk_rows, core
+        )
+
+    decoded = natural(decoded)
+    input_grad = natural(input_grads)
+
+    def scattered(parts):
+        return lax.psum_scatter(
+            jnp.concatenate(parts, axis=1), "dp", scatter_dimension=0, tiled=True
+        ).astype(jnp.float32)
+
+    dec_sum_rows = scattered(dec_grads)
+    late_rows = scattered(enc_grads[:2] + [bridge_grad])
+    early_rows = scattered(enc_grads[2:])
+    enc_sum_rows = jnp.concatenate(
+        [late_rows[:, :first_cols], early_rows, late_rows[:, first_cols:]], axis=1
+    )
+    norm_sums = sum_everywhere(jnp.concatenate([enc_norm_grads, dec_norm_grads], axis=1))
+    data_rank = lax.axis_index("dp")
+    enc_norm_rows = lax.dynamic_slice_in_dim(norm_sums[:, :D], data_rank * enc_share, enc_share, 1)
+    dec_norm_rows = lax.dynamic_slice_in_dim(norm_sums[:, D:], data_rank * dec_share, dec_share, 1)
+    local_sum = jnp.sum(enc_sum_rows * enc_sum_rows) + jnp.sum(dec_sum_rows * dec_sum_rows)
+    squares = sum_everywhere(jnp.full((8, 128), local_sum))[0, 0] + jnp.sum(norm_sums * norm_sums)
     grad_norm = jnp.sqrt(squares)
     factor = clip_bound * lax.rsqrt(squares + 1e-06)
     enc_grad = enc_sum_rows * factor
@@ -446,7 +621,6 @@
         ),
         "mp",
     )
-    data_rank = lax.axis_index("dp")
     paired = jnp.logical_and(
         data_rank >= len(enc_widths), data_rank < len(enc_widths) + len(dec_widths) // 2
     )

time: 1510 us -> 908 us (0.60)
  waiting for transfers between devices: 958 us -> 429 us
  blocking collectives: 134 us -> 47.9 us
  starting transfers between devices: 7.68 us -> 52.3 us
  matrix products: 231 us -> 187 us
    reduce_scatter x11 -> x3, waiting for transfers between devices: 426 us -> 120 us  [scattered(): lax.psum_scatter(jnp.concatenate(parts, axis=1), 'dp', scatter_dimension=...]
    all_gather x11 -> x2, waiting for transfers between devices: 242 us -> 52.5 us  [the longest x1 28 us: local(): lax.all_gather(enc_master[:, :first_cols].astype(jnp.bfloat16), 'dp', axi...]
    ppermute x0 -> x65, waiting for transfers between devices: none -> 141 us  [pair_swap(): lax.ppermute(array, axis, [(rank, rank ^ bit) for rank in range(size)])]
    unnamed x28 -> x7, waiting for transfers between devices: 126 us -> 0.11 us
    ppermute x0 -> x65, starting transfers between devices: none -> 45.7 us  [pair_swap(): lax.ppermute(array, axis, [(rank, rank ^ bit) for rank in range(size)])]
    all_gather x2 -> x0, blocking collectives: 43.3 us -> none  [the longest x1 22.6 us: local(): lax.all_gather(enc_norms.astype(jnp.bfloat16), 'dp', axis=1, tiled=True)]
    psum x1 -> x0, blocking collectives: 39.4 us -> none  [local(): squares = lax.psum(local_sum, ('dp', 'mp'))]
    all_gather x1, waiting for transfers between devices: 39.1 us -> 0.02 us  [local(): lax.all_gather(dec_master.astype(jnp.bfloat16), 'dp', axis=0, tiled=True)]
  transfers between devices with their start and end apart: 27 -> 73, of which waited for: 25 -> 39; matrix products, arithmetic and copies ran while one was open for 5% -> 22% of each run, Pallas kernels for 0% -> 0%
where the time goes in v2:
time: 908 us; the launch traced here: 897 us
  waiting for transfers between devices  429 us (47%)
  matrix products  187 us (21%)
  other arithmetic  106 us (12%)
  starting transfers between devices  52.3 us (6%)
  local copies, waits for them, and re-layouts  50.1 us (6%)
  blocking collectives  47.9 us (5%)
  between operations  22.9 us (3%)
    ppermute x65, waiting for transfers between devices, pair_swap(): lax.ppermute(array, axis, [(rank, rank ^ bit) for rank in range(size)])  141 us
    reduce_scatter x3, waiting for transfers between devices, scattered(): lax.psum_scatter(jnp.concatenate(parts, axis=1), 'dp', scatter_dimension=...  120 us
    psum x1, waiting for transfers between devices, local(): lax.psum(lax.dot_general(own, own, (((1,), (1,)), ((), ())), preferred_el...  84.6 us
    all_to_all x1, blocking collectives, local(): lax.all_to_all(slots, 'dp', 0, 0).reshape(data_ranks * enc_rows, slot_width)  47.9 us
    ppermute x65, starting transfers between devices, pair_swap(): lax.ppermute(array, axis, [(rank, rank ^ bit) for rank in range(size)])  45.7 us
    all_to_all x1, waiting for transfers between devices, local(): lax.all_to_all(orthogonal.reshape(data_ranks, enc_rows, slot_width), 'dp'...  30 us
    unnamed x331, local copies, waits for them, and re-layouts  29.3 us
    all_gather x1, waiting for transfers between devices, local(): lax.all_gather(enc_master[:, :first_cols].astype(jnp.bfloat16), 'dp', axi...  28 us
  transfers between devices with their start and end apart: 73, of which 39 were waited for; matrix products, arithmetic and copies ran while one was open for 22% of the time, Pallas kernels for 0%

profile of v2, /device:TPU:0, one launch (start us, length us, event | category | flops | bytes accessed | tf_op | source)
XLA Modules:
  0.0 896.9 jit_solution(5250255690942079947)
XLA Ops:
  29.6 5.4 add_convert_fusion.5
  35.0 28.0 %all-gather.4.cloned.1.call-done = bf16[1024,1024]{1,0:T(8,128)(2,1)} async-done(((bf16[128,1024]{1,0:T(8,128)(2,1)}), bf16[1024,1024]{1,0:T(8,128)(2,1)}) %all-gather.4.cloned.1.call-update) | async-done | bytes 2097168 | tf_op jit(solution)/shard_map/all_gather | solution.py:464
  67.2 15.0 %while.54 = (s32[]{:T(128)}, bf16[2,512,4,64]{1,3,2,0:T(8,128)(2,1)S(1)}, f32[2,4,512,1]{2,1,3,0:T(4,128)S(1)}, s32[2,512]{1,0:T(2,128)S(1)}, s32[2,2,256]{2,1,0...) while((s32[]{:T(128)}, ...), condition=%wide.region_9.10_spmd, body=%wide.region_6.9_spmd.sunk | while | flops 562690048 | bytes 28919924 | solution.py:156
  90.4 11.8 %collective-permute-done.12 = bf16[256,1024]{1,0:T(8,128)(2,1)S(1)} collective-permute-done((bf16[256,1024]{1,0:T(8,128)(2,1)S(1)}, bf16[256,1024]{1,0:T(8,128)(2,1)S(1)}, u32[]{:S(2)}, u32[]{:S(2)}) %collective-permute-start.12) | collective-permute-done | bytes 524320 | tf_op jit(solution)/shard_map/ppermute | solution.py:41
  102.7 9.8 %collective-permute-done.4 = bf16[256,1024]{1,0:T(8,128)(2,1)S(1)} collective-permute-done((bf16[256,1024]{1,0:T(8,128)(2,1)S(1)}, bf16[256,1024]{1,0:T(8,128)(2,1)S(1)}, u32[]{:S(2)}, u32[]{:S(2)}) %collective-permute-start.4) | collective-permute-done | bytes 524320 | tf_op jit(solution)/shard_map/ppermute | solution.py:41
  116.4 24.5 %all-gather.6.cloned.1.call-done = bf16[1024,2176]{1,0:T(8,128)(2,1)} async-done(((bf16[128,2176]{1,0:T(8,128)(2,1)}), bf16[1024,2176]{1,0:T(8,128)(2,1)}) %all-gather.6.cloned.1.call-update) | async-done | bytes 4456464 | tf_op jit(solution)/shard_map/all_gather | solution.py:467
  143.5 4.4 multiply_convert_fusion.4
  149.4 4.5 multiply_convert_fusion.5
  167.3 8.4 collective-permute-done.15
  177.9 8.2 collective-permute-done.7
  195.0 15.1 %while.55 = (s32[]{:T(128)}, bf16[2,512,4,32]{1,3,2,0:T(8,128)(2,1)S(1)}, f32[2,4,512,1]{2,1,3,0:T(4,128)S(1)}, s32[2,512]{1,0:T(2,128)S(1)}, s32[2,2,256]{2,1,0...) while((s32[]{:T(128)}, ...), condition=%wide.region_21.22_spmd, body=%wide.region_18.21_spmd.sunk | while | flops 294189056 | bytes 28133492 | solution.py:156
  222.5 5.2 collective-permute-done.24
  245.6 4.6 collective-permute-done.33
  250.2 5.6 collective-permute-done.27
  255.8 5.6 collective-permute-done.30
  275.5 24.6 %while.56 = (s32[]{:T(128)}, f32[1024,4,32]{0,2,1:T(8,128)S(1)}, f32[1024,4,32]{0,2,1:T(8,128)}, bf16[2,512,4,32]{1,3,2,0:T(8,128)(2,1)}, bf16[2,512,4,32]{1,3,2...) while((s32[]{:T(128)}, f32[1024,4,32]{0,2,1:T(8,128)S(1)}, ...), condition=%wide.region_32.33_spmd.clone, body=%wide.region_30.32_spmd.clone.sunk | while | flops 703854592 | bytes 74918168 | solution.py:214
  306.4 7.0 collective-permute-done.42
  344.7 9.0 %collective-permute-done.39 = bf16[256,1024]{1,0:T(8,128)(2,1)S(1)} collective-permute-done((bf16[256,1024]{1,0:T(8,128)(2,1)S(1)}, bf16[256,1024]{1,0:T(8,128)(2,1)S(1)}, u32[]{:S(2)}, u32[]{:S(2)}) %collective-permute-start.39) | collective-permute-done | bytes 524320 | tf_op jit(solution)/shard_map/ppermute | solution.py:41
  353.7 10.4 %collective-permute-done.45 = bf16[256,1024]{1,0:T(8,128)(2,1)S(1)} collective-permute-done((bf16[256,1024]{1,0:T(8,128)(2,1)S(1)}, bf16[256,1024]{1,0:T(8,128)(2,1)S(1)}, u32[]{:S(2)}, u32[]{:S(2)}) %collective-permute-start.45) | collective-permute-done | bytes 524320 | tf_op jit(solution)/shard_map/ppermute | solution.py:41
  380.7 24.9 %while.57 = (s32[]{:T(128)}, f32[1024,4,64]{0,2,1:T(8,128)S(1)}, f32[1024,4,64]{0,2,1:T(8,128)}, bf16[2,512,4,64]{1,3,2,0:T(8,128)(2,1)}, bf16[2,512,4,64]{1,3,2...) while((s32[]{:T(128)}, f32[1024,4,64]{0,2,1:T(8,128)S(1)}, ...), condition=%wide.region_43.44_spmd.clone, body=%wide.region_41.43_spmd.clone.sunk | while | flops 1375729664 | bytes 84748568 | solution.py:214
  427.8 6.5 copy.102
  442.7 12.3 %collective-permute-done.48 = bf16[256,1024]{1,0:T(8,128)(2,1)S(1)} collective-permute-done((bf16[256,1024]{1,0:T(8,128)(2,1)S(1)}, bf16[256,1024]{1,0:T(8,128)(2,1)S(1)}, u32[]{:S(2)}, u32[]{:S(2)}) %collective-permute-start.48) | collective-permute-done | bytes 524320 | tf_op jit(solution)/shard_map/ppermute | solution.py:41
  455.6 9.8 %collective-permute-done.51 = bf16[256,1024]{1,0:T(8,128)(2,1)S(1)} collective-permute-done((bf16[256,1024]{1,0:T(8,128)(2,1)S(1)}, bf16[256,1024]{1,0:T(8,128)(2,1)S(1)}, u32[]{:S(2)}, u32[]{:S(2)}) %collective-permute-start.51) | collective-permute-done | bytes 524320 | tf_op jit(solution)/shard_map/ppermute | solution.py:41
  473.0 31.8 %reduce-scatter.10.cloned.1.call-done = bf16[128,1152]{1,0:T(8,128)(2,1)} async-done(((bf16[1024,1152]{1,0:T(8,128)(2,1)}), bf16[128,1152]{1,0:T(8,128)(2,1)}) %reduce-scatter.10.cloned.1.call-update) | async-done | bytes 294928 | tf_op jit(solution)/shard_map/reduce_scatter | solution.py:579
  507.3 88.3 %reduce-scatter.12.cloned.1.call-done = bf16[128,2048]{1,0:T(8,128)(2,1)} async-done(((bf16[1024,2048]{1,0:T(8,128)(2,1)}), bf16[128,2048]{1,0:T(8,128)(2,1)}) %reduce-scatter.12.cloned.1.call-update) | async-done | bytes 524304 | tf_op jit(solution)/shard_map/reduce_scatter | solution.py:579
  625.0 47.9 %all_to_all.10 = bf16[8,128,1024]{2,1,0:T(8,128)(2,1)S(1)} all-to-all(bf16[8,128,1024]{2,1,0:T(8,128)(2,1)S(1)} %broadcast_dynamic-update-slice_fusion), channel_id=1, replica_groups=mesh['dp'=8,'mp'=4] {'dp'}, dimensions={0} | all-to-all | bytes 4194304 | tf_op jit(solution)/shard_map/all_to_all | solution.py:617
  678.6 84.6 %all-reduce.9.cloned.1.call-done = f32[1024,1024]{1,0:T(8,128)} async-done(((f32[1024,1024]{1,0:T(8,128)}), f32[1024,1024]{1,0:T(8,128)}) %all-reduce.9.cloned.1.call-update) | async-done | bytes 4194320 | tf_op jit(solution)/shard_map/psum | solution.py:618
  768.8 7.5 multiply_add_fusion.11
  806.4 4.7 multiply_add_fusion.4
  817.5 10.5 %fusion.190 = bf16[1024,1024]{1,0:T(8,128)(2,1)} fusion(bf16[1024,1024]{1,0:T(8,128)(2,1)} %bitcast.427, f32[1024,1024]{1,0:T(8,128)} %multiply_add_fusion.4, f32[1024]{0:T(1024)S(1)} %add_divide_fusion, bf16[1024,1024]{1,0:T(8,128)(2,1)} %add_convert_fusion), kind=kOutput, calls=%fused_computation.228 | convolution fusion | flops 4301258752 | bytes 10489856 | tf_op jit(solution)/shard_map/dot_general | solution.py:637
  828.0 6.0 all-to-all-start.1
  852.2 30.0 %all-to-all-done.1 = bf16[8,128,1024]{2,1,0:T(8,128)(2,1)} async-done(((bf16[8,128,1024]{2,1,0:T(8,128)(2,1)}), bf16[8,128,1024]{2,1,0:T(8,128)(2,1)}, u32[]{:S(2)}, u32[]{:S(2)}) %all-to-all-start.1) | async-done | bytes 2097184 | tf_op jit(solution)/shard_map/all_to_all | solution.py:642
  (849 shorter events, 380.5 us)
Async XLA Ops:
  7.2 55.7 %all-gather.4.cloned.1.call-start = ((), (), s32[]{:S(2)}) async-start(), calls=%async_computation.5 | async-start | bytes 2359296 | tf_op jit(solution)/shard_map/all_gather | solution.py:464
  9.5 131.4 %all-gather.6.cloned.1.call-start = ((), (), s32[]{:S(2)}) async-start(), calls=%async_computation.6 | async-start | bytes 5013504 | tf_op jit(solution)/shard_map/all_gather | solution.py:467
  9.6 11.5 %collective-permute-start = (bf16[1,4,192]{2,1,0:T(4,128)(2,1)S(1)}, bf16[1,4,192]{2,1,0:T(4,128)(2,1)S(1)}, u32[]{:S(2)}, u32[]{:S(2)}) collective-permute-start(bf16[1,4,192]{2,1,0:T(4,128)(2,1)S(1)} %pad_maximum_fusion.19), channel_id=1, source_target_pairs={{0,4},{4,0},{8,12},{12,8},{16,20},{20,16},{24,28},{28,24},{1,5},{5... | collective-permute-start | bytes 4616 | tf_op jit(solution)/shard_map/ppermute | solution.py:41
  13.5 177.9 %all-gather.8.cloned.1.call-start = ((), (), s32[]{:S(2)}) async-start(), calls=%async_computation.7 | async-start | bytes 1769472 | tf_op jit(solution)/shard_map/all_gather | solution.py:470
  87.3 14.8 %collective-permute-start.12 = (bf16[256,1024]{1,0:T(8,128)(2,1)S(1)}, bf16[256,1024]{1,0:T(8,128)(2,1)S(1)}, u32[]{:S(2)}, u32[]{:S(2)}) collective-permute-start(bf16[256,1024]{1,0:T(8,128)(2,1)S(1)} %fusion.242), channel_id=1, source_target_pairs={{0,2},{1,3},{2,0},{3,1},{4,6},{5,7},{6,4},{7,5},{8,10},{9,11},{10,... | collective-permute-start | bytes 1572872 | tf_op jit(solution)/shard_map/ppermute | solution.py:41
  89.0 23.4 %collective-permute-start.4 = (bf16[256,1024]{1,0:T(8,128)(2,1)S(1)}, bf16[256,1024]{1,0:T(8,128)(2,1)S(1)}, u32[]{:S(2)}, u32[]{:S(2)}) collective-permute-start(bf16[256,1024]{1,0:T(8,128)(2,1)S(1)} %fusion.245), channel_id=1, source_target_pairs={{0,2},{1,3},{2,0},{3,1},{4,6},{5,7},{6,4},{7,5},{8,10},{9,11},{10,... | collective-permute-start | bytes 1572872 | tf_op jit(solution)/shard_map/ppermute | solution.py:41
  114.3 29.2 %collective-permute-start.13 = (bf16[256,1024]{1,0:T(8,128)(2,1)S(1)}, bf16[256,1024]{1,0:T(8,128)(2,1)}, u32[]{:S(2)}, u32[]{:S(2)}) collective-permute-start(bf16[256,1024]{1,0:T(8,128)(2,1)S(1)} %get-tuple-element.707), channel_id=1, source_target_pairs={{0,1},{1,0},{2,3},{3,2},{4,5},{5,4},{6,7},{7,6},{8,9},{9,8},{10,11... | collective-permute-start | bytes 1572872 | tf_op jit(solution)/shard_map/ppermute | solution.py:41
  115.1 354.3 %reduce-scatter.14.cloned.1.call-start = ((), (), s32[]{:S(2)}) async-start(), calls=%async_computation.11 | async-start | bytes 1769472 | tf_op jit(solution)/shard_map/reduce_scatter | solution.py:579
  116.0 33.5 %collective-permute-start.5 = (bf16[256,1024]{1,0:T(8,128)(2,1)}, bf16[256,1024]{1,0:T(8,128)(2,1)}, u32[]{:S(2)}, u32[]{:S(2)}) collective-permute-start(bf16[256,1024]{1,0:T(8,128)(2,1)} %get-tuple-element.706), channel_id=1, source_target_pairs={{0,1},{1,0},{2,3},{3,2},{4,5},{5,4},{6,7},{7,6},{8,9},{9,8},{10,11... | collective-permute-start | bytes 1572872 | tf_op jit(solution)/shard_map/ppermute | solution.py:41
  142.0 15.7 %collective-permute-start.8 = (bf16[1024,128]{1,0:T(8,128)(2,1)S(1)}, bf16[1024,128]{1,0:T(8,128)(2,1)S(1)}, u32[]{:S(2)}, u32[]{:S(2)}) collective-permute-start(bf16[1024,128]{1,0:T(8,128)(2,1)S(1)} %get-tuple-element.671), channel_id=1, source_target_pairs={{0,2},{1,3},{2,0},{3,1},{4,6},{5,7},{6,4},{7,5},{8,10},{9,11},{10,... | collective-permute-start | bytes 786440 | tf_op jit(solution)/shard_map/ppermute | solution.py:41
  160.6 15.1 %collective-permute-start.15 = (bf16[256,1024]{1,0:T(8,128)(2,1)}, bf16[256,1024]{1,0:T(8,128)(2,1)}, u32[]{:S(2)}, u32[]{:S(2)}) collective-permute-start(bf16[256,1024]{1,0:T(8,128)(2,1)} %fusion.241), channel_id=1, source_target_pairs={{0,2},{1,3},{2,0},{3,1},{4,6},{5,7},{6,4},{7,5},{8,10},{9,11},{10,... | collective-permute-start | bytes 1572872 | tf_op jit(solution)/shard_map/ppermute | solution.py:41
  163.5 22.7 %collective-permute-start.7 = (bf16[256,1024]{1,0:T(8,128)(2,1)}, bf16[256,1024]{1,0:T(8,128)(2,1)}, u32[]{:S(2)}, u32[]{:S(2)}) collective-permute-start(bf16[256,1024]{1,0:T(8,128)(2,1)} %fusion.244), channel_id=1, source_target_pairs={{0,2},{1,3},{2,0},{3,1},{4,6},{5,7},{6,4},{7,5},{8,10},{9,11},{10,... | collective-permute-start | bytes 1572872 | tf_op jit(solution)/shard_map/ppermute | solution.py:41
  218.3 9.3 %collective-permute-start.24 = (bf16[256,512]{1,0:T(8,128)(2,1)S(1)}, bf16[256,512]{1,0:T(8,128)(2,1)}, u32[]{:S(2)}, u32[]{:S(2)}) collective-permute-start(bf16[256,512]{1,0:T(8,128)(2,1)S(1)} %fusion.314), channel_id=1, source_target_pairs={{0,2},{1,3},{2,0},{3,1},{4,6},{5,7},{6,4},{7,5},{8,10},{9,11},{10,... | collective-permute-start | bytes 786440 | tf_op jit(solution)/shard_map/ppermute | solution.py:41
  221.3 11.1 %collective-permute-start.18 = (bf16[256,512]{1,0:T(8,128)(2,1)S(1)}, bf16[256,512]{1,0:T(8,128)(2,1)S(1)}, u32[]{:S(2)}, u32[]{:S(2)}) collective-permute-start(bf16[256,512]{1,0:T(8,128)(2,1)S(1)} %fusion.316), channel_id=1, source_target_pairs={{0,2},{1,3},{2,0},{3,1},{4,6},{5,7},{6,4},{7,5},{8,10},{9,11},{10,... | collective-permute-start | bytes 786440 | tf_op jit(solution)/shard_map/ppermute | solution.py:41
  241.0 9.2 %collective-permute-start.33 = (bf16[256,512]{1,0:T(8,128)(2,1)S(1)}, bf16[256,512]{1,0:T(8,128)(2,1)S(1)}, u32[]{:S(2)}, u32[]{:S(2)}) collective-permute-start(bf16[256,512]{1,0:T(8,128)(2,1)S(1)} %fusion.396), channel_id=1, source_target_pairs={{0,2},{1,3},{2,0},{3,1},{4,6},{5,7},{6,4},{7,5},{8,10},{9,11},{10,... | collective-permute-start | bytes 786440 | tf_op jit(solution)/shard_map/ppermute | solution.py:41
  242.0 13.8 %collective-permute-start.27 = (bf16[256,512]{1,0:T(8,128)(2,1)S(1)}, bf16[256,512]{1,0:T(8,128)(2,1)S(1)}, u32[]{:S(2)}, u32[]{:S(2)}) collective-permute-start(bf16[256,512]{1,0:T(8,128)(2,1)S(1)} %fusion.313), channel_id=1, source_target_pairs={{0,2},{1,3},{2,0},{3,1},{4,6},{5,7},{6,4},{7,5},{8,10},{9,11},{10,... | collective-permute-start | bytes 786440 | tf_op jit(solution)/shard_map/ppermute | solution.py:41
  243.4 18.1 %collective-permute-start.30 = (bf16[256,512]{1,0:T(8,128)(2,1)S(1)}, bf16[256,512]{1,0:T(8,128)(2,1)S(1)}, u32[]{:S(2)}, u32[]{:S(2)}) collective-permute-start(bf16[256,512]{1,0:T(8,128)(2,1)S(1)} %fusion.394), channel_id=1, source_target_pairs={{0,2},{1,3},{2,0},{3,1},{4,6},{5,7},{6,4},{7,5},{8,10},{9,11},{10,... | collective-permute-start | bytes 786440 | tf_op jit(solution)/shard_map/ppermute | solution.py:41
  244.3 21.9 %collective-permute-start.21 = (bf16[256,512]{1,0:T(8,128)(2,1)S(1)}, bf16[256,512]{1,0:T(8,128)(2,1)S(1)}, u32[]{:S(2)}, u32[]{:S(2)}) collective-permute-start(bf16[256,512]{1,0:T(8,128)(2,1)S(1)} %fusion.315), channel_id=1, source_target_pairs={{0,2},{1,3},{2,0},{3,1},{4,6},{5,7},{6,4},{7,5},{8,10},{9,11},{10,... | collective-permute-start | bytes 786440 | tf_op jit(solution)/shard_map/ppermute | solution.py:41
  304.2 9.2 %collective-permute-start.42 = (bf16[256,512]{1,0:T(8,128)(2,1)S(1)}, bf16[256,512]{1,0:T(8,128)(2,1)S(1)}, u32[]{:S(2)}, u32[]{:S(2)}) collective-permute-start(bf16[256,512]{1,0:T(8,128)(2,1)S(1)} %fusion.400), channel_id=1, source_target_pairs={{0,2},{1,3},{2,0},{3,1},{4,6},{5,7},{6,4},{7,5},{8,10},{9,11},{10,... | collective-permute-start | bytes 786440 | tf_op jit(solution)/shard_map/ppermute | solution.py:41
  305.1 13.0 %collective-permute-start.36 = (bf16[256,512]{1,0:T(8,128)(2,1)S(1)}, bf16[256,512]{1,0:T(8,128)(2,1)S(1)}, u32[]{:S(2)}, u32[]{:S(2)}) collective-permute-start(bf16[256,512]{1,0:T(8,128)(2,1)S(1)} %fusion.398), channel_id=1, source_target_pairs={{0,2},{1,3},{2,0},{3,1},{4,6},{5,7},{6,4},{7,5},{8,10},{9,11},{10,... | collective-permute-start | bytes 786440 | tf_op jit(solution)/shard_map/ppermute | solution.py:41
  323.6 46.6 %collective-permute-start.54 = (bf16[256,1024]{1,0:T(8,128)(2,1)S(1)}, bf16[256,1024]{1,0:T(8,128)(2,1)}, u32[]{:S(2)}, u32[]{:S(2)}) collective-permute-start(bf16[256,1024]{1,0:T(8,128)(2,1)S(1)} %copy-done.37), channel_id=1, source_target_pairs={{0,1},{1,0},{2,3},{3,2},{4,5},{5,4},{6,7},{7,6},{8,9},{9,8},{10,11... | collective-permute-start | bytes 1572872 | tf_op jit(solution)/shard_map/ppermute | solution.py:41
  324.1 46.1 %collective-permute-start.53 = (bf16[256,1024]{1,0:T(8,128)(2,1)}, bf16[256,1024]{1,0:T(8,128)(2,1)}, u32[]{:S(2)}, u32[]{:S(2)}) collective-permute-start(bf16[256,1024]{1,0:T(8,128)(2,1)} %add_convert_fusion.8), channel_id=1, source_target_pairs={{0,1},{1,0},{2,3},{3,2},{4,5},{5,4},{6,7},{7,6},{8,9},{9,8},{10,11... | collective-permute-start | bytes 1572872 | tf_op jit(solution)/shard_map/ppermute | solution.py:41
  338.8 14.8 %collective-permute-start.39 = (bf16[256,1024]{1,0:T(8,128)(2,1)S(1)}, bf16[256,1024]{1,0:T(8,128)(2,1)S(1)}, u32[]{:S(2)}, u32[]{:S(2)}) collective-permute-start(bf16[256,1024]{1,0:T(8,128)(2,1)S(1)} %fusion.372), channel_id=1, source_target_pairs={{0,2},{1,3},{2,0},{3,1},{4,6},{5,7},{6,4},{7,5},{8,10},{9,11},{10,... | collective-permute-start | bytes 1572872 | tf_op jit(solution)/shard_map/ppermute | solution.py:41
  340.0 24.1 %collective-permute-start.45 = (bf16[256,1024]{1,0:T(8,128)(2,1)S(1)}, bf16[256,1024]{1,0:T(8,128)(2,1)S(1)}, u32[]{:S(2)}, u32[]{:S(2)}) collective-permute-start(bf16[256,1024]{1,0:T(8,128)(2,1)S(1)} %fusion.374), channel_id=1, source_target_pairs={{0,2},{1,3},{2,0},{3,1},{4,6},{5,7},{6,4},{7,5},{8,10},{9,11},{10,... | collective-permute-start | bytes 1572872 | tf_op jit(solution)/shard_map/ppermute | solution.py:41
  370.2 134.6 %reduce-scatter.10.cloned.1.call-start = ((), (), s32[]{:S(2)}) async-start(), calls=%async_computation.9 | async-start | bytes 2654208 | tf_op jit(solution)/shard_map/reduce_scatter | solution.py:579
  416.0 179.7 %reduce-scatter.12.cloned.1.call-start = ((), (), s32[]{:S(2)}) async-start(), calls=%async_computation.10 | async-start | bytes 4718592 | tf_op jit(solution)/shard_map/reduce_scatter | solution.py:579
  434.3 328.9 %all-reduce.9.cloned.1.call-start = ((), (), s32[]{:S(2)}) async-start(), calls=%async_computation.8 | async-start | bytes 8388608 | tf_op jit(solution)/shard_map/psum | solution.py:618
  440.2 14.8 %collective-permute-start.48 = (bf16[256,1024]{1,0:T(8,128)(2,1)S(1)}, bf16[256,1024]{1,0:T(8,128)(2,1)S(1)}, u32[]{:S(2)}, u32[]{:S(2)}) collective-permute-start(bf16[256,1024]{1,0:T(8,128)(2,1)S(1)} %fusion.376), channel_id=1, source_target_pairs={{0,2},{1,3},{2,0},{3,1},{4,6},{5,7},{6,4},{7,5},{8,10},{9,11},{10,... | collective-permute-start | bytes 1572872 | tf_op jit(solution)/shard_map/ppermute | solution.py:41
  441.7 23.8 %collective-permute-start.51 = (bf16[256,1024]{1,0:T(8,128)(2,1)S(1)}, bf16[256,1024]{1,0:T(8,128)(2,1)S(1)}, u32[]{:S(2)}, u32[]{:S(2)}) collective-permute-start(bf16[256,1024]{1,0:T(8,128)(2,1)S(1)} %fusion.378), channel_id=1, source_target_pairs={{0,2},{1,3},{2,0},{3,1},{4,6},{5,7},{6,4},{7,5},{8,10},{9,11},{10,... | collective-permute-start | bytes 1572872 | tf_op jit(solution)/shard_map/ppermute | solution.py:41
  472.5 127.8 %collective-permute-start.62 = (f32[4,1536]{1,0:T(4,128)S(1)}, f32[4,1536]{1,0:T(4,128)S(1)}, u32[]{:S(2)}, u32[]{:S(2)}) collective-permute-start(f32[4,1536]{1,0:T(4,128)S(1)} %fusion.531), channel_id=1, source_target_pairs={{0,4},{4,0},{8,12},{12,8},{16,20},{20,16},{24,28},{28,24},{1,5},{5... | collective-permute-start | bytes 73736 | tf_op jit(solution)/shard_map/ppermute | solution.py:41
  604.2 10.2 %collective-permute-start.64 = (f32[4,1536]{1,0:T(4,128)S(1)}, f32[4,1536]{1,0:T(4,128)S(1)}, u32[]{:S(2)}, u32[]{:S(2)}) collective-permute-start(f32[4,1536]{1,0:T(4,128)S(1)} %add.751), channel_id=1, source_target_pairs={{0,16},{4,20},{8,24},{12,28},{16,0},{20,4},{24,8},{28,12},{1,17},{... | collective-permute-start | bytes 73736 | tf_op jit(solution)/shard_map/ppermute | solution.py:41
  828.0 54.1 %all-to-all-start.1 = ((bf16[8,128,1024]{2,1,0:T(8,128)(2,1)}), bf16[8,128,1024]{2,1,0:T(8,128)(2,1)}, u32[]{:S(2)}, u32[]{:S(2)}) async-start(bf16[8,128,1024]{2,1,0:T(8,128)(2,1)} %bitcast.424), calls=%async_computation.1 | async-start | bytes 4194304 | tf_op jit(solution)/shard_map/all_to_all | solution.py:642
  (213 other events, 1503.8 us)
Sparse Core Ops, SparseCore 0:
  10.7 52.1 all-gather.3
  65.7 75.1 all-gather.5
  143.7 42.5 all-gather.7
  370.3 62.6 reduce-scatter.13
  436.7 68.0 reduce-scatter.9
  508.7 86.9 reduce-scatter.11
  678.7 84.4 all-reduce.8

commit v3 on v2

v3 whole, which is shorter than its diff:
```python
import functools
import math

import jax
import jax.numpy as jnp
from jax import lax
from jax.experimental import pallas as pl
from jax.experimental.pallas import tpu as pltpu
from jax.sharding import PartitionSpec as P

D = 1024
HD = 64
FF = 4096
DD = 512
DHD = 32
DFF = 2048
NS_STEPS = 5


highest = lax.Precision.HIGHEST
ln_eps = 1e-06
masked_score = -1e30
newton_first = 3.4445
newton_second = -4.775
newton_third = 2.0315
momentum_keep = 0.5
clip_bound = 100.0
rate_enc = 0.2
rate_dec = 0.3
rate_norm = 1.0
decay_rate = 0.01
kernel_vmem = 32 * 1024 * 1024
newton_vmem = 48 * 1024 * 1024


def shortened(array):

    def short(part):
        return part.astype(jnp.bfloat16) if part.dtype == jnp.float32 else part

    return jax.tree.map(short, array)


def pair_swap(array, axis, bit):
    size = lax.axis_size(axis)
    return lax.ppermute(array, axis, [(rank, rank ^ bit) for rank in range(size)])


def core_swap(array):
    return pair_swap(array, "mp", 1)


def far_swap(array):
    return pair_swap(array, "mp", 2)


def far_sum(chip_term):
    half = chip_term.astype(jnp.bfloat16)
    return half.astype(jnp.float32) + far_swap(half).astype(jnp.float32)


def chip_sum(partial_term):
    own_rows = partial_term.shape[0] // 2
    received = core_swap(partial_term[own_rows:].astype(jnp.bfloat16))
    return partial_term[:own_rows] + received.astype(jnp.float32)


def both_halves(own_part):
    return jnp.concatenate([own_part, core_swap(own_part)], axis=0)


def sum_everywhere(array):
    for axis in ("mp", "dp"):
        bit = 1
        while bit < lax.axis_size(axis):
            array = array + pair_swap(array, axis, bit)
            bit *= 2
    return array


def gather_small(array):
    rank = lax.axis_index("dp")
    gathered = array[None]
    bit = 1
    while bit < lax.axis_size("dp"):
        other = pair_swap(gathered, "dp", bit)
        lower = (rank & bit) == 0
        gathered = jnp.concatenate(
            [jnp.where(lower, gathered, other), jnp.where(lower, other, gathered)], axis=0
        )
        bit *= 2
    return gathered


def assemble_kernel(rank_ref, *refs):
    whole_ref = refs[-1]
    rows = refs[0].shape[0]
    for bit, part_ref in enumerate(refs[:-1]):
        place = pl.multiple_of((rank_ref[0] ^ bit) * rows, rows)
        whole_ref[pl.ds(place, rows), :] = part_ref[...]


def assemble(parts):
    rows, columns = parts[0].shape
    spec = pl.BlockSpec(memory_space=pltpu.VMEM)
    return pl.pallas_call(
        assemble_kernel,
        in_specs=[pl.BlockSpec(memory_space=pltpu.SMEM)] + [spec] * len(parts),
        out_specs=spec,
        out_shape=jax.ShapeDtypeStruct((len(parts) * rows, columns), parts[0].dtype),
        compiler_params=pltpu.CompilerParams(vmem_limit_bytes=kernel_vmem),
        cost_estimate=pl.CostEstimate(
            flops=0, bytes_accessed=4 * len(parts) * rows * columns, transcendentals=0
        ),
        name="assemble",
    )(lax.axis_index("dp").reshape(1), *parts)


class Gather:
    def __init__(self, array):
        self.general = lax.axis_size("dp") != 8
        if self.general:
            self.whole = lax.all_gather(array, "dp", axis=0, tiled=True)
            self.lined = [array]
        else:
            self.lined = [array] + [pair_swap(array, "dp", 2 * bit) for bit in (1, 2, 3)]
            self.crossed = None

    def turn(self, values):
        if self.general:
            return values
        values, self.lined = lax.optimization_barrier((values, self.lined))
        self.cross()
        return values

    def cross(self):
        self.crossed = [pair_swap(part, "dp", 1) for part in self.lined]

    def result(self):
        if self.general:
            return self.whole
        if self.crossed is None:
            self.cross()
        return assemble([part for pair in zip(self.lined, self.crossed) for part in pair])


def collect(slots):
    ranks = lax.axis_size("dp")
    rank = lax.axis_index("dp")
    width = max(rows.shape[1] for rows in slots.values())
    padded = {
        owner: jnp.pad(rows, ((0, 0), (0, width - rows.shape[1])))
        for owner, rows in slots.items()
    }
    parts = []
    for bit in range(ranks):
        value = None
        for owner, rows in padded.items():
            value = rows if value is None else jnp.where(rank ^ bit == owner, rows, value)
        if bit:
            value = lax.ppermute(value, "dp", [(owner ^ bit, owner) for owner in padded])
        parts.append(value)
    return assemble(parts)


def after(value, anchor):
    return lax.optimization_barrier((value, anchor))[0]


def fold(kept, received):
    return (kept.astype(jnp.float32) + received.astype(jnp.float32)).astype(jnp.bfloat16)


def split_rows(array, place):
    half = array.shape[0] // 2
    return (
        lax.dynamic_slice_in_dim(array, (1 - place) * half, half, 0),
        lax.dynamic_slice_in_dim(array, place * half, half, 0),
    )


class Scatter:
    def __init__(self, groups):
        self.phase = 0
        self.general = lax.axis_size("dp") != 8
        self.rank = lax.axis_index("dp")
        if self.general:
            whole = jnp.concatenate(
                [
                    sum(
                        jnp.einsum("td,tf->df", left, right, preferred_element_type=jnp.float32)
                        for left, right in zip(lefts, rights)
                    ).astype(jnp.bfloat16)
                    for lefts, rights in groups
                ],
                axis=1,
            )
            self.total = lax.psum_scatter(whole, "dp", scatter_dimension=0, tiled=True)
            self.received = self.total
        else:
            self.sent, self.kept = weight_grads(groups, self.rank % 2)
            self.received = pair_swap(self.sent, "dp", 1)

    def turn(self, values):
        if self.general or self.phase == 2:
            return values
        values, self.received = lax.optimization_barrier((values, self.received))
        self.advance()
        return values

    def advance(self):
        place = self.rank // 2 % 2 if self.phase == 0 else self.rank // 4
        self.sent, self.kept = split_rows(fold(self.kept, self.received), place)
        self.received = pair_swap(self.sent, "dp", 2 << self.phase)
        self.phase += 1

    def result(self):
        if self.general:
            return self.total.astype(jnp.float32)
        while self.phase < 2:
            self.advance()
        return self.kept.astype(jnp.float32) + self.received.astype(jnp.float32)

    def direct_result(self):
        if self.general:
            return self.total.astype(jnp.float32)
        pairs = fold(self.kept, self.received)
        rows = pairs.shape[0] // 4
        outer = self.rank // 2

        def block(place):
            return lax.dynamic_slice_in_dim(pairs, (place % 2 * 2 + place // 2) * rows, rows, 0)

        total = block(outer).astype(jnp.float32)
        for bit in (3, 2, 1):
            total = total + pair_swap(block(outer ^ bit), "dp", 2 * bit).astype(jnp.float32)
        return total


def normalize(values):
    center = values - jnp.mean(values, axis=-1, keepdims=True)
    inverse = lax.rsqrt(jnp.mean(center * center, axis=-1, keepdims=True) + ln_eps)
    return center * inverse, inverse


def normalize_back(normal, inverse, gain_row, out_grad):
    scaled = out_grad * gain_row
    mean_grad = jnp.mean(scaled, axis=-1, keepdims=True)
    mean_dot = jnp.mean(scaled * normal, axis=-1, keepdims=True)
    return inverse * (scaled - mean_grad - normal * mean_dot)


def gelu_and_slope(hidden):
    spread = 0.5 + 0.5 * lax.erf(hidden * math.sqrt(0.5))
    density = jnp.exp(-0.5 * hidden * hidden) * (1.0 / math.sqrt(2.0 * math.pi))
    return hidden * spread, spread + hidden * density


def swap_halves(array, chunk_rows, core):
    parts = array.reshape((-1, 2, chunk_rows // 2) + array.shape[1:])
    return jnp.where(core == 0, parts, parts[:, ::-1]).reshape(array.shape)


def segments_of(lengths, row_count):
    item_ends = jnp.cumsum(lengths)
    position = jnp.arange(row_count, dtype=jnp.int32)
    segment = jnp.sum((position[:, None] >= item_ends[None, :]).astype(jnp.int32), axis=1)
    live_mask = (position < item_ends[-1]).astype(jnp.float32)
    return (segment, live_mask)


def split_columns(whole_cols, widths):
    pieces = []
    start_col = 0
    for piece_width in widths:
        pieces.append(whole_cols[:, start_col : start_col + piece_width])
        start_col += piece_width
    return pieces


def head_mask(head, head_width, inner_width):
    lane = lax.broadcasted_iota(jnp.int32, (1, inner_width), 1)
    inside = jnp.logical_and(lane >= head * head_width, lane < (head + 1) * head_width)
    return jnp.where(inside, 1.0, 0.0)


def masked_rows(rows, head, head_width):
    mask = head_mask(head, head_width, rows.shape[1])
    return (rows.astype(jnp.float32) * mask).astype(jnp.bfloat16)


def last_dims(left, right):
    return lax.dot_general(
        left, right, (((1,), (1,)), ((), ())), preferred_element_type=jnp.float32
    )


def segment_bias(key_segment_ref, query_segment_ref):
    return jnp.where(key_segment_ref[...] == query_segment_ref[...], 0.0, masked_score)


def attend_forward_kernel(
    head_width, key_segment_ref, query_segment_ref, query_ref, key_ref, value_ref, out_ref,
    logsum_ref,
):
    block_rows, inner_width = query_ref.shape
    score_scale = head_width ** (-0.5)
    bias = segment_bias(key_segment_ref, query_segment_ref)
    joined = jnp.zeros((block_rows, inner_width), jnp.float32)
    logsums = []
    for head in range(inner_width // head_width):
        query = masked_rows(query_ref[...], head, head_width)
        scores = last_dims(query, key_ref[...]) * score_scale + bias
        top = jnp.max(scores, axis=1, keepdims=True)
        shifted = jnp.exp(scores - top)
        total = jnp.sum(shifted, axis=1, keepdims=True)
        part = jnp.dot(
            shifted.astype(jnp.bfloat16), value_ref[...], preferred_element_type=jnp.float32
        )
        joined += part * (head_mask(head, head_width, inner_width) / total)
        logsums.append(jnp.broadcast_to(top + jnp.log(total), (block_rows, 128)))
    out_ref[...] = joined.astype(jnp.bfloat16)
    lane = lax.broadcasted_iota(jnp.int32, (block_rows, 128), 1)
    stacked = logsums[0]
    for head in range(1, len(logsums)):
        stacked = jnp.where(lane == head, logsums[head], stacked)
    logsum_ref[...] = stacked.T[: len(logsums), :]


def attend_forward(mixed_all, segment, first_block, block_count, head_width, block_rows):
    row_count = mixed_all.shape[0]
    inner_width = mixed_all.shape[1] // 3
    head_count = inner_width // head_width
    return pl.pallas_call(
        functools.partial(attend_forward_kernel, head_width),
        grid=(block_count,),
        in_specs=[
            pl.BlockSpec((1, row_count), lambda i: (0, 0)),
            pl.BlockSpec((block_rows, 1), lambda i: (first_block + i, 0)),
            pl.BlockSpec((block_rows, inner_width), lambda i: (first_block + i, 0)),
            pl.BlockSpec((row_count, inner_width), lambda i: (0, 1)),
            pl.BlockSpec((row_count, inner_width), lambda i: (0, 2)),
        ],
        out_specs=[
            pl.BlockSpec((block_rows, inner_width), lambda i: (i, 0)),
            pl.BlockSpec((head_count, block_rows), lambda i: (0, i)),
        ],
        out_shape=[
            jax.ShapeDtypeStruct((block_count * block_rows, inner_width), jnp.bfloat16),
            jax.ShapeDtypeStruct((head_count, block_count * block_rows), jnp.float32),
        ],
        compiler_params=pltpu.CompilerParams(
            dimension_semantics=("arbitrary",), vmem_limit_bytes=kernel_vmem
        ),
        cost_estimate=pl.CostEstimate(
            flops=4 * block_count * block_rows * row_count * inner_width * head_count,
            bytes_accessed=8 * row_count * inner_width,
            transcendentals=block_count * block_rows * row_count * head_count,
        ),
        name="attend_forward",
    )(segment.reshape(1, row_count), segment.reshape(row_count, 1), mixed_all, mixed_all, mixed_all)


def attend_backward_kernel(
    head_width, key_segment_ref, query_segment_ref, grad_ref, logsum_ref, query_ref, key_ref,
    value_ref, out_ref, turned_ref, key_total_ref, value_total_ref,
):
    step = pl.program_id(0)
    block_rows, inner_width = query_ref.shape

    @pl.when(step == 0)
    def begin():
        turned_ref[...] = key_ref[...].astype(jnp.float32).T.astype(jnp.bfloat16)
        key_total_ref[...] = jnp.zeros_like(key_total_ref)
        value_total_ref[...] = jnp.zeros_like(value_total_ref)

    score_scale = head_width ** (-0.5)
    bias = segment_bias(key_segment_ref, query_segment_ref)
    parts = []
    for head in range(inner_width // head_width):
        query = masked_rows(query_ref[...], head, head_width)
        grad = masked_rows(grad_ref[...], head, head_width)
        scores = last_dims(key_ref[...], query) * score_scale + bias
        attention = jnp.exp(scores - logsum_ref[head : head + 1, :])
        weighted = attention * last_dims(value_ref[...], grad)
        row_dot = jnp.sum(weighted, axis=0, keepdims=True)
        score_grad = (weighted - attention * row_dot).astype(jnp.bfloat16)
        value_total_ref[...] += jnp.dot(
            attention.astype(jnp.bfloat16), grad, preferred_element_type=jnp.float32
        )
        key_total_ref[...] += jnp.dot(score_grad, query, preferred_element_type=jnp.float32)
        parts.append(
            jnp.dot(
                turned_ref[head * head_width : (head + 1) * head_width, :],
                score_grad,
                preferred_element_type=jnp.float32,
            )
        )
    query_grad = (jnp.concatenate(parts, axis=0) * score_scale).T
    rows = pl.ds(pl.multiple_of(step * block_rows, block_rows), block_rows)
    out_ref[rows, :inner_width] = query_grad.astype(jnp.bfloat16)

    @pl.when(step == pl.num_programs(0) - 1)
    def finish():
        out_ref[:, inner_width : 2 * inner_width] = (key_total_ref[...] * score_scale).astype(
            jnp.bfloat16
        )
        out_ref[:, 2 * inner_width :] = value_total_ref[...].astype(jnp.bfloat16)


def attend_backward(heads_grad, mixed_all, logsum, segment, head_width, block_rows):
    row_count, inner_width = heads_grad.shape
    head_count = inner_width // head_width
    return pl.pallas_call(
        functools.partial(attend_backward_kernel, head_width),
        grid=(row_count // block_rows,),
        in_specs=[
            pl.BlockSpec((row_count, 1), lambda i: (0, 0)),
            pl.BlockSpec((1, block_rows), lambda i: (0, i)),
            pl.BlockSpec((block_rows, inner_width), lambda i: (i, 0)),
            pl.BlockSpec((head_count, block_rows), lambda i: (0, i)),
            pl.BlockSpec((block_rows, inner_width), lambda i: (i, 0)),
            pl.BlockSpec((row_count, inner_width), lambda i: (0, 1)),
            pl.BlockSpec((row_count, inner_width), lambda i: (0, 2)),
        ],
        out_specs=pl.BlockSpec((row_count, 3 * inner_width), lambda i: (0, 0)),
        out_shape=jax.ShapeDtypeStruct((row_count, 3 * inner_width), jnp.bfloat16),
        scratch_shapes=[
            pltpu.VMEM((inner_width, row_count), jnp.bfloat16),
            pltpu.VMEM((row_count, inner_width), jnp.float32),
            pltpu.VMEM((row_count, inner_width), jnp.float32),
        ],
        compiler_params=pltpu.CompilerParams(
            dimension_semantics=("arbitrary",), vmem_limit_bytes=kernel_vmem
        ),
        cost_estimate=pl.CostEstimate(
            flops=10 * row_count * row_count * inner_width * head_count,
            bytes_accessed=14 * row_count * inner_width,
            transcendentals=row_count * row_count * head_count,
        ),
        name="attend_backward",
    )(
        segment.reshape(row_count, 1),
        segment.reshape(1, row_count),
        heads_grad,
        logsum,
        mixed_all,
        mixed_all,
        mixed_all,
    )


def attention_input(own_chunks, norm_values):
    normals = [normalize(own) for own in own_chunks]
    halves = [
        both_halves((normal * norm_values[0] + norm_values[1]).astype(jnp.bfloat16))
        for normal, _ in normals
    ]
    return normals, halves


def block_forward(own_chunks, halves, segment, pieces, norm_values, head_width, hook):
    halves = hook("input", halves)
    qkv_proj, out_proj = pieces[:2]
    chunk_rows = halves[0].shape[0]
    normed_half = jnp.concatenate(halves, axis=0)
    mixed_all = jnp.dot(normed_half, qkv_proj, preferred_element_type=jnp.float32).astype(
        jnp.bfloat16
    )
    heads_out, logsums, middles = [], [], []
    for place, own in enumerate(own_chunks):
        rows, logsum = attend_forward(mixed_all, segment, place, 1, head_width, chunk_rows)
        if place == 0:
            rows = hook("heads", rows)
        heads_out.append(rows)
        logsums.append(logsum)
        chip_term = chip_sum(
            jnp.einsum("ti,di->td", rows, out_proj, preferred_element_type=jnp.float32)
        )
        middles.append(own + far_sum(chip_term))
    middles = hook("middle", middles)
    up_proj, down_proj = pieces[2:4]
    seconds, outputs, ups = [], [], []
    for middle in middles:
        normal, inverse = normalize(middle)
        normed_two = both_halves((normal * norm_values[2] + norm_values[3]).astype(jnp.bfloat16))
        hidden = jnp.dot(normed_two, up_proj, preferred_element_type=jnp.float32)
        activated, slope = gelu_and_slope(hidden)
        activated = activated.astype(jnp.bfloat16)
        chip_term = chip_sum(
            jnp.einsum("tf,df->td", activated, down_proj, preferred_element_type=jnp.float32)
        )
        outputs.append(middle + far_sum(chip_term))
        seconds.append((normal, inverse))
        ups.append((normed_two, activated, slope))
    return (
        outputs,
        (normed_half, mixed_all, heads_out, logsums, seconds, ups),
    )


def block_backward(
    own_grads, half_grads, saved, firsts, pieces, norm_values, segment, head_width, hook
):
    normed_half, mixed_all, heads_out, logsums, seconds, ups = saved
    qkv_proj, out_proj, up_proj, down_proj = pieces
    chunk_rows = half_grads[0].shape[0]
    down_group = (half_grads, [activated for _, activated, _ in ups])
    half_grads = hook("start", half_grads, down_group)
    hidden_halves, chip_terms = [], []
    for half_grad, (_, _, slope) in zip(half_grads, ups):
        act_grad = jnp.einsum("td,df->tf", half_grad, down_proj, preferred_element_type=jnp.float32)
        hidden_half = (act_grad * slope).astype(jnp.bfloat16)
        hidden_halves.append(hidden_half)
        chip_terms.append(
            chip_sum(
                jnp.einsum("tf,df->td", hidden_half, up_proj, preferred_element_type=jnp.float32)
            )
        )
    up_group = ([normed_two for normed_two, _, _ in ups], hidden_halves)
    normed_grads = hook("sums", [far_sum(chip_term) for chip_term in chip_terms], up_group)
    middle_grads, middle_halves, gain_two, shift_two = [], [], 0.0, 0.0
    for own_grad, chip_term, normed_grad, (normal, inverse) in zip(
        own_grads, chip_terms, normed_grads, seconds
    ):
        gain_two = gain_two + jnp.sum(chip_term * normal, axis=0)
        shift_two = shift_two + jnp.sum(chip_term, axis=0)
        middle_grad = own_grad + normalize_back(normal, inverse, norm_values[2], normed_grad)
        middle_grads.append(middle_grad)
        middle_halves.append(both_halves(middle_grad.astype(jnp.bfloat16)))
    out_group = (middle_halves, heads_out)
    middle_halves = hook("middle", middle_halves, out_group)
    heads_grad = jnp.concatenate(
        [
            jnp.einsum("td,di->ti", half, out_proj, preferred_element_type=jnp.float32).astype(
                jnp.bfloat16
            )
            for half in middle_halves
        ],
        axis=0,
    )
    mixed_grad = attend_backward(
        heads_grad, mixed_all, jnp.concatenate(logsums, axis=1), segment, head_width, chunk_rows
    )
    qkv_group = ([normed_half], [mixed_grad])
    mixed_grad = hook("mixed", mixed_grad, qkv_group)
    chip_terms = [
        chip_sum(
            jnp.einsum(
                "tf,df->td",
                mixed_grad[place * chunk_rows : (place + 1) * chunk_rows],
                qkv_proj,
                preferred_element_type=jnp.float32,
            )
        )
        for place in range(len(own_grads))
    ]
    input_grads, gain_one, shift_one = [], 0.0, 0.0
    for middle_grad, chip_term, (normal, inverse) in zip(middle_grads, chip_terms, firsts):
        gain_one = gain_one + jnp.sum(chip_term * normal, axis=0)
        shift_one = shift_one + jnp.sum(chip_term, axis=0)
        input_grads.append(
            middle_grad
            + normalize_back(normal, inverse, norm_values[0], far_sum(chip_term))
        )
    return (
        input_grads,
        [qkv_group, out_group, up_group, down_group],
        jnp.stack([gain_one, shift_one, gain_two, shift_two]),
    )


def weight_grads_kernel(counts, parity_ref, *refs):
    sent_ref, kept_ref = refs[-2:]
    even = parity_ref[0] == 0
    place, column = 0, 0
    for count in counts:
        total = 0.0
        for k in range(count):
            total = total + lax.dot_general(
                refs[place + k][...],
                refs[place + count + k][...],
                (((0,), (0,)), ((), ())),
                preferred_element_type=jnp.float32,
            )
        half = total.shape[0] // 2
        columns = slice(column, column + total.shape[1])
        upper, lower = total[:half], total[half:]
        sent_ref[:, columns] = jnp.where(even, lower, upper).astype(jnp.bfloat16)
        kept_ref[:, columns] = jnp.where(even, upper, lower).astype(jnp.bfloat16)
        place += 2 * count
        column += total.shape[1]


def weight_grads(groups, parity):
    width = groups[0][0][0].shape[1]
    specs, operands, flops = [], [], 0
    for lefts, rights in groups:
        for left in lefts:
            specs.append(
                pl.BlockSpec((left.shape[0], width // 4), lambda i: (0, i % 2 * 2 + i // 2))
            )
            operands.append(left)
        for right in rights:
            specs.append(pl.BlockSpec(right.shape, lambda i: (0, 0)))
            operands.append(right)
            flops += 2 * width * right.shape[0] * right.shape[1]
    columns = sum(rights[0].shape[1] for _, rights in groups)
    half = jax.ShapeDtypeStruct((width // 2, columns), jnp.bfloat16)
    return pl.pallas_call(
        functools.partial(weight_grads_kernel, [len(lefts) for lefts, _ in groups]),
        grid=(4,),
        in_specs=[pl.BlockSpec(memory_space=pltpu.SMEM)] + specs,
        out_specs=[pl.BlockSpec((width // 8, columns), lambda i: (i, 0))] * 2,
        out_shape=[half, half],
        compiler_params=pltpu.CompilerParams(
            dimension_semantics=("arbitrary",), vmem_limit_bytes=kernel_vmem
        ),
        cost_estimate=pl.CostEstimate(
            flops=flops,
            bytes_accessed=2 * sum(operand.size for operand in operands) + 2 * width * columns,
            transcendentals=0,
        ),
        name="weight_grads",
    )(parity.reshape(1), *operands)


low_set = ((0, 0), (0, 1), (0, 2), (0, 3), (1, 1))
high_set = ((2, 2), (2, 3), (3, 3), (1, 2), (1, 3))


def newton_kernel(
    enc_rows, dec_rows, paired_ref, low_ref, high_ref, own_ref, out_ref, gram_ref, total_ref,
    mix_ref, gram_half_ref, total_half_ref,
):
    size = gram_ref.shape[0]
    block = size // 4
    tile = size // 2

    def in_upper(axis, count, start):
        shape = (count, 1) if axis == 0 else (1, count)
        place = start + lax.broadcasted_iota(jnp.int32, shape, axis)
        return place % enc_rows < dec_rows

    row = lax.broadcasted_iota(jnp.int32, (block, block), 0)
    column = lax.broadcasted_iota(jnp.int32, (block, block), 1)
    upper_trace, whole_trace = 0.0, 0.0
    for places, blocks_ref in ((low_set, low_ref), (high_set, high_ref)):
        for k, (i, j) in enumerate(places):
            value = blocks_ref[k * block : (k + 1) * block, :]
            gram_ref[i * block : (i + 1) * block, j * block : (j + 1) * block] = value
            if i != j:
                gram_ref[j * block : (j + 1) * block, i * block : (i + 1) * block] = value.T
            else:
                diagonal = jnp.where(row == column, value, 0.0)
                whole_trace += jnp.sum(diagonal)
                upper_trace += jnp.sum(
                    jnp.where(in_upper(0, block, i * block), diagonal, 0.0)
                )
    paired = paired_ref[0] == 1
    upper_scale = 1.0 / (jnp.sqrt(jnp.where(paired, upper_trace, whole_trace)) + 1e-07)
    lower_scale = 1.0 / (
        jnp.sqrt(jnp.where(paired, whole_trace - upper_trace, whole_trace)) + 1e-07
    )
    column_scale = jnp.where(in_upper(1, size, 0), upper_scale, lower_scale)

    def rows_of(step):
        return pl.ds(pl.multiple_of(step * tile, tile), tile)

    def times(left, right):
        return jnp.dot(left, right, preferred_element_type=jnp.float32)

    @pl.loop(0, size // tile)
    def _(step):
        rows = rows_of(step)
        row_scale = jnp.where(in_upper(0, tile, step * tile), upper_scale, lower_scale)
        scaled = gram_ref[rows, :] * row_scale * column_scale
        gram_ref[rows, :] = scaled
        gram_half_ref[0, rows, :] = scaled.astype(jnp.bfloat16)

    for newton_step in range(NS_STEPS):
        now, later = newton_step % 2, (newton_step + 1) % 2

        @pl.loop(0, size // tile)
        def _(step):
            rows = rows_of(step)
            square = times(gram_half_ref[now, rows, :], gram_half_ref[now])
            mix = newton_second * gram_ref[rows, :] + newton_third * square
            mix_ref[rows, :] = mix.astype(jnp.bfloat16)
            if newton_step == 0:
                same = lax.broadcasted_iota(
                    jnp.int32, (tile, size), 0
                ) + step * tile == lax.broadcasted_iota(jnp.int32, (tile, size), 1)
                total = jnp.where(same, newton_first, 0.0) + mix
                total_ref[rows, :] = total
                total_half_ref[later, rows, :] = total.astype(jnp.bfloat16)

        @pl.loop(0, size // tile)
        def _(step):
            rows = rows_of(step)
            mix = mix_ref[rows, :]
            if newton_step > 0:
                total = newton_first * total_ref[rows, :] + times(mix, total_half_ref[now])
                if newton_step == NS_STEPS - 1:
                    out_ref[rows, :] = times(
                        (total * column_scale).astype(jnp.bfloat16), own_ref[...]
                    ).astype(jnp.bfloat16)
                else:
                    total_ref[rows, :] = total
                    total_half_ref[later, rows, :] = total.astype(jnp.bfloat16)
            if newton_step < NS_STEPS - 1:
                left = newton_first * gram_ref[rows, :] + times(mix, gram_half_ref[now])
                gram = newton_first * left + times(left.astype(jnp.bfloat16), mix_ref[...])
                gram_ref[rows, :] = gram
                gram_half_ref[later, rows, :] = gram.astype(jnp.bfloat16)


def newton(low_blocks, high_blocks, own, paired, enc_rows, dec_rows):
    size, width = own.shape
    whole = pl.BlockSpec(memory_space=pltpu.VMEM)
    return pl.pallas_call(
        functools.partial(newton_kernel, enc_rows, dec_rows),
        in_specs=[pl.BlockSpec(memory_space=pltpu.SMEM)] + [whole] * 3,
        out_specs=whole,
        out_shape=jax.ShapeDtypeStruct((size, width), jnp.bfloat16),
        scratch_shapes=[
            pltpu.VMEM((size, size), jnp.float32),
            pltpu.VMEM((size, size), jnp.float32),
            pltpu.VMEM((size, size), jnp.bfloat16),
            pltpu.VMEM((2, size, size), jnp.bfloat16),
            pltpu.VMEM((2, size, size), jnp.bfloat16),
        ],
        compiler_params=pltpu.CompilerParams(vmem_limit_bytes=newton_vmem),
        cost_estimate=pl.CostEstimate(
            flops=36 * size * size * size, bytes_accessed=20 * size * size, transcendentals=0
        ),
        name="newton",
    )(paired.astype(jnp.int32).reshape(1), low_blocks, high_blocks, own)


def gram_sum(gram):
    size = gram.shape[0] // 4

    def packed(places):
        return jnp.concatenate(
            [gram[i * size : (i + 1) * size, j * size : (j + 1) * size] for i, j in places],
            axis=0,
        )

    lower_core = lax.axis_index("mp") % 2 == 0
    low_blocks, high_blocks = packed(low_set), packed(high_set)
    own = jnp.where(lower_core, low_blocks, high_blocks)
    own = own + core_swap(jnp.where(lower_core, high_blocks, low_blocks))
    own = own + far_swap(own)
    other = core_swap(own)
    return jnp.where(lower_core, own, other), jnp.where(lower_core, other, own)


enc_slots = (2, 5, 3, 4, 7)
dec_slots = (0, 6)


def slot_rows(enc_rows_half, dec_rows_half, enc_widths, dec_widths, slot_width, data_ranks):
    enc_parts = split_columns(enc_rows_half, enc_widths)
    dec_parts = split_columns(dec_rows_half, dec_widths)
    half_width = slot_width // 2

    def widened(part, width):
        return jnp.pad(part, ((0, 0), (0, width - part.shape[1])))

    empty = jnp.zeros((enc_rows_half.shape[0], slot_width), enc_rows_half.dtype)
    slots = [empty] * data_ranks
    for part, slot in zip(enc_parts, enc_slots):
        slots[slot] = widened(part, slot_width)
    for place, slot in enumerate(dec_slots):
        upper = jnp.pad(widened(dec_parts[2 * place], half_width), ((0, 0), (0, half_width)))
        lower = jnp.pad(widened(dec_parts[2 * place + 1], half_width), ((0, 0), (half_width, 0)))
        slots[slot] = jnp.concatenate([upper, lower], axis=0)
    return jnp.stack(slots)


def unslot(rows_back, enc_widths, dec_widths, dec_rows):
    slot_width = rows_back.shape[2]
    enc_results = [rows_back[slot][:, :width] for slot, width in zip(enc_slots, enc_widths)]
    dec_results = []
    for place, width in enumerate(dec_widths):
        slot = rows_back[dec_slots[place // 2]]
        odd = place % 2
        dec_results.append(
            slot[
                odd * dec_rows : (odd + 1) * dec_rows,
                odd * (slot_width // 2) : odd * (slot_width // 2) + width,
            ]
        )
    return enc_results, dec_results


def apply_step(master, ortho_rows, widths, model_width, rate, model_ranks):
    steps_all = [
        orthogonal * (0.2 * math.sqrt(max(model_width, piece_width * model_ranks)))
        for orthogonal, piece_width in zip(ortho_rows, widths)
    ]
    return master * (1.0 - rate * decay_rate) - rate * jnp.concatenate(steps_all, axis=1)


def local(
    patches,
    cotangent,
    item_lengths,
    enc_master,
    dec_master,
    enc_norms,
    dec_norms,
    enc_moment,
    dec_moment,
    enc_norm_moment,
    dec_norm_moment,
):
    model_ranks = lax.axis_size("mp")
    data_ranks = lax.axis_size("dp")
    enc_widths = [
        3 * D // model_ranks,
        D // model_ranks,
        FF // model_ranks,
        FF // model_ranks,
        DD // model_ranks,
    ]
    dec_widths = [3 * DD // model_ranks, DD // model_ranks, DFF // model_ranks, DFF // model_ranks]
    first_cols = enc_widths[0] + enc_widths[1]
    norm_parts = gather_small(
        jnp.concatenate([enc_norms, dec_norms], axis=1).astype(jnp.bfloat16)
    ).astype(jnp.float32)
    enc_share, dec_share = enc_norms.shape[1], dec_norms.shape[1]
    enc_norm_values = jnp.moveaxis(norm_parts[:, :, :enc_share], 0, 1).reshape(4, D)
    dec_norm_values = jnp.moveaxis(norm_parts[:, :, enc_share:], 0, 1).reshape(4, DD)
    enc_half = enc_master.astype(jnp.bfloat16)
    up_cols = first_cols + enc_widths[2]
    first_gather = Gather(enc_half[:, :first_cols])
    up_gather = Gather(after(enc_half[:, first_cols:up_cols], first_gather.lined))
    rest_gather = Gather(after(enc_half[:, up_cols:], up_gather.lined))
    dec_low = lax.all_gather(
        after(dec_master.astype(jnp.bfloat16), rest_gather.lined), "dp", axis=0, tiled=True
    )
    enc_pieces = split_columns(first_gather.result(), enc_widths[:2])
    dec_pieces = split_columns(dec_low, dec_widths)
    model_rank = lax.axis_index("mp")
    core = model_rank % 2
    upper_chip = model_rank // 2
    row_count = patches.shape[0]
    enc_rows = enc_master.shape[0]
    dec_rows = dec_master.shape[0]
    chunk_count = 2
    chunk_rows = row_count // chunk_count
    own_count = chunk_rows // 2
    segment, live_mask = segments_of(item_lengths[0], row_count)
    segment = swap_halves(segment, chunk_rows, core)
    live_mask = swap_halves(live_mask, chunk_rows, core)
    inputs = swap_halves(patches, chunk_rows, core)
    upstream = swap_halves(cotangent, chunk_rows, core) * live_mask.astype(jnp.bfloat16)[:, None]

    def chunked(array):
        return [array[k * chunk_rows : (k + 1) * chunk_rows] for k in range(chunk_count)]

    slot_width = max(enc_widths)

    def to_owners(enc_part, dec_part):
        slots = slot_rows(
            enc_part.astype(jnp.bfloat16),
            dec_part.astype(jnp.bfloat16),
            enc_widths,
            dec_widths,
            slot_width,
            data_ranks,
        )
        moved = lax.all_to_all(slots, "dp", 0, 0)
        return moved.reshape(-1, slot_width)

    input_chunks = [chunk.astype(jnp.float32) for chunk in chunked(inputs)]
    normals_all = [normalize(chunk) for chunk in input_chunks]
    enc_firsts = [(normal[:own_count], inverse[:own_count]) for normal, inverse in normals_all]
    enc_halves = [
        (normal * enc_norm_values[0] + enc_norm_values[1]).astype(jnp.bfloat16)
        for normal, _ in normals_all
    ]
    late_pieces = {}

    def enc_forward_hook(name, values):
        if name == "input":
            values = up_gather.turn(values)
        if name == "heads":
            values = rest_gather.turn(values)
        if name == "middle":
            down_low, bridge = split_columns(rest_gather.result(), enc_widths[3:])
            enc_pieces.extend([up_gather.result(), down_low, bridge])
            late_pieces["bridge"] = whole_bridge(bridge)
        return values

    def whole_bridge(bridge):
        bridge_far = far_swap(bridge)
        bridge_pair = jnp.where(
            upper_chip == 0, jnp.stack([bridge, bridge_far]), jnp.stack([bridge_far, bridge])
        )
        pair_other = core_swap(bridge_pair)
        bridge_all = jnp.stack(
            [
                jnp.where(core == 0, bridge_pair, pair_other),
                jnp.where(core == 0, pair_other, bridge_pair),
            ],
            axis=1,
        )
        share_width = bridge.shape[1]
        return jnp.moveaxis(bridge_all.reshape(-1, D, share_width), 0, 1).reshape(D, DD)

    encoded, enc_saved = block_forward(
        [chunk[:own_count] for chunk in input_chunks],
        enc_halves,
        segment,
        enc_pieces,
        enc_norm_values,
        HD,
        enc_forward_hook,
    )
    bridge_all = late_pieces["bridge"]
    encoded_own = [chunk.astype(jnp.bfloat16) for chunk in encoded]
    decoder_in = [
        jnp.dot(chunk, bridge_all, preferred_element_type=jnp.float32)
        .astype(jnp.bfloat16)
        .astype(jnp.float32)
        for chunk in encoded_own
    ]
    encoded_halves = [both_halves(chunk) for chunk in encoded_own]
    dec_firsts, dec_halves = attention_input(decoder_in, dec_norm_values)
    decoded, dec_saved = block_forward(
        decoder_in,
        dec_halves,
        segment,
        dec_pieces,
        dec_norm_values,
        DHD,
        lambda name, values: values,
    )
    old_enc, old_dec, _ = lax.optimization_barrier((enc_moment, dec_moment, encoded_own[0]))
    old_slots = to_owners(old_enc, old_dec)
    upstream_halves = chunked(upstream)
    dec_in_grads, dec_groups, dec_norm_grads = block_backward(
        [half[:own_count].astype(jnp.float32) for half in upstream_halves],
        upstream_halves,
        dec_saved,
        dec_firsts,
        dec_pieces,
        dec_norm_values,
        segment,
        DHD,
        lambda name, values, group: values,
    )
    dec_scatter = Scatter(dec_groups)
    bridge_halves = [both_halves(grad.astype(jnp.bfloat16)) for grad in dec_in_grads]
    bridge_halves, old_slots = lax.optimization_barrier((bridge_halves, old_slots))
    encoded_grads = [
        jnp.einsum("tf,df->td", half, bridge_all, preferred_element_type=jnp.float32)
        for half in bridge_halves
    ]
    share_width = enc_widths[4]
    bridge_in_grad = [
        lax.dynamic_slice_in_dim(half, model_rank * share_width, share_width, 1)
        for half in bridge_halves
    ]
    scatters = {}

    def enc_hook(name, values, group):
        if name == "start":
            scatters["down"] = Scatter([group, (encoded_halves, bridge_in_grad)])
        if name == "sums":
            values = dec_scatter.turn(values)
            scatters["up"] = Scatter([group])
        if name == "middle":
            values = dec_scatter.turn(values)
            values = scatters["down"].turn(values)
            scatters["out"] = group
        if name == "mixed":
            values = scatters["down"].turn(values)
            values = scatters["up"].turn(values)
            scatters["late"] = Scatter([group, scatters["out"]])
        return values

    input_grads, _, enc_norm_grads = block_backward(
        [grad[:own_count] for grad in encoded_grads],
        [grad.astype(jnp.bfloat16) for grad in encoded_grads],
        enc_saved,
        enc_firsts,
        enc_pieces[:4],
        enc_norm_values,
        segment,
        HD,
        enc_hook,
    )
    dec_sum_rows = dec_scatter.result()
    up_rows = scatters["up"].result()
    down_rows, bridge_rows = split_columns(scatters["down"].result(), enc_widths[3:])

    half_width = slot_width // 2
    half_rows = [
        jnp.pad(part, ((0, 0), (0, half_width - part.shape[1])))
        for part in split_columns(dec_sum_rows, dec_widths)
    ]

    def owned(slots):
        whole = collect({slot: rows.astype(jnp.bfloat16) for slot, rows in slots.items()})
        return jnp.pad(whole, ((0, 0), (0, slot_width - whole.shape[1])))

    wide_slots = owned(
        {
            enc_slots[2]: up_rows,
            enc_slots[3]: down_rows,
            dec_slots[0]: jnp.concatenate(half_rows[:2], axis=0),
            dec_slots[1]: jnp.concatenate(half_rows[2:], axis=0),
        }
    )

    def natural(own_chunks):
        return swap_halves(
            jnp.concatenate([both_halves(own) for own in own_chunks], axis=0), chunk_rows, core
        )

    decoded = natural(decoded)
    input_grad = natural(input_grads)

    qkv_rows, out_rows = split_columns(scatters["late"].result(), enc_widths[:2])
    enc_sum_rows = jnp.concatenate([qkv_rows, out_rows, up_rows, down_rows, bridge_rows], axis=1)
    norm_sums = sum_everywhere(jnp.concatenate([enc_norm_grads, dec_norm_grads], axis=1))
    data_rank = lax.axis_index("dp")
    enc_norm_rows = lax.dynamic_slice_in_dim(norm_sums[:, :D], data_rank * enc_share, enc_share, 1)
    dec_norm_rows = lax.dynamic_slice_in_dim(norm_sums[:, D:], data_rank * dec_share, dec_share, 1)
    local_sum = jnp.sum(enc_sum_rows * enc_sum_rows) + jnp.sum(dec_sum_rows * dec_sum_rows)
    squares = sum_everywhere(jnp.full((8, 128), local_sum))[0, 0] + jnp.sum(norm_sums * norm_sums)
    (qkv_rows, out_rows), wide_slots = lax.optimization_barrier(((qkv_rows, out_rows), wide_slots))
    late_slots = owned({enc_slots[0]: qkv_rows, enc_slots[1]: out_rows, enc_slots[4]: bridge_rows})
    data_rank = lax.axis_index("dp")

    def is_rank(*slots):
        return functools.reduce(jnp.logical_or, [data_rank == slot for slot in slots])

    lower_row = (jnp.arange(wide_slots.shape[0], dtype=jnp.int32) % enc_rows >= dec_rows)[:, None]
    shifted = jnp.where(
        lower_row, jnp.roll(wide_slots, half_width, axis=1), wide_slots
    )
    grad_slots = jnp.where(
        is_rank(*enc_slots[2:4]),
        wide_slots,
        jnp.where(is_rank(*dec_slots), shifted, late_slots),
    )
    grad_norm = jnp.sqrt(squares)
    factor = clip_bound * lax.rsqrt(squares + 1e-06)
    enc_grad = enc_sum_rows * factor
    dec_grad = dec_sum_rows * factor
    enc_norm_grad = enc_norm_rows * factor
    dec_norm_grad = dec_norm_rows * factor
    dec_shift_grad = dec_norm_grad[3]
    enc_moment_new = momentum_keep * enc_moment + enc_grad
    dec_moment_new = momentum_keep * dec_moment + dec_grad
    enc_norm_moment_new = momentum_keep * enc_norm_moment + enc_norm_grad
    dec_norm_moment_new = momentum_keep * dec_norm_moment + dec_norm_grad
    own = (
        momentum_keep * old_slots.astype(jnp.float32)
        + factor * grad_slots.astype(jnp.float32)
    ).astype(jnp.bfloat16)
    low_blocks, high_blocks = gram_sum(
        lax.dot_general(own, own, (((1,), (1,)), ((), ())), preferred_element_type=jnp.float32)
    )
    orthogonal = newton(low_blocks, high_blocks, own, is_rank(*dec_slots), enc_rows, dec_rows)
    rows_back = lax.all_to_all(
        orthogonal.reshape(data_ranks, enc_rows, slot_width), "dp", 0, 0
    ).astype(jnp.float32)
    enc_results, dec_results = unslot(rows_back, enc_widths, dec_widths, dec_rows)
    enc_master_new = apply_step(enc_master, enc_results, enc_widths, D, rate_enc, model_ranks)
    dec_master_new = apply_step(dec_master, dec_results, dec_widths, DD, rate_dec, model_ranks)
    enc_norms_new = enc_norms - rate_norm * enc_norm_moment_new
    dec_norms_new = dec_norms - rate_norm * dec_norm_moment_new
    return (
        decoded,
        input_grad,
        enc_grad,
        dec_grad,
        enc_norm_grad,
        dec_norm_grad,
        dec_shift_grad,
        enc_moment_new,
        dec_moment_new,
        enc_norm_moment_new,
        dec_norm_moment_new,
        enc_master_new,
        dec_master_new,
        enc_norms_new,
        dec_norms_new,
        enc_master_new.astype(jnp.bfloat16),
        dec_master_new.astype(jnp.bfloat16),
        enc_norms_new.astype(jnp.bfloat16),
        dec_norms_new.astype(jnp.bfloat16),
        grad_norm,
    )


def solution(mesh):
    return jax.shard_map(
        local,
        mesh=mesh,
        in_specs=(
            P("dp", None),
            P("dp", None),
            P("dp", None),
            P("dp", "mp"),
            P("dp", "mp"),
            P(None, "dp"),
            P(None, "dp"),
            P("dp", "mp"),
            P("dp", "mp"),
            P(None, "dp"),
            P(None, "dp"),
        ),
        out_specs=(
            P("dp", None),
            P("dp", None),
            P("dp", "mp"),
            P("dp", "mp"),
            P(None, "dp"),
            P(None, "dp"),
            P("dp"),
            P("dp", "mp"),
            P("dp", "mp"),
            P(None, "dp"),
            P(None, "dp"),
            P("dp", "mp"),
            P("dp", "mp"),
            P(None, "dp"),
            P(None, "dp"),
            P("dp", "mp"),
            P("dp", "mp"),
            P(None, "dp"),
            P(None, "dp"),
            P(),
        ),
        check_vma=False,
    )
```

time: 908 us -> 708 us (0.78)
  waiting for transfers between devices: 429 us -> 250 us
  matrix products: 187 us -> 41.9 us
  Pallas kernels: 0 us -> 109 us
  starting transfers between devices: 52.3 us -> 136 us
  blocking collectives: 47.9 us -> 0 us
  local copies, waits for them, and re-layouts: 50.1 us -> 37.1 us
    dot_general x54 -> x0, matrix products: 134 us -> none  [the longest x5 19 us: gram_newton(): square = jnp.dot(gram_half, gram_half, preferred_element_type=jnp.float32)]
    reduce_scatter x3 -> x0, waiting for transfers between devices: 120 us -> none  [scattered(): lax.psum_scatter(jnp.concatenate(parts, axis=1), 'dp', scatter_dimension=...]
    pallas_call x0 -> x16, Pallas kernels: none -> 109 us  [the longest x1 47.7 us: newton(): pl.pallas_call(functools.partial(newton_kernel, enc_rows, dec_rows), in_s...]
    psum x1 -> x0, waiting for transfers between devices: 84.6 us -> none  [local(): lax.psum(lax.dot_general(own, own, (((1,), (1,)), ((), ())), preferred_el...]
    ppermute x65 -> x101, waiting for transfers between devices: 141 us -> 208 us  [pair_swap(): lax.ppermute(array, axis, [(rank, rank ^ bit) for rank in range(size)])]
    all_gather x3 -> x1, waiting for transfers between devices: 52.5 us -> 0.01 us  [local(): lax.all_gather(after(dec_master.astype(jnp.bfloat16), rest_gather.lined),...]
    all_to_all x1 -> x0, blocking collectives: 47.9 us -> none  [local(): lax.all_to_all(slots, 'dp', 0, 0).reshape(data_ranks * enc_rows, slot_width)]
    ppermute x65 -> x101, starting transfers between devices: 45.7 us -> 83.4 us  [pair_swap(): lax.ppermute(array, axis, [(rank, rank ^ bit) for rank in range(size)])]
  transfers between devices with their start and end apart: 73 -> 118, of which waited for: 39 -> 42; matrix products, arithmetic and copies ran while one was open for 22% -> 21% of each run, Pallas kernels for 0% -> 9%
where the time goes in v3:
time: 708 us; the launch traced here: 703 us
  waiting for transfers between devices  250 us (35%)
  starting transfers between devices  136 us (19%)
  Pallas kernels  109 us (15%)
  other arithmetic  107 us (15%)
  matrix products  41.9 us (6%)
  local copies, waits for them, and re-layouts  37.1 us (5%)
  between operations  21.9 us (3%)
    ppermute x101, waiting for transfers between devices, pair_swap(): lax.ppermute(array, axis, [(rank, rank ^ bit) for rank in range(size)])  208 us
    ppermute x101, starting transfers between devices, pair_swap(): lax.ppermute(array, axis, [(rank, rank ^ bit) for rank in range(size)])  83.4 us
    pallas_call x1, Pallas kernels, newton(): pl.pallas_call(functools.partial(newton_kernel, enc_rows, dec_rows), in_s...  47.7 us
    ppermute x14, starting transfers between devices, collect(): lax.ppermute(value, 'dp', [(owner ^ bit, owner) for owner in padded])  34.5 us
    all_to_all x1, waiting for transfers between devices, local(): lax.all_to_all(orthogonal.reshape(data_ranks, enc_rows, slot_width), 'dp'...  29.8 us
    pallas_call x2, Pallas kernels, attend_backward(): pl.pallas_call(functools.partial(attend_backward_kernel, head_width), gri...  26.2 us
    unnamed x322, local copies, waits for them, and re-layouts  19 us
    pallas_call x4, Pallas kernels, attend_forward(): pl.pallas_call(functools.partial(attend_forward_kernel, head_width), grid...  15.2 us
  transfers between devices with their start and end apart: 118, of which 42 were waited for; matrix products, arithmetic and copies ran while one was open for 21% of the time, Pallas kernels for 9%

profile of v3, /device:TPU:0, one launch (start us, length us, event | category | flops | bytes accessed | tf_op | source)
XLA Modules:
  0.0 702.5 jit_solution(8051634183968215659)
XLA Ops:
  43.6 5.0 add_convert_fusion.4
  52.3 8.5 %collective-permute-done.7.refs_4_ = bf16[128,1024]{1,0:T(8,128)(2,1)S(1)} collective-permute-done((bf16[128,1024]{1,0:T(8,128)(2,1)S(1)}, bf16[128,1024]{1,0:T(8,128)(2,1)S(1)}, u32[]{:S(2)}, u32[]{:S(2)}) %collective-permute-start.7) | collective-permute-done | bytes 262176 | tf_op jit(solution)/shard_map/ppermute | solution.py:46
  80.7 7.0 %collective-permute-done.14.refs_4_ = bf16[128,1152]{1,0:T(8,128)(2,1)} collective-permute-done((bf16[128,1152]{1,0:T(8,128)(2,1)S(1)}, bf16[128,1152]{1,0:T(8,128)(2,1)}, u32[]{:S(2)}, u32[]{:S(2)}) %collective-permute-start.14) | collective-permute-done | bytes 294944 | tf_op jit(solution)/shard_map/ppermute | solution.py:46
  125.5 8.5 %collective-permute-done.17 = bf16[256,1024]{1,0:T(8,128)(2,1)S(1)} collective-permute-done((bf16[256,1024]{1,0:T(8,128)(2,1)S(1)}, bf16[256,1024]{1,0:T(8,128)(2,1)S(1)}, u32[]{:S(2)}, u32[]{:S(2)}) %collective-permute-start.17) | collective-permute-done | bytes 524320 | tf_op jit(solution)/shard_map/ppermute | solution.py:46
  147.3 4.7 multiply_convert_fusion.1
  173.1 8.1 %collective-permute-done.28 = bf16[256,1024]{1,0:T(8,128)(2,1)S(1)} collective-permute-done((bf16[256,1024]{1,0:T(8,128)(2,1)S(1)}, bf16[256,1024]{1,0:T(8,128)(2,1)S(1)}, u32[]{:S(2)}, u32[]{:S(2)}) %collective-permute-start.28) | collective-permute-done | bytes 524320 | tf_op jit(solution)/shard_map/ppermute | solution.py:46
  182.5 9.5 %collective-permute-done.36 = bf16[256,1024]{1,0:T(8,128)(2,1)S(1)} collective-permute-done((bf16[256,1024]{1,0:T(8,128)(2,1)S(1)}, bf16[256,1024]{1,0:T(8,128)(2,1)S(1)}, u32[]{:S(2)}, u32[]{:S(2)}) %collective-permute-start.36) | collective-permute-done | bytes 524320 | tf_op jit(solution)/shard_map/ppermute | solution.py:46
  219.7 6.2 collective-permute-done.39
  226.3 4.8 collective-permute-done.45
  233.2 7.2 %all-to-all-start = ((bf16[8,128,1024]{2,1,0:T(8,128)(2,1)}), bf16[8,128,1024]{2,1,0:T(8,128)(2,1)}, u32[]{:S(2)}, u32[]{:S(2)}) async-start(bf16[8,128,1024]{2,1,0:T(8,128)(2,1)} %bitcast_dynamic-update-slice_fusion), calls=%async_computation | async-start | bytes 4194304 | tf_op jit(solution)/shard_map/all_to_all | solution.py:875
  258.8 5.6 collective-permute-done.48
  264.4 5.6 collective-permute-done.54
  280.6 12.5 %attend_backward.2.refs_1_ = bf16[1024,384]{1,0:T(8,128)(2,1)S(1)} custom-call(s32[1024,1]{1,0:T(8,128)S(1)} %copy-done.29, s32[1,1024]{1,0:T(1,128)S(1)} %reshape_reshape.4.key_segment_ref.query_segment_ref, bf16[1024,128]{1,0:T(8,128)(2,1)S(1)} %pad_maximum_fusion.19.grad_ref, f32[4,1024]{1,0:T(4,128)S(1)} %pad_maximum_fusion.20.logsum_ref, ...), custom_call_target="tpu_custom_call" | custom-call | flops 5368709120 | bytes 1835008 | tf_op jit(solution)/shard_map/attend_backward/pallas_call | solution.py:414
  299.5 5.1 collective-permute-done.60
  305.0 4.6 collective-permute-done.57
  341.1 7.2 %collective-permute-done.65 = bf16[256,1024]{1,0:T(8,128)(2,1)S(1)} collective-permute-done((bf16[256,1024]{1,0:T(8,128)(2,1)S(1)}, bf16[256,1024]{1,0:T(8,128)(2,1)S(1)}, u32[]{:S(2)}, u32[]{:S(2)}) %collective-permute-start.65) | collective-permute-done | bytes 524320 | tf_op jit(solution)/shard_map/ppermute | solution.py:46
  348.4 10.2 %collective-permute-done.63 = bf16[256,1024]{1,0:T(8,128)(2,1)S(1)} collective-permute-done((bf16[256,1024]{1,0:T(8,128)(2,1)S(1)}, bf16[256,1024]{1,0:T(8,128)(2,1)S(1)}, u32[]{:S(2)}, u32[]{:S(2)}) %collective-permute-start.63) | collective-permute-done | bytes 524320 | tf_op jit(solution)/shard_map/ppermute | solution.py:46
  368.2 5.4 collective-permute-done.69
  382.8 13.7 %attend_backward.3.refs_1_ = bf16[1024,768]{1,0:T(8,128)(2,1)S(1)} custom-call(s32[1024,1]{1,0:T(8,128)S(1)} %copy-done.30, s32[1,1024]{1,0:T(1,128)S(1)} %reshape_reshape.4.key_segment_ref.query_segment_ref, bf16[1024,256]{1,0:T(8,128)(2,1)S(1)} %pad_maximum_fusion.18.grad_ref, f32[4,1024]{1,0:T(4,128)S(1)} %pad_maximum_fusion.21.logsum_ref, ...), custom_call_target="tpu_custom_call" | custom-call | flops 10737418240 | bytes 3670016 | tf_op jit(solution)/shard_map/attend_backward/pallas_call | solution.py:414
  407.8 11.9 %collective-permute-done.86 = bf16[128,1152]{1,0:T(8,128)(2,1)S(1)} collective-permute-done((bf16[128,1152]{1,0:T(8,128)(2,1)S(1)}, bf16[128,1152]{1,0:T(8,128)(2,1)S(1)}, u32[]{:S(2)}, u32[]{:S(2)}) %collective-permute-start.86) | collective-permute-done | bytes 294944 | tf_op jit(solution)/shard_map/ppermute | solution.py:46
  429.0 10.6 %collective-permute-done.85 = bf16[128,1024]{1,0:T(8,128)(2,1)S(1)} collective-permute-done((bf16[128,1024]{1,0:T(8,128)(2,1)S(1)}, bf16[128,1024]{1,0:T(8,128)(2,1)S(1)}, u32[]{:S(2)}, u32[]{:S(2)}) %collective-permute-start.85) | collective-permute-done | bytes 262176 | tf_op jit(solution)/shard_map/ppermute | solution.py:46
  440.7 6.1 collective-permute-start.100
  463.7 11.4 %collective-permute-done.83 = bf16[128,1024]{1,0:T(8,128)(2,1)S(1)} collective-permute-done((bf16[128,1024]{1,0:T(8,128)(2,1)S(1)}, bf16[128,1024]{1,0:T(8,128)(2,1)S(1)}, u32[]{:S(2)}, u32[]{:S(2)}) %collective-permute-start.83) | collective-permute-done | bytes 262176 | tf_op jit(solution)/shard_map/ppermute | solution.py:46
  479.1 5.4 collective-permute-start.103
  491.8 8.7 %collective-permute-done.98.refs_1_ = bf16[128,1024]{1,0:T(8,128)(2,1)S(1)} collective-permute-done((bf16[128,1024]{1,0:T(8,128)(2,1)S(1)}, bf16[128,1024]{1,0:T(8,128)(2,1)S(1)}, u32[]{:S(2)}, u32[]{:S(2)}) %collective-permute-start.98) | collective-permute-done | bytes 262176 | tf_op jit(solution)/shard_map/ppermute | solution.py:161
  500.9 4.6 collective-permute-done.97
  507.8 4.5 collective-permute-start.106
  520.8 5.4 collective-permute-start.109
  543.0 30.3 %collective-permute-done.113 = f32[1280,256]{1,0:T(8,128)S(1)} collective-permute-done((f32[1280,256]{1,0:T(8,128)S(1)}, f32[1280,256]{1,0:T(8,128)S(1)}, u32[]{:S(2)}, u32[]{:S(2)}) %collective-permute-start.113) | collective-permute-done | bytes 1310752 | tf_op jit(solution)/shard_map/ppermute | solution.py:46
  581.0 47.7 %newton.1 = bf16[1024,1024]{1,0:T(8,128)(2,1)} custom-call(s32[1]{0:T(128)} %bitcast.51.paired_ref, f32[1280,256]{1,0:T(8,128)S(1)} %get-tuple-element.223.low_ref, f32[1280,256]{1,0:T(8,128)S(1)} %get-tuple-element.222.high_ref, bf16[1024,1024]{1,0:T(8,128)(2,1)} %copy-done.115), custom_call_target="tpu_custom_call" | custom-call | flops 38654705664 | bytes 20971520 | tf_op jit(solution)/shard_map/newton/pallas_call | solution.py:721
  628.7 10.4 %all-to-all-start.1 = ((bf16[8,128,1024]{2,1,0:T(8,128)(2,1)}), bf16[8,128,1024]{2,1,0:T(8,128)(2,1)}, u32[]{:S(2)}, u32[]{:S(2)}) async-start(bf16[8,128,1024]{2,1,0:T(8,128)(2,1)} %bitcast.52), calls=%async_computation.1 | async-start | bytes 4194304 | tf_op jit(solution)/shard_map/all_to_all | solution.py:1071
  657.9 29.8 %all-to-all-done.1 = bf16[8,128,1024]{2,1,0:T(8,128)(2,1)} async-done(((bf16[8,128,1024]{2,1,0:T(8,128)(2,1)}), bf16[8,128,1024]{2,1,0:T(8,128)(2,1)}, u32[]{:S(2)}, u32[]{:S(2)}) %all-to-all-start.1) | async-done | bytes 2097184 | tf_op jit(solution)/shard_map/all_to_all | solution.py:1071
  (836 shorter events, 354.5 us)
Async XLA Ops:
  7.2 196.1 %all-gather.2.cloned.1.call-start = ((), (), s32[]{:S(2)}) async-start(), calls=%async_computation.2 | async-start | bytes 1769472 | tf_op jit(solution)/shard_map/all_gather | solution.py:841
  9.7 29.3 %collective-permute-start.3 = (bf16[128,1024]{1,0:T(8,128)(2,1)S(1)}, bf16[128,1024]{1,0:T(8,128)(2,1)S(1)}, u32[]{:S(2)}, u32[]{:S(2)}) collective-permute-start(bf16[128,1024]{1,0:T(8,128)(2,1)S(1)} %get-tuple-element.242.refs_0_), channel_id=1, source_target_pairs={{0,8},{4,12},{8,0},{12,4},{16,24},{20,28},{24,16},{28,20},{1,9},{5... | collective-permute-start | bytes 786440 | tf_op jit(solution)/shard_map/ppermute | solution.py:46
  12.7 26.3 %collective-permute-start.4 = (bf16[128,1024]{1,0:T(8,128)(2,1)S(1)}, bf16[128,1024]{1,0:T(8,128)(2,1)S(1)}, u32[]{:S(2)}, u32[]{:S(2)}) collective-permute-start(bf16[128,1024]{1,0:T(8,128)(2,1)S(1)} %get-tuple-element.242.refs_0_), channel_id=1, source_target_pairs={{0,16},{4,20},{8,24},{12,28},{16,0},{20,4},{24,8},{28,12},{1,17},{... | collective-permute-start | bytes 786440 | tf_op jit(solution)/shard_map/ppermute | solution.py:46
  15.3 23.8 %collective-permute-start.5 = (bf16[128,1024]{1,0:T(8,128)(2,1)S(1)}, bf16[128,1024]{1,0:T(8,128)(2,1)S(1)}, u32[]{:S(2)}, u32[]{:S(2)}) collective-permute-start(bf16[128,1024]{1,0:T(8,128)(2,1)S(1)} %get-tuple-element.242.refs_0_), channel_id=1, source_target_pairs={{0,24},{4,28},{8,16},{12,20},{16,8},{20,12},{24,0},{28,4},{1,25},{... | collective-permute-start | bytes 786440 | tf_op jit(solution)/shard_map/ppermute | solution.py:46
  15.3 49.2 %collective-permute-start.9 = (bf16[128,1024]{1,0:T(8,128)(2,1)S(1)}, bf16[128,1024]{1,0:T(8,128)(2,1)S(1)}, u32[]{:S(2)}, u32[]{:S(2)}) collective-permute-start(bf16[128,1024]{1,0:T(8,128)(2,1)S(1)} %get-tuple-element.242.refs_0_), channel_id=1, source_target_pairs={{0,4},{4,0},{8,12},{12,8},{16,20},{20,16},{24,28},{28,24},{1,5},{5... | collective-permute-start | bytes 786440 | tf_op jit(solution)/shard_map/ppermute | solution.py:46
  65.3 22.4 %collective-permute-start.14 = (bf16[128,1152]{1,0:T(8,128)(2,1)S(1)}, bf16[128,1152]{1,0:T(8,128)(2,1)}, u32[]{:S(2)}, u32[]{:S(2)}) collective-permute-start(bf16[128,1152]{1,0:T(8,128)(2,1)S(1)} %slice.552.refs_0_), channel_id=1, source_target_pairs={{0,16},{4,20},{8,24},{12,28},{16,0},{20,4},{24,8},{28,12},{1,17},{... | collective-permute-start | bytes 884744 | tf_op jit(solution)/shard_map/ppermute | solution.py:46
  66.0 21.7 %collective-permute-start.15 = (bf16[128,1152]{1,0:T(8,128)(2,1)S(1)}, bf16[128,1152]{1,0:T(8,128)(2,1)}, u32[]{:S(2)}, u32[]{:S(2)}) collective-permute-start(bf16[128,1152]{1,0:T(8,128)(2,1)S(1)} %slice.552.refs_0_), channel_id=1, source_target_pairs={{0,24},{4,28},{8,16},{12,20},{16,8},{20,12},{24,0},{28,4},{1,25},{... | collective-permute-start | bytes 884744 | tf_op jit(solution)/shard_map/ppermute | solution.py:46
  90.6 29.4 %collective-permute-start.16 = (bf16[256,1024]{1,0:T(8,128)(2,1)}, bf16[256,1024]{1,0:T(8,128)(2,1)}, u32[]{:S(2)}, u32[]{:S(2)}) collective-permute-start(bf16[256,1024]{1,0:T(8,128)(2,1)} %slice.915), channel_id=1, source_target_pairs={{0,1},{1,0},{2,3},{3,2},{4,5},{5,4},{6,7},{7,6},{8,9},{9,8},{10,11... | collective-permute-start | bytes 1572872 | tf_op jit(solution)/shard_map/ppermute | solution.py:46
  95.7 26.4 %collective-permute-start.33 = (bf16[256,1024]{1,0:T(8,128)(2,1)}, bf16[256,1024]{1,0:T(8,128)(2,1)}, u32[]{:S(2)}, u32[]{:S(2)}) collective-permute-start(bf16[256,1024]{1,0:T(8,128)(2,1)} %fusion.43), channel_id=1, source_target_pairs={{0,2},{1,3},{2,0},{3,1},{4,6},{5,7},{6,4},{7,5},{8,10},{9,11},{10,... | collective-permute-start | bytes 1572872 | tf_op jit(solution)/shard_map/ppermute | solution.py:46
  101.4 36.0 %collective-permute-start.19 = (bf16[128,1024]{1,0:T(8,128)(2,1)S(1)}, bf16[128,1024]{1,0:T(8,128)(2,1)S(1)}, u32[]{:S(2)}, u32[]{:S(2)}) collective-permute-start(bf16[128,1024]{1,0:T(8,128)(2,1)S(1)} %get-tuple-element.77.refs_0_), channel_id=1, source_target_pairs={{0,4},{4,0},{8,12},{12,8},{16,20},{20,16},{24,28},{28,24},{1,5},{5... | collective-permute-start | bytes 786440 | tf_op jit(solution)/shard_map/ppermute | solution.py:46
  107.7 31.4 %collective-permute-start.20 = (bf16[128,1024]{1,0:T(8,128)(2,1)S(1)}, bf16[128,1024]{1,0:T(8,128)(2,1)}, u32[]{:S(2)}, u32[]{:S(2)}) collective-permute-start(bf16[128,1024]{1,0:T(8,128)(2,1)S(1)} %copy-done.38), channel_id=1, source_target_pairs={{0,4},{4,0},{8,12},{12,8},{16,20},{20,16},{24,28},{28,24},{1,5},{5... | collective-permute-start | bytes 786440 | tf_op jit(solution)/shard_map/ppermute | solution.py:46
  114.0 25.1 %collective-permute-start.21 = (bf16[128,1024]{1,0:T(8,128)(2,1)}, bf16[128,1024]{1,0:T(8,128)(2,1)}, u32[]{:S(2)}, u32[]{:S(2)}) collective-permute-start(bf16[128,1024]{1,0:T(8,128)(2,1)} %copy-done.39), channel_id=1, source_target_pairs={{0,4},{4,0},{8,12},{12,8},{16,20},{20,16},{24,28},{28,24},{1,5},{5... | collective-permute-start | bytes 786440 | tf_op jit(solution)/shard_map/ppermute | solution.py:46
  168.2 23.8 %collective-permute-start.36 = (bf16[256,1024]{1,0:T(8,128)(2,1)S(1)}, bf16[256,1024]{1,0:T(8,128)(2,1)S(1)}, u32[]{:S(2)}, u32[]{:S(2)}) collective-permute-start(bf16[256,1024]{1,0:T(8,128)(2,1)S(1)} %fusion.42), channel_id=1, source_target_pairs={{0,2},{1,3},{2,0},{3,1},{4,6},{5,7},{6,4},{7,5},{8,10},{9,11},{10,... | collective-permute-start | bytes 1572872 | tf_op jit(solution)/shard_map/ppermute | solution.py:46
  182.3 69.6 %collective-permute-start.70 = (bf16[256,1024]{1,0:T(8,128)(2,1)}, bf16[256,1024]{1,0:T(8,128)(2,1)}, u32[]{:S(2)}, u32[]{:S(2)}) collective-permute-start(bf16[256,1024]{1,0:T(8,128)(2,1)} %add_convert_fusion.12), channel_id=1, source_target_pairs={{0,1},{1,0},{2,3},{3,2},{4,5},{5,4},{6,7},{7,6},{8,9},{9,8},{10,11... | collective-permute-start | bytes 1572872 | tf_op jit(solution)/shard_map/ppermute | solution.py:46
  193.1 83.2 %collective-permute-start.71 = (bf16[256,1024]{1,0:T(8,128)(2,1)}, bf16[256,1024]{1,0:T(8,128)(2,1)}, u32[]{:S(2)}, u32[]{:S(2)}) collective-permute-start(bf16[256,1024]{1,0:T(8,128)(2,1)} %add_convert_fusion.10), channel_id=1, source_target_pairs={{0,1},{1,0},{2,3},{3,2},{4,5},{5,4},{6,7},{7,6},{8,9},{9,8},{10,11... | collective-permute-start | bytes 1572872 | tf_op jit(solution)/shard_map/ppermute | solution.py:46
  233.2 81.3 %all-to-all-start = ((bf16[8,128,1024]{2,1,0:T(8,128)(2,1)}), bf16[8,128,1024]{2,1,0:T(8,128)(2,1)}, u32[]{:S(2)}, u32[]{:S(2)}) async-start(bf16[8,128,1024]{2,1,0:T(8,128)(2,1)} %bitcast_dynamic-update-slice_fusion), calls=%async_computation | async-start | bytes 4194304 | tf_op jit(solution)/shard_map/all_to_all | solution.py:875
  331.1 27.7 %collective-permute-start.66 = (bf16[256,1536]{1,0:T(8,128)(2,1)S(1)}, bf16[256,1536]{1,0:T(8,128)(2,1)S(1)}, u32[]{:S(2)}, u32[]{:S(2)}) collective-permute-start(bf16[256,1536]{1,0:T(8,128)(2,1)S(1)} %get-tuple-element.95), channel_id=1, source_target_pairs={{0,4},{4,0},{8,12},{12,8},{16,20},{20,16},{24,28},{28,24},{1,5},{5... | collective-permute-start | bytes 2359304 | tf_op jit(solution)/shard_map/ppermute | solution.py:46
  334.2 24.4 %collective-permute-start.63 = (bf16[256,1024]{1,0:T(8,128)(2,1)S(1)}, bf16[256,1024]{1,0:T(8,128)(2,1)S(1)}, u32[]{:S(2)}, u32[]{:S(2)}) collective-permute-start(bf16[256,1024]{1,0:T(8,128)(2,1)S(1)} %fusion.109), channel_id=1, source_target_pairs={{0,2},{1,3},{2,0},{3,1},{4,6},{5,7},{6,4},{7,5},{8,10},{9,11},{10,... | collective-permute-start | bytes 1572872 | tf_op jit(solution)/shard_map/ppermute | solution.py:46
  340.9 35.9 %collective-permute-start.72 = (bf16[512,1152]{1,0:T(8,128)(2,1)S(1)}, bf16[512,1152]{1,0:T(8,128)(2,1)S(1)}, u32[]{:S(2)}, u32[]{:S(2)}) collective-permute-start(bf16[512,1152]{1,0:T(8,128)(2,1)S(1)} %get-tuple-element.102), channel_id=1, source_target_pairs={{0,4},{4,0},{8,12},{12,8},{16,20},{20,16},{24,28},{28,24},{1,5},{5... | collective-permute-start | bytes 3538952 | tf_op jit(solution)/shard_map/ppermute | solution.py:46
  367.4 35.4 %collective-permute-start.74 = (bf16[512,1024]{1,0:T(8,128)(2,1)S(1)}, bf16[512,1024]{1,0:T(8,128)(2,1)S(1)}, u32[]{:S(2)}, u32[]{:S(2)}) collective-permute-start(bf16[512,1024]{1,0:T(8,128)(2,1)S(1)} %get-tuple-element.110), channel_id=1, source_target_pairs={{0,4},{4,0},{8,12},{12,8},{16,20},{20,16},{24,28},{28,24},{1,5},{5... | collective-permute-start | bytes 3145736 | tf_op jit(solution)/shard_map/ppermute | solution.py:46
  377.2 25.6 %collective-permute-start.73 = (bf16[256,1152]{1,0:T(8,128)(2,1)S(1)}, bf16[256,1152]{1,0:T(8,128)(2,1)S(1)}, u32[]{:S(2)}, u32[]{:S(2)}) collective-permute-start(bf16[256,1152]{1,0:T(8,128)(2,1)S(1)} %constant_dynamic-slice_fusion.8), channel_id=1, source_target_pairs={{0,8},{4,12},{8,0},{12,4},{16,24},{20,28},{24,16},{28,20},{1,9},{5... | collective-permute-start | bytes 1769480 | tf_op jit(solution)/shard_map/ppermute | solution.py:46
  400.4 23.6 %collective-permute-start.81 = (bf16[512,1024]{1,0:T(8,128)(2,1)S(1)}, bf16[512,1024]{1,0:T(8,128)(2,1)S(1)}, u32[]{:S(2)}, u32[]{:S(2)}) collective-permute-start(bf16[512,1024]{1,0:T(8,128)(2,1)S(1)} %get-tuple-element.113), channel_id=1, source_target_pairs={{0,4},{4,0},{8,12},{12,8},{16,20},{20,16},{24,28},{28,24},{1,5},{5... | collective-permute-start | bytes 3145736 | tf_op jit(solution)/shard_map/ppermute | solution.py:46
  403.3 21.8 %collective-permute-start.84 = (bf16[256,1024]{1,0:T(8,128)(2,1)S(1)}, bf16[256,1024]{1,0:T(8,128)(2,1)S(1)}, u32[]{:S(2)}, u32[]{:S(2)}) collective-permute-start(bf16[256,1024]{1,0:T(8,128)(2,1)S(1)} %constant_dynamic-slice_fusion.5), channel_id=1, source_target_pairs={{0,8},{4,12},{8,0},{12,4},{16,24},{20,28},{24,16},{28,20},{1,9},{5... | collective-permute-start | bytes 1572872 | tf_op jit(solution)/shard_map/ppermute | solution.py:46
  424.4 30.5 %collective-permute-start.82 = (bf16[256,1024]{1,0:T(8,128)(2,1)S(1)}, bf16[256,1024]{1,0:T(8,128)(2,1)S(1)}, u32[]{:S(2)}, u32[]{:S(2)}) collective-permute-start(bf16[256,1024]{1,0:T(8,128)(2,1)S(1)} %constant_dynamic-slice_fusion.7), channel_id=1, source_target_pairs={{0,8},{4,12},{8,0},{12,4},{16,24},{20,28},{24,16},{28,20},{1,9},{5... | collective-permute-start | bytes 1572872 | tf_op jit(solution)/shard_map/ppermute | solution.py:46
  426.6 23.1 %collective-permute-start.76 = (bf16[256,1024]{1,0:T(8,128)(2,1)S(1)}, bf16[256,1024]{1,0:T(8,128)(2,1)S(1)}, u32[]{:S(2)}, u32[]{:S(2)}) collective-permute-start(bf16[256,1024]{1,0:T(8,128)(2,1)S(1)} %fusion.113), channel_id=1, source_target_pairs={{0,2},{1,3},{2,0},{3,1},{4,6},{5,7},{6,4},{7,5},{8,10},{9,11},{10,... | collective-permute-start | bytes 1572872 | tf_op jit(solution)/shard_map/ppermute | solution.py:46
  427.4 24.3 %collective-permute-start.79 = (bf16[256,1024]{1,0:T(8,128)(2,1)S(1)}, bf16[256,1024]{1,0:T(8,128)(2,1)S(1)}, u32[]{:S(2)}, u32[]{:S(2)}) collective-permute-start(bf16[256,1024]{1,0:T(8,128)(2,1)S(1)} %fusion.115), channel_id=1, source_target_pairs={{0,2},{1,3},{2,0},{3,1},{4,6},{5,7},{6,4},{7,5},{8,10},{9,11},{10,... | collective-permute-start | bytes 1572872 | tf_op jit(solution)/shard_map/ppermute | solution.py:46
  440.7 38.4 %collective-permute-start.100 = (bf16[128,1024]{1,0:T(8,128)(2,1)}, bf16[128,1024]{1,0:T(8,128)(2,1)S(1)}, u32[]{:S(2)}, u32[]{:S(2)}) collective-permute-start(bf16[128,1024]{1,0:T(8,128)(2,1)} %get-tuple-element.241), channel_id=1, source_target_pairs={{0,12},{28,16},{12,0},{20,24},{1,13},{29,17},{13,1},{21,25},{2,14}... | collective-permute-start | bytes 786440 | tf_op jit(solution)/shard_map/ppermute | solution.py:161
  446.8 37.7 %collective-permute-start.101 = (bf16[128,1024]{1,0:T(8,128)(2,1)}, bf16[128,1024]{1,0:T(8,128)(2,1)S(1)}, u32[]{:S(2)}, u32[]{:S(2)}) collective-permute-start(bf16[128,1024]{1,0:T(8,128)(2,1)} %get-tuple-element.240), channel_id=1, source_target_pairs={{28,12},{0,16},{16,0},{8,24},{29,13},{1,17},{17,1},{9,25},{30,14},... | collective-permute-start | bytes 786440 | tf_op jit(solution)/shard_map/ppermute | solution.py:161
  449.7 37.5 %collective-permute-start.102 = (bf16[128,1024]{1,0:T(8,128)(2,1)}, bf16[128,1024]{1,0:T(8,128)(2,1)S(1)}, u32[]{:S(2)}, u32[]{:S(2)}) collective-permute-start(bf16[128,1024]{1,0:T(8,128)(2,1)} %get-tuple-element.238), channel_id=1, source_target_pairs={{24,12},{4,16},{20,0},{12,24},{25,13},{5,17},{21,1},{13,25},{26,14... | collective-permute-start | bytes 786440 | tf_op jit(solution)/shard_map/ppermute | solution.py:161
  451.7 35.5 %collective-permute-start.99 = (bf16[128,1024]{1,0:T(8,128)(2,1)}, bf16[128,1024]{1,0:T(8,128)(2,1)S(1)}, u32[]{:S(2)}, u32[]{:S(2)}) collective-permute-start(bf16[128,1024]{1,0:T(8,128)(2,1)} %get-tuple-element.239), channel_id=1, source_target_pairs={{4,12},{24,16},{8,0},{16,24},{5,13},{25,17},{9,1},{17,25},{6,14},{... | collective-permute-start | bytes 786440 | tf_op jit(solution)/shard_map/ppermute | solution.py:161
  542.4 30.9 %collective-permute-start.113 = (f32[1280,256]{1,0:T(8,128)S(1)}, f32[1280,256]{1,0:T(8,128)S(1)}, u32[]{:S(2)}, u32[]{:S(2)}) collective-permute-start(f32[1280,256]{1,0:T(8,128)S(1)} %select_add_fusion), channel_id=1, source_target_pairs={{0,2},{1,3},{2,0},{3,1},{4,6},{5,7},{6,4},{7,5},{8,10},{9,11},{10,... | collective-permute-start | bytes 3932168 | tf_op jit(solution)/shard_map/ppermute | solution.py:46
  628.7 59.0 %all-to-all-start.1 = ((bf16[8,128,1024]{2,1,0:T(8,128)(2,1)}), bf16[8,128,1024]{2,1,0:T(8,128)(2,1)}, u32[]{:S(2)}, u32[]{:S(2)}) async-start(bf16[8,128,1024]{2,1,0:T(8,128)(2,1)} %bitcast.52), calls=%async_computation.1 | async-start | bytes 4194304 | tf_op jit(solution)/shard_map/all_to_all | solution.py:1071
  (241 other events, 2082.9 us)
Sparse Core Ops, SparseCore 0:
  145.4 45.8 all-gather.1

commit v4 on v3

v4 whole, which is shorter than its diff:
```python
import functools
import math

import jax
import jax.numpy as jnp
from jax import lax
from jax.experimental import pallas as pl
from jax.experimental.pallas import tpu as pltpu
from jax.sharding import PartitionSpec as P

D = 1024
HD = 64
FF = 4096
DD = 512
DHD = 32
DFF = 2048
NS_STEPS = 5


highest = lax.Precision.HIGHEST
ln_eps = 1e-06
masked_score = -1e30
newton_first = 3.4445
newton_second = -4.775
newton_third = 2.0315
momentum_keep = 0.5
clip_bound = 100.0
rate_enc = 0.2
rate_dec = 0.3
rate_norm = 1.0
decay_rate = 0.01
kernel_vmem = 32 * 1024 * 1024
newton_vmem = 48 * 1024 * 1024
grads_vmem = 58 * 1024 * 1024


def shortened(array):

    def short(part):
        return part.astype(jnp.bfloat16) if part.dtype == jnp.float32 else part

    return jax.tree.map(short, array)


def pair_swap(array, axis, bit):
    size = lax.axis_size(axis)
    return lax.ppermute(array, axis, [(rank, rank ^ bit) for rank in range(size)])


def core_swap(array):
    return pair_swap(array, "mp", 1)


def far_swap(array):
    return pair_swap(array, "mp", 2)


def far_sum(chip_term):
    half = chip_term.astype(jnp.bfloat16)
    return half.astype(jnp.float32) + far_swap(half).astype(jnp.float32)


def chip_sum(own_term, other_term):
    return own_term + core_swap(other_term.astype(jnp.bfloat16)).astype(jnp.float32)


def shared(own_parts):
    return [part for own in own_parts for part in (own, core_swap(own))]


def paired(parts):
    return list(zip(parts[::2], parts[1::2]))


def times(left, right):
    return jnp.dot(left, right, preferred_element_type=jnp.float32)


def times_turned(left, right):
    return jnp.einsum("tf,df->td", left, right, preferred_element_type=jnp.float32)


def gather_small(array):
    rank = lax.axis_index("dp")
    gathered = array[None]
    bit = 1
    while bit < lax.axis_size("dp"):
        other = pair_swap(gathered, "dp", bit)
        lower = (rank & bit) == 0
        gathered = jnp.concatenate(
            [jnp.where(lower, gathered, other), jnp.where(lower, other, gathered)], axis=0
        )
        bit *= 2
    return gathered


def assemble_kernel(rank_ref, *refs):
    whole_ref = refs[-1]
    rows = refs[0].shape[0]
    for bit, part_ref in enumerate(refs[:-1]):
        place = pl.multiple_of((rank_ref[0] ^ bit) * rows, rows)
        whole_ref[pl.ds(place, rows), :] = part_ref[...]


def assemble(parts, place):
    rows, columns = parts[0].shape
    spec = pl.BlockSpec(memory_space=pltpu.VMEM)
    return pl.pallas_call(
        assemble_kernel,
        in_specs=[pl.BlockSpec(memory_space=pltpu.SMEM)] + [spec] * len(parts),
        out_specs=spec,
        out_shape=jax.ShapeDtypeStruct((len(parts) * rows, columns), parts[0].dtype),
        compiler_params=pltpu.CompilerParams(vmem_limit_bytes=grads_vmem),
        cost_estimate=pl.CostEstimate(
            flops=0, bytes_accessed=4 * len(parts) * rows * columns, transcendentals=0
        ),
        name="assemble",
    )(place.reshape(1), *parts)


class Gather:
    def __init__(self, array):
        self.general = lax.axis_size("dp") != 8
        if self.general:
            self.whole = lax.all_gather(array, "dp", axis=0, tiled=True)
            self.lined = [array]
        else:
            self.lined = [array] + [pair_swap(array, "dp", 2 * bit) for bit in (1, 2, 3)]
            self.crossed = None

    def turn(self, values):
        if self.general:
            return values
        values, self.lined = lax.optimization_barrier((values, self.lined))
        self.cross()
        return values

    def cross(self):
        self.crossed = [pair_swap(part, "dp", 1) for part in self.lined]

    def result(self):
        if self.general:
            return self.whole
        if self.crossed is None:
            self.cross()
        parts = [part for pair in zip(self.lined, self.crossed) for part in pair]
        return assemble(parts, lax.axis_index("dp"))


def collect_values(slots):
    ranks = lax.axis_size("dp")
    rank = lax.axis_index("dp")
    width = max(rows.shape[1] for rows in slots.values())
    padded = {
        owner: jnp.pad(rows.astype(jnp.bfloat16), ((0, 0), (0, width - rows.shape[1])))
        for owner, rows in slots.items()
    }
    values = []
    for bit in range(ranks):
        value = None
        for owner, rows in padded.items():
            value = rows if value is None else jnp.where(rank ^ bit == owner, rows, value)
        values.append(value)
    return values


def collect_parts(values, owners):
    return values[:1] + [
        lax.ppermute(value, "dp", [(owner ^ bit, owner) for owner in owners])
        for bit, value in enumerate(values)
        if bit
    ]


def cross_pair(even_rows, odd_rows):
    even = lax.axis_index("dp") % 2 == 0
    kept = jnp.where(even, even_rows, odd_rows)
    return kept, pair_swap(jnp.where(even, odd_rows, even_rows), "dp", 1)


def line_pair(kept, crossed, owners):
    even = lax.axis_index("dp") % 2 == 0
    lined = jnp.concatenate(
        [jnp.where(even, kept, crossed), jnp.where(even, crossed, kept)], axis=0
    )
    return [lined] + [
        lax.ppermute(lined, "dp", [(owner ^ (2 * bit), owner) for owner in owners])
        for bit in range(1, lax.axis_size("dp") // 2)
    ]


def after(value, anchor):
    return lax.optimization_barrier((value, anchor))[0]


def fold(kept, received):
    return (kept.astype(jnp.float32) + received.astype(jnp.float32)).astype(jnp.bfloat16)


def split_rows(array, place):
    half = array.shape[0] // 2
    return (
        lax.dynamic_slice_in_dim(array, (1 - place) * half, half, 0),
        lax.dynamic_slice_in_dim(array, place * half, half, 0),
    )


class Scatter:
    def __init__(self, groups):
        self.phase = 0
        self.general = lax.axis_size("dp") != 8
        self.rank = lax.axis_index("dp")
        self.sent = self.kept = self.received = None
        if self.general:
            whole = jnp.concatenate(
                [
                    jnp.einsum(
                        "td,tf->df",
                        jnp.concatenate(lefts, axis=0),
                        jnp.concatenate(rights, axis=0),
                        preferred_element_type=jnp.float32,
                    ).astype(jnp.bfloat16)
                    for lefts, rights in groups
                ],
                axis=1,
            )
            self.total = lax.psum_scatter(whole, "dp", scatter_dimension=0, tiled=True)
        else:
            self.sent, self.kept = weight_grads(groups, self.rank % 2)

    def send(self):
        if not self.general:
            self.received = pair_swap(self.sent, "dp", 1 << self.phase)

    def fold(self):
        if not self.general:
            place = self.rank // 2 % 2 if self.phase == 0 else self.rank // 4
            self.sent, self.kept = split_rows(fold(self.kept, self.received), place)
            self.phase += 1

    def result(self):
        if self.general:
            return self.total.astype(jnp.float32)
        return self.kept.astype(jnp.float32) + self.received.astype(jnp.float32)


class HopSum:
    def __init__(self, value):
        self.value = value
        self.hops = [
            (axis, 1 << bit)
            for axis in ("mp", "dp")
            for bit in range(lax.axis_size(axis).bit_length() - 1)
        ]

    def step(self, count):
        for axis, bit in self.hops[:count]:
            self.value = self.value + pair_swap(self.value, axis, bit)
        self.hops = self.hops[count:]

    def finish(self):
        self.step(len(self.hops))
        return self.value


def normalize(values):
    center = values - jnp.mean(values, axis=-1, keepdims=True)
    inverse = lax.rsqrt(jnp.mean(center * center, axis=-1, keepdims=True) + ln_eps)
    return center * inverse, inverse


def normalize_back(normal, inverse, gain_row, out_grad):
    scaled = out_grad * gain_row
    mean_grad = jnp.mean(scaled, axis=-1, keepdims=True)
    mean_dot = jnp.mean(scaled * normal, axis=-1, keepdims=True)
    return inverse * (scaled - mean_grad - normal * mean_dot)


def gelu_and_slope(hidden):
    spread = 0.5 + 0.5 * lax.erf(hidden * math.sqrt(0.5))
    density = jnp.exp(-0.5 * hidden * hidden) * (1.0 / math.sqrt(2.0 * math.pi))
    return hidden * spread, spread + hidden * density


def swap_halves(array, chunk_rows, core):
    parts = array.reshape((-1, 2, chunk_rows // 2) + array.shape[1:])
    return jnp.where(core == 0, parts, parts[:, ::-1]).reshape(array.shape)


def segments_of(lengths, row_count):
    item_ends = jnp.cumsum(lengths)
    position = jnp.arange(row_count, dtype=jnp.int32)
    segment = jnp.sum((position[:, None] >= item_ends[None, :]).astype(jnp.int32), axis=1)
    live_mask = (position < item_ends[-1]).astype(jnp.float32)
    return (segment, live_mask)


def split_columns(whole_cols, widths):
    pieces = []
    start_col = 0
    for piece_width in widths:
        pieces.append(whole_cols[:, start_col : start_col + piece_width])
        start_col += piece_width
    return pieces


def head_mask(head, head_width, inner_width):
    lane = lax.broadcasted_iota(jnp.int32, (1, inner_width), 1)
    inside = jnp.logical_and(lane >= head * head_width, lane < (head + 1) * head_width)
    return jnp.where(inside, 1.0, 0.0)


def masked_rows(rows, head, head_width):
    mask = head_mask(head, head_width, rows.shape[1])
    return (rows.astype(jnp.float32) * mask).astype(jnp.bfloat16)


def last_dims(left, right):
    return lax.dot_general(
        left, right, (((1,), (1,)), ((), ())), preferred_element_type=jnp.float32
    )


def segment_bias(key_segment_ref, query_segment_ref):
    return jnp.where(key_segment_ref[...] == query_segment_ref[...], 0.0, masked_score)


def joined_columns(refs, first, last):
    return jnp.concatenate([ref[:, first:last] for ref in refs], axis=0)


def attend_forward_kernel(
    head_width, place, count, key_segment_ref, query_segment_ref, *refs
):
    mixed_refs, (own_ref, other_ref, logsum_ref) = refs[:count], refs[count:]
    block_rows = query_segment_ref.shape[0]
    half_rows, inner_width = own_ref.shape
    score_scale = head_width ** (-0.5)
    bias = segment_bias(key_segment_ref, query_segment_ref)
    if count == 1:
        rows = mixed_refs[0][place * block_rows : (place + 1) * block_rows, :inner_width]
    else:
        rows = joined_columns(mixed_refs[2 * place : 2 * place + 2], 0, inner_width)
    keys = joined_columns(mixed_refs, inner_width, 2 * inner_width)
    values = joined_columns(mixed_refs, 2 * inner_width, 3 * inner_width)
    total_out = jnp.zeros((block_rows, inner_width), jnp.float32)
    logsums = []
    for head in range(inner_width // head_width):
        scores = last_dims(masked_rows(rows, head, head_width), keys) * score_scale + bias
        top = jnp.max(scores, axis=1, keepdims=True)
        shifted = jnp.exp(scores - top)
        total = jnp.sum(shifted, axis=1, keepdims=True)
        part = times(shifted.astype(jnp.bfloat16), values)
        total_out += part * (head_mask(head, head_width, inner_width) / total)
        logsums.append(jnp.broadcast_to(top + jnp.log(total), (block_rows, 128)))
    own_ref[...] = total_out[:half_rows].astype(jnp.bfloat16)
    other_ref[...] = total_out[half_rows:].astype(jnp.bfloat16)
    lane = lax.broadcasted_iota(jnp.int32, (block_rows, 128), 1)
    stacked = logsums[0]
    for head in range(1, len(logsums)):
        stacked = jnp.where(lane == head, logsums[head], stacked)
    logsum_ref[...] = stacked.T[: len(logsums), :]


def attend_forward(mixed, segment, place, head_width, block_rows):
    row_count = segment.shape[0]
    inner_width = mixed[0].shape[1] // 3
    head_count = inner_width // head_width
    whole = pl.BlockSpec(memory_space=pltpu.VMEM)
    half = jax.ShapeDtypeStruct((block_rows // 2, inner_width), jnp.bfloat16)
    return pl.pallas_call(
        functools.partial(attend_forward_kernel, head_width, place, len(mixed)),
        in_specs=[whole] * (2 + len(mixed)),
        out_specs=[whole] * 3,
        out_shape=[half, half, jax.ShapeDtypeStruct((head_count, block_rows), jnp.float32)],
        compiler_params=pltpu.CompilerParams(vmem_limit_bytes=kernel_vmem),
        cost_estimate=pl.CostEstimate(
            flops=4 * block_rows * row_count * inner_width * head_count,
            bytes_accessed=8 * row_count * inner_width,
            transcendentals=block_rows * row_count * head_count,
        ),
        name="attend_forward",
    )(
        segment.reshape(1, row_count),
        segment[place * block_rows : (place + 1) * block_rows].reshape(block_rows, 1),
        *mixed,
    )


def attend_backward_kernel(head_width, count, key_segment_ref, query_segment_ref, *refs):
    grad_refs, logsum_refs, refs = refs[:4], refs[4:6], refs[6:]
    mixed_refs, out_refs, refs = refs[:count], refs[count : count + 4], refs[count + 4 :]
    turned_ref, grad_ref, query_ref, bias_ref, query_grad_ref, key_total_ref, value_total_ref = refs
    row_count, inner_width = grad_ref.shape
    part_rows = row_count // 4
    block_rows = row_count // 2
    score_scale = head_width ** (-0.5)
    keys = joined_columns(mixed_refs, inner_width, 2 * inner_width)
    values = joined_columns(mixed_refs, 2 * inner_width, 3 * inner_width)
    turned_ref[...] = keys.astype(jnp.float32).T.astype(jnp.bfloat16)
    for k in range(4):
        grad_ref[k * part_rows : (k + 1) * part_rows, :] = grad_refs[k][...]
    query_ref[...] = joined_columns(mixed_refs, 0, inner_width)
    key_total_ref[...] = jnp.zeros_like(key_total_ref)
    value_total_ref[...] = jnp.zeros_like(value_total_ref)
    for block in range(2):
        bias_ref[block] = jnp.where(
            key_segment_ref[...]
            == query_segment_ref[:, block * block_rows : (block + 1) * block_rows],
            0.0,
            masked_score,
        )

    @pl.loop(0, 2)
    def _(block):
        rows = pl.ds(pl.multiple_of(block * block_rows, block_rows), block_rows)
        parts = []
        for head in range(inner_width // head_width):
            query = masked_rows(query_ref[rows, :], head, head_width)
            grad = masked_rows(grad_ref[rows, :], head, head_width)
            logsum = jnp.where(
                block == 0,
                logsum_refs[0][head : head + 1, :],
                logsum_refs[1][head : head + 1, :],
            )
            scores = last_dims(keys, query) * score_scale + bias_ref[block]
            attention = jnp.exp(scores - logsum)
            weighted = attention * last_dims(values, grad)
            row_dot = jnp.sum(weighted, axis=0, keepdims=True)
            score_grad = (weighted - attention * row_dot).astype(jnp.bfloat16)
            value_total_ref[...] += times(attention.astype(jnp.bfloat16), grad)
            key_total_ref[...] += times(score_grad, query)
            parts.append(
                times(turned_ref[head * head_width : (head + 1) * head_width, :], score_grad)
            )
        query_grad_ref[rows, :] = (jnp.concatenate(parts, axis=0) * score_scale).T

    for k, out_ref in enumerate(out_refs):
        rows = slice(k * part_rows, (k + 1) * part_rows)
        out_ref[:, :inner_width] = query_grad_ref[rows, :].astype(jnp.bfloat16)
        out_ref[:, inner_width : 2 * inner_width] = (key_total_ref[rows, :] * score_scale).astype(
            jnp.bfloat16
        )
        out_ref[:, 2 * inner_width :] = value_total_ref[rows, :].astype(jnp.bfloat16)


def attend_backward(heads_grads, mixed, logsums, segment, head_width):
    row_count = segment.shape[0]
    part_rows, inner_width = heads_grads[0].shape
    head_count = inner_width // head_width
    whole = pl.BlockSpec(memory_space=pltpu.VMEM)
    part = jax.ShapeDtypeStruct((part_rows, 3 * inner_width), jnp.bfloat16)
    return pl.pallas_call(
        functools.partial(attend_backward_kernel, head_width, len(mixed)),
        in_specs=[whole] * (8 + len(mixed)),
        out_specs=[whole] * 4,
        out_shape=[part] * 4,
        scratch_shapes=[
            pltpu.VMEM((inner_width, row_count), jnp.bfloat16),
            pltpu.VMEM((row_count, inner_width), jnp.bfloat16),
            pltpu.VMEM((row_count, inner_width), jnp.bfloat16),
            pltpu.VMEM((2, row_count, row_count // 2), jnp.float32),
            pltpu.VMEM((row_count, inner_width), jnp.float32),
            pltpu.VMEM((row_count, inner_width), jnp.float32),
            pltpu.VMEM((row_count, inner_width), jnp.float32),
        ],
        compiler_params=pltpu.CompilerParams(vmem_limit_bytes=kernel_vmem),
        cost_estimate=pl.CostEstimate(
            flops=10 * row_count * row_count * inner_width * head_count,
            bytes_accessed=14 * row_count * inner_width,
            transcendentals=row_count * row_count * head_count,
        ),
        name="attend_backward",
    )(
        segment.reshape(row_count, 1),
        segment.reshape(1, row_count),
        *heads_grads,
        *logsums,
        *mixed,
    )


def block_forward(own_chunks, rows, segment, pieces, norm_values, head_width, hook):
    qkv_proj, out_proj = pieces[:2]
    mixed = [times(part, qkv_proj).astype(jnp.bfloat16) for part in rows]
    block_rows = segment.shape[0] // len(own_chunks)
    heads, logsums, middles = [], [], []
    for place, own in enumerate(own_chunks):
        own_heads, other_heads, logsum = attend_forward(
            mixed, segment, place, head_width, block_rows
        )
        heads += [own_heads, other_heads]
        logsums.append(logsum)
        chip_term = chip_sum(
            times_turned(own_heads, out_proj), times_turned(other_heads, out_proj)
        )
        middles.append(own + far_sum(chip_term))
    middles = hook("middle", middles)
    up_proj, down_proj = pieces[2:4]
    seconds, chip_terms, ups, activated, slopes = [], [], [], [], []
    for middle in middles:
        normal, inverse = normalize(middle)
        parts = shared([(normal * norm_values[2] + norm_values[3]).astype(jnp.bfloat16)])
        partials = []
        for part in parts:
            value, slope = gelu_and_slope(times(part, up_proj))
            value = value.astype(jnp.bfloat16)
            partials.append(times_turned(value, down_proj))
            activated.append(value)
            slopes.append(slope)
        ups += parts
        chip_terms.append(chip_sum(*partials))
        seconds.append((normal, inverse))
    return middles, chip_terms, (rows, mixed, heads, logsums, seconds, ups, activated, slopes)


def block_backward(
    own_grads, half_rows, saved, firsts, pieces, norm_values, segment, head_width, hook
):
    rows, mixed, heads, logsums, seconds, ups, activated, slopes = saved
    qkv_proj, out_proj, up_proj, down_proj = pieces
    down_group = (half_rows, activated)
    half_rows = hook("start", half_rows, down_group)
    hidden_rows = [
        (times(half, down_proj) * slope).astype(jnp.bfloat16)
        for half, slope in zip(half_rows, slopes)
    ]
    chip_terms = [
        chip_sum(times_turned(own, up_proj), times_turned(other, up_proj))
        for own, other in paired(hidden_rows)
    ]
    up_group = (ups, hidden_rows)
    normed_grads = hook("sums", [far_sum(chip_term) for chip_term in chip_terms], up_group)
    middle_grads, gain_two, shift_two = [], 0.0, 0.0
    for own_grad, chip_term, normed_grad, (normal, inverse) in zip(
        own_grads, chip_terms, normed_grads, seconds
    ):
        gain_two = gain_two + jnp.sum(chip_term * normal, axis=0)
        shift_two = shift_two + jnp.sum(chip_term, axis=0)
        middle_grads.append(
            own_grad + normalize_back(normal, inverse, norm_values[2], normed_grad)
        )
    middle_rows = shared([grad.astype(jnp.bfloat16) for grad in middle_grads])
    out_group = (middle_rows, heads)
    middle_rows = hook("middle", middle_rows, out_group)
    heads_grads = [times(part, out_proj).astype(jnp.bfloat16) for part in middle_rows]
    mixed_grads = attend_backward(heads_grads, mixed, logsums, segment, head_width)
    qkv_group = (rows, mixed_grads)
    mixed_grads = hook("mixed", mixed_grads, qkv_group)
    chip_terms = [
        chip_sum(times_turned(own, qkv_proj), times_turned(other, qkv_proj))
        for own, other in paired(mixed_grads)
    ]
    gain_one, shift_one = 0.0, 0.0
    for chip_term, (normal, _) in zip(chip_terms, firsts):
        gain_one = gain_one + jnp.sum(chip_term * normal, axis=0)
        shift_one = shift_one + jnp.sum(chip_term, axis=0)
    norm_grads = jnp.stack([gain_one, shift_one, gain_two, shift_two])
    groups = [qkv_group, out_group, up_group, down_group]
    return chip_terms, middle_grads, groups, norm_grads


def block_input_grads(far_sums, middle_grads, firsts, norm_values):
    return [
        middle_grad + normalize_back(normal, inverse, norm_values[0], normed_grad)
        for middle_grad, normed_grad, (normal, inverse) in zip(middle_grads, far_sums, firsts)
    ]


def row_pieces(refs, count):
    if len(refs) == count:
        return [ref[...] for ref in refs]
    rows = refs[0].shape[0] // count
    return [refs[0][k * rows : (k + 1) * rows, :] for k in range(count)]


def weight_grads_kernel(counts, parity_ref, *refs):
    sent_ref, kept_ref = refs[-2:]
    even = parity_ref[0] == 0
    place, column = 0, 0
    for left_count, right_count in counts:
        count = max(left_count, right_count)
        lefts = row_pieces(refs[place : place + left_count], count)
        place += left_count
        rights = row_pieces(refs[place : place + right_count], count)
        place += right_count
        total = 0.0
        for left, right in zip(lefts, rights):
            total = total + lax.dot_general(
                left, right, (((0,), (0,)), ((), ())), preferred_element_type=jnp.float32
            )
        half = total.shape[0] // 2
        columns = slice(column, column + total.shape[1])
        upper, lower = total[:half], total[half:]
        sent_ref[:, columns] = jnp.where(even, lower, upper).astype(jnp.bfloat16)
        kept_ref[:, columns] = jnp.where(even, upper, lower).astype(jnp.bfloat16)
        column += total.shape[1]


def weight_grads(groups, parity):
    width = groups[0][0][0].shape[1]
    specs, operands, flops = [], [], 0
    for lefts, rights in groups:
        for left in lefts:
            specs.append(
                pl.BlockSpec((left.shape[0], width // 4), lambda i: (0, i % 2 * 2 + i // 2))
            )
            operands.append(left)
        for right in rights:
            specs.append(pl.BlockSpec(right.shape, lambda i: (0, 0)))
            operands.append(right)
            flops += 2 * width * right.shape[0] * right.shape[1]
    columns = sum(rights[0].shape[1] for _, rights in groups)
    half = jax.ShapeDtypeStruct((width // 2, columns), jnp.bfloat16)
    return pl.pallas_call(
        functools.partial(
            weight_grads_kernel, [(len(lefts), len(rights)) for lefts, rights in groups]
        ),
        grid=(4,),
        in_specs=[pl.BlockSpec(memory_space=pltpu.SMEM)] + specs,
        out_specs=[pl.BlockSpec((width // 8, columns), lambda i: (i, 0))] * 2,
        out_shape=[half, half],
        compiler_params=pltpu.CompilerParams(
            dimension_semantics=("arbitrary",), vmem_limit_bytes=grads_vmem
        ),
        cost_estimate=pl.CostEstimate(
            flops=flops,
            bytes_accessed=2 * sum(operand.size for operand in operands) + 2 * width * columns,
            transcendentals=0,
        ),
        name="weight_grads",
    )(parity.reshape(1), *operands)


low_set = ((0, 0), (0, 1), (0, 2), (0, 3), (1, 1))
high_set = ((2, 2), (2, 3), (3, 3), (1, 2), (1, 3))


def newton_kernel(
    enc_rows, dec_rows, paired_ref, low_ref, high_ref, own_ref, out_ref, gram_ref, total_ref,
    mix_ref, gram_half_ref, total_half_ref,
):
    size = gram_ref.shape[0]
    block = size // 4
    tile = size // 2

    def in_upper(axis, count, start):
        shape = (count, 1) if axis == 0 else (1, count)
        place = start + lax.broadcasted_iota(jnp.int32, shape, axis)
        return place % enc_rows < dec_rows

    row = lax.broadcasted_iota(jnp.int32, (block, block), 0)
    column = lax.broadcasted_iota(jnp.int32, (block, block), 1)
    upper_trace, whole_trace = 0.0, 0.0
    for places, blocks_ref in ((low_set, low_ref), (high_set, high_ref)):
        for k, (i, j) in enumerate(places):
            value = blocks_ref[k * block : (k + 1) * block, :]
            gram_ref[i * block : (i + 1) * block, j * block : (j + 1) * block] = value
            if i != j:
                gram_ref[j * block : (j + 1) * block, i * block : (i + 1) * block] = value.T
            else:
                diagonal = jnp.where(row == column, value, 0.0)
                whole_trace += jnp.sum(diagonal)
                upper_trace += jnp.sum(
                    jnp.where(in_upper(0, block, i * block), diagonal, 0.0)
                )
    paired = paired_ref[0] == 1
    upper_scale = 1.0 / (jnp.sqrt(jnp.where(paired, upper_trace, whole_trace)) + 1e-07)
    lower_scale = 1.0 / (
        jnp.sqrt(jnp.where(paired, whole_trace - upper_trace, whole_trace)) + 1e-07
    )
    column_scale = jnp.where(in_upper(1, size, 0), upper_scale, lower_scale)

    def rows_of(step):
        return pl.ds(pl.multiple_of(step * tile, tile), tile)

    def times(left, right):
        return jnp.dot(left, right, preferred_element_type=jnp.float32)

    @pl.loop(0, size // tile)
    def _(step):
        rows = rows_of(step)
        row_scale = jnp.where(in_upper(0, tile, step * tile), upper_scale, lower_scale)
        scaled = gram_ref[rows, :] * row_scale * column_scale
        gram_ref[rows, :] = scaled
        gram_half_ref[0, rows, :] = scaled.astype(jnp.bfloat16)

    for newton_step in range(NS_STEPS):
        now, later = newton_step % 2, (newton_step + 1) % 2

        @pl.loop(0, size // tile)
        def _(step):
            rows = rows_of(step)
            square = times(gram_half_ref[now, rows, :], gram_half_ref[now])
            mix = newton_second * gram_ref[rows, :] + newton_third * square
            mix_ref[rows, :] = mix.astype(jnp.bfloat16)
            if newton_step == 0:
                same = lax.broadcasted_iota(
                    jnp.int32, (tile, size), 0
                ) + step * tile == lax.broadcasted_iota(jnp.int32, (tile, size), 1)
                total = jnp.where(same, newton_first, 0.0) + mix
                total_ref[rows, :] = total
                total_half_ref[later, rows, :] = total.astype(jnp.bfloat16)

        @pl.loop(0, size // tile)
        def _(step):
            rows = rows_of(step)
            mix = mix_ref[rows, :]
            if newton_step > 0:
                total = newton_first * total_ref[rows, :] + times(mix, total_half_ref[now])
                if newton_step == NS_STEPS - 1:
                    out_ref[rows, :] = times(
                        (total * column_scale).astype(jnp.bfloat16), own_ref[...]
                    ).astype(jnp.bfloat16)
                else:
                    total_ref[rows, :] = total
                    total_half_ref[later, rows, :] = total.astype(jnp.bfloat16)
            if newton_step < NS_STEPS - 1:
                left = newton_first * gram_ref[rows, :] + times(mix, gram_half_ref[now])
                gram = newton_first * left + times(left.astype(jnp.bfloat16), mix_ref[...])
                gram_ref[rows, :] = gram
                gram_half_ref[later, rows, :] = gram.astype(jnp.bfloat16)


def newton(low_blocks, high_blocks, own, paired, enc_rows, dec_rows):
    size, width = own.shape
    whole = pl.BlockSpec(memory_space=pltpu.VMEM)
    return pl.pallas_call(
        functools.partial(newton_kernel, enc_rows, dec_rows),
        in_specs=[pl.BlockSpec(memory_space=pltpu.SMEM)] + [whole] * 3,
        out_specs=whole,
        out_shape=jax.ShapeDtypeStruct((size, width), jnp.bfloat16),
        scratch_shapes=[
            pltpu.VMEM((size, size), jnp.float32),
            pltpu.VMEM((size, size), jnp.float32),
            pltpu.VMEM((size, size), jnp.bfloat16),
            pltpu.VMEM((2, size, size), jnp.bfloat16),
            pltpu.VMEM((2, size, size), jnp.bfloat16),
        ],
        compiler_params=pltpu.CompilerParams(vmem_limit_bytes=newton_vmem),
        cost_estimate=pl.CostEstimate(
            flops=36 * size * size * size, bytes_accessed=20 * size * size, transcendentals=0
        ),
        name="newton",
    )(paired.astype(jnp.int32).reshape(1), low_blocks, high_blocks, own)


def gram_sum(gram):
    size = gram.shape[0] // 4

    def packed(places):
        return jnp.concatenate(
            [gram[i * size : (i + 1) * size, j * size : (j + 1) * size] for i, j in places],
            axis=0,
        )

    lower_core = lax.axis_index("mp") % 2 == 0
    low_blocks, high_blocks = packed(low_set), packed(high_set)
    own = jnp.where(lower_core, low_blocks, high_blocks)
    own = own + core_swap(jnp.where(lower_core, high_blocks, low_blocks))
    own = own + far_swap(own)
    other = core_swap(own)
    return jnp.where(lower_core, own, other), jnp.where(lower_core, other, own)


enc_slots = (2, 5, 3, 4, 6)
dec_slots = (0, 7)


def slot_rows(enc_rows_half, dec_rows_half, enc_widths, dec_widths, slot_width, data_ranks):
    enc_parts = split_columns(enc_rows_half, enc_widths)
    dec_parts = split_columns(dec_rows_half, dec_widths)
    half_width = slot_width // 2

    def widened(part, width):
        return jnp.pad(part, ((0, 0), (0, width - part.shape[1])))

    empty = jnp.zeros((enc_rows_half.shape[0], slot_width), enc_rows_half.dtype)
    slots = [empty] * data_ranks
    for part, slot in zip(enc_parts, enc_slots):
        slots[slot] = widened(part, slot_width)
    for place, slot in enumerate(dec_slots):
        upper = jnp.pad(widened(dec_parts[2 * place], half_width), ((0, 0), (0, half_width)))
        lower = jnp.pad(widened(dec_parts[2 * place + 1], half_width), ((0, 0), (half_width, 0)))
        slots[slot] = jnp.concatenate([upper, lower], axis=0)
    return jnp.stack(slots)


def unslot(rows_back, enc_widths, dec_widths, dec_rows):
    slot_width = rows_back.shape[2]
    enc_results = [rows_back[slot][:, :width] for slot, width in zip(enc_slots, enc_widths)]
    dec_results = []
    for place, width in enumerate(dec_widths):
        slot = rows_back[dec_slots[place // 2]]
        odd = place % 2
        dec_results.append(
            slot[
                odd * dec_rows : (odd + 1) * dec_rows,
                odd * (slot_width // 2) : odd * (slot_width // 2) + width,
            ]
        )
    return enc_results, dec_results


def apply_step(master, ortho_rows, widths, model_width, rate, model_ranks):
    steps_all = [
        orthogonal * (0.2 * math.sqrt(max(model_width, piece_width * model_ranks)))
        for orthogonal, piece_width in zip(ortho_rows, widths)
    ]
    return master * (1.0 - rate * decay_rate) - rate * jnp.concatenate(steps_all, axis=1)


def local(
    patches,
    cotangent,
    item_lengths,
    enc_master,
    dec_master,
    enc_norms,
    dec_norms,
    enc_moment,
    dec_moment,
    enc_norm_moment,
    dec_norm_moment,
):
    model_ranks = lax.axis_size("mp")
    data_ranks = lax.axis_size("dp")
    enc_widths = [
        3 * D // model_ranks,
        D // model_ranks,
        FF // model_ranks,
        FF // model_ranks,
        DD // model_ranks,
    ]
    dec_widths = [3 * DD // model_ranks, DD // model_ranks, DFF // model_ranks, DFF // model_ranks]
    first_cols = enc_widths[0] + enc_widths[1]
    norm_parts = gather_small(
        jnp.concatenate([enc_norms, dec_norms], axis=1).astype(jnp.bfloat16)
    ).astype(jnp.float32)
    enc_share, dec_share = enc_norms.shape[1], dec_norms.shape[1]
    enc_norm_values = jnp.moveaxis(norm_parts[:, :, :enc_share], 0, 1).reshape(4, D)
    dec_norm_values = jnp.moveaxis(norm_parts[:, :, enc_share:], 0, 1).reshape(4, DD)
    enc_half = enc_master.astype(jnp.bfloat16)
    first_gather = Gather(enc_half[:, :first_cols])
    rest_low = lax.all_gather(
        after(enc_half[:, first_cols:], first_gather.lined), "dp", axis=0, tiled=True
    )
    dec_low = lax.all_gather(
        after(dec_master.astype(jnp.bfloat16), first_gather.lined), "dp", axis=0, tiled=True
    )
    enc_pieces = split_columns(first_gather.result(), enc_widths[:2])
    dec_pieces = split_columns(dec_low, dec_widths)
    model_rank = lax.axis_index("mp")
    core = model_rank % 2
    upper_chip = model_rank // 2
    row_count = patches.shape[0]
    enc_rows = enc_master.shape[0]
    dec_rows = dec_master.shape[0]
    chunk_count = 2
    chunk_rows = row_count // chunk_count
    own_count = chunk_rows // 2
    segment, live_mask = segments_of(item_lengths[0], row_count)
    segment = swap_halves(segment, chunk_rows, core)
    live_mask = swap_halves(live_mask, chunk_rows, core)
    inputs = swap_halves(patches, chunk_rows, core)
    upstream = swap_halves(cotangent, chunk_rows, core) * live_mask.astype(jnp.bfloat16)[:, None]

    slot_width = max(enc_widths)

    def to_owners(enc_part, dec_part):
        slots = slot_rows(
            enc_part.astype(jnp.bfloat16),
            dec_part.astype(jnp.bfloat16),
            enc_widths,
            dec_widths,
            slot_width,
            data_ranks,
        )
        moved = lax.all_to_all(slots, "dp", 0, 0)
        return moved.reshape(-1, slot_width)

    input_normal, input_inverse = normalize(inputs.astype(jnp.float32))
    own_places = [slice(k * chunk_rows, k * chunk_rows + own_count) for k in range(chunk_count)]
    enc_firsts = [(input_normal[place], input_inverse[place]) for place in own_places]
    enc_rows_in = [
        (input_normal * enc_norm_values[0] + enc_norm_values[1]).astype(jnp.bfloat16)
    ]
    late_pieces = {}

    def enc_forward_hook(name, values):
        if name == "middle":
            enc_pieces.extend(split_columns(rest_low, enc_widths[2:]))
            late_pieces["bridge"] = whole_bridge(enc_pieces[4])
        return values

    def whole_bridge(bridge):
        bridge_far = far_swap(bridge)
        bridge_pair = jnp.where(
            upper_chip == 0, jnp.stack([bridge, bridge_far]), jnp.stack([bridge_far, bridge])
        )
        pair_other = core_swap(bridge_pair)
        bridge_all = jnp.stack(
            [
                jnp.where(core == 0, bridge_pair, pair_other),
                jnp.where(core == 0, pair_other, bridge_pair),
            ],
            axis=1,
        )
        share_width = bridge.shape[1]
        return jnp.moveaxis(bridge_all.reshape(-1, D, share_width), 0, 1).reshape(D, DD)

    enc_middles, enc_terms, enc_saved = block_forward(
        [inputs[place].astype(jnp.float32) for place in own_places],
        enc_rows_in,
        segment,
        enc_pieces,
        enc_norm_values,
        HD,
        enc_forward_hook,
    )
    bridge_all = late_pieces["bridge"]
    encoded_own = [
        (middle + far_sum(term)).astype(jnp.bfloat16)
        for middle, term in zip(enc_middles, enc_terms)
    ]
    decoder_in = [
        times(chunk, bridge_all).astype(jnp.bfloat16).astype(jnp.float32) for chunk in encoded_own
    ]
    encoded_rows = shared(encoded_own)
    dec_firsts = [normalize(chunk) for chunk in decoder_in]
    dec_rows_in = shared(
        [
            (normal * dec_norm_values[0] + dec_norm_values[1]).astype(jnp.bfloat16)
            for normal, _ in dec_firsts
        ]
    )
    dec_outs, dec_out_terms, dec_saved = block_forward(
        decoder_in,
        dec_rows_in,
        segment,
        dec_pieces,
        dec_norm_values,
        DHD,
        lambda name, values: values,
    )
    old_enc, old_dec, _ = lax.optimization_barrier((enc_moment, dec_moment, encoded_own[0]))
    old_slots = to_owners(old_enc, old_dec)
    upstream_rows = [
        upstream[k * own_count : (k + 1) * own_count] for k in range(2 * chunk_count)
    ]
    dec_terms, dec_middles, dec_groups, dec_norm_grads = block_backward(
        [half.astype(jnp.float32) for half in upstream_rows[::2]],
        upstream_rows,
        dec_saved,
        dec_firsts,
        dec_pieces,
        dec_norm_values,
        segment,
        DHD,
        lambda name, values, group: values,
    )
    dec_scatter = Scatter(dec_groups)
    dec_far_sums, dec_scatter.sent = lax.optimization_barrier(
        ([far_sum(term) for term in dec_terms], dec_scatter.sent)
    )
    dec_scatter.send()
    dec_in_grads = block_input_grads(dec_far_sums, dec_middles, dec_firsts, dec_norm_values)
    bridge_rows_in = shared([grad.astype(jnp.bfloat16) for grad in dec_in_grads])
    bridge_rows_in, old_slots = lax.optimization_barrier((bridge_rows_in, old_slots))
    encoded_grads = [times_turned(part, bridge_all) for part in bridge_rows_in]
    share_width = enc_widths[4]
    bridge_in_grad = [
        lax.dynamic_slice_in_dim(part, model_rank * share_width, share_width, 1)
        for part in bridge_rows_in
    ]
    scatters = {}

    def joined(values, *background):
        values, received = lax.optimization_barrier(
            (values, [scatter.received for scatter in background])
        )
        for scatter, piece in zip(background, received):
            scatter.received = piece
            scatter.fold()
        return values

    def enc_hook(name, values, group):
        if name == "start":
            scatters["down"] = Scatter([group, (encoded_rows, bridge_in_grad)])
            scatters["down"].send()
        if name == "sums":
            values = joined(values, dec_scatter)
            dec_scatter.send()
            scatters["up"] = Scatter([group])
            values, scatters["up"].sent = lax.optimization_barrier((values, scatters["up"].sent))
            scatters["up"].send()
        if name == "middle":
            values = joined(values, dec_scatter, scatters["down"])
            dec_scatter.send()
            scatters["down"].send()
            scatters["out"] = group
        if name == "mixed":
            late = scatters["late"] = Scatter([group, scatters["out"]])
            late.send()
            values = after(values, late.sent)
            values, dec_scatter.received = joined(
                (values, dec_scatter.received), scatters["down"], scatters["up"]
            )
            scatters["up"].send()
            scatters["down"].send()
        return values

    enc_back_terms, enc_middle_grads, _, enc_norm_grads = block_backward(
        encoded_grads[::2],
        [grad.astype(jnp.bfloat16) for grad in encoded_grads],
        enc_saved,
        enc_firsts,
        enc_pieces[:4],
        enc_norm_values,
        segment,
        HD,
        enc_hook,
    )
    late, up, down = (scatters[name] for name in ("late", "up", "down"))
    norm_hops = HopSum(jnp.concatenate([enc_norm_grads, dec_norm_grads], axis=1))
    norm_hops.step(2)
    enc_back_terms, norm_hops.value, down.received = joined(
        (enc_back_terms, norm_hops.value, down.received), late, up
    )
    late.send()
    up.send()
    norm_hops.step(1)
    enc_far_sums = [far_sum(term) for term in enc_back_terms]
    dec_sum_rows = dec_scatter.result()
    down_rows, bridge_rows = split_columns(down.result(), enc_widths[3:])
    half_width = slot_width // 2
    half_rows = [
        jnp.pad(part, ((0, 0), (0, half_width - part.shape[1])))
        for part in split_columns(dec_sum_rows, dec_widths)
    ]
    narrow = {
        dec_slots[0]: jnp.concatenate(half_rows[:2], axis=0),
        dec_slots[1]: jnp.concatenate(half_rows[2:], axis=0),
        enc_slots[4]: bridge_rows,
    }
    narrow_parts = collect_parts(collect_values(narrow), narrow)
    norm_hops.value, up.received = joined((norm_hops.value, up.received), late)
    up_rows = up.result()
    up_half, down_half = up_rows.astype(jnp.bfloat16), down_rows.astype(jnp.bfloat16)
    late.sent, up_half, down_half = lax.optimization_barrier((late.sent, up_half, down_half))
    late.send()
    wide_crossed = cross_pair(down_half, up_half)
    norm_hops.step(1)
    late.received, wide_crossed, norm_hops.value, enc_far_sums, narrow_parts = (
        lax.optimization_barrier(
            (late.received, wide_crossed, norm_hops.value, enc_far_sums, narrow_parts)
        )
    )
    qkv_rows, out_rows = split_columns(late.result(), enc_widths[:2])
    out_padded = jnp.pad(out_rows, ((0, 0), (0, enc_widths[0] - enc_widths[1])))
    tail_crossed = cross_pair(qkv_rows.astype(jnp.bfloat16), out_padded.astype(jnp.bfloat16))
    wide_parts = line_pair(*wide_crossed, enc_slots[2:4])
    norm_sums = norm_hops.finish()
    data_rank = lax.axis_index("dp")
    enc_sum_rows = jnp.concatenate([qkv_rows, out_rows, up_rows, down_rows, bridge_rows], axis=1)
    local_sum = jnp.sum(enc_sum_rows * enc_sum_rows) + jnp.sum(dec_sum_rows * dec_sum_rows)
    square_hops = HopSum(jnp.full((8, 128), local_sum))
    squares = square_hops.finish()[0, 0]
    tail_crossed, squares, norm_sums = lax.optimization_barrier((tail_crossed, squares, norm_sums))
    squares = squares + jnp.sum(norm_sums * norm_sums)
    tail_parts = line_pair(*tail_crossed, enc_slots[:2])

    def owned(parts, place):
        whole = assemble(parts, place)
        return jnp.pad(whole, ((0, 0), (0, slot_width - whole.shape[1])))

    late_slots = owned(tail_parts, data_rank // 2)
    wide_slots = owned(wide_parts, data_rank // 2)
    narrow_slots = owned(narrow_parts, data_rank)
    enc_norm_rows = lax.dynamic_slice_in_dim(norm_sums[:, :D], data_rank * enc_share, enc_share, 1)
    dec_norm_rows = lax.dynamic_slice_in_dim(norm_sums[:, D:], data_rank * dec_share, dec_share, 1)
    input_grads = block_input_grads(
        enc_far_sums, enc_middle_grads, enc_firsts, enc_norm_values
    )

    def natural(own_chunks):
        return swap_halves(jnp.concatenate(shared(own_chunks), axis=0), chunk_rows, core)

    dec_out_terms, _ = lax.optimization_barrier((dec_out_terms, late.received))
    decoded = [middle + far_sum(term) for middle, term in zip(dec_outs, dec_out_terms)]
    decoded = natural(decoded)
    input_grad = natural(input_grads)
    data_rank = lax.axis_index("dp")

    def is_rank(*slots):
        return functools.reduce(jnp.logical_or, [data_rank == slot for slot in slots])

    lower_row = (jnp.arange(wide_slots.shape[0], dtype=jnp.int32) % enc_rows >= dec_rows)[:, None]
    shifted = jnp.where(
        jnp.logical_and(lower_row, is_rank(*dec_slots)),
        jnp.roll(narrow_slots, half_width, axis=1),
        narrow_slots,
    )
    grad_slots = jnp.where(
        is_rank(*enc_slots[2:4]),
        wide_slots,
        jnp.where(is_rank(*enc_slots[:2]), late_slots, shifted),
    )
    grad_norm = jnp.sqrt(squares)
    factor = clip_bound * lax.rsqrt(squares + 1e-06)
    enc_grad = enc_sum_rows * factor
    dec_grad = dec_sum_rows * factor
    enc_norm_grad = enc_norm_rows * factor
    dec_norm_grad = dec_norm_rows * factor
    dec_shift_grad = dec_norm_grad[3]
    enc_moment_new = momentum_keep * enc_moment + enc_grad
    dec_moment_new = momentum_keep * dec_moment + dec_grad
    enc_norm_moment_new = momentum_keep * enc_norm_moment + enc_norm_grad
    dec_norm_moment_new = momentum_keep * dec_norm_moment + dec_norm_grad
    own = (
        momentum_keep * old_slots.astype(jnp.float32)
        + factor * grad_slots.astype(jnp.float32)
    ).astype(jnp.bfloat16)
    low_blocks, high_blocks = gram_sum(
        lax.dot_general(own, own, (((1,), (1,)), ((), ())), preferred_element_type=jnp.float32)
    )
    orthogonal = newton(low_blocks, high_blocks, own, is_rank(*dec_slots), enc_rows, dec_rows)
    rows_back = lax.all_to_all(
        orthogonal.reshape(data_ranks, enc_rows, slot_width), "dp", 0, 0
    ).astype(jnp.float32)
    enc_results, dec_results = unslot(rows_back, enc_widths, dec_widths, dec_rows)
    enc_master_new = apply_step(enc_master, enc_results, enc_widths, D, rate_enc, model_ranks)
    dec_master_new = apply_step(dec_master, dec_results, dec_widths, DD, rate_dec, model_ranks)
    enc_norms_new = enc_norms - rate_norm * enc_norm_moment_new
    dec_norms_new = dec_norms - rate_norm * dec_norm_moment_new
    return (
        decoded,
        input_grad,
        enc_grad,
        dec_grad,
        enc_norm_grad,
        dec_norm_grad,
        dec_shift_grad,
        enc_moment_new,
        dec_moment_new,
        enc_norm_moment_new,
        dec_norm_moment_new,
        enc_master_new,
        dec_master_new,
        enc_norms_new,
        dec_norms_new,
        enc_master_new.astype(jnp.bfloat16),
        dec_master_new.astype(jnp.bfloat16),
        enc_norms_new.astype(jnp.bfloat16),
        dec_norms_new.astype(jnp.bfloat16),
        grad_norm,
    )


def solution(mesh):
    return jax.shard_map(
        local,
        mesh=mesh,
        in_specs=(
            P("dp", None),
            P("dp", None),
            P("dp", None),
            P("dp", "mp"),
            P("dp", "mp"),
            P(None, "dp"),
            P(None, "dp"),
            P("dp", "mp"),
            P("dp", "mp"),
            P(None, "dp"),
            P(None, "dp"),
        ),
        out_specs=(
            P("dp", None),
            P("dp", None),
            P("dp", "mp"),
            P("dp", "mp"),
            P(None, "dp"),
            P(None, "dp"),
            P("dp"),
            P("dp", "mp"),
            P("dp", "mp"),
            P(None, "dp"),
            P(None, "dp"),
            P("dp", "mp"),
            P("dp", "mp"),
            P(None, "dp"),
            P(None, "dp"),
            P("dp", "mp"),
            P("dp", "mp"),
            P(None, "dp"),
            P(None, "dp"),
            P(),
        ),
        check_vma=False,
    )
```

time: 708 us -> 672 us (0.949)
  waiting for transfers between devices: 250 us -> 197 us
  matrix products: 41.9 us -> 74.7 us
  other arithmetic: 107 us -> 85.3 us
  Pallas kernels: 109 us -> 129 us
  starting transfers between devices: 136 us -> 128 us
    ppermute x101 -> x89, waiting for transfers between devices: 208 us -> 162 us  [pair_swap(): lax.ppermute(array, axis, [(rank, rank ^ bit) for rank in range(size)])]
    dot_general x34 -> x67, matrix products: 39.5 us -> 72.3 us  [the longest x31 36.6 us: times(): return jnp.dot(left, right, preferred_element_type=jnp.float32)]
    concatenate x20 -> x4, other arithmetic: 19.7 us -> 5.1 us  [the longest x2 4.3 us: natural(): jnp.concatenate(shared(own_chunks), axis=0)]
    pallas_call x10, Pallas kernels: 56.6 us -> 69.7 us  [the longest x4 27.5 us: weight_grads(): pl.pallas_call(functools.partial(weight_grads_kernel, [(len(lefts), len(r...]
    convert_element_type x16 -> x1, other arithmetic: 7.41 us -> 0.07 us  [far_sum(): half = chip_term.astype(jnp.bfloat16)]
    ppermute x14 -> x13, waiting for transfers between devices: 12.6 us -> 5.26 us  [the longest x7 5.24 us: collect_parts(): lax.ppermute(value, 'dp', [(owner ^ bit, owner) for owner in owners])]
    ppermute x14 -> x13, starting transfers between devices: 34.5 us -> 28.4 us  [the longest x7 14.5 us: collect_parts(): lax.ppermute(value, 'dp', [(owner ^ bit, owner) for owner in owners])]
    unnamed x322 -> x323, local copies, waits for them, and re-layouts: 19 us -> 17.9 us
  transfers between devices with their start and end apart: 118 -> 106, of which waited for: 42 -> 40; matrix products, arithmetic and copies ran while one was open for 21% -> 24% of each run, Pallas kernels for 9% -> 18%
where the time goes in v4:
time: 672 us; the launch traced here: 667 us
  waiting for transfers between devices  197 us (29%)
  Pallas kernels  129 us (19%)
  starting transfers between devices  128 us (19%)
  other arithmetic  85.3 us (13%)
  matrix products  74.7 us (11%)
  local copies, waits for them, and re-layouts  31.8 us (5%)
  between operations  21.4 us (3%)
    ppermute x89, waiting for transfers between devices, pair_swap(): lax.ppermute(array, axis, [(rank, rank ^ bit) for rank in range(size)])  162 us
    ppermute x89, starting transfers between devices, pair_swap(): lax.ppermute(array, axis, [(rank, rank ^ bit) for rank in range(size)])  84.3 us
    pallas_call x1, Pallas kernels, newton(): pl.pallas_call(functools.partial(newton_kernel, enc_rows, dec_rows), in_s...  48.6 us
    dot_general x31, matrix products, times(): return jnp.dot(left, right, preferred_element_type=jnp.float32)  36.6 us
    dot_general x36, matrix products, times_turned(): jnp.einsum('tf,df->td', left, right, preferred_element_type=jnp.float32)  35.7 us
    all_to_all x1, waiting for transfers between devices, local(): lax.all_to_all(orthogonal.reshape(data_ranks, enc_rows, slot_width), 'dp'...  28.3 us
    pallas_call x4, Pallas kernels, weight_grads(): pl.pallas_call(functools.partial(weight_grads_kernel, [(len(lefts), len(r...  27.5 us
    pallas_call x2, Pallas kernels, attend_backward(): pl.pallas_call(functools.partial(attend_backward_kernel, head_width, len(...  26.8 us
  transfers between devices with their start and end apart: 106, of which 40 were waited for; matrix products, arithmetic and copies ran while one was open for 24% of the time, Pallas kernels for 18%

profile of v4, /device:TPU:0, one launch (start us, length us, event | category | flops | bytes accessed | tf_op | source)
XLA Modules:
  0.0 667.2 jit_solution(13979074005007016979)
XLA Ops:
  24.6 10.5 %collective-permute-done.6.refs_4_ = bf16[128,1024]{1,0:T(8,128)(2,1)} collective-permute-done((bf16[128,1024]{1,0:T(8,128)(2,1)S(1)}, bf16[128,1024]{1,0:T(8,128)(2,1)}, u32[]{:S(2)}, u32[]{:S(2)}) %collective-permute-start.6) | collective-permute-done | bytes 262176 | tf_op jit(solution)/shard_map/ppermute | solution.py:47
  35.6 4.5 collective-permute-start.1
  49.1 4.5 subtract_multiply_fusion
  53.6 6.9 %collective-permute-done.5.refs_3_ = bf16[128,1024]{1,0:T(8,128)(2,1)S(1)} collective-permute-done((bf16[128,1024]{1,0:T(8,128)(2,1)}, bf16[128,1024]{1,0:T(8,128)(2,1)S(1)}, u32[]{:S(2)}, u32[]{:S(2)}) %collective-permute-start.5) | collective-permute-done | bytes 262176 | tf_op jit(solution)/shard_map/ppermute | solution.py:47
  60.6 5.2 collective-permute-done.7.refs_5_
  92.8 7.7 %collective-permute-done.11 = bf16[256,1024]{1,0:T(8,128)(2,1)S(1)} collective-permute-done((bf16[256,1024]{1,0:T(8,128)(2,1)S(1)}, bf16[256,1024]{1,0:T(8,128)(2,1)S(1)}, u32[]{:S(2)}, u32[]{:S(2)}) %collective-permute-start.11) | collective-permute-done | bytes 524320 | tf_op jit(solution)/shard_map/ppermute | solution.py:47
  100.5 10.4 %collective-permute-done.19 = bf16[256,1024]{1,0:T(8,128)(2,1)} collective-permute-done((bf16[256,1024]{1,0:T(8,128)(2,1)S(1)}, bf16[256,1024]{1,0:T(8,128)(2,1)}, u32[]{:S(2)}, u32[]{:S(2)}) %collective-permute-start.19) | collective-permute-done | bytes 524320 | tf_op jit(solution)/shard_map/ppermute | solution.py:47
  139.9 8.3 %collective-permute-done.22 = bf16[256,1024]{1,0:T(8,128)(2,1)} collective-permute-done((bf16[256,1024]{1,0:T(8,128)(2,1)}, bf16[256,1024]{1,0:T(8,128)(2,1)}, u32[]{:S(2)}, u32[]{:S(2)}) %collective-permute-start.22) | collective-permute-done | bytes 524320 | tf_op jit(solution)/shard_map/ppermute | solution.py:47
  150.5 8.3 %collective-permute-done.14 = bf16[256,1024]{1,0:T(8,128)(2,1)} collective-permute-done((bf16[256,1024]{1,0:T(8,128)(2,1)}, bf16[256,1024]{1,0:T(8,128)(2,1)}, u32[]{:S(2)}, u32[]{:S(2)}) %collective-permute-start.14) | collective-permute-done | bytes 524320 | tf_op jit(solution)/shard_map/ppermute | solution.py:47
  184.5 6.1 collective-permute-done.29
  210.5 4.3 all-to-all-start
  226.9 13.0 %attend_backward.2 = (bf16[256,384]{1,0:T(8,128)(2,1)S(1)}, bf16[256,384]{1,0:T(8,128)(2,1)S(1)}, bf16[256,384]{1,0:T(8,128)(2,1)S(1)}, bf16[256,384]{1,0:T(8,128)(2,1)S(1)}) custom-call(s32[1024,1]{1,0:T(8,128)S(1)} %reshape_reshape.6.key_segment_ref, s32[1,1024]{1,0:T(1,128)S(1)} %reshape_reshape.4.key_segment_ref.query_segment_ref, ...), custom_call_target="tpu_custom_call" | custom-call | flops 5368709120 | bytes 1835008 | tf_op jit(solution)/shard_map/attend_backward/pallas_call | solution.py:453
  248.2 7.1 %weight_grads.4 = (bf16[256,1536]{1,0:T(8,128)(2,1)}, bf16[256,1536]{1,0:T(8,128)(2,1)}) custom-call(s32[1]{0:T(128)} %bitcast.20.parity_ref, bf16[256,512]{1,0:T(8,128)(2,1)} %get-tuple-element.365.refs_0_, bf16[256,512]{1,0:T(8,128)(2,1)} %collective-permute-done.17.refs_1_, bf16[256,512]{1,0:T(8,128)(2,1)} %get-tuple-element.364.refs_2_, ...), custom_call_target="tpu_custom_call" | custom-call | flops 1610612736 | bytes 8912896 | tf_op jit(solution)/shard_map/weight_grads/pallas_call | solution.py:615
  285.1 7.2 %weight_grads.6 = (bf16[512,1152]{1,0:T(8,128)(2,1)}, bf16[512,1152]{1,0:T(8,128)(2,1)}) custom-call(s32[1]{0:T(128)} %bitcast.20.parity_ref, bf16[256,1024]{1,0:T(8,128)(2,1)} %copy-done.102, bf16[256,1024]{1,0:T(8,128)(2,1)} %copy-done.95, bf16[256,1024]{1,0:T(8,128)(2,1)} %copy-done.103, bf16[256,1024]{1,0:T(8,128)(2,1)} %copy-done.98, ...), custom_call_target="tpu_custom_call" | custom-call | flops 2415919104 | bytes 8912896 | tf_op jit(solution)/shard_map/weight_grads/pallas_call | solution.py:615
  293.9 6.3 weight_grads.5
  301.8 5.5 collective-permute-done.47
  317.0 4.6 collective-permute-done.54
  321.6 4.7 collective-permute-done.51
  337.7 13.8 %attend_backward.3 = (bf16[256,768]{1,0:T(8,128)(2,1)S(1)}, bf16[256,768]{1,0:T(8,128)(2,1)S(1)}, bf16[256,768]{1,0:T(8,128)(2,1)S(1)}, bf16[256,768]{1,0:T(8,128)(2,1)S(1)}) custom-call(s32[1024,1]{1,0:T(8,128)S(1)} %reshape_reshape.6.key_segment_ref, s32[1,1024]{1,0:T(1,128)S(1)} %reshape_reshape.4.key_segment_ref.query_segment_ref, ...), custom_call_target="tpu_custom_call" | custom-call | flops 10737418240 | bytes 3670016 | tf_op jit(solution)/shard_map/attend_backward/pallas_call | solution.py:453
  354.5 6.8 %weight_grads.7 = (bf16[512,1024]{1,0:T(8,128)(2,1)}, bf16[512,1024]{1,0:T(8,128)(2,1)}) custom-call(s32[1]{0:T(128)} %bitcast.20.parity_ref, bf16[1024,1024]{1,0:T(8,128)(2,1)} %copy-done.67, bf16[256,768]{1,0:T(8,128)(2,1)} %copy-done.4, bf16[256,768]{1,0:T(8,128)(2,1)} %copy-done.18, bf16[256,768]{1,0:T(8,128)(2,1)} %copy-done.14, ...), custom_call_target="tpu_custom_call" | custom-call | flops 2147483648 | bytes 8388608 | tf_op jit(solution)/shard_map/weight_grads/pallas_call | solution.py:615
  376.6 14.2 %collective-permute-done.62 = bf16[128,1152]{1,0:T(8,128)(2,1)S(1)} collective-permute-done((bf16[128,1152]{1,0:T(8,128)(2,1)S(1)}, bf16[128,1152]{1,0:T(8,128)(2,1)S(1)}, u32[]{:S(2)}, u32[]{:S(2)}) %collective-permute-start.62) | collective-permute-done | bytes 294944 | tf_op jit(solution)/shard_map/ppermute | solution.py:47
  400.8 7.1 %collective-permute-done.66 = bf16[128,1024]{1,0:T(8,128)(2,1)S(1)} collective-permute-done((bf16[128,1024]{1,0:T(8,128)(2,1)S(1)}, bf16[128,1024]{1,0:T(8,128)(2,1)S(1)}, u32[]{:S(2)}, u32[]{:S(2)}) %collective-permute-start.66) | collective-permute-done | bytes 262176 | tf_op jit(solution)/shard_map/ppermute | solution.py:47
  409.2 6.4 collective-permute-done.67
  427.1 4.3 collective-permute-start.79
  440.7 5.4 collective-permute-start.86
  462.6 6.3 collective-permute-start.91
  475.4 6.3 collective-permute-start.96
  495.4 4.7 add_convert_fusion.own_ref
  521.2 19.3 %collective-permute-done.100 = f32[1280,256]{1,0:T(8,128)} collective-permute-done((f32[1280,256]{1,0:T(8,128)}, f32[1280,256]{1,0:T(8,128)}, u32[]{:S(2)}, u32[]{:S(2)}) %collective-permute-start.100) | collective-permute-done | bytes 1310752 | tf_op jit(solution)/shard_map/ppermute | solution.py:47
  546.5 48.6 %newton.1 = bf16[1024,1024]{1,0:T(8,128)(2,1)} custom-call(s32[1]{0:T(128)} %bitcast.48.paired_ref, f32[1280,256]{1,0:T(8,128)S(1)} %get-tuple-element.310.low_ref, f32[1280,256]{1,0:T(8,128)S(1)} %get-tuple-element.309.high_ref, bf16[1024,1024]{1,0:T(8,128)(2,1)} %copy-done.60), custom_call_target="tpu_custom_call" | custom-call | flops 38654705664 | bytes 20971520 | tf_op jit(solution)/shard_map/newton/pallas_call | solution.py:728
  595.1 10.8 %all-to-all-start.1 = ((bf16[8,128,1024]{2,1,0:T(8,128)(2,1)}), bf16[8,128,1024]{2,1,0:T(8,128)(2,1)S(1)}, u32[]{:S(2)}, u32[]{:S(2)}) async-start(bf16[8,128,1024]{2,1,0:T(8,128)(2,1)} %bitcast.50), calls=%async_computation.1 | async-start | bytes 4194304 | tf_op jit(solution)/shard_map/all_to_all | solution.py:1128
  625.9 28.3 %all-to-all-done.1 = bf16[8,128,1024]{2,1,0:T(8,128)(2,1)S(1)} async-done(((bf16[8,128,1024]{2,1,0:T(8,128)(2,1)}), bf16[8,128,1024]{2,1,0:T(8,128)(2,1)S(1)}, u32[]{:S(2)}, u32[]{:S(2)}) %all-to-all-start.1) | async-done | bytes 2097184 | tf_op jit(solution)/shard_map/all_to_all | solution.py:1128
  (804 shorter events, 338.2 us)
Async XLA Ops:
  7.2 109.8 %all-gather.3.cloned.1.call-start = ((), (), s32[]{:S(2)}) async-start(), calls=%async_computation.2 | async-start | bytes 5013504 | tf_op jit(solution)/shard_map/all_gather | solution.py:845
  9.0 44.6 %collective-permute-start.3 = (bf16[128,1024]{1,0:T(8,128)(2,1)S(1)}, bf16[128,1024]{1,0:T(8,128)(2,1)S(1)}, u32[]{:S(2)}, u32[]{:S(2)}) collective-permute-start(bf16[128,1024]{1,0:T(8,128)(2,1)S(1)} %slice.364.refs_0_), channel_id=1, source_target_pairs={{0,4},{4,0},{8,12},{12,8},{16,20},{20,16},{24,28},{28,24},{1,5},{5... | collective-permute-start | bytes 786440 | tf_op jit(solution)/shard_map/ppermute | solution.py:47
  13.6 21.5 %collective-permute-start.6 = (bf16[128,1024]{1,0:T(8,128)(2,1)S(1)}, bf16[128,1024]{1,0:T(8,128)(2,1)}, u32[]{:S(2)}, u32[]{:S(2)}) collective-permute-start(bf16[128,1024]{1,0:T(8,128)(2,1)S(1)} %slice.364.refs_0_), channel_id=1, source_target_pairs={{0,16},{4,20},{8,24},{12,28},{16,0},{20,4},{24,8},{28,12},{1,17},{... | collective-permute-start | bytes 786440 | tf_op jit(solution)/shard_map/ppermute | solution.py:47
  35.1 130.3 %all-gather.5.cloned.1.call-start = ((), (), s32[]{:S(2)}) async-start(), calls=%async_computation.3 | async-start | bytes 1769472 | tf_op jit(solution)/shard_map/all_gather | solution.py:848
  48.6 20.0 %collective-permute-start.9 = (bf16[128,1024]{1,0:T(8,128)(2,1)}, bf16[128,1024]{1,0:T(8,128)(2,1)S(1)}, u32[]{:S(2)}, u32[]{:S(2)}) collective-permute-start(bf16[128,1024]{1,0:T(8,128)(2,1)} %collective-permute-done.8.refs_6_), channel_id=1, source_target_pairs={{0,4},{4,0},{8,12},{12,8},{16,20},{20,16},{24,28},{28,24},{1,5},{5... | collective-permute-start | bytes 786440 | tf_op jit(solution)/shard_map/ppermute | solution.py:47
  87.8 23.1 %collective-permute-start.19 = (bf16[256,1024]{1,0:T(8,128)(2,1)S(1)}, bf16[256,1024]{1,0:T(8,128)(2,1)}, u32[]{:S(2)}, u32[]{:S(2)}) collective-permute-start(bf16[256,1024]{1,0:T(8,128)(2,1)S(1)} %fusion.5), channel_id=1, source_target_pairs={{0,2},{1,3},{2,0},{3,1},{4,6},{5,7},{6,4},{7,5},{8,10},{9,11},{10,... | collective-permute-start | bytes 1572872 | tf_op jit(solution)/shard_map/ppermute | solution.py:47
  135.2 23.5 %collective-permute-start.14 = (bf16[256,1024]{1,0:T(8,128)(2,1)}, bf16[256,1024]{1,0:T(8,128)(2,1)}, u32[]{:S(2)}, u32[]{:S(2)}) collective-permute-start(bf16[256,1024]{1,0:T(8,128)(2,1)} %add_convert_fusion.13), channel_id=1, source_target_pairs={{0,2},{1,3},{2,0},{3,1},{4,6},{5,7},{6,4},{7,5},{8,10},{9,11},{10,... | collective-permute-start | bytes 1572872 | tf_op jit(solution)/shard_map/ppermute | solution.py:47
  210.5 52.6 %all-to-all-start = ((bf16[8,128,1024]{2,1,0:T(8,128)(2,1)}), bf16[8,128,1024]{2,1,0:T(8,128)(2,1)}, u32[]{:S(2)}, u32[]{:S(2)}) async-start(bf16[8,128,1024]{2,1,0:T(8,128)(2,1)} %fusion.112), calls=%async_computation | async-start | bytes 4194304 | tf_op jit(solution)/shard_map/all_to_all | solution.py:879
  261.0 24.1 %collective-permute-start.52 = (bf16[256,1024]{1,0:T(8,128)(2,1)S(1)}, bf16[256,1024]{1,0:T(8,128)(2,1)}, u32[]{:S(2)}, u32[]{:S(2)}) collective-permute-start(bf16[256,1024]{1,0:T(8,128)(2,1)S(1)} %copy-done.66), channel_id=1, source_target_pairs={{0,1},{1,0},{2,3},{3,2},{4,5},{5,4},{6,7},{7,6},{8,9},{9,8},{10,11... | collective-permute-start | bytes 1572872 | tf_op jit(solution)/shard_map/ppermute | solution.py:47
  261.1 24.0 %collective-permute-start.53 = (bf16[256,1024]{1,0:T(8,128)(2,1)S(1)}, bf16[256,1024]{1,0:T(8,128)(2,1)}, u32[]{:S(2)}, u32[]{:S(2)}) collective-permute-start(bf16[256,1024]{1,0:T(8,128)(2,1)S(1)} %copy-done.64), channel_id=1, source_target_pairs={{0,1},{1,0},{2,3},{3,2},{4,5},{5,4},{6,7},{7,6},{8,9},{9,8},{10,11... | collective-permute-start | bytes 1572872 | tf_op jit(solution)/shard_map/ppermute | solution.py:47
  261.5 47.2 %collective-permute-start.48 = (bf16[256,1536]{1,0:T(8,128)(2,1)}, bf16[256,1536]{1,0:T(8,128)(2,1)}, u32[]{:S(2)}, u32[]{:S(2)}) collective-permute-start(bf16[256,1536]{1,0:T(8,128)(2,1)} %get-tuple-element.140), channel_id=1, source_target_pairs={{0,4},{4,0},{8,12},{12,8},{16,20},{20,16},{24,28},{28,24},{1,5},{5... | collective-permute-start | bytes 2359304 | tf_op jit(solution)/shard_map/ppermute | solution.py:47
  283.7 23.6 %collective-permute-start.47 = (bf16[256,1024]{1,0:T(8,128)(2,1)}, bf16[256,1024]{1,0:T(8,128)(2,1)}, u32[]{:S(2)}, u32[]{:S(2)}) collective-permute-start(bf16[256,1024]{1,0:T(8,128)(2,1)} %get-tuple-element.411), channel_id=1, source_target_pairs={{0,2},{1,3},{2,0},{3,1},{4,6},{5,7},{6,4},{7,5},{8,10},{9,11},{10,... | collective-permute-start | bytes 1572872 | tf_op jit(solution)/shard_map/ppermute | solution.py:47
  292.3 29.2 %collective-permute-start.54 = (bf16[512,1152]{1,0:T(8,128)(2,1)}, bf16[512,1152]{1,0:T(8,128)(2,1)}, u32[]{:S(2)}, u32[]{:S(2)}) collective-permute-start(bf16[512,1152]{1,0:T(8,128)(2,1)} %get-tuple-element.148), channel_id=1, source_target_pairs={{0,4},{4,0},{8,12},{12,8},{16,20},{20,16},{24,28},{28,24},{1,5},{5... | collective-permute-start | bytes 3538952 | tf_op jit(solution)/shard_map/ppermute | solution.py:47
  315.9 46.2 %collective-permute-start.57 = (bf16[512,1024]{1,0:T(8,128)(2,1)}, bf16[512,1024]{1,0:T(8,128)(2,1)}, u32[]{:S(2)}, u32[]{:S(2)}) collective-permute-start(bf16[512,1024]{1,0:T(8,128)(2,1)} %get-tuple-element.168), channel_id=1, source_target_pairs={{0,4},{4,0},{8,12},{12,8},{16,20},{20,16},{24,28},{28,24},{1,5},{5... | collective-permute-start | bytes 3145736 | tf_op jit(solution)/shard_map/ppermute | solution.py:47
  333.0 29.0 %collective-permute-start.55 = (bf16[64,1536]{1,0:T(8,128)(2,1)S(1)}, bf16[64,1536]{1,0:T(8,128)(2,1)}, u32[]{:S(2)}, u32[]{:S(2)}) collective-permute-start(bf16[64,1536]{1,0:T(8,128)(2,1)S(1)} %constant_dynamic-slice_fusion.8), channel_id=1, source_target_pairs={{0,16},{4,20},{8,24},{12,28},{16,0},{20,4},{24,8},{28,12},{1,17},{... | collective-permute-start | bytes 589832 | tf_op jit(solution)/shard_map/ppermute | solution.py:47
  336.6 25.5 %collective-permute-start.56 = (bf16[256,1152]{1,0:T(8,128)(2,1)S(1)}, bf16[256,1152]{1,0:T(8,128)(2,1)S(1)}, u32[]{:S(2)}, u32[]{:S(2)}) collective-permute-start(bf16[256,1152]{1,0:T(8,128)(2,1)S(1)} %constant_dynamic-slice_fusion.7), channel_id=1, source_target_pairs={{0,8},{4,12},{8,0},{12,4},{16,24},{20,28},{24,16},{28,20},{1,9},{5... | collective-permute-start | bytes 1769480 | tf_op jit(solution)/shard_map/ppermute | solution.py:47
  361.4 29.5 %collective-permute-start.63 = (bf16[512,1024]{1,0:T(8,128)(2,1)}, bf16[512,1024]{1,0:T(8,128)(2,1)S(1)}, u32[]{:S(2)}, u32[]{:S(2)}) collective-permute-start(bf16[512,1024]{1,0:T(8,128)(2,1)} %get-tuple-element.160), channel_id=1, source_target_pairs={{0,4},{4,0},{8,12},{12,8},{16,20},{20,16},{24,28},{28,24},{1,5},{5... | collective-permute-start | bytes 3145736 | tf_op jit(solution)/shard_map/ppermute | solution.py:47
  371.2 20.7 %collective-permute-start.64 = (bf16[256,1024]{1,0:T(8,128)(2,1)S(1)}, bf16[256,1024]{1,0:T(8,128)(2,1)S(1)}, u32[]{:S(2)}, u32[]{:S(2)}) collective-permute-start(bf16[256,1024]{1,0:T(8,128)(2,1)S(1)} %constant_dynamic-slice_fusion.5), channel_id=1, source_target_pairs={{0,8},{4,12},{8,0},{12,4},{16,24},{20,28},{24,16},{28,20},{1,9},{5... | collective-permute-start | bytes 1572872 | tf_op jit(solution)/shard_map/ppermute | solution.py:47
  396.0 19.7 %collective-permute-start.67 = (bf16[256,1024]{1,0:T(8,128)(2,1)S(1)}, bf16[256,1024]{1,0:T(8,128)(2,1)S(1)}, u32[]{:S(2)}, u32[]{:S(2)}) collective-permute-start(bf16[256,1024]{1,0:T(8,128)(2,1)S(1)} %constant_dynamic-slice_fusion.3), channel_id=1, source_target_pairs={{0,8},{4,12},{8,0},{12,4},{16,24},{20,28},{24,16},{28,20},{1,9},{5... | collective-permute-start | bytes 1572872 | tf_op jit(solution)/shard_map/ppermute | solution.py:47
  396.4 20.8 %collective-permute-start.71 = (bf16[256,1024]{1,0:T(8,128)(2,1)S(1)}, bf16[256,1024]{1,0:T(8,128)(2,1)S(1)}, u32[]{:S(2)}, u32[]{:S(2)}) collective-permute-start(bf16[256,1024]{1,0:T(8,128)(2,1)S(1)} %convert_element_type.777), channel_id=1, source_target_pairs={{0,2},{1,3},{2,0},{3,1},{4,6},{5,7},{6,4},{7,5},{8,10},{9,11},{10,... | collective-permute-start | bytes 1572872 | tf_op jit(solution)/shard_map/ppermute | solution.py:47
  397.1 34.4 %collective-permute-start.72 = (bf16[256,1024]{1,0:T(8,128)(2,1)S(1)}, bf16[256,1024]{1,0:T(8,128)(2,1)S(1)}, u32[]{:S(2)}, u32[]{:S(2)}) collective-permute-start(bf16[256,1024]{1,0:T(8,128)(2,1)S(1)} %get-tuple-element.187), channel_id=1, source_target_pairs={{0,2},{1,3},{2,0},{3,1},{4,6},{5,7},{6,4},{7,5},{8,10},{9,11},{10,... | collective-permute-start | bytes 1572872 | tf_op jit(solution)/shard_map/ppermute | solution.py:47
  399.5 19.2 %collective-permute-start.73 = (bf16[128,512]{1,0:T(8,128)(2,1)S(1)}, bf16[128,512]{1,0:T(8,128)(2,1)S(1)}, u32[]{:S(2)}, u32[]{:S(2)}) collective-permute-start(bf16[128,512]{1,0:T(8,128)(2,1)S(1)} %get-tuple-element.334), channel_id=1, source_target_pairs={{4,0},{24,28},{28,24},{5,1},{25,29},{29,25},{6,2},{26,30},{30,26},... | collective-permute-start | bytes 393224 | tf_op jit(solution)/shard_map/ppermute | solution.py:169
  440.7 33.0 %collective-permute-start.86 = (bf16[128,768]{1,0:T(8,128)(2,1)}, bf16[128,768]{1,0:T(8,128)(2,1)}, u32[]{:S(2)}, u32[]{:S(2)}) collective-permute-start(bf16[128,768]{1,0:T(8,128)(2,1)} %get-tuple-element.331), channel_id=1, source_target_pairs={{0,4},{4,0},{8,12},{12,8},{16,20},{20,16},{24,28},{28,24},{1,5},{5... | collective-permute-start | bytes 589832 | tf_op jit(solution)/shard_map/ppermute | solution.py:47
  448.5 25.2 %collective-permute-start.92 = (f32[4,1536]{1,0:T(4,128)S(1)}, f32[4,1536]{1,0:T(4,128)S(1)}, u32[]{:S(2)}, u32[]{:S(2)}) collective-permute-start(f32[4,1536]{1,0:T(4,128)S(1)} %add.740), channel_id=1, source_target_pairs={{0,16},{4,20},{8,24},{12,28},{16,0},{20,4},{24,8},{28,12},{1,17},{... | collective-permute-start | bytes 73736 | tf_op jit(solution)/shard_map/ppermute | solution.py:47
  450.3 32.8 %collective-permute-start.93 = (bf16[256,1024]{1,0:T(8,128)(2,1)S(1)}, bf16[256,1024]{1,0:T(8,128)(2,1)S(1)}, u32[]{:S(2)}, u32[]{:S(2)}) collective-permute-start(bf16[256,1024]{1,0:T(8,128)(2,1)S(1)} %pad_maximum_fusion.5.refs_0_), channel_id=1, source_target_pairs={{4,12},{24,16},{5,13},{25,17},{6,14},{26,18},{7,15},{27,19}} | collective-permute-start | bytes 1572872 | tf_op jit(solution)/shard_map/ppermute | solution.py:187
  468.9 20.6 %collective-permute-start.94 = (bf16[256,1024]{1,0:T(8,128)(2,1)S(1)}, bf16[256,1024]{1,0:T(8,128)(2,1)}, u32[]{:S(2)}, u32[]{:S(2)}) collective-permute-start(bf16[256,1024]{1,0:T(8,128)(2,1)S(1)} %pad_maximum_fusion.5.refs_0_), channel_id=1, source_target_pairs={{28,12},{0,16},{29,13},{1,17},{30,14},{2,18},{31,15},{3,19}} | collective-permute-start | bytes 1572872 | tf_op jit(solution)/shard_map/ppermute | solution.py:187
  508.6 31.9 %collective-permute-start.100 = (f32[1280,256]{1,0:T(8,128)}, f32[1280,256]{1,0:T(8,128)}, u32[]{:S(2)}, u32[]{:S(2)}) collective-permute-start(f32[1280,256]{1,0:T(8,128)} %select_add_fusion), channel_id=1, source_target_pairs={{0,2},{1,3},{2,0},{3,1},{4,6},{5,7},{6,4},{7,5},{8,10},{9,11},{10,... | collective-permute-start | bytes 3932168 | tf_op jit(solution)/shard_map/ppermute | solution.py:47
  519.2 91.9 %collective-permute-start.82 = (bf16[256,512]{1,0:T(8,128)(2,1)}, bf16[256,512]{1,0:T(8,128)(2,1)}, u32[]{:S(2)}, u32[]{:S(2)}) collective-permute-start(bf16[256,512]{1,0:T(8,128)(2,1)} %convert_add_fusion.15), channel_id=1, source_target_pairs={{0,2},{1,3},{2,0},{3,1},{4,6},{5,7},{6,4},{7,5},{8,10},{9,11},{10,... | collective-permute-start | bytes 786440 | tf_op jit(solution)/shard_map/ppermute | solution.py:47
  519.8 93.2 %collective-permute-start.80 = (bf16[256,512]{1,0:T(8,128)(2,1)}, bf16[256,512]{1,0:T(8,128)(2,1)}, u32[]{:S(2)}, u32[]{:S(2)}) collective-permute-start(bf16[256,512]{1,0:T(8,128)(2,1)} %convert_add_fusion.16), channel_id=1, source_target_pairs={{0,2},{1,3},{2,0},{3,1},{4,6},{5,7},{6,4},{7,5},{8,10},{9,11},{10,... | collective-permute-start | bytes 786440 | tf_op jit(solution)/shard_map/ppermute | solution.py:47
  545.8 74.5 %collective-permute-start.85 = (f32[256,1024]{1,0:T(8,128)}, f32[256,1024]{1,0:T(8,128)}, u32[]{:S(2)}, u32[]{:S(2)}) collective-permute-start(f32[256,1024]{1,0:T(8,128)} %get-tuple-element.299), channel_id=1, source_target_pairs={{0,1},{1,0},{2,3},{3,2},{4,5},{5,4},{6,7},{7,6},{8,9},{9,8},{10,11... | collective-permute-start | bytes 3145736 | tf_op jit(solution)/shard_map/ppermute | solution.py:47
  545.8 74.5 %collective-permute-start.84 = (f32[256,1024]{1,0:T(8,128)}, f32[256,1024]{1,0:T(8,128)}, u32[]{:S(2)}, u32[]{:S(2)}) collective-permute-start(f32[256,1024]{1,0:T(8,128)} %get-tuple-element.298), channel_id=1, source_target_pairs={{0,1},{1,0},{2,3},{3,2},{4,5},{5,4},{6,7},{7,6},{8,9},{9,8},{10,11... | collective-permute-start | bytes 3145736 | tf_op jit(solution)/shard_map/ppermute | solution.py:47
  595.1 59.2 %all-to-all-start.1 = ((bf16[8,128,1024]{2,1,0:T(8,128)(2,1)}), bf16[8,128,1024]{2,1,0:T(8,128)(2,1)S(1)}, u32[]{:S(2)}, u32[]{:S(2)}) async-start(bf16[8,128,1024]{2,1,0:T(8,128)(2,1)} %bitcast.50), calls=%async_computation.1 | async-start | bytes 4194304 | tf_op jit(solution)/shard_map/all_to_all | solution.py:1128
  (231 other events, 1695.6 us)
Sparse Core Ops, SparseCore 0:
  35.2 81.7 all-gather.2
  119.8 42.3 all-gather.4

commit v5 on v4

--- a/solution.py
+++ b/solution.py
@@ -544,6 +544,7 @@
     out_group = (middle_rows, heads)
     middle_rows = hook("middle", middle_rows, out_group)
     heads_grads = [times(part, out_proj).astype(jnp.bfloat16) for part in middle_rows]
+    heads_grads = hook("heads", heads_grads, None)
     mixed_grads = attend_backward(heads_grads, mixed, logsums, segment, head_width)
     qkv_group = (rows, mixed_grads)
     mixed_grads = hook("mixed", mixed_grads, qkv_group)
@@ -672,13 +673,9 @@
     column_scale = jnp.where(in_upper(1, size, 0), upper_scale, lower_scale)
 
     def rows_of(step):
-        return pl.ds(pl.multiple_of(step * tile, tile), tile)
-
-    def times(left, right):
-        return jnp.dot(left, right, preferred_element_type=jnp.float32)
-
-    @pl.loop(0, size // tile)
-    def _(step):
+        return slice(step * tile, (step + 1) * tile)
+
+    for step in range(size // tile):
         rows = rows_of(step)
         row_scale = jnp.where(in_upper(0, tile, step * tile), upper_scale, lower_scale)
         scaled = gram_ref[rows, :] * row_scale * column_scale
@@ -688,8 +685,7 @@
     for newton_step in range(NS_STEPS):
         now, later = newton_step % 2, (newton_step + 1) % 2
 
-        @pl.loop(0, size // tile)
-        def _(step):
+        for step in range(size // tile):
             rows = rows_of(step)
             square = times(gram_half_ref[now, rows, :], gram_half_ref[now])
             mix = newton_second * gram_ref[rows, :] + newton_third * square
@@ -702,8 +698,7 @@
                 total_ref[rows, :] = total
                 total_half_ref[later, rows, :] = total.astype(jnp.bfloat16)
 
-        @pl.loop(0, size // tile)
-        def _(step):
+        for step in range(size // tile):
             rows = rows_of(step)
             mix = mix_ref[rows, :]
             if newton_step > 0:
@@ -995,19 +990,17 @@
             values, scatters["up"].sent = lax.optimization_barrier((values, scatters["up"].sent))
             scatters["up"].send()
         if name == "middle":
-            values = joined(values, dec_scatter, scatters["down"])
-            dec_scatter.send()
+            scatters["out"] = group
+        if name == "heads":
+            values = joined(values, scatters["down"])
             scatters["down"].send()
-            scatters["out"] = group
         if name == "mixed":
             late = scatters["late"] = Scatter([group, scatters["out"]])
             late.send()
             values = after(values, late.sent)
-            values, dec_scatter.received = joined(
-                (values, dec_scatter.received), scatters["down"], scatters["up"]
-            )
-            scatters["up"].send()
-            scatters["down"].send()
+            values = joined(values, scatters["down"], scatters["up"], dec_scatter)
+            for scatter in (scatters["up"], scatters["down"], dec_scatter):
+                scatter.send()
         return values
 
     enc_back_terms, enc_middle_grads, _, enc_norm_grads = block_backward(
@@ -1024,8 +1017,8 @@
     late, up, down = (scatters[name] for name in ("late", "up", "down"))
     norm_hops = HopSum(jnp.concatenate([enc_norm_grads, dec_norm_grads], axis=1))
     norm_hops.step(2)
-    enc_back_terms, norm_hops.value, down.received = joined(
-        (enc_back_terms, norm_hops.value, down.received), late, up
+    enc_back_terms, norm_hops.value, down.received, dec_scatter.received = joined(
+        (enc_back_terms, norm_hops.value, down.received, dec_scatter.received), late, up
     )
     late.send()
     up.send()
@@ -1038,12 +1031,14 @@
         jnp.pad(part, ((0, 0), (0, half_width - part.shape[1])))
         for part in split_columns(dec_sum_rows, dec_widths)
     ]
-    narrow = {
-        dec_slots[0]: jnp.concatenate(half_rows[:2], axis=0),
-        dec_slots[1]: jnp.concatenate(half_rows[2:], axis=0),
-        enc_slots[4]: bridge_rows,
-    }
-    narrow_parts = collect_parts(collect_values(narrow), narrow)
+    narrow_rows = [
+        jnp.concatenate(half_rows[:2], axis=0),
+        jnp.concatenate(half_rows[2:], axis=0),
+        bridge_rows,
+    ]
+    narrow_all = lax.all_gather(
+        jnp.concatenate(narrow_rows, axis=1).astype(jnp.bfloat16), "dp", axis=0, tiled=True
+    )
     norm_hops.value, up.received = joined((norm_hops.value, up.received), late)
     up_rows = up.result()
     up_half, down_half = up_rows.astype(jnp.bfloat16), down_rows.astype(jnp.bfloat16)
@@ -1051,10 +1046,8 @@
     late.send()
     wide_crossed = cross_pair(down_half, up_half)
     norm_hops.step(1)
-    late.received, wide_crossed, norm_hops.value, enc_far_sums, narrow_parts = (
-        lax.optimization_barrier(
-            (late.received, wide_crossed, norm_hops.value, enc_far_sums, narrow_parts)
-        )
+    late.received, wide_crossed, norm_hops.value, enc_far_sums = lax.optimization_barrier(
+        (late.received, wide_crossed, norm_hops.value, enc_far_sums)
     )
     qkv_rows, out_rows = split_columns(late.result(), enc_widths[:2])
     out_padded = jnp.pad(out_rows, ((0, 0), (0, enc_widths[0] - enc_widths[1])))
@@ -1076,7 +1069,16 @@
 
     late_slots = owned(tail_parts, data_rank // 2)
     wide_slots = owned(wide_parts, data_rank // 2)
-    narrow_slots = owned(narrow_parts, data_rank)
+    dec_parts = [narrow_all[:, k * half_width : (k + 1) * half_width] for k in range(2)]
+    bridge_part = jnp.pad(
+        narrow_all[:, slot_width:], ((0, 0), (0, half_width - enc_widths[4]))
+    )
+    narrow_slots = jnp.where(
+        data_rank == dec_slots[0],
+        dec_parts[0],
+        jnp.where(data_rank == dec_slots[1], dec_parts[1], bridge_part),
+    )
+    narrow_slots = jnp.pad(narrow_slots, ((0, 0), (0, slot_width - half_width)))
     enc_norm_rows = lax.dynamic_slice_in_dim(norm_sums[:, :D], data_rank * enc_share, enc_share, 1)
     dec_norm_rows = lax.dynamic_slice_in_dim(norm_sums[:, D:], data_rank * dec_share, dec_share, 1)
     input_grads = block_input_grads(

time: 672 us -> 658 us (0.979)
  starting transfers between devices: 128 us -> 110 us
  Pallas kernels: 129 us -> 122 us
  waiting for transfers between devices: 197 us -> 204 us
    ppermute x7 -> x0, starting transfers between devices: 14.5 us -> none  [collect_parts(): lax.ppermute(value, 'dp', [(owner ^ bit, owner) for owner in owners])]
    ppermute x89, waiting for transfers between devices: 162 us -> 175 us  [pair_swap(): lax.ppermute(array, axis, [(rank, rank ^ bit) for rank in range(size)])]
    unnamed x323 -> x343, local copies, waits for them, and re-layouts: 17.9 us -> 20.1 us
  transfers between devices with their start and end apart: 106 -> 100, of which waited for: 40 -> 37; matrix products, arithmetic and copies ran while one was open for 24% -> 24% of each run, Pallas kernels for 18% -> 18%
where the time goes in v5:
time: 658 us; the launch traced here: 653 us
  waiting for transfers between devices  204 us (31%)
  Pallas kernels  122 us (19%)
  starting transfers between devices  110 us (17%)
  other arithmetic  89.1 us (14%)
  matrix products  69.9 us (11%)
  local copies, waits for them, and re-layouts  36.6 us (6%)
  between operations  21 us (3%)
    ppermute x89, waiting for transfers between devices, pair_swap(): lax.ppermute(array, axis, [(rank, rank ^ bit) for rank in range(size)])  175 us
    ppermute x89, starting transfers between devices, pair_swap(): lax.ppermute(array, axis, [(rank, rank ^ bit) for rank in range(size)])  78.5 us
    pallas_call x1, Pallas kernels, newton(): pl.pallas_call(functools.partial(newton_kernel, enc_rows, dec_rows), in_s...  44 us
    dot_general x36, matrix products, times_turned(): jnp.einsum('tf,df->td', left, right, preferred_element_type=jnp.float32)  33.9 us
    dot_general x31, matrix products, times(): return jnp.dot(left, right, preferred_element_type=jnp.float32)  33.6 us
    all_to_all x1, waiting for transfers between devices, local(): lax.all_to_all(orthogonal.reshape(data_ranks, enc_rows, slot_width), 'dp'...  28.4 us
    pallas_call x4, Pallas kernels, weight_grads(): pl.pallas_call(functools.partial(weight_grads_kernel, [(len(lefts), len(r...  27.5 us
    pallas_call x2, Pallas kernels, attend_backward(): pl.pallas_call(functools.partial(attend_backward_kernel, head_width, len(...  27 us
  transfers between devices with their start and end apart: 100, of which 37 were waited for; matrix products, arithmetic and copies ran while one was open for 24% of the time, Pallas kernels for 18%

profile of v5, /device:TPU:0, one launch (start us, length us, event | category | flops | bytes accessed | tf_op | source)
XLA Modules:
  0.0 653.1 jit_solution(9509212303677685329)
XLA Ops:
  20.6 4.0 collective-permute-done.4.refs_2_
  24.6 10.5 %collective-permute-done.6.refs_4_ = bf16[128,1024]{1,0:T(8,128)(2,1)} collective-permute-done((bf16[128,1024]{1,0:T(8,128)(2,1)S(1)}, bf16[128,1024]{1,0:T(8,128)(2,1)}, u32[]{:S(2)}, u32[]{:S(2)}) %collective-permute-start.6) | collective-permute-done | bytes 262176 | tf_op jit(solution)/shard_map/ppermute | solution.py:47
  35.6 4.5 collective-permute-start.1
  49.1 4.5 subtract_multiply_fusion
  53.6 6.9 %collective-permute-done.5.refs_3_ = bf16[128,1024]{1,0:T(8,128)(2,1)S(1)} collective-permute-done((bf16[128,1024]{1,0:T(8,128)(2,1)}, bf16[128,1024]{1,0:T(8,128)(2,1)S(1)}, u32[]{:S(2)}, u32[]{:S(2)}) %collective-permute-start.5) | collective-permute-done | bytes 262176 | tf_op jit(solution)/shard_map/ppermute | solution.py:47
  60.6 5.2 collective-permute-done.7.refs_5_
  75.5 3.9 attend_forward.4
  92.7 7.8 %collective-permute-done.11 = bf16[256,1024]{1,0:T(8,128)(2,1)S(1)} collective-permute-done((bf16[256,1024]{1,0:T(8,128)(2,1)S(1)}, bf16[256,1024]{1,0:T(8,128)(2,1)S(1)}, u32[]{:S(2)}, u32[]{:S(2)}) %collective-permute-start.11) | collective-permute-done | bytes 524320 | tf_op jit(solution)/shard_map/ppermute | solution.py:47
  100.5 10.4 %collective-permute-done.19 = bf16[256,1024]{1,0:T(8,128)(2,1)} collective-permute-done((bf16[256,1024]{1,0:T(8,128)(2,1)S(1)}, bf16[256,1024]{1,0:T(8,128)(2,1)}, u32[]{:S(2)}, u32[]{:S(2)}) %collective-permute-start.19) | collective-permute-done | bytes 524320 | tf_op jit(solution)/shard_map/ppermute | solution.py:47
  139.8 8.3 %collective-permute-done.22 = bf16[256,1024]{1,0:T(8,128)(2,1)} collective-permute-done((bf16[256,1024]{1,0:T(8,128)(2,1)}, bf16[256,1024]{1,0:T(8,128)(2,1)}, u32[]{:S(2)}, u32[]{:S(2)}) %collective-permute-start.22) | collective-permute-done | bytes 524320 | tf_op jit(solution)/shard_map/ppermute | solution.py:47
  150.4 8.3 %collective-permute-done.14 = bf16[256,1024]{1,0:T(8,128)(2,1)} collective-permute-done((bf16[256,1024]{1,0:T(8,128)(2,1)}, bf16[256,1024]{1,0:T(8,128)(2,1)}, u32[]{:S(2)}, u32[]{:S(2)}) %collective-permute-start.14) | collective-permute-done | bytes 524320 | tf_op jit(solution)/shard_map/ppermute | solution.py:47
  186.6 6.1 collective-permute-done.29
  193.1 4.3 collective-permute-done.25
  212.6 4.4 all-to-all-start
  217.1 4.1 collective-permute-done.33
  228.9 13.2 %attend_backward.2 = (bf16[256,384]{1,0:T(8,128)(2,1)S(1)}, bf16[256,384]{1,0:T(8,128)(2,1)S(1)}, bf16[256,384]{1,0:T(8,128)(2,1)S(1)}, bf16[256,384]{1,0:T(8,128)(2,1)S(1)}) custom-call(s32[1024,1]{1,0:T(8,128)S(1)} %reshape_reshape.6.key_segment_ref, s32[1,1024]{1,0:T(1,128)S(1)} %reshape_reshape.4.key_segment_ref.query_segment_ref, ...), custom_call_target="tpu_custom_call" | custom-call | flops 5368709120 | bytes 1835008 | tf_op jit(solution)/shard_map/attend_backward/pallas_call | solution.py:453
  251.1 7.1 %weight_grads.4 = (bf16[256,1536]{1,0:T(8,128)(2,1)}, bf16[256,1536]{1,0:T(8,128)(2,1)}) custom-call(s32[1]{0:T(128)} %bitcast.20.parity_ref, bf16[256,512]{1,0:T(8,128)(2,1)} %get-tuple-element.341.refs_0_, bf16[256,512]{1,0:T(8,128)(2,1)} %collective-permute-done.17.refs_1_, bf16[256,512]{1,0:T(8,128)(2,1)} %get-tuple-element.340.refs_2_, ...), custom_call_target="tpu_custom_call" | custom-call | flops 1610612736 | bytes 8912896 | tf_op jit(solution)/shard_map/weight_grads/pallas_call | solution.py:616
  284.3 7.2 %weight_grads.6 = (bf16[512,1152]{1,0:T(8,128)(2,1)}, bf16[512,1152]{1,0:T(8,128)(2,1)}) custom-call(s32[1]{0:T(128)} %bitcast.20.parity_ref, bf16[256,1024]{1,0:T(8,128)(2,1)} %copy-done.113, bf16[256,1024]{1,0:T(8,128)(2,1)} %copy-done.104, bf16[256,1024]{1,0:T(8,128)(2,1)} %copy-done.114, bf16[256,1024]{1,0:T(8,128)(2,1)} %copy-done.107, ...), custom_call_target="tpu_custom_call" | custom-call | flops 2415919104 | bytes 8912896 | tf_op jit(solution)/shard_map/weight_grads/pallas_call | solution.py:616
  292.8 6.3 weight_grads.5
  300.6 6.2 collective-permute-done.47
  324.6 13.8 %attend_backward.3 = (bf16[256,768]{1,0:T(8,128)(2,1)S(1)}, bf16[256,768]{1,0:T(8,128)(2,1)S(1)}, bf16[256,768]{1,0:T(8,128)(2,1)S(1)}, bf16[256,768]{1,0:T(8,128)(2,1)S(1)}) custom-call(s32[1024,1]{1,0:T(8,128)S(1)} %reshape_reshape.6.key_segment_ref, s32[1,1024]{1,0:T(1,128)S(1)} %reshape_reshape.4.key_segment_ref.query_segment_ref, ...), custom_call_target="tpu_custom_call" | custom-call | flops 10737418240 | bytes 3670016 | tf_op jit(solution)/shard_map/attend_backward/pallas_call | solution.py:453
  341.5 6.8 %weight_grads.7 = (bf16[512,1024]{1,0:T(8,128)(2,1)}, bf16[512,1024]{1,0:T(8,128)(2,1)}) custom-call(s32[1]{0:T(128)} %bitcast.20.parity_ref, bf16[1024,1024]{1,0:T(8,128)(2,1)} %copy-done.70, bf16[256,768]{1,0:T(8,128)(2,1)} %copy-done.4, bf16[256,768]{1,0:T(8,128)(2,1)} %copy-done.18, bf16[256,768]{1,0:T(8,128)(2,1)} %copy-done.14, ...), custom_call_target="tpu_custom_call" | custom-call | flops 2147483648 | bytes 8388608 | tf_op jit(solution)/shard_map/weight_grads/pallas_call | solution.py:616
  366.7 10.4 %collective-permute-done.62 = bf16[64,1536]{1,0:T(8,128)(2,1)S(1)} collective-permute-done((bf16[64,1536]{1,0:T(8,128)(2,1)S(1)}, bf16[64,1536]{1,0:T(8,128)(2,1)S(1)}, u32[]{:S(2)}, u32[]{:S(2)}) %collective-permute-start.62) | collective-permute-done | bytes 196640 | tf_op jit(solution)/shard_map/ppermute | solution.py:47
  391.8 16.1 %collective-permute-done.66 = bf16[128,1024]{1,0:T(8,128)(2,1)} collective-permute-done((bf16[128,1024]{1,0:T(8,128)(2,1)}, bf16[128,1024]{1,0:T(8,128)(2,1)}, u32[]{:S(2)}, u32[]{:S(2)}) %collective-permute-start.66) | collective-permute-done | bytes 262176 | tf_op jit(solution)/shard_map/ppermute | solution.py:47
  416.1 7.9 %collective-permute-done.70 = f32[4,1536]{1,0:T(4,128)S(1)} collective-permute-done((f32[4,1536]{1,0:T(4,128)S(1)}, f32[4,1536]{1,0:T(4,128)S(1)}, u32[]{:S(2)}, u32[]{:S(2)}) %collective-permute-start.70) | collective-permute-done | bytes 24608 | tf_op jit(solution)/shard_map/ppermute | solution.py:47
  424.0 10.4 %collective-permute-done.68 = bf16[128,1024]{1,0:T(8,128)(2,1)S(1)} collective-permute-done((bf16[128,1024]{1,0:T(8,128)(2,1)S(1)}, bf16[128,1024]{1,0:T(8,128)(2,1)S(1)}, u32[]{:S(2)}, u32[]{:S(2)}) %collective-permute-start.68) | collective-permute-done | bytes 262176 | tf_op jit(solution)/shard_map/ppermute | solution.py:47
  451.0 7.3 %collective-permute-start.84 = (f32[8,128]{1,0:T(8,128)S(1)}, f32[8,128]{1,0:T(8,128)S(1)}, u32[]{:S(2)}, u32[]{:S(2)}) collective-permute-start(f32[8,128]{1,0:T(8,128)S(1)} %add.756), channel_id=1, source_target_pairs={{0,16},{4,20},{8,24},{12,28},{16,0},{20,4},{24,8},{28,12},{1,17},{... | collective-permute-start | bytes 12296 | tf_op jit(solution)/shard_map/ppermute | solution.py:47
  464.8 6.2 collective-permute-start.89
  509.5 19.0 %collective-permute-done.93 = f32[1280,256]{1,0:T(8,128)} collective-permute-done((f32[1280,256]{1,0:T(8,128)}, f32[1280,256]{1,0:T(8,128)}, u32[]{:S(2)}, u32[]{:S(2)}) %collective-permute-start.93) | collective-permute-done | bytes 1310752 | tf_op jit(solution)/shard_map/ppermute | solution.py:47
  534.4 44.0 %newton.1 = bf16[1024,1024]{1,0:T(8,128)(2,1)} custom-call(s32[1]{0:T(128)} %bitcast.48.paired_ref, f32[1280,256]{1,0:T(8,128)S(1)} %get-tuple-element.294.low_ref, f32[1280,256]{1,0:T(8,128)S(1)} %get-tuple-element.293.high_ref, bf16[1024,1024]{1,0:T(8,128)(2,1)} %copy-done.63), custom_call_target="tpu_custom_call" | custom-call | flops 38654705664 | bytes 20971520 | tf_op jit(solution)/shard_map/newton/pallas_call | solution.py:723
  578.4 13.5 %all-to-all-start.1 = ((bf16[8,128,1024]{2,1,0:T(8,128)(2,1)}), bf16[8,128,1024]{2,1,0:T(8,128)(2,1)S(1)}, u32[]{:S(2)}, u32[]{:S(2)}) async-start(bf16[8,128,1024]{2,1,0:T(8,128)(2,1)} %bitcast.50), calls=%async_computation.1 | async-start | bytes 4194304 | tf_op jit(solution)/shard_map/all_to_all | solution.py:1130
  611.9 28.4 %all-to-all-done.1 = bf16[8,128,1024]{2,1,0:T(8,128)(2,1)S(1)} async-done(((bf16[8,128,1024]{2,1,0:T(8,128)(2,1)}), bf16[8,128,1024]{2,1,0:T(8,128)(2,1)S(1)}, u32[]{:S(2)}, u32[]{:S(2)}) %all-to-all-start.1) | async-done | bytes 2097184 | tf_op jit(solution)/shard_map/all_to_all | solution.py:1130
  (811 shorter events, 315.0 us)
Async XLA Ops:
  7.2 109.8 %all-gather.4.cloned.1.call-start = ((), (), s32[]{:S(2)}) async-start(), calls=%async_computation.2 | async-start | bytes 5013504 | tf_op jit(solution)/shard_map/all_gather | solution.py:840
  9.0 44.6 %collective-permute-start.3 = (bf16[128,1024]{1,0:T(8,128)(2,1)S(1)}, bf16[128,1024]{1,0:T(8,128)(2,1)S(1)}, u32[]{:S(2)}, u32[]{:S(2)}) collective-permute-start(bf16[128,1024]{1,0:T(8,128)(2,1)S(1)} %slice.376.refs_0_), channel_id=1, source_target_pairs={{0,4},{4,0},{8,12},{12,8},{16,20},{20,16},{24,28},{28,24},{1,5},{5... | collective-permute-start | bytes 786440 | tf_op jit(solution)/shard_map/ppermute | solution.py:47
  13.6 21.5 %collective-permute-start.6 = (bf16[128,1024]{1,0:T(8,128)(2,1)S(1)}, bf16[128,1024]{1,0:T(8,128)(2,1)}, u32[]{:S(2)}, u32[]{:S(2)}) collective-permute-start(bf16[128,1024]{1,0:T(8,128)(2,1)S(1)} %slice.376.refs_0_), channel_id=1, source_target_pairs={{0,16},{4,20},{8,24},{12,28},{16,0},{20,4},{24,8},{28,12},{1,17},{... | collective-permute-start | bytes 786440 | tf_op jit(solution)/shard_map/ppermute | solution.py:47
  35.1 132.3 %all-gather.6.cloned.1.call-start = ((), (), s32[]{:S(2)}) async-start(), calls=%async_computation.3 | async-start | bytes 1769472 | tf_op jit(solution)/shard_map/all_gather | solution.py:843
  87.8 23.2 %collective-permute-start.19 = (bf16[256,1024]{1,0:T(8,128)(2,1)S(1)}, bf16[256,1024]{1,0:T(8,128)(2,1)}, u32[]{:S(2)}, u32[]{:S(2)}) collective-permute-start(bf16[256,1024]{1,0:T(8,128)(2,1)S(1)} %fusion.5), channel_id=1, source_target_pairs={{0,2},{1,3},{2,0},{3,1},{4,6},{5,7},{6,4},{7,5},{8,10},{9,11},{10,... | collective-permute-start | bytes 1572872 | tf_op jit(solution)/shard_map/ppermute | solution.py:47
  135.2 23.5 %collective-permute-start.14 = (bf16[256,1024]{1,0:T(8,128)(2,1)}, bf16[256,1024]{1,0:T(8,128)(2,1)}, u32[]{:S(2)}, u32[]{:S(2)}) collective-permute-start(bf16[256,1024]{1,0:T(8,128)(2,1)} %add_convert_fusion.13), channel_id=1, source_target_pairs={{0,2},{1,3},{2,0},{3,1},{4,6},{5,7},{6,4},{7,5},{8,10},{9,11},{10,... | collective-permute-start | bytes 1572872 | tf_op jit(solution)/shard_map/ppermute | solution.py:47
  212.6 52.7 %all-to-all-start = ((bf16[8,128,1024]{2,1,0:T(8,128)(2,1)}), bf16[8,128,1024]{2,1,0:T(8,128)(2,1)}, u32[]{:S(2)}, u32[]{:S(2)}) async-start(bf16[8,128,1024]{2,1,0:T(8,128)(2,1)} %fusion.119), calls=%async_computation | async-start | bytes 4194304 | tf_op jit(solution)/shard_map/all_to_all | solution.py:874
  217.0 265.2 %all-gather.8.cloned.1.call-start = ((), (), s32[]{:S(2)}) async-start(), calls=%async_computation.4 | async-start | bytes 2654208 | tf_op jit(solution)/shard_map/all_gather | solution.py:1039
  264.5 43.5 %collective-permute-start.48 = (bf16[256,1536]{1,0:T(8,128)(2,1)}, bf16[256,1536]{1,0:T(8,128)(2,1)}, u32[]{:S(2)}, u32[]{:S(2)}) collective-permute-start(bf16[256,1536]{1,0:T(8,128)(2,1)} %get-tuple-element.132), channel_id=1, source_target_pairs={{0,4},{4,0},{8,12},{12,8},{16,20},{20,16},{24,28},{28,24},{1,5},{5... | collective-permute-start | bytes 2359304 | tf_op jit(solution)/shard_map/ppermute | solution.py:47
  282.9 23.9 %collective-permute-start.47 = (bf16[256,1024]{1,0:T(8,128)(2,1)S(1)}, bf16[256,1024]{1,0:T(8,128)(2,1)}, u32[]{:S(2)}, u32[]{:S(2)}) collective-permute-start(bf16[256,1024]{1,0:T(8,128)(2,1)S(1)} %get-tuple-element.387), channel_id=1, source_target_pairs={{0,2},{1,3},{2,0},{3,1},{4,6},{5,7},{6,4},{7,5},{8,10},{9,11},{10,... | collective-permute-start | bytes 1572872 | tf_op jit(solution)/shard_map/ppermute | solution.py:47
  291.5 29.3 %collective-permute-start.53 = (bf16[512,1152]{1,0:T(8,128)(2,1)}, bf16[512,1152]{1,0:T(8,128)(2,1)}, u32[]{:S(2)}, u32[]{:S(2)}) collective-permute-start(bf16[512,1152]{1,0:T(8,128)(2,1)} %get-tuple-element.138), channel_id=1, source_target_pairs={{0,4},{4,0},{8,12},{12,8},{16,20},{20,16},{24,28},{28,24},{1,5},{5... | collective-permute-start | bytes 3538952 | tf_op jit(solution)/shard_map/ppermute | solution.py:47
  312.3 37.3 %collective-permute-start.55 = (bf16[512,1024]{1,0:T(8,128)(2,1)}, bf16[512,1024]{1,0:T(8,128)(2,1)S(1)}, u32[]{:S(2)}, u32[]{:S(2)}) collective-permute-start(bf16[512,1024]{1,0:T(8,128)(2,1)} %get-tuple-element.157), channel_id=1, source_target_pairs={{0,4},{4,0},{8,12},{12,8},{16,20},{20,16},{24,28},{28,24},{1,5},{5... | collective-permute-start | bytes 3145736 | tf_op jit(solution)/shard_map/ppermute | solution.py:47
  315.7 34.0 %collective-permute-start.56 = (bf16[128,1536]{1,0:T(8,128)(2,1)}, bf16[128,1536]{1,0:T(8,128)(2,1)}, u32[]{:S(2)}, u32[]{:S(2)}) collective-permute-start(bf16[128,1536]{1,0:T(8,128)(2,1)} %constant_dynamic-slice_fusion.8), channel_id=1, source_target_pairs={{0,8},{4,12},{8,0},{12,4},{16,24},{20,28},{24,16},{28,20},{1,9},{5... | collective-permute-start | bytes 1179656 | tf_op jit(solution)/shard_map/ppermute | solution.py:47
  323.3 26.3 %collective-permute-start.54 = (bf16[256,1152]{1,0:T(8,128)(2,1)}, bf16[256,1152]{1,0:T(8,128)(2,1)}, u32[]{:S(2)}, u32[]{:S(2)}) collective-permute-start(bf16[256,1152]{1,0:T(8,128)(2,1)} %constant_dynamic-slice_fusion.9), channel_id=1, source_target_pairs={{0,8},{4,12},{8,0},{12,4},{16,24},{20,28},{24,16},{28,20},{1,9},{5... | collective-permute-start | bytes 1769480 | tf_op jit(solution)/shard_map/ppermute | solution.py:47
  348.3 28.8 %collective-permute-start.63 = (bf16[512,1024]{1,0:T(8,128)(2,1)}, bf16[512,1024]{1,0:T(8,128)(2,1)S(1)}, u32[]{:S(2)}, u32[]{:S(2)}) collective-permute-start(bf16[512,1024]{1,0:T(8,128)(2,1)} %get-tuple-element.150), channel_id=1, source_target_pairs={{0,4},{4,0},{8,12},{12,8},{16,20},{20,16},{24,28},{28,24},{1,5},{5... | collective-permute-start | bytes 3145736 | tf_op jit(solution)/shard_map/ppermute | solution.py:47
  353.8 23.3 %collective-permute-start.61 = (bf16[128,1152]{1,0:T(8,128)(2,1)S(1)}, bf16[128,1152]{1,0:T(8,128)(2,1)S(1)}, u32[]{:S(2)}, u32[]{:S(2)}) collective-permute-start(bf16[128,1152]{1,0:T(8,128)(2,1)S(1)} %constant_dynamic-slice_fusion.7), channel_id=1, source_target_pairs={{0,16},{4,20},{8,24},{12,28},{16,0},{20,4},{24,8},{28,12},{1,17},{... | collective-permute-start | bytes 884744 | tf_op jit(solution)/shard_map/ppermute | solution.py:47
  355.7 23.9 %collective-permute-start.64 = (bf16[256,1024]{1,0:T(8,128)(2,1)S(1)}, bf16[256,1024]{1,0:T(8,128)(2,1)S(1)}, u32[]{:S(2)}, u32[]{:S(2)}) collective-permute-start(bf16[256,1024]{1,0:T(8,128)(2,1)S(1)} %constant_dynamic-slice_fusion.5), channel_id=1, source_target_pairs={{0,8},{4,12},{8,0},{12,4},{16,24},{20,28},{24,16},{28,20},{1,9},{5... | collective-permute-start | bytes 1572872 | tf_op jit(solution)/shard_map/ppermute | solution.py:47
  381.6 28.1 %collective-permute-start.67 = (bf16[256,1024]{1,0:T(8,128)(2,1)}, bf16[256,1024]{1,0:T(8,128)(2,1)}, u32[]{:S(2)}, u32[]{:S(2)}) collective-permute-start(bf16[256,1024]{1,0:T(8,128)(2,1)} %constant_dynamic-slice_fusion.3), channel_id=1, source_target_pairs={{0,8},{4,12},{8,0},{12,4},{16,24},{20,28},{24,16},{28,20},{1,9},{5... | collective-permute-start | bytes 1572872 | tf_op jit(solution)/shard_map/ppermute | solution.py:47
  385.8 22.1 %collective-permute-start.66 = (bf16[128,1024]{1,0:T(8,128)(2,1)}, bf16[128,1024]{1,0:T(8,128)(2,1)}, u32[]{:S(2)}, u32[]{:S(2)}) collective-permute-start(bf16[128,1024]{1,0:T(8,128)(2,1)} %constant_dynamic-slice_fusion.4), channel_id=1, source_target_pairs={{0,16},{4,20},{8,24},{12,28},{16,0},{20,4},{24,8},{28,12},{1,17},{... | collective-permute-start | bytes 786440 | tf_op jit(solution)/shard_map/ppermute | solution.py:47
  389.6 26.1 %collective-permute-start.71 = (bf16[256,1024]{1,0:T(8,128)(2,1)S(1)}, bf16[256,1024]{1,0:T(8,128)(2,1)S(1)}, u32[]{:S(2)}, u32[]{:S(2)}) collective-permute-start(bf16[256,1024]{1,0:T(8,128)(2,1)S(1)} %convert_element_type.775), channel_id=1, source_target_pairs={{0,2},{1,3},{2,0},{3,1},{4,6},{5,7},{6,4},{7,5},{8,10},{9,11},{10,... | collective-permute-start | bytes 1572872 | tf_op jit(solution)/shard_map/ppermute | solution.py:47
  390.3 25.6 %collective-permute-start.72 = (bf16[256,1024]{1,0:T(8,128)(2,1)S(1)}, bf16[256,1024]{1,0:T(8,128)(2,1)S(1)}, u32[]{:S(2)}, u32[]{:S(2)}) collective-permute-start(bf16[256,1024]{1,0:T(8,128)(2,1)S(1)} %copy-done.112), channel_id=1, source_target_pairs={{0,2},{1,3},{2,0},{3,1},{4,6},{5,7},{6,4},{7,5},{8,10},{9,11},{10,... | collective-permute-start | bytes 1572872 | tf_op jit(solution)/shard_map/ppermute | solution.py:47
  412.1 22.3 %collective-permute-start.68 = (bf16[128,1024]{1,0:T(8,128)(2,1)S(1)}, bf16[128,1024]{1,0:T(8,128)(2,1)S(1)}, u32[]{:S(2)}, u32[]{:S(2)}) collective-permute-start(bf16[128,1024]{1,0:T(8,128)(2,1)S(1)} %constant_dynamic-slice_fusion.2), channel_id=1, source_target_pairs={{0,16},{4,20},{8,24},{12,28},{16,0},{20,4},{24,8},{28,12},{1,17},{... | collective-permute-start | bytes 786440 | tf_op jit(solution)/shard_map/ppermute | solution.py:47
  413.7 20.7 %collective-permute-start.69 = (bf16[128,1024]{1,0:T(8,128)(2,1)S(1)}, bf16[128,1024]{1,0:T(8,128)(2,1)S(1)}, u32[]{:S(2)}, u32[]{:S(2)}) collective-permute-start(bf16[128,1024]{1,0:T(8,128)(2,1)S(1)} %get-tuple-element.311), channel_id=1, source_target_pairs={{0,4},{4,0},{8,12},{12,8},{16,20},{20,16},{24,28},{28,24},{1,5},{5... | collective-permute-start | bytes 786440 | tf_op jit(solution)/shard_map/ppermute | solution.py:47
  435.4 27.6 %collective-permute-start.79 = (bf16[128,768]{1,0:T(8,128)(2,1)}, bf16[128,768]{1,0:T(8,128)(2,1)}, u32[]{:S(2)}, u32[]{:S(2)}) collective-permute-start(bf16[128,768]{1,0:T(8,128)(2,1)} %get-tuple-element.315), channel_id=1, source_target_pairs={{0,4},{4,0},{8,12},{12,8},{16,20},{20,16},{24,28},{28,24},{1,5},{5... | collective-permute-start | bytes 589832 | tf_op jit(solution)/shard_map/ppermute | solution.py:47
  438.1 24.9 %collective-permute-start.85 = (f32[4,1536]{1,0:T(4,128)S(1)}, f32[4,1536]{1,0:T(4,128)S(1)}, u32[]{:S(2)}, u32[]{:S(2)}) collective-permute-start(f32[4,1536]{1,0:T(4,128)S(1)} %add.740), channel_id=1, source_target_pairs={{0,16},{4,20},{8,24},{12,28},{16,0},{20,4},{24,8},{28,12},{1,17},{... | collective-permute-start | bytes 73736 | tf_op jit(solution)/shard_map/ppermute | solution.py:47
  439.3 33.1 %collective-permute-start.86 = (bf16[256,1024]{1,0:T(8,128)(2,1)S(1)}, bf16[256,1024]{1,0:T(8,128)(2,1)S(1)}, u32[]{:S(2)}, u32[]{:S(2)}) collective-permute-start(bf16[256,1024]{1,0:T(8,128)(2,1)S(1)} %pad_maximum_fusion.5.refs_0_), channel_id=1, source_target_pairs={{4,12},{24,16},{5,13},{25,17},{6,14},{26,18},{7,15},{27,19}} | collective-permute-start | bytes 1572872 | tf_op jit(solution)/shard_map/ppermute | solution.py:187
  496.5 31.9 %collective-permute-start.93 = (f32[1280,256]{1,0:T(8,128)}, f32[1280,256]{1,0:T(8,128)}, u32[]{:S(2)}, u32[]{:S(2)}) collective-permute-start(f32[1280,256]{1,0:T(8,128)} %select_add_fusion), channel_id=1, source_target_pairs={{0,2},{1,3},{2,0},{3,1},{4,6},{5,7},{6,4},{7,5},{8,10},{9,11},{10,... | collective-permute-start | bytes 3932168 | tf_op jit(solution)/shard_map/ppermute | solution.py:47
  507.4 89.7 %collective-permute-start.75 = (bf16[256,512]{1,0:T(8,128)(2,1)}, bf16[256,512]{1,0:T(8,128)(2,1)}, u32[]{:S(2)}, u32[]{:S(2)}) collective-permute-start(bf16[256,512]{1,0:T(8,128)(2,1)} %convert_add_fusion.15), channel_id=1, source_target_pairs={{0,2},{1,3},{2,0},{3,1},{4,6},{5,7},{6,4},{7,5},{8,10},{9,11},{10,... | collective-permute-start | bytes 786440 | tf_op jit(solution)/shard_map/ppermute | solution.py:47
  507.7 91.3 %collective-permute-start.73 = (bf16[256,512]{1,0:T(8,128)(2,1)}, bf16[256,512]{1,0:T(8,128)(2,1)}, u32[]{:S(2)}, u32[]{:S(2)}) collective-permute-start(bf16[256,512]{1,0:T(8,128)(2,1)} %convert_add_fusion.16), channel_id=1, source_target_pairs={{0,2},{1,3},{2,0},{3,1},{4,6},{5,7},{6,4},{7,5},{8,10},{9,11},{10,... | collective-permute-start | bytes 786440 | tf_op jit(solution)/shard_map/ppermute | solution.py:47
  533.7 72.6 %collective-permute-start.78 = (f32[256,1024]{1,0:T(8,128)}, f32[256,1024]{1,0:T(8,128)}, u32[]{:S(2)}, u32[]{:S(2)}) collective-permute-start(f32[256,1024]{1,0:T(8,128)} %get-tuple-element.283), channel_id=1, source_target_pairs={{0,1},{1,0},{2,3},{3,2},{4,5},{5,4},{6,7},{7,6},{8,9},{9,8},{10,11... | collective-permute-start | bytes 3145736 | tf_op jit(solution)/shard_map/ppermute | solution.py:47
  533.7 72.6 %collective-permute-start.77 = (f32[256,1024]{1,0:T(8,128)}, f32[256,1024]{1,0:T(8,128)}, u32[]{:S(2)}, u32[]{:S(2)}) collective-permute-start(f32[256,1024]{1,0:T(8,128)} %get-tuple-element.282), channel_id=1, source_target_pairs={{0,1},{1,0},{2,3},{3,2},{4,5},{5,4},{6,7},{7,6},{8,9},{9,8},{10,11... | collective-permute-start | bytes 3145736 | tf_op jit(solution)/shard_map/ppermute | solution.py:47
  578.4 62.0 %all-to-all-start.1 = ((bf16[8,128,1024]{2,1,0:T(8,128)(2,1)}), bf16[8,128,1024]{2,1,0:T(8,128)(2,1)S(1)}, u32[]{:S(2)}, u32[]{:S(2)}) async-start(bf16[8,128,1024]{2,1,0:T(8,128)(2,1)} %bitcast.50), calls=%async_computation.1 | async-start | bytes 4194304 | tf_op jit(solution)/shard_map/all_to_all | solution.py:1130
  (235 other events, 1568.1 us)
Sparse Core Ops, SparseCore 0:
  35.2 81.7 all-gather.3
  119.8 42.1 all-gather.5
  383.0 60.3 all-gather.7

commit v6 on v5

--- a/solution.py
+++ b/solution.py
@@ -1023,7 +1023,6 @@
     late.send()
     up.send()
     norm_hops.step(1)
-    enc_far_sums = [far_sum(term) for term in enc_back_terms]
     dec_sum_rows = dec_scatter.result()
     down_rows, bridge_rows = split_columns(down.result(), enc_widths[3:])
     half_width = slot_width // 2
@@ -1036,32 +1035,39 @@
         jnp.concatenate(half_rows[2:], axis=0),
         bridge_rows,
     ]
-    narrow_all = lax.all_gather(
-        jnp.concatenate(narrow_rows, axis=1).astype(jnp.bfloat16), "dp", axis=0, tiled=True
-    )
     norm_hops.value, up.received = joined((norm_hops.value, up.received), late)
     up_rows = up.result()
     up_half, down_half = up_rows.astype(jnp.bfloat16), down_rows.astype(jnp.bfloat16)
-    late.sent, up_half, down_half = lax.optimization_barrier((late.sent, up_half, down_half))
+    late.sent, up_half, down_half, narrow_rows = lax.optimization_barrier(
+        (late.sent, up_half, down_half, narrow_rows)
+    )
+    narrow_all = lax.all_gather(
+        jnp.concatenate(narrow_rows, axis=1).astype(jnp.bfloat16), "dp", axis=0, tiled=True
+    )
     late.send()
     wide_crossed = cross_pair(down_half, up_half)
     norm_hops.step(1)
-    late.received, wide_crossed, norm_hops.value, enc_far_sums = lax.optimization_barrier(
-        (late.received, wide_crossed, norm_hops.value, enc_far_sums)
+    late.received, wide_crossed, norm_hops.value = lax.optimization_barrier(
+        (late.received, wide_crossed, norm_hops.value)
     )
     qkv_rows, out_rows = split_columns(late.result(), enc_widths[:2])
     out_padded = jnp.pad(out_rows, ((0, 0), (0, enc_widths[0] - enc_widths[1])))
-    tail_crossed = cross_pair(qkv_rows.astype(jnp.bfloat16), out_padded.astype(jnp.bfloat16))
-    wide_parts = line_pair(*wide_crossed, enc_slots[2:4])
     norm_sums = norm_hops.finish()
     data_rank = lax.axis_index("dp")
     enc_sum_rows = jnp.concatenate([qkv_rows, out_rows, up_rows, down_rows, bridge_rows], axis=1)
     local_sum = jnp.sum(enc_sum_rows * enc_sum_rows) + jnp.sum(dec_sum_rows * dec_sum_rows)
     square_hops = HopSum(jnp.full((8, 128), local_sum))
+    square_hops.step(3)
+    tail_rows = (qkv_rows.astype(jnp.bfloat16), out_padded.astype(jnp.bfloat16))
+    square_hops.value, tail_rows = lax.optimization_barrier((square_hops.value, tail_rows))
+    tail_crossed = cross_pair(*tail_rows)
     squares = square_hops.finish()[0, 0]
-    tail_crossed, squares, norm_sums = lax.optimization_barrier((tail_crossed, squares, norm_sums))
+    tail_crossed, wide_crossed, squares, norm_sums = lax.optimization_barrier(
+        (tail_crossed, wide_crossed, squares, norm_sums)
+    )
     squares = squares + jnp.sum(norm_sums * norm_sums)
     tail_parts = line_pair(*tail_crossed, enc_slots[:2])
+    wide_parts = line_pair(*wide_crossed, enc_slots[2:4])
 
     def owned(parts, place):
         whole = assemble(parts, place)
@@ -1081,17 +1087,12 @@
     narrow_slots = jnp.pad(narrow_slots, ((0, 0), (0, slot_width - half_width)))
     enc_norm_rows = lax.dynamic_slice_in_dim(norm_sums[:, :D], data_rank * enc_share, enc_share, 1)
     dec_norm_rows = lax.dynamic_slice_in_dim(norm_sums[:, D:], data_rank * dec_share, dec_share, 1)
-    input_grads = block_input_grads(
-        enc_far_sums, enc_middle_grads, enc_firsts, enc_norm_values
-    )
-
     def natural(own_chunks):
         return swap_halves(jnp.concatenate(shared(own_chunks), axis=0), chunk_rows, core)
 
     dec_out_terms, _ = lax.optimization_barrier((dec_out_terms, late.received))
     decoded = [middle + far_sum(term) for middle, term in zip(dec_outs, dec_out_terms)]
     decoded = natural(decoded)
-    input_grad = natural(input_grads)
     data_rank = lax.axis_index("dp")
 
     def is_rank(*slots):
@@ -1127,6 +1128,11 @@
         lax.dot_general(own, own, (((1,), (1,)), ((), ())), preferred_element_type=jnp.float32)
     )
     orthogonal = newton(low_blocks, high_blocks, own, is_rank(*dec_slots), enc_rows, dec_rows)
+    enc_far_sums = [far_sum(term) for term in after(enc_back_terms, low_blocks)]
+    enc_far_sums, orthogonal = lax.optimization_barrier((enc_far_sums, orthogonal))
+    input_grad = natural(
+        block_input_grads(enc_far_sums, enc_middle_grads, enc_firsts, enc_norm_values)
+    )
     rows_back = lax.all_to_all(
         orthogonal.reshape(data_ranks, enc_rows, slot_width), "dp", 0, 0
     ).astype(jnp.float32)

time: 658 us -> 655 us (level)
  waiting for transfers between devices: 204 us -> 222 us
  starting transfers between devices: 110 us -> 97 us
    ppermute x6, waiting for transfers between devices: 0.02 us -> 12 us  [line_pair(): lax.ppermute(lined, 'dp', [(owner ^ 2 * bit, owner) for owner in owners])]
    ppermute x89, starting transfers between devices: 78.5 us -> 70.4 us  [pair_swap(): lax.ppermute(array, axis, [(rank, rank ^ bit) for rank in range(size)])]
    unnamed x343 -> x337, local copies, waits for them, and re-layouts: 20.1 us -> 20.7 us
  transfers between devices with their start and end apart: 100 -> 100, of which waited for: 37 -> 42; matrix products, arithmetic and copies ran while one was open for 24% -> 23% of each run, Pallas kernels for 18% -> 18%
where the time goes in v6:
time: 655 us; the launch traced here: 651 us
  waiting for transfers between devices  222 us (34%)
  Pallas kernels  122 us (19%)
  starting transfers between devices  97 us (15%)
  other arithmetic  85 us (13%)
  matrix products  66.6 us (10%)
  local copies, waits for them, and re-layouts  36.5 us (6%)
  between operations  21 us (3%)
    ppermute x89, waiting for transfers between devices, pair_swap(): lax.ppermute(array, axis, [(rank, rank ^ bit) for rank in range(size)])  180 us
    ppermute x89, starting transfers between devices, pair_swap(): lax.ppermute(array, axis, [(rank, rank ^ bit) for rank in range(size)])  70.4 us
    pallas_call x1, Pallas kernels, newton(): pl.pallas_call(functools.partial(newton_kernel, enc_rows, dec_rows), in_s...  44 us
    dot_general x31, matrix products, times(): return jnp.dot(left, right, preferred_element_type=jnp.float32)  33.5 us
    dot_general x36, matrix products, times_turned(): jnp.einsum('tf,df->td', left, right, preferred_element_type=jnp.float32)  30.7 us
    all_to_all x1, waiting for transfers between devices, local(): lax.all_to_all(orthogonal.reshape(data_ranks, enc_rows, slot_width), 'dp'...  29.2 us
    pallas_call x4, Pallas kernels, weight_grads(): pl.pallas_call(functools.partial(weight_grads_kernel, [(len(lefts), len(r...  27.5 us
    pallas_call x2, Pallas kernels, attend_backward(): pl.pallas_call(functools.partial(attend_backward_kernel, head_width, len(...  27 us
  transfers between devices with their start and end apart: 100, of which 42 were waited for; matrix products, arithmetic and copies ran while one was open for 23% of the time, Pallas kernels for 18%

profile of v6, /device:TPU:0, one launch (start us, length us, event | category | flops | bytes accessed | tf_op | source)
XLA Modules:
  0.0 650.7 jit_solution(2442140293978576719)
XLA Ops:
  20.6 4.0 collective-permute-done.4.refs_2_
  24.6 10.5 %collective-permute-done.6.refs_4_ = bf16[128,1024]{1,0:T(8,128)(2,1)} collective-permute-done((bf16[128,1024]{1,0:T(8,128)(2,1)S(1)}, bf16[128,1024]{1,0:T(8,128)(2,1)}, u32[]{:S(2)}, u32[]{:S(2)}) %collective-permute-start.6) | collective-permute-done | bytes 262176 | tf_op jit(solution)/shard_map/ppermute | solution.py:47
  35.6 4.5 collective-permute-start.1
  49.2 4.5 subtract_multiply_fusion
  53.6 6.9 %collective-permute-done.5.refs_3_ = bf16[128,1024]{1,0:T(8,128)(2,1)S(1)} collective-permute-done((bf16[128,1024]{1,0:T(8,128)(2,1)}, bf16[128,1024]{1,0:T(8,128)(2,1)S(1)}, u32[]{:S(2)}, u32[]{:S(2)}) %collective-permute-start.5) | collective-permute-done | bytes 262176 | tf_op jit(solution)/shard_map/ppermute | solution.py:47
  60.6 5.2 collective-permute-done.7.refs_5_
  79.9 3.9 attend_forward.5
  92.7 7.8 %collective-permute-done.11 = bf16[256,1024]{1,0:T(8,128)(2,1)S(1)} collective-permute-done((bf16[256,1024]{1,0:T(8,128)(2,1)S(1)}, bf16[256,1024]{1,0:T(8,128)(2,1)S(1)}, u32[]{:S(2)}, u32[]{:S(2)}) %collective-permute-start.11) | collective-permute-done | bytes 524320 | tf_op jit(solution)/shard_map/ppermute | solution.py:47
  100.5 10.4 %collective-permute-done.19 = bf16[256,1024]{1,0:T(8,128)(2,1)} collective-permute-done((bf16[256,1024]{1,0:T(8,128)(2,1)S(1)}, bf16[256,1024]{1,0:T(8,128)(2,1)}, u32[]{:S(2)}, u32[]{:S(2)}) %collective-permute-start.19) | collective-permute-done | bytes 524320 | tf_op jit(solution)/shard_map/ppermute | solution.py:47
  139.8 8.3 %collective-permute-done.22 = bf16[256,1024]{1,0:T(8,128)(2,1)} collective-permute-done((bf16[256,1024]{1,0:T(8,128)(2,1)}, bf16[256,1024]{1,0:T(8,128)(2,1)}, u32[]{:S(2)}, u32[]{:S(2)}) %collective-permute-start.22) | collective-permute-done | bytes 524320 | tf_op jit(solution)/shard_map/ppermute | solution.py:47
  150.4 8.3 %collective-permute-done.14 = bf16[256,1024]{1,0:T(8,128)(2,1)} collective-permute-done((bf16[256,1024]{1,0:T(8,128)(2,1)}, bf16[256,1024]{1,0:T(8,128)(2,1)}, u32[]{:S(2)}, u32[]{:S(2)}) %collective-permute-start.14) | collective-permute-done | bytes 524320 | tf_op jit(solution)/shard_map/ppermute | solution.py:47
  189.0 6.1 collective-permute-done.29
  195.6 4.3 collective-permute-done.25
  215.1 4.3 all-to-all-start
  219.5 4.1 collective-permute-done.33
  231.4 13.2 %attend_backward.2 = (bf16[256,384]{1,0:T(8,128)(2,1)S(1)}, bf16[256,384]{1,0:T(8,128)(2,1)S(1)}, bf16[256,384]{1,0:T(8,128)(2,1)S(1)}, bf16[256,384]{1,0:T(8,128)(2,1)S(1)}) custom-call(s32[1024,1]{1,0:T(8,128)S(1)} %reshape_reshape.6.key_segment_ref, s32[1,1024]{1,0:T(1,128)S(1)} %reshape_reshape.4.key_segment_ref.query_segment_ref, ...), custom_call_target="tpu_custom_call" | custom-call | flops 5368709120 | bytes 1835008 | tf_op jit(solution)/shard_map/attend_backward/pallas_call | solution.py:453
  253.6 7.1 %weight_grads.4 = (bf16[256,1536]{1,0:T(8,128)(2,1)}, bf16[256,1536]{1,0:T(8,128)(2,1)}) custom-call(s32[1]{0:T(128)} %bitcast.20.parity_ref, bf16[256,512]{1,0:T(8,128)(2,1)} %copy-done.95, bf16[256,512]{1,0:T(8,128)(2,1)} %collective-permute-done.17.refs_1_, bf16[256,512]{1,0:T(8,128)(2,1)} %get-tuple-element.361.refs_2_, ...), custom_call_target="tpu_custom_call" | custom-call | flops 1610612736 | bytes 8912896 | tf_op jit(solution)/shard_map/weight_grads/pallas_call | solution.py:616
  286.8 7.2 %weight_grads.6 = (bf16[512,1152]{1,0:T(8,128)(2,1)}, bf16[512,1152]{1,0:T(8,128)(2,1)}) custom-call(s32[1]{0:T(128)} %bitcast.20.parity_ref, bf16[256,1024]{1,0:T(8,128)(2,1)} %copy-done.111, bf16[256,1024]{1,0:T(8,128)(2,1)} %copy-done.101, bf16[256,1024]{1,0:T(8,128)(2,1)} %copy-done.112, bf16[256,1024]{1,0:T(8,128)(2,1)} %copy-done.106, ...), custom_call_target="tpu_custom_call" | custom-call | flops 2415919104 | bytes 8912896 | tf_op jit(solution)/shard_map/weight_grads/pallas_call | solution.py:616
  295.3 6.3 weight_grads.5
  303.1 6.1 collective-permute-done.47
  319.3 3.9 collective-permute-done.53
  327.2 13.8 %attend_backward.3 = (bf16[256,768]{1,0:T(8,128)(2,1)S(1)}, bf16[256,768]{1,0:T(8,128)(2,1)S(1)}, bf16[256,768]{1,0:T(8,128)(2,1)S(1)}, bf16[256,768]{1,0:T(8,128)(2,1)S(1)}) custom-call(s32[1024,1]{1,0:T(8,128)S(1)} %reshape_reshape.6.key_segment_ref, s32[1,1024]{1,0:T(1,128)S(1)} %reshape_reshape.4.key_segment_ref.query_segment_ref, ...), custom_call_target="tpu_custom_call" | custom-call | flops 10737418240 | bytes 3670016 | tf_op jit(solution)/shard_map/attend_backward/pallas_call | solution.py:453
  344.0 6.8 %weight_grads.7 = (bf16[512,1024]{1,0:T(8,128)(2,1)}, bf16[512,1024]{1,0:T(8,128)(2,1)}) custom-call(s32[1]{0:T(128)} %bitcast.20.parity_ref, bf16[1024,1024]{1,0:T(8,128)(2,1)} %copy-done.70, bf16[256,768]{1,0:T(8,128)(2,1)} %copy-done.4, bf16[256,768]{1,0:T(8,128)(2,1)} %copy-done.18, bf16[256,768]{1,0:T(8,128)(2,1)} %copy-done.14, ...), custom_call_target="tpu_custom_call" | custom-call | flops 2147483648 | bytes 8388608 | tf_op jit(solution)/shard_map/weight_grads/pallas_call | solution.py:616
  368.2 10.4 %collective-permute-done.62 = bf16[64,1536]{1,0:T(8,128)(2,1)S(1)} collective-permute-done((bf16[64,1536]{1,0:T(8,128)(2,1)S(1)}, bf16[64,1536]{1,0:T(8,128)(2,1)S(1)}, u32[]{:S(2)}, u32[]{:S(2)}) %collective-permute-start.62) | collective-permute-done | bytes 196640 | tf_op jit(solution)/shard_map/ppermute | solution.py:47
  386.3 9.4 %collective-permute-done.66 = bf16[128,1024]{1,0:T(8,128)(2,1)S(1)} collective-permute-done((bf16[128,1024]{1,0:T(8,128)(2,1)S(1)}, bf16[128,1024]{1,0:T(8,128)(2,1)S(1)}, u32[]{:S(2)}, u32[]{:S(2)}) %collective-permute-start.66) | collective-permute-done | bytes 262176 | tf_op jit(solution)/shard_map/ppermute | solution.py:47
  395.6 5.9 collective-permute-done.67
  409.0 12.3 %collective-permute-done.68 = bf16[128,1024]{1,0:T(8,128)(2,1)S(1)} collective-permute-done((bf16[128,1024]{1,0:T(8,128)(2,1)}, bf16[128,1024]{1,0:T(8,128)(2,1)S(1)}, u32[]{:S(2)}, u32[]{:S(2)}) %collective-permute-start.68) | collective-permute-done | bytes 262176 | tf_op jit(solution)/shard_map/ppermute | solution.py:47
  452.6 11.4 %collective-permute-done.85.refs_1_ = bf16[256,768]{1,0:T(8,128)(2,1)S(1)} collective-permute-done((bf16[256,768]{1,0:T(8,128)(2,1)S(1)}, bf16[256,768]{1,0:T(8,128)(2,1)S(1)}, u32[]{:S(2)}, u32[]{:S(2)}) %collective-permute-start.85) | collective-permute-done | bytes 393248 | tf_op jit(solution)/shard_map/ppermute | solution.py:187
  498.9 23.2 %collective-permute-done.89 = f32[1280,256]{1,0:T(8,128)} collective-permute-done((f32[1280,256]{1,0:T(8,128)}, f32[1280,256]{1,0:T(8,128)}, u32[]{:S(2)}, u32[]{:S(2)}) %collective-permute-start.89) | collective-permute-done | bytes 1310752 | tf_op jit(solution)/shard_map/ppermute | solution.py:47
  530.4 44.0 %newton.1 = bf16[1024,1024]{1,0:T(8,128)(2,1)} custom-call(s32[1]{0:T(128)} %bitcast.45.paired_ref, f32[1280,256]{1,0:T(8,128)S(1)} %get-tuple-element.314.low_ref, f32[1280,256]{1,0:T(8,128)S(1)} %get-tuple-element.313.high_ref, bf16[1024,1024]{1,0:T(8,128)(2,1)} %copy-done.65), custom_call_target="tpu_custom_call" | custom-call | flops 38654705664 | bytes 20971520 | tf_op jit(solution)/shard_map/newton/pallas_call | solution.py:723
  574.8 13.2 %all-to-all-start.1 = ((bf16[8,128,1024]{2,1,0:T(8,128)(2,1)}), bf16[8,128,1024]{2,1,0:T(8,128)(2,1)}, u32[]{:S(2)}, u32[]{:S(2)}) async-start(bf16[8,128,1024]{2,1,0:T(8,128)(2,1)} %bitcast.50), calls=%async_computation.1 | async-start | bytes 4194304 | tf_op jit(solution)/shard_map/all_to_all | solution.py:1136
  607.2 29.2 %all-to-all-done.1 = bf16[8,128,1024]{2,1,0:T(8,128)(2,1)} async-done(((bf16[8,128,1024]{2,1,0:T(8,128)(2,1)}), bf16[8,128,1024]{2,1,0:T(8,128)(2,1)}, u32[]{:S(2)}, u32[]{:S(2)}) %all-to-all-start.1) | async-done | bytes 2097184 | tf_op jit(solution)/shard_map/all_to_all | solution.py:1136
  (807 shorter events, 312.9 us)
Async XLA Ops:
  7.2 109.8 %all-gather.4.cloned.1.call-start = ((), (), s32[]{:S(2)}) async-start(), calls=%async_computation.2 | async-start | bytes 5013504 | tf_op jit(solution)/shard_map/all_gather | solution.py:840
  9.0 44.6 %collective-permute-start.3 = (bf16[128,1024]{1,0:T(8,128)(2,1)S(1)}, bf16[128,1024]{1,0:T(8,128)(2,1)S(1)}, u32[]{:S(2)}, u32[]{:S(2)}) collective-permute-start(bf16[128,1024]{1,0:T(8,128)(2,1)S(1)} %slice.372.refs_0_), channel_id=1, source_target_pairs={{0,4},{4,0},{8,12},{12,8},{16,20},{20,16},{24,28},{28,24},{1,5},{5... | collective-permute-start | bytes 786440 | tf_op jit(solution)/shard_map/ppermute | solution.py:47
  13.6 21.5 %collective-permute-start.6 = (bf16[128,1024]{1,0:T(8,128)(2,1)S(1)}, bf16[128,1024]{1,0:T(8,128)(2,1)}, u32[]{:S(2)}, u32[]{:S(2)}) collective-permute-start(bf16[128,1024]{1,0:T(8,128)(2,1)S(1)} %slice.372.refs_0_), channel_id=1, source_target_pairs={{0,16},{4,20},{8,24},{12,28},{16,0},{20,4},{24,8},{28,12},{1,17},{... | collective-permute-start | bytes 786440 | tf_op jit(solution)/shard_map/ppermute | solution.py:47
  16.4 19.1 %collective-permute-start = (bf16[1,4,192]{2,1,0:T(4,128)(2,1)S(1)}, bf16[1,4,192]{2,1,0:T(4,128)(2,1)S(1)}, u32[]{:S(2)}, u32[]{:S(2)}) collective-permute-start(bf16[1,4,192]{2,1,0:T(4,128)(2,1)S(1)} %pad_maximum_fusion.11), channel_id=1, source_target_pairs={{0,4},{4,0},{8,12},{12,8},{16,20},{20,16},{24,28},{28,24},{1,5},{5... | collective-permute-start | bytes 4616 | tf_op jit(solution)/shard_map/ppermute | solution.py:47
  35.1 133.0 %all-gather.6.cloned.1.call-start = ((), (), s32[]{:S(2)}) async-start(), calls=%async_computation.3 | async-start | bytes 1769472 | tf_op jit(solution)/shard_map/all_gather | solution.py:843
  48.6 20.0 %collective-permute-start.9 = (bf16[128,1024]{1,0:T(8,128)(2,1)}, bf16[128,1024]{1,0:T(8,128)(2,1)S(1)}, u32[]{:S(2)}, u32[]{:S(2)}) collective-permute-start(bf16[128,1024]{1,0:T(8,128)(2,1)} %collective-permute-done.8.refs_6_), channel_id=1, source_target_pairs={{0,4},{4,0},{8,12},{12,8},{16,20},{20,16},{24,28},{28,24},{1,5},{5... | collective-permute-start | bytes 786440 | tf_op jit(solution)/shard_map/ppermute | solution.py:47
  87.8 23.1 %collective-permute-start.19 = (bf16[256,1024]{1,0:T(8,128)(2,1)S(1)}, bf16[256,1024]{1,0:T(8,128)(2,1)}, u32[]{:S(2)}, u32[]{:S(2)}) collective-permute-start(bf16[256,1024]{1,0:T(8,128)(2,1)S(1)} %fusion.5), channel_id=1, source_target_pairs={{0,2},{1,3},{2,0},{3,1},{4,6},{5,7},{6,4},{7,5},{8,10},{9,11},{10,... | collective-permute-start | bytes 1572872 | tf_op jit(solution)/shard_map/ppermute | solution.py:47
  135.2 23.4 %collective-permute-start.14 = (bf16[256,1024]{1,0:T(8,128)(2,1)}, bf16[256,1024]{1,0:T(8,128)(2,1)}, u32[]{:S(2)}, u32[]{:S(2)}) collective-permute-start(bf16[256,1024]{1,0:T(8,128)(2,1)} %add_convert_fusion.13), channel_id=1, source_target_pairs={{0,2},{1,3},{2,0},{3,1},{4,6},{5,7},{6,4},{7,5},{8,10},{9,11},{10,... | collective-permute-start | bytes 1572872 | tf_op jit(solution)/shard_map/ppermute | solution.py:47
  215.1 52.8 %all-to-all-start = ((bf16[8,128,1024]{2,1,0:T(8,128)(2,1)}), bf16[8,128,1024]{2,1,0:T(8,128)(2,1)}, u32[]{:S(2)}, u32[]{:S(2)}) async-start(bf16[8,128,1024]{2,1,0:T(8,128)(2,1)} %fusion.113), calls=%async_computation | async-start | bytes 4194304 | tf_op jit(solution)/shard_map/all_to_all | solution.py:874
  219.4 256.4 %all-gather.8.cloned.1.call-start = ((), (), s32[]{:S(2)}) async-start(), calls=%async_computation.4 | async-start | bytes 2654208 | tf_op jit(solution)/shard_map/all_gather | solution.py:1044
  266.4 20.4 %collective-permute-start.51 = (bf16[256,1024]{1,0:T(8,128)(2,1)}, bf16[256,1024]{1,0:T(8,128)(2,1)}, u32[]{:S(2)}, u32[]{:S(2)}) collective-permute-start(bf16[256,1024]{1,0:T(8,128)(2,1)} %add_convert_fusion.12.refs_8_), channel_id=1, source_target_pairs={{0,1},{1,0},{2,3},{3,2},{4,5},{5,4},{6,7},{7,6},{8,9},{9,8},{10,11... | collective-permute-start | bytes 1572872 | tf_op jit(solution)/shard_map/ppermute | solution.py:47
  266.5 20.3 %collective-permute-start.52 = (bf16[256,1024]{1,0:T(8,128)(2,1)S(1)}, bf16[256,1024]{1,0:T(8,128)(2,1)}, u32[]{:S(2)}, u32[]{:S(2)}) collective-permute-start(bf16[256,1024]{1,0:T(8,128)(2,1)S(1)} %copy-done.69), channel_id=1, source_target_pairs={{0,1},{1,0},{2,3},{3,2},{4,5},{5,4},{6,7},{7,6},{8,9},{9,8},{10,11... | collective-permute-start | bytes 1572872 | tf_op jit(solution)/shard_map/ppermute | solution.py:47
  267.0 42.4 %collective-permute-start.48 = (bf16[256,1536]{1,0:T(8,128)(2,1)}, bf16[256,1536]{1,0:T(8,128)(2,1)}, u32[]{:S(2)}, u32[]{:S(2)}) collective-permute-start(bf16[256,1536]{1,0:T(8,128)(2,1)} %get-tuple-element.143), channel_id=1, source_target_pairs={{0,4},{4,0},{8,12},{12,8},{16,20},{20,16},{24,28},{28,24},{1,5},{5... | collective-permute-start | bytes 2359304 | tf_op jit(solution)/shard_map/ppermute | solution.py:47
  285.4 23.8 %collective-permute-start.47 = (bf16[256,1024]{1,0:T(8,128)(2,1)S(1)}, bf16[256,1024]{1,0:T(8,128)(2,1)S(1)}, u32[]{:S(2)}, u32[]{:S(2)}) collective-permute-start(bf16[256,1024]{1,0:T(8,128)(2,1)S(1)} %get-tuple-element.408), channel_id=1, source_target_pairs={{0,2},{1,3},{2,0},{3,1},{4,6},{5,7},{6,4},{7,5},{8,10},{9,11},{10,... | collective-permute-start | bytes 1572872 | tf_op jit(solution)/shard_map/ppermute | solution.py:47
  294.0 29.3 %collective-permute-start.53 = (bf16[512,1152]{1,0:T(8,128)(2,1)}, bf16[512,1152]{1,0:T(8,128)(2,1)}, u32[]{:S(2)}, u32[]{:S(2)}) collective-permute-start(bf16[512,1152]{1,0:T(8,128)(2,1)} %get-tuple-element.149), channel_id=1, source_target_pairs={{0,4},{4,0},{8,12},{12,8},{16,20},{20,16},{24,28},{28,24},{1,5},{5... | collective-permute-start | bytes 3538952 | tf_op jit(solution)/shard_map/ppermute | solution.py:47
  313.6 38.5 %collective-permute-start.55 = (bf16[512,1024]{1,0:T(8,128)(2,1)}, bf16[512,1024]{1,0:T(8,128)(2,1)S(1)}, u32[]{:S(2)}, u32[]{:S(2)}) collective-permute-start(bf16[512,1024]{1,0:T(8,128)(2,1)} %get-tuple-element.168), channel_id=1, source_target_pairs={{0,4},{4,0},{8,12},{12,8},{16,20},{20,16},{24,28},{28,24},{1,5},{5... | collective-permute-start | bytes 3145736 | tf_op jit(solution)/shard_map/ppermute | solution.py:47
  317.0 35.2 %collective-permute-start.56 = (bf16[128,1536]{1,0:T(8,128)(2,1)}, bf16[128,1536]{1,0:T(8,128)(2,1)}, u32[]{:S(2)}, u32[]{:S(2)}) collective-permute-start(bf16[128,1536]{1,0:T(8,128)(2,1)} %constant_dynamic-slice_fusion.8), channel_id=1, source_target_pairs={{0,8},{4,12},{8,0},{12,4},{16,24},{20,28},{24,16},{28,20},{1,9},{5... | collective-permute-start | bytes 1179656 | tf_op jit(solution)/shard_map/ppermute | solution.py:47
  325.8 26.3 %collective-permute-start.54 = (bf16[256,1152]{1,0:T(8,128)(2,1)}, bf16[256,1152]{1,0:T(8,128)(2,1)}, u32[]{:S(2)}, u32[]{:S(2)}) collective-permute-start(bf16[256,1152]{1,0:T(8,128)(2,1)} %constant_dynamic-slice_fusion.9), channel_id=1, source_target_pairs={{0,8},{4,12},{8,0},{12,4},{16,24},{20,28},{24,16},{28,20},{1,9},{5... | collective-permute-start | bytes 1769480 | tf_op jit(solution)/shard_map/ppermute | solution.py:47
  350.8 27.8 %collective-permute-start.63 = (bf16[512,1024]{1,0:T(8,128)(2,1)}, bf16[512,1024]{1,0:T(8,128)(2,1)S(1)}, u32[]{:S(2)}, u32[]{:S(2)}) collective-permute-start(bf16[512,1024]{1,0:T(8,128)(2,1)} %get-tuple-element.161), channel_id=1, source_target_pairs={{0,4},{4,0},{8,12},{12,8},{16,20},{20,16},{24,28},{28,24},{1,5},{5... | collective-permute-start | bytes 3145736 | tf_op jit(solution)/shard_map/ppermute | solution.py:47
  355.3 23.3 %collective-permute-start.61 = (bf16[128,1152]{1,0:T(8,128)(2,1)S(1)}, bf16[128,1152]{1,0:T(8,128)(2,1)S(1)}, u32[]{:S(2)}, u32[]{:S(2)}) collective-permute-start(bf16[128,1152]{1,0:T(8,128)(2,1)S(1)} %constant_dynamic-slice_fusion.7), channel_id=1, source_target_pairs={{0,16},{4,20},{8,24},{12,28},{16,0},{20,4},{24,8},{28,12},{1,17},{... | collective-permute-start | bytes 884744 | tf_op jit(solution)/shard_map/ppermute | solution.py:47
  357.2 24.0 %collective-permute-start.64 = (bf16[256,1024]{1,0:T(8,128)(2,1)S(1)}, bf16[256,1024]{1,0:T(8,128)(2,1)S(1)}, u32[]{:S(2)}, u32[]{:S(2)}) collective-permute-start(bf16[256,1024]{1,0:T(8,128)(2,1)S(1)} %constant_dynamic-slice_fusion.5), channel_id=1, source_target_pairs={{0,8},{4,12},{8,0},{12,4},{16,24},{20,28},{24,16},{28,20},{1,9},{5... | collective-permute-start | bytes 1572872 | tf_op jit(solution)/shard_map/ppermute | solution.py:47
  444.0 20.0 %collective-permute-start.85 = (bf16[256,768]{1,0:T(8,128)(2,1)S(1)}, bf16[256,768]{1,0:T(8,128)(2,1)S(1)}, u32[]{:S(2)}, u32[]{:S(2)}) collective-permute-start(bf16[256,768]{1,0:T(8,128)(2,1)S(1)} %pad_maximum_fusion.6.refs_0_), channel_id=1, source_target_pairs={{0,8},{28,20},{1,9},{29,21},{2,10},{30,22},{3,11},{31,23}} | collective-permute-start | bytes 1179656 | tf_op jit(solution)/shard_map/ppermute | solution.py:187
  448.0 23.4 %collective-permute-start.82 = (bf16[256,1024]{1,0:T(8,128)(2,1)S(1)}, bf16[256,1024]{1,0:T(8,128)(2,1)S(1)}, u32[]{:S(2)}, u32[]{:S(2)}) collective-permute-start(bf16[256,1024]{1,0:T(8,128)(2,1)S(1)} %pad_maximum_fusion.5.refs_0_), channel_id=1, source_target_pairs={{4,12},{24,16},{5,13},{25,17},{6,14},{26,18},{7,15},{27,19}} | collective-permute-start | bytes 1572872 | tf_op jit(solution)/shard_map/ppermute | solution.py:187
  448.8 23.3 %collective-permute-start.83 = (bf16[256,1024]{1,0:T(8,128)(2,1)S(1)}, bf16[256,1024]{1,0:T(8,128)(2,1)S(1)}, u32[]{:S(2)}, u32[]{:S(2)}) collective-permute-start(bf16[256,1024]{1,0:T(8,128)(2,1)S(1)} %pad_maximum_fusion.5.refs_0_), channel_id=1, source_target_pairs={{28,12},{0,16},{29,13},{1,17},{30,14},{2,18},{31,15},{3,19}} | collective-permute-start | bytes 1572872 | tf_op jit(solution)/shard_map/ppermute | solution.py:187
  450.4 21.6 %collective-permute-start.84 = (bf16[256,1024]{1,0:T(8,128)(2,1)S(1)}, bf16[256,1024]{1,0:T(8,128)(2,1)}, u32[]{:S(2)}, u32[]{:S(2)}) collective-permute-start(bf16[256,1024]{1,0:T(8,128)(2,1)S(1)} %pad_maximum_fusion.5.refs_0_), channel_id=1, source_target_pairs={{20,12},{8,16},{21,13},{9,17},{22,14},{10,18},{23,15},{11,19}} | collective-permute-start | bytes 1572872 | tf_op jit(solution)/shard_map/ppermute | solution.py:187
  490.1 31.9 %collective-permute-start.89 = (f32[1280,256]{1,0:T(8,128)}, f32[1280,256]{1,0:T(8,128)}, u32[]{:S(2)}, u32[]{:S(2)}) collective-permute-start(f32[1280,256]{1,0:T(8,128)} %select_add_fusion), channel_id=1, source_target_pairs={{0,2},{1,3},{2,0},{3,1},{4,6},{5,7},{6,4},{7,5},{8,10},{9,11},{10,... | collective-permute-start | bytes 3932168 | tf_op jit(solution)/shard_map/ppermute | solution.py:47
  496.8 30.8 %collective-permute-start.73 = (bf16[256,512]{1,0:T(8,128)(2,1)S(1)}, bf16[256,512]{1,0:T(8,128)(2,1)S(1)}, u32[]{:S(2)}, u32[]{:S(2)}) collective-permute-start(bf16[256,512]{1,0:T(8,128)(2,1)S(1)} %convert_add_fusion.15), channel_id=1, source_target_pairs={{0,2},{1,3},{2,0},{3,1},{4,6},{5,7},{6,4},{7,5},{8,10},{9,11},{10,... | collective-permute-start | bytes 786440 | tf_op jit(solution)/shard_map/ppermute | solution.py:47
  498.8 89.2 %collective-permute-start.71 = (bf16[256,512]{1,0:T(8,128)(2,1)S(1)}, bf16[256,512]{1,0:T(8,128)(2,1)}, u32[]{:S(2)}, u32[]{:S(2)}) collective-permute-start(bf16[256,512]{1,0:T(8,128)(2,1)S(1)} %convert_add_fusion.16), channel_id=1, source_target_pairs={{0,2},{1,3},{2,0},{3,1},{4,6},{5,7},{6,4},{7,5},{8,10},{9,11},{10,... | collective-permute-start | bytes 786440 | tf_op jit(solution)/shard_map/ppermute | solution.py:47
  527.7 71.2 %collective-permute-start.74 = (f32[256,512]{1,0:T(8,128)S(1)}, f32[256,512]{1,0:T(8,128)}, u32[]{:S(2)}, u32[]{:S(2)}) collective-permute-start(f32[256,512]{1,0:T(8,128)S(1)} %add_add_fusion.2), channel_id=1, source_target_pairs={{0,1},{1,0},{2,3},{3,2},{4,5},{5,4},{6,7},{7,6},{8,9},{9,8},{10,11... | collective-permute-start | bytes 1572872 | tf_op jit(solution)/shard_map/ppermute | solution.py:47
  528.3 46.1 %collective-permute-start.91 = (bf16[256,1024]{1,0:T(8,128)(2,1)S(1)}, bf16[256,1024]{1,0:T(8,128)(2,1)S(1)}, u32[]{:S(2)}, u32[]{:S(2)}) collective-permute-start(bf16[256,1024]{1,0:T(8,128)(2,1)S(1)} %convert_element_type.788), channel_id=1, source_target_pairs={{0,2},{1,3},{2,0},{3,1},{4,6},{5,7},{6,4},{7,5},{8,10},{9,11},{10,... | collective-permute-start | bytes 1572872 | tf_op jit(solution)/shard_map/ppermute | solution.py:47
  528.7 45.8 %collective-permute-start.92 = (bf16[256,1024]{1,0:T(8,128)(2,1)S(1)}, bf16[256,1024]{1,0:T(8,128)(2,1)S(1)}, u32[]{:S(2)}, u32[]{:S(2)}) collective-permute-start(bf16[256,1024]{1,0:T(8,128)(2,1)S(1)} %copy-done.110), channel_id=1, source_target_pairs={{0,2},{1,3},{2,0},{3,1},{4,6},{5,7},{6,4},{7,5},{8,10},{9,11},{10,... | collective-permute-start | bytes 1572872 | tf_op jit(solution)/shard_map/ppermute | solution.py:47
  574.8 61.7 %all-to-all-start.1 = ((bf16[8,128,1024]{2,1,0:T(8,128)(2,1)}), bf16[8,128,1024]{2,1,0:T(8,128)(2,1)}, u32[]{:S(2)}, u32[]{:S(2)}) async-start(bf16[8,128,1024]{2,1,0:T(8,128)(2,1)} %bitcast.50), calls=%async_computation.1 | async-start | bytes 4194304 | tf_op jit(solution)/shard_map/all_to_all | solution.py:1136
  (232 other events, 1671.9 us)
Sparse Core Ops, SparseCore 0:
  35.2 81.7 all-gather.3
  119.8 42.3 all-gather.5
  403.6 60.0 all-gather.7

commit v7 on v6

--- a/solution.py
+++ b/solution.py
@@ -414,7 +414,7 @@
     @pl.loop(0, 2)
     def _(block):
         rows = pl.ds(pl.multiple_of(block * block_rows, block_rows), block_rows)
-        parts = []
+        parts, attentions, score_grads, grads, queries = [], [], [], [], []
         for head in range(inner_width // head_width):
             query = masked_rows(query_ref[rows, :], head, head_width)
             grad = masked_rows(grad_ref[rows, :], head, head_width)
@@ -428,11 +428,19 @@
             weighted = attention * last_dims(values, grad)
             row_dot = jnp.sum(weighted, axis=0, keepdims=True)
             score_grad = (weighted - attention * row_dot).astype(jnp.bfloat16)
-            value_total_ref[...] += times(attention.astype(jnp.bfloat16), grad)
-            key_total_ref[...] += times(score_grad, query)
+            attentions.append(attention.astype(jnp.bfloat16))
+            score_grads.append(score_grad)
+            grads.append(grad)
+            queries.append(query)
             parts.append(
                 times(turned_ref[head * head_width : (head + 1) * head_width, :], score_grad)
             )
+        value_total_ref[...] += times(
+            jnp.concatenate(attentions, axis=1), jnp.concatenate(grads, axis=0)
+        )
+        key_total_ref[...] += times(
+            jnp.concatenate(score_grads, axis=1), jnp.concatenate(queries, axis=0)
+        )
         query_grad_ref[rows, :] = (jnp.concatenate(parts, axis=0) * score_scale).T
 
     for k, out_ref in enumerate(out_refs):

time: 655 us -> 661 us (level)
  transfers between devices with their start and end apart: 100 -> 100, of which waited for: 42 -> 42; matrix products, arithmetic and copies ran while one was open for 23% -> 23% of each run, Pallas kernels for 18% -> 19%
where the time goes in v7:
time: 661 us; the launch traced here: 657 us
  waiting for transfers between devices  222 us (34%)
  Pallas kernels  128 us (19%)
  starting transfers between devices  97.1 us (15%)
  other arithmetic  85 us (13%)
  matrix products  66.6 us (10%)
  local copies, waits for them, and re-layouts  36.5 us (6%)
  between operations  21 us (3%)
    ppermute x89, waiting for transfers between devices, pair_swap(): lax.ppermute(array, axis, [(rank, rank ^ bit) for rank in range(size)])  180 us
    ppermute x89, starting transfers between devices, pair_swap(): lax.ppermute(array, axis, [(rank, rank ^ bit) for rank in range(size)])  70.5 us
    pallas_call x1, Pallas kernels, newton(): pl.pallas_call(functools.partial(newton_kernel, enc_rows, dec_rows), in_s...  44 us
    dot_general x31, matrix products, times(): return jnp.dot(left, right, preferred_element_type=jnp.float32)  33.5 us
    pallas_call x2, Pallas kernels, attend_backward(): pl.pallas_call(functools.partial(attend_backward_kernel, head_width, len(...  32.9 us
    dot_general x36, matrix products, times_turned(): jnp.einsum('tf,df->td', left, right, preferred_element_type=jnp.float32)  30.7 us
    all_to_all x1, waiting for transfers between devices, local(): lax.all_to_all(orthogonal.reshape(data_ranks, enc_rows, slot_width), 'dp'...  29.3 us
    pallas_call x4, Pallas kernels, weight_grads(): pl.pallas_call(functools.partial(weight_grads_kernel, [(len(lefts), len(r...  27.5 us
  transfers between devices with their start and end apart: 100, of which 42 were waited for; matrix products, arithmetic and copies ran while one was open for 23% of the time, Pallas kernels for 19%

profile of v7, /device:TPU:0, one launch (start us, length us, event | category | flops | bytes accessed | tf_op | source)
XLA Modules:
  0.0 656.5 jit_solution(8511396957594510561)
XLA Ops:
  20.6 4.0 collective-permute-done.4.refs_2_
  24.6 10.5 %collective-permute-done.6.refs_4_ = bf16[128,1024]{1,0:T(8,128)(2,1)} collective-permute-done((bf16[128,1024]{1,0:T(8,128)(2,1)S(1)}, bf16[128,1024]{1,0:T(8,128)(2,1)}, u32[]{:S(2)}, u32[]{:S(2)}) %collective-permute-start.6) | collective-permute-done | bytes 262176 | tf_op jit(solution)/shard_map/ppermute | solution.py:47
  35.6 4.5 collective-permute-start.1
  49.2 4.5 subtract_multiply_fusion
  53.6 6.9 %collective-permute-done.5.refs_3_ = bf16[128,1024]{1,0:T(8,128)(2,1)S(1)} collective-permute-done((bf16[128,1024]{1,0:T(8,128)(2,1)}, bf16[128,1024]{1,0:T(8,128)(2,1)S(1)}, u32[]{:S(2)}, u32[]{:S(2)}) %collective-permute-start.5) | collective-permute-done | bytes 262176 | tf_op jit(solution)/shard_map/ppermute | solution.py:47
  60.6 5.2 collective-permute-done.7.refs_5_
  79.9 3.9 attend_forward.5
  92.7 7.8 %collective-permute-done.11 = bf16[256,1024]{1,0:T(8,128)(2,1)S(1)} collective-permute-done((bf16[256,1024]{1,0:T(8,128)(2,1)S(1)}, bf16[256,1024]{1,0:T(8,128)(2,1)S(1)}, u32[]{:S(2)}, u32[]{:S(2)}) %collective-permute-start.11) | collective-permute-done | bytes 524320 | tf_op jit(solution)/shard_map/ppermute | solution.py:47
  100.5 10.4 %collective-permute-done.19 = bf16[256,1024]{1,0:T(8,128)(2,1)} collective-permute-done((bf16[256,1024]{1,0:T(8,128)(2,1)S(1)}, bf16[256,1024]{1,0:T(8,128)(2,1)}, u32[]{:S(2)}, u32[]{:S(2)}) %collective-permute-start.19) | collective-permute-done | bytes 524320 | tf_op jit(solution)/shard_map/ppermute | solution.py:47
  139.8 8.3 %collective-permute-done.22 = bf16[256,1024]{1,0:T(8,128)(2,1)} collective-permute-done((bf16[256,1024]{1,0:T(8,128)(2,1)}, bf16[256,1024]{1,0:T(8,128)(2,1)}, u32[]{:S(2)}, u32[]{:S(2)}) %collective-permute-start.22) | collective-permute-done | bytes 524320 | tf_op jit(solution)/shard_map/ppermute | solution.py:47
  150.4 8.3 %collective-permute-done.14 = bf16[256,1024]{1,0:T(8,128)(2,1)} collective-permute-done((bf16[256,1024]{1,0:T(8,128)(2,1)}, bf16[256,1024]{1,0:T(8,128)(2,1)}, u32[]{:S(2)}, u32[]{:S(2)}) %collective-permute-start.14) | collective-permute-done | bytes 524320 | tf_op jit(solution)/shard_map/ppermute | solution.py:47
  189.0 6.1 collective-permute-done.29
  195.6 4.3 collective-permute-done.25
  215.1 4.3 all-to-all-start
  219.5 4.1 collective-permute-done.33
  231.4 16.5 %attend_backward.2 = (bf16[256,384]{1,0:T(8,128)(2,1)S(1)}, bf16[256,384]{1,0:T(8,128)(2,1)S(1)}, bf16[256,384]{1,0:T(8,128)(2,1)S(1)}, bf16[256,384]{1,0:T(8,128)(2,1)S(1)}) custom-call(s32[1024,1]{1,0:T(8,128)S(1)} %reshape_reshape.6.key_segment_ref, s32[1,1024]{1,0:T(1,128)S(1)} %reshape_reshape.4.key_segment_ref.query_segment_ref, ...), custom_call_target="tpu_custom_call" | custom-call | flops 5368709120 | bytes 1835008 | tf_op jit(solution)/shard_map/attend_backward/pallas_call | solution.py:461
  256.9 7.1 %weight_grads.4 = (bf16[256,1536]{1,0:T(8,128)(2,1)}, bf16[256,1536]{1,0:T(8,128)(2,1)}) custom-call(s32[1]{0:T(128)} %bitcast.20.parity_ref, bf16[256,512]{1,0:T(8,128)(2,1)} %copy-done.95, bf16[256,512]{1,0:T(8,128)(2,1)} %collective-permute-done.17.refs_1_, bf16[256,512]{1,0:T(8,128)(2,1)} %get-tuple-element.361.refs_2_, ...), custom_call_target="tpu_custom_call" | custom-call | flops 1610612736 | bytes 8912896 | tf_op jit(solution)/shard_map/weight_grads/pallas_call | solution.py:624
  290.1 7.2 %weight_grads.6 = (bf16[512,1152]{1,0:T(8,128)(2,1)}, bf16[512,1152]{1,0:T(8,128)(2,1)}) custom-call(s32[1]{0:T(128)} %bitcast.20.parity_ref, bf16[256,1024]{1,0:T(8,128)(2,1)} %copy-done.111, bf16[256,1024]{1,0:T(8,128)(2,1)} %copy-done.101, bf16[256,1024]{1,0:T(8,128)(2,1)} %copy-done.112, bf16[256,1024]{1,0:T(8,128)(2,1)} %copy-done.106, ...), custom_call_target="tpu_custom_call" | custom-call | flops 2415919104 | bytes 8912896 | tf_op jit(solution)/shard_map/weight_grads/pallas_call | solution.py:624
  298.6 6.3 weight_grads.5
  306.4 6.1 collective-permute-done.47
  322.6 3.9 collective-permute-done.53
  330.5 16.4 %attend_backward.3 = (bf16[256,768]{1,0:T(8,128)(2,1)S(1)}, bf16[256,768]{1,0:T(8,128)(2,1)S(1)}, bf16[256,768]{1,0:T(8,128)(2,1)S(1)}, bf16[256,768]{1,0:T(8,128)(2,1)S(1)}) custom-call(s32[1024,1]{1,0:T(8,128)S(1)} %reshape_reshape.6.key_segment_ref, s32[1,1024]{1,0:T(1,128)S(1)} %reshape_reshape.4.key_segment_ref.query_segment_ref, ...), custom_call_target="tpu_custom_call" | custom-call | flops 10737418240 | bytes 3670016 | tf_op jit(solution)/shard_map/attend_backward/pallas_call | solution.py:461
  349.9 6.8 %weight_grads.7 = (bf16[512,1024]{1,0:T(8,128)(2,1)}, bf16[512,1024]{1,0:T(8,128)(2,1)}) custom-call(s32[1]{0:T(128)} %bitcast.20.parity_ref, bf16[1024,1024]{1,0:T(8,128)(2,1)} %copy-done.70, bf16[256,768]{1,0:T(8,128)(2,1)} %copy-done.4, bf16[256,768]{1,0:T(8,128)(2,1)} %copy-done.18, bf16[256,768]{1,0:T(8,128)(2,1)} %copy-done.14, ...), custom_call_target="tpu_custom_call" | custom-call | flops 2147483648 | bytes 8388608 | tf_op jit(solution)/shard_map/weight_grads/pallas_call | solution.py:624
  374.1 10.4 %collective-permute-done.62 = bf16[64,1536]{1,0:T(8,128)(2,1)S(1)} collective-permute-done((bf16[64,1536]{1,0:T(8,128)(2,1)S(1)}, bf16[64,1536]{1,0:T(8,128)(2,1)S(1)}, u32[]{:S(2)}, u32[]{:S(2)}) %collective-permute-start.62) | collective-permute-done | bytes 196640 | tf_op jit(solution)/shard_map/ppermute | solution.py:47
  392.1 9.4 %collective-permute-done.66 = bf16[128,1024]{1,0:T(8,128)(2,1)S(1)} collective-permute-done((bf16[128,1024]{1,0:T(8,128)(2,1)S(1)}, bf16[128,1024]{1,0:T(8,128)(2,1)S(1)}, u32[]{:S(2)}, u32[]{:S(2)}) %collective-permute-start.66) | collective-permute-done | bytes 262176 | tf_op jit(solution)/shard_map/ppermute | solution.py:47
  401.5 5.9 collective-permute-done.67
  414.9 12.2 %collective-permute-done.68 = bf16[128,1024]{1,0:T(8,128)(2,1)S(1)} collective-permute-done((bf16[128,1024]{1,0:T(8,128)(2,1)}, bf16[128,1024]{1,0:T(8,128)(2,1)S(1)}, u32[]{:S(2)}, u32[]{:S(2)}) %collective-permute-start.68) | collective-permute-done | bytes 262176 | tf_op jit(solution)/shard_map/ppermute | solution.py:47
  458.4 11.4 %collective-permute-done.85.refs_1_ = bf16[256,768]{1,0:T(8,128)(2,1)S(1)} collective-permute-done((bf16[256,768]{1,0:T(8,128)(2,1)S(1)}, bf16[256,768]{1,0:T(8,128)(2,1)S(1)}, u32[]{:S(2)}, u32[]{:S(2)}) %collective-permute-start.85) | collective-permute-done | bytes 393248 | tf_op jit(solution)/shard_map/ppermute | solution.py:187
  504.7 23.2 %collective-permute-done.89 = f32[1280,256]{1,0:T(8,128)} collective-permute-done((f32[1280,256]{1,0:T(8,128)}, f32[1280,256]{1,0:T(8,128)}, u32[]{:S(2)}, u32[]{:S(2)}) %collective-permute-start.89) | collective-permute-done | bytes 1310752 | tf_op jit(solution)/shard_map/ppermute | solution.py:47
  536.2 44.0 %newton.1 = bf16[1024,1024]{1,0:T(8,128)(2,1)} custom-call(s32[1]{0:T(128)} %bitcast.45.paired_ref, f32[1280,256]{1,0:T(8,128)S(1)} %get-tuple-element.314.low_ref, f32[1280,256]{1,0:T(8,128)S(1)} %get-tuple-element.313.high_ref, bf16[1024,1024]{1,0:T(8,128)(2,1)} %copy-done.65), custom_call_target="tpu_custom_call" | custom-call | flops 38654705664 | bytes 20971520 | tf_op jit(solution)/shard_map/newton/pallas_call | solution.py:731
  580.6 13.2 %all-to-all-start.1 = ((bf16[8,128,1024]{2,1,0:T(8,128)(2,1)}), bf16[8,128,1024]{2,1,0:T(8,128)(2,1)}, u32[]{:S(2)}, u32[]{:S(2)}) async-start(bf16[8,128,1024]{2,1,0:T(8,128)(2,1)} %bitcast.50), calls=%async_computation.1 | async-start | bytes 4194304 | tf_op jit(solution)/shard_map/all_to_all | solution.py:1144
  613.0 29.3 %all-to-all-done.1 = bf16[8,128,1024]{2,1,0:T(8,128)(2,1)} async-done(((bf16[8,128,1024]{2,1,0:T(8,128)(2,1)}), bf16[8,128,1024]{2,1,0:T(8,128)(2,1)}, u32[]{:S(2)}, u32[]{:S(2)}) %all-to-all-start.1) | async-done | bytes 2097184 | tf_op jit(solution)/shard_map/all_to_all | solution.py:1144
  (807 shorter events, 313.0 us)
Async XLA Ops:
  7.2 109.8 %all-gather.4.cloned.1.call-start = ((), (), s32[]{:S(2)}) async-start(), calls=%async_computation.2 | async-start | bytes 5013504 | tf_op jit(solution)/shard_map/all_gather | solution.py:848
  9.0 44.6 %collective-permute-start.3 = (bf16[128,1024]{1,0:T(8,128)(2,1)S(1)}, bf16[128,1024]{1,0:T(8,128)(2,1)S(1)}, u32[]{:S(2)}, u32[]{:S(2)}) collective-permute-start(bf16[128,1024]{1,0:T(8,128)(2,1)S(1)} %slice.372.refs_0_), channel_id=1, source_target_pairs={{0,4},{4,0},{8,12},{12,8},{16,20},{20,16},{24,28},{28,24},{1,5},{5... | collective-permute-start | bytes 786440 | tf_op jit(solution)/shard_map/ppermute | solution.py:47
  13.6 21.5 %collective-permute-start.6 = (bf16[128,1024]{1,0:T(8,128)(2,1)S(1)}, bf16[128,1024]{1,0:T(8,128)(2,1)}, u32[]{:S(2)}, u32[]{:S(2)}) collective-permute-start(bf16[128,1024]{1,0:T(8,128)(2,1)S(1)} %slice.372.refs_0_), channel_id=1, source_target_pairs={{0,16},{4,20},{8,24},{12,28},{16,0},{20,4},{24,8},{28,12},{1,17},{... | collective-permute-start | bytes 786440 | tf_op jit(solution)/shard_map/ppermute | solution.py:47
  16.4 19.1 %collective-permute-start = (bf16[1,4,192]{2,1,0:T(4,128)(2,1)S(1)}, bf16[1,4,192]{2,1,0:T(4,128)(2,1)S(1)}, u32[]{:S(2)}, u32[]{:S(2)}) collective-permute-start(bf16[1,4,192]{2,1,0:T(4,128)(2,1)S(1)} %pad_maximum_fusion.11), channel_id=1, source_target_pairs={{0,4},{4,0},{8,12},{12,8},{16,20},{20,16},{24,28},{28,24},{1,5},{5... | collective-permute-start | bytes 4616 | tf_op jit(solution)/shard_map/ppermute | solution.py:47
  35.1 133.0 %all-gather.6.cloned.1.call-start = ((), (), s32[]{:S(2)}) async-start(), calls=%async_computation.3 | async-start | bytes 1769472 | tf_op jit(solution)/shard_map/all_gather | solution.py:851
  48.6 20.0 %collective-permute-start.9 = (bf16[128,1024]{1,0:T(8,128)(2,1)}, bf16[128,1024]{1,0:T(8,128)(2,1)S(1)}, u32[]{:S(2)}, u32[]{:S(2)}) collective-permute-start(bf16[128,1024]{1,0:T(8,128)(2,1)} %collective-permute-done.8.refs_6_), channel_id=1, source_target_pairs={{0,4},{4,0},{8,12},{12,8},{16,20},{20,16},{24,28},{28,24},{1,5},{5... | collective-permute-start | bytes 786440 | tf_op jit(solution)/shard_map/ppermute | solution.py:47
  87.8 23.1 %collective-permute-start.19 = (bf16[256,1024]{1,0:T(8,128)(2,1)S(1)}, bf16[256,1024]{1,0:T(8,128)(2,1)}, u32[]{:S(2)}, u32[]{:S(2)}) collective-permute-start(bf16[256,1024]{1,0:T(8,128)(2,1)S(1)} %fusion.5), channel_id=1, source_target_pairs={{0,2},{1,3},{2,0},{3,1},{4,6},{5,7},{6,4},{7,5},{8,10},{9,11},{10,... | collective-permute-start | bytes 1572872 | tf_op jit(solution)/shard_map/ppermute | solution.py:47
  135.2 23.4 %collective-permute-start.14 = (bf16[256,1024]{1,0:T(8,128)(2,1)}, bf16[256,1024]{1,0:T(8,128)(2,1)}, u32[]{:S(2)}, u32[]{:S(2)}) collective-permute-start(bf16[256,1024]{1,0:T(8,128)(2,1)} %add_convert_fusion.13), channel_id=1, source_target_pairs={{0,2},{1,3},{2,0},{3,1},{4,6},{5,7},{6,4},{7,5},{8,10},{9,11},{10,... | collective-permute-start | bytes 1572872 | tf_op jit(solution)/shard_map/ppermute | solution.py:47
  215.1 56.1 %all-to-all-start = ((bf16[8,128,1024]{2,1,0:T(8,128)(2,1)}), bf16[8,128,1024]{2,1,0:T(8,128)(2,1)}, u32[]{:S(2)}, u32[]{:S(2)}) async-start(bf16[8,128,1024]{2,1,0:T(8,128)(2,1)} %fusion.113), calls=%async_computation | async-start | bytes 4194304 | tf_op jit(solution)/shard_map/all_to_all | solution.py:882
  219.4 262.3 %all-gather.8.cloned.1.call-start = ((), (), s32[]{:S(2)}) async-start(), calls=%async_computation.4 | async-start | bytes 2654208 | tf_op jit(solution)/shard_map/all_gather | solution.py:1052
  269.7 20.4 %collective-permute-start.51 = (bf16[256,1024]{1,0:T(8,128)(2,1)}, bf16[256,1024]{1,0:T(8,128)(2,1)}, u32[]{:S(2)}, u32[]{:S(2)}) collective-permute-start(bf16[256,1024]{1,0:T(8,128)(2,1)} %add_convert_fusion.12.refs_8_), channel_id=1, source_target_pairs={{0,1},{1,0},{2,3},{3,2},{4,5},{5,4},{6,7},{7,6},{8,9},{9,8},{10,11... | collective-permute-start | bytes 1572872 | tf_op jit(solution)/shard_map/ppermute | solution.py:47
  269.8 20.3 %collective-permute-start.52 = (bf16[256,1024]{1,0:T(8,128)(2,1)S(1)}, bf16[256,1024]{1,0:T(8,128)(2,1)}, u32[]{:S(2)}, u32[]{:S(2)}) collective-permute-start(bf16[256,1024]{1,0:T(8,128)(2,1)S(1)} %copy-done.69), channel_id=1, source_target_pairs={{0,1},{1,0},{2,3},{3,2},{4,5},{5,4},{6,7},{7,6},{8,9},{9,8},{10,11... | collective-permute-start | bytes 1572872 | tf_op jit(solution)/shard_map/ppermute | solution.py:47
  270.2 42.4 %collective-permute-start.48 = (bf16[256,1536]{1,0:T(8,128)(2,1)}, bf16[256,1536]{1,0:T(8,128)(2,1)}, u32[]{:S(2)}, u32[]{:S(2)}) collective-permute-start(bf16[256,1536]{1,0:T(8,128)(2,1)} %get-tuple-element.143), channel_id=1, source_target_pairs={{0,4},{4,0},{8,12},{12,8},{16,20},{20,16},{24,28},{28,24},{1,5},{5... | collective-permute-start | bytes 2359304 | tf_op jit(solution)/shard_map/ppermute | solution.py:47
  288.7 23.8 %collective-permute-start.47 = (bf16[256,1024]{1,0:T(8,128)(2,1)S(1)}, bf16[256,1024]{1,0:T(8,128)(2,1)S(1)}, u32[]{:S(2)}, u32[]{:S(2)}) collective-permute-start(bf16[256,1024]{1,0:T(8,128)(2,1)S(1)} %get-tuple-element.408), channel_id=1, source_target_pairs={{0,2},{1,3},{2,0},{3,1},{4,6},{5,7},{6,4},{7,5},{8,10},{9,11},{10,... | collective-permute-start | bytes 1572872 | tf_op jit(solution)/shard_map/ppermute | solution.py:47
  297.3 29.3 %collective-permute-start.53 = (bf16[512,1152]{1,0:T(8,128)(2,1)}, bf16[512,1152]{1,0:T(8,128)(2,1)}, u32[]{:S(2)}, u32[]{:S(2)}) collective-permute-start(bf16[512,1152]{1,0:T(8,128)(2,1)} %get-tuple-element.149), channel_id=1, source_target_pairs={{0,4},{4,0},{8,12},{12,8},{16,20},{20,16},{24,28},{28,24},{1,5},{5... | collective-permute-start | bytes 3538952 | tf_op jit(solution)/shard_map/ppermute | solution.py:47
  316.9 41.1 %collective-permute-start.55 = (bf16[512,1024]{1,0:T(8,128)(2,1)}, bf16[512,1024]{1,0:T(8,128)(2,1)S(1)}, u32[]{:S(2)}, u32[]{:S(2)}) collective-permute-start(bf16[512,1024]{1,0:T(8,128)(2,1)} %get-tuple-element.168), channel_id=1, source_target_pairs={{0,4},{4,0},{8,12},{12,8},{16,20},{20,16},{24,28},{28,24},{1,5},{5... | collective-permute-start | bytes 3145736 | tf_op jit(solution)/shard_map/ppermute | solution.py:47
  320.3 37.7 %collective-permute-start.56 = (bf16[128,1536]{1,0:T(8,128)(2,1)}, bf16[128,1536]{1,0:T(8,128)(2,1)}, u32[]{:S(2)}, u32[]{:S(2)}) collective-permute-start(bf16[128,1536]{1,0:T(8,128)(2,1)} %constant_dynamic-slice_fusion.8), channel_id=1, source_target_pairs={{0,8},{4,12},{8,0},{12,4},{16,24},{20,28},{24,16},{28,20},{1,9},{5... | collective-permute-start | bytes 1179656 | tf_op jit(solution)/shard_map/ppermute | solution.py:47
  329.1 28.9 %collective-permute-start.54 = (bf16[256,1152]{1,0:T(8,128)(2,1)}, bf16[256,1152]{1,0:T(8,128)(2,1)}, u32[]{:S(2)}, u32[]{:S(2)}) collective-permute-start(bf16[256,1152]{1,0:T(8,128)(2,1)} %constant_dynamic-slice_fusion.9), channel_id=1, source_target_pairs={{0,8},{4,12},{8,0},{12,4},{16,24},{20,28},{24,16},{28,20},{1,9},{5... | collective-permute-start | bytes 1769480 | tf_op jit(solution)/shard_map/ppermute | solution.py:47
  356.7 27.8 %collective-permute-start.63 = (bf16[512,1024]{1,0:T(8,128)(2,1)}, bf16[512,1024]{1,0:T(8,128)(2,1)S(1)}, u32[]{:S(2)}, u32[]{:S(2)}) collective-permute-start(bf16[512,1024]{1,0:T(8,128)(2,1)} %get-tuple-element.161), channel_id=1, source_target_pairs={{0,4},{4,0},{8,12},{12,8},{16,20},{20,16},{24,28},{28,24},{1,5},{5... | collective-permute-start | bytes 3145736 | tf_op jit(solution)/shard_map/ppermute | solution.py:47
  361.2 23.3 %collective-permute-start.61 = (bf16[128,1152]{1,0:T(8,128)(2,1)S(1)}, bf16[128,1152]{1,0:T(8,128)(2,1)S(1)}, u32[]{:S(2)}, u32[]{:S(2)}) collective-permute-start(bf16[128,1152]{1,0:T(8,128)(2,1)S(1)} %constant_dynamic-slice_fusion.7), channel_id=1, source_target_pairs={{0,16},{4,20},{8,24},{12,28},{16,0},{20,4},{24,8},{28,12},{1,17},{... | collective-permute-start | bytes 884744 | tf_op jit(solution)/shard_map/ppermute | solution.py:47
  363.0 23.9 %collective-permute-start.64 = (bf16[256,1024]{1,0:T(8,128)(2,1)S(1)}, bf16[256,1024]{1,0:T(8,128)(2,1)S(1)}, u32[]{:S(2)}, u32[]{:S(2)}) collective-permute-start(bf16[256,1024]{1,0:T(8,128)(2,1)S(1)} %constant_dynamic-slice_fusion.5), channel_id=1, source_target_pairs={{0,8},{4,12},{8,0},{12,4},{16,24},{20,28},{24,16},{28,20},{1,9},{5... | collective-permute-start | bytes 1572872 | tf_op jit(solution)/shard_map/ppermute | solution.py:47
  449.8 20.1 %collective-permute-start.85 = (bf16[256,768]{1,0:T(8,128)(2,1)S(1)}, bf16[256,768]{1,0:T(8,128)(2,1)S(1)}, u32[]{:S(2)}, u32[]{:S(2)}) collective-permute-start(bf16[256,768]{1,0:T(8,128)(2,1)S(1)} %pad_maximum_fusion.6.refs_0_), channel_id=1, source_target_pairs={{0,8},{28,20},{1,9},{29,21},{2,10},{30,22},{3,11},{31,23}} | collective-permute-start | bytes 1179656 | tf_op jit(solution)/shard_map/ppermute | solution.py:187
  453.9 23.4 %collective-permute-start.82 = (bf16[256,1024]{1,0:T(8,128)(2,1)S(1)}, bf16[256,1024]{1,0:T(8,128)(2,1)S(1)}, u32[]{:S(2)}, u32[]{:S(2)}) collective-permute-start(bf16[256,1024]{1,0:T(8,128)(2,1)S(1)} %pad_maximum_fusion.5.refs_0_), channel_id=1, source_target_pairs={{4,12},{24,16},{5,13},{25,17},{6,14},{26,18},{7,15},{27,19}} | collective-permute-start | bytes 1572872 | tf_op jit(solution)/shard_map/ppermute | solution.py:187
  454.6 23.3 %collective-permute-start.83 = (bf16[256,1024]{1,0:T(8,128)(2,1)S(1)}, bf16[256,1024]{1,0:T(8,128)(2,1)S(1)}, u32[]{:S(2)}, u32[]{:S(2)}) collective-permute-start(bf16[256,1024]{1,0:T(8,128)(2,1)S(1)} %pad_maximum_fusion.5.refs_0_), channel_id=1, source_target_pairs={{28,12},{0,16},{29,13},{1,17},{30,14},{2,18},{31,15},{3,19}} | collective-permute-start | bytes 1572872 | tf_op jit(solution)/shard_map/ppermute | solution.py:187
  456.3 21.6 %collective-permute-start.84 = (bf16[256,1024]{1,0:T(8,128)(2,1)S(1)}, bf16[256,1024]{1,0:T(8,128)(2,1)}, u32[]{:S(2)}, u32[]{:S(2)}) collective-permute-start(bf16[256,1024]{1,0:T(8,128)(2,1)S(1)} %pad_maximum_fusion.5.refs_0_), channel_id=1, source_target_pairs={{20,12},{8,16},{21,13},{9,17},{22,14},{10,18},{23,15},{11,19}} | collective-permute-start | bytes 1572872 | tf_op jit(solution)/shard_map/ppermute | solution.py:187
  496.0 31.9 %collective-permute-start.89 = (f32[1280,256]{1,0:T(8,128)}, f32[1280,256]{1,0:T(8,128)}, u32[]{:S(2)}, u32[]{:S(2)}) collective-permute-start(f32[1280,256]{1,0:T(8,128)} %select_add_fusion), channel_id=1, source_target_pairs={{0,2},{1,3},{2,0},{3,1},{4,6},{5,7},{6,4},{7,5},{8,10},{9,11},{10,... | collective-permute-start | bytes 3932168 | tf_op jit(solution)/shard_map/ppermute | solution.py:47
  502.6 30.8 %collective-permute-start.73 = (bf16[256,512]{1,0:T(8,128)(2,1)S(1)}, bf16[256,512]{1,0:T(8,128)(2,1)S(1)}, u32[]{:S(2)}, u32[]{:S(2)}) collective-permute-start(bf16[256,512]{1,0:T(8,128)(2,1)S(1)} %convert_add_fusion.15), channel_id=1, source_target_pairs={{0,2},{1,3},{2,0},{3,1},{4,6},{5,7},{6,4},{7,5},{8,10},{9,11},{10,... | collective-permute-start | bytes 786440 | tf_op jit(solution)/shard_map/ppermute | solution.py:47
  504.6 89.2 %collective-permute-start.71 = (bf16[256,512]{1,0:T(8,128)(2,1)S(1)}, bf16[256,512]{1,0:T(8,128)(2,1)}, u32[]{:S(2)}, u32[]{:S(2)}) collective-permute-start(bf16[256,512]{1,0:T(8,128)(2,1)S(1)} %convert_add_fusion.16), channel_id=1, source_target_pairs={{0,2},{1,3},{2,0},{3,1},{4,6},{5,7},{6,4},{7,5},{8,10},{9,11},{10,... | collective-permute-start | bytes 786440 | tf_op jit(solution)/shard_map/ppermute | solution.py:47
  533.5 71.2 %collective-permute-start.74 = (f32[256,512]{1,0:T(8,128)S(1)}, f32[256,512]{1,0:T(8,128)}, u32[]{:S(2)}, u32[]{:S(2)}) collective-permute-start(f32[256,512]{1,0:T(8,128)S(1)} %add_add_fusion.2), channel_id=1, source_target_pairs={{0,1},{1,0},{2,3},{3,2},{4,5},{5,4},{6,7},{7,6},{8,9},{9,8},{10,11... | collective-permute-start | bytes 1572872 | tf_op jit(solution)/shard_map/ppermute | solution.py:47
  534.1 46.1 %collective-permute-start.91 = (bf16[256,1024]{1,0:T(8,128)(2,1)S(1)}, bf16[256,1024]{1,0:T(8,128)(2,1)S(1)}, u32[]{:S(2)}, u32[]{:S(2)}) collective-permute-start(bf16[256,1024]{1,0:T(8,128)(2,1)S(1)} %convert_element_type.788), channel_id=1, source_target_pairs={{0,2},{1,3},{2,0},{3,1},{4,6},{5,7},{6,4},{7,5},{8,10},{9,11},{10,... | collective-permute-start | bytes 1572872 | tf_op jit(solution)/shard_map/ppermute | solution.py:47
  534.6 45.8 %collective-permute-start.92 = (bf16[256,1024]{1,0:T(8,128)(2,1)S(1)}, bf16[256,1024]{1,0:T(8,128)(2,1)S(1)}, u32[]{:S(2)}, u32[]{:S(2)}) collective-permute-start(bf16[256,1024]{1,0:T(8,128)(2,1)S(1)} %copy-done.110), channel_id=1, source_target_pairs={{0,2},{1,3},{2,0},{3,1},{4,6},{5,7},{6,4},{7,5},{8,10},{9,11},{10,... | collective-permute-start | bytes 1572872 | tf_op jit(solution)/shard_map/ppermute | solution.py:47
  580.6 61.7 %all-to-all-start.1 = ((bf16[8,128,1024]{2,1,0:T(8,128)(2,1)}), bf16[8,128,1024]{2,1,0:T(8,128)(2,1)}, u32[]{:S(2)}, u32[]{:S(2)}) async-start(bf16[8,128,1024]{2,1,0:T(8,128)(2,1)} %bitcast.50), calls=%async_computation.1 | async-start | bytes 4194304 | tf_op jit(solution)/shard_map/all_to_all | solution.py:1144
  (232 other events, 1671.6 us)
Sparse Core Ops, SparseCore 0:
  35.2 81.7 all-gather.3
  119.8 42.3 all-gather.5
  409.4 60.0 all-gather.7
